TPU v7x, 256 devices: a whole 4x4x8 slice. The times are simulated.
256 devices in a mesh: lon: 64 (over y, x_lo, z), lat: 4 (over x_hi, core).
Axes of the slice: x: 4 (x_hi: 2, x_lo: 2; x = x_hi * 2 + x_lo), y: 4, z: 8, core: 2. Of those that a mesh axis runs over, the one named last changes fastest.
Arguments:
- height: float32 [4096, 1024], P('lon', 'lat')
- albedo: float32 [4096, 1024], P('lon', 'lat'), may hold values from 0.6 to 1.4
- images: bfloat16 [12, 4096, 1024], P(None, 'lon', 'lat'), may hold values from 0.049804688 to 0.59765625
- lit_mask: int32 [12, 4096, 1024], P(None, 'lon', 'lat'), may hold values from 0 to 1, as said below
- lit_count: int32 [12, 64, 4], P(None, 'lon', 'lat'), may hold values from 0 to 16384, as said below
- geometry: float32 [12, 4], replicated, may hold values from -1 to 1, as said below
- owner_column: int32 [4096, 1024], P('lon', 'lat'), may hold values from 0 to 1023, as said below
- altimetry: float32 [1024, 256], P('lon', 'lat'), may hold values from -30 to 30, as said below
Outputs:
- refined: float32 [4096, 1024], P('lon', 'lat')
Inputs may be any that keep to these rules, and one draw needn't show every extreme that they name: lit_mask is 0 or 1; the share of lit cells differs between sectors and images. lit_count[k, a, b] is the number of ones of lit_mask[k] in sector a (rows a * 64 to (a + 1) * 64 - 1) and band b (columns b * 256 to (b + 1) * 256 - 1). owner_column[i, j] = ((i + s_j) // 4) mod 1024, where s_j, from 0 to 3, depends on the column j only; every owner has exactly 4^2 cells. Rows of geometry hold a unit sun direction of low elevation and an emission cosine between 0.8 and 1. `altimetry`: elevations in metres.
All inputs are finite; a program needn't handle non-finite values.
Results may differ from a plain program's by a relative error of at most 0.0003.
Values sent between devices are 32-bit elements; how exact they have to be, the bound alone decides.
No kernel may reach another device: no remote copies, remote signals or barrier semaphores. Data moves between devices by JAX's collectives and lax.ppermute only.
A program may use at most 64 MiB of HBM per device.

v0:
```python
import jax
import jax.numpy as jnp
from jax import lax
from jax.sharding import PartitionSpec as P

IMAGES = 12
RAD = 16
OWN = 4
ITERS = 3


STEP_SIZE = 0.05
ALT_WEIGHT = 64.0
DATA_GAIN = 160.0
LUNAR_MIX = 0.6
SHARPNESS = 20.0


def padded(cells, sides, width):
    for axis, dim in sides:
        count = lax.axis_size(axis)
        head = lax.slice_in_dim(cells, 0, width, axis=dim)
        tail = lax.slice_in_dim(cells, cells.shape[dim] - width, cells.shape[dim], axis=dim)
        cells = jnp.concatenate(
            [
                lax.ppermute(tail, axis, [(i, (i + 1) % count) for i in range(count)]),
                cells,
                lax.ppermute(head, axis, [((i + 1) % count, i) for i in range(count)]),
            ],
            axis=dim,
        )
    return cells


def from_behind(value, axis, steps):
    count = lax.axis_size(axis)
    pairs = [(source, (source + steps) % count) for source in range(count)]
    return lax.ppermute(value, axis, pairs)


def band_entries(offsets, derivative):
    inside = (offsets >= 0) & (offsets <= 2 * RAD)
    if derivative:
        denom = float(RAD * (RAD + 1) * (2 * RAD + 1)) / 3.0
        entries = (offsets - RAD).astype(jnp.float32) / denom
    else:
        entries = jnp.full(offsets.shape, 1.0 / (2 * RAD + 1), jnp.float32)
    return jnp.where(inside, entries, 0.0)


def band_left(row_count, derivative):
    row_ids = jnp.arange(row_count, dtype=jnp.int32)[:, None]
    col_ids = jnp.arange(row_count + 2 * RAD, dtype=jnp.int32)[None, :]
    return band_entries(col_ids - row_ids, derivative)


def band_right(col_count, derivative):
    row_ids = jnp.arange(col_count + 2 * RAD, dtype=jnp.int32)[:, None]
    col_ids = jnp.arange(col_count, dtype=jnp.int32)[None, :]
    return band_entries(row_ids - col_ids, derivative)


def slopes(surface_ext, row_count, col_count):
    right_band = jnp.concatenate(
        [band_right(col_count, False), band_right(col_count, True)], axis=1
    )
    combined = jnp.dot(surface_ext, right_band, precision=lax.Precision.HIGHEST)
    slope_lon = jnp.dot(
        band_left(row_count, True), combined[:, :col_count], precision=lax.Precision.HIGHEST
    )
    slope_lat = jnp.dot(
        band_left(row_count, False), combined[:, col_count:], precision=lax.Precision.HIGHEST
    )
    return (slope_lon, slope_lat)


def adjoint(grad_lon_ext, grad_lat_ext, row_count, col_count):
    left_part = jnp.concatenate(
        [
            jnp.dot(band_left(row_count, True), grad_lon_ext, precision=lax.Precision.HIGHEST),
            jnp.dot(band_left(row_count, False), grad_lat_ext, precision=lax.Precision.HIGHEST),
        ],
        axis=1,
    )
    right_band = jnp.concatenate(
        [band_right(col_count, False), band_right(col_count, True)], axis=0
    )
    return -jnp.dot(left_part, right_band, precision=lax.Precision.HIGHEST)


def lat_keep(width, lat_cells):
    lat_index = lax.axis_index("lat")
    positions = jnp.arange(lat_cells + 2 * width, dtype=jnp.int32)
    global_row = lat_index * lat_cells - width + positions
    return (global_row >= 0) & (global_row < lat_cells * lax.axis_size("lat"))


def gradients(slope_lon, slope_lat, albedo, images, weights, geometry):
    norm = jnp.sqrt(1.0 + slope_lon * slope_lon + slope_lat * slope_lat)

    def accumulate(image_index, running):
        grad_lon, grad_lat = running
        sun_row = lax.dynamic_index_in_dim(geometry, image_index, 0, keepdims=False)
        observed = lax.dynamic_index_in_dim(images, image_index, 0, keepdims=False).astype(
            jnp.float32
        )
        weight = lax.dynamic_index_in_dim(weights, image_index, 0, keepdims=False)
        facing = sun_row[2] - sun_row[0] * slope_lon - sun_row[1] * slope_lat
        lit_part = jax.nn.softplus(SHARPNESS * facing) / SHARPNESS
        view_cos = sun_row[3]
        shading = LUNAR_MIX * lit_part / (lit_part + view_cos) + (1.0 - LUNAR_MIX) * lit_part / norm
        rendered = albedo * shading
        residual_scale = 2.0 * weight * (rendered - observed) * albedo
        lit_slope = (
            LUNAR_MIX * view_cos / ((lit_part + view_cos) * (lit_part + view_cos))
            + (1.0 - LUNAR_MIX) / norm
        ) * jax.nn.sigmoid(SHARPNESS * facing)
        norm_slope = (1.0 - LUNAR_MIX) * lit_part / (norm * norm * norm)
        grad_lon = grad_lon + residual_scale * (-sun_row[0] * lit_slope - norm_slope * slope_lon)
        grad_lat = grad_lat + residual_scale * (-sun_row[1] * lit_slope - norm_slope * slope_lat)
        return (grad_lon, grad_lat)

    zeros_field = jnp.zeros_like(slope_lon)
    return lax.fori_loop(0, IMAGES, accumulate, (zeros_field, zeros_field))


def per_device(height, albedo, images, lit_mask, lit_count, geometry, owner_column, altimetry):
    lon_cells, lat_cells = height.shape
    lon_devices = lax.axis_size("lon")
    totals = lax.psum(lit_count.reshape(IMAGES), ("lon", "lat")).astype(jnp.float32)
    cells_all = float(lon_cells * lat_cells * lon_devices * lax.axis_size("lat"))
    image_weight = DATA_GAIN * cells_all / totals
    weights = lit_mask.astype(jnp.float32) * image_weight[:, None, None]
    owner_cols = lon_cells // OWN
    owner_total = owner_cols * lon_devices
    local_bin = (owner_column - lax.axis_index("lon") * owner_cols) % owner_total
    slot_hits = jnp.arange(owner_cols + 1, dtype=jnp.int32)[:, None, None] == local_bin[None]
    surface = height
    for iteration in range(ITERS):
        extended = padded(surface, (("lon", 0), ("lat", 1)), RAD)
        extended = jnp.where(lat_keep(RAD, lat_cells)[None, :], extended, 0.0)
        slope_lon, slope_lat = slopes(extended, lon_cells, lat_cells)
        grad_lon, grad_lat = gradients(slope_lon, slope_lat, albedo, images, weights, geometry)
        slope_pair = padded(jnp.stack([grad_lon, grad_lat]), (("lon", 1), ("lat", 2)), RAD)
        slope_pair = jnp.where(lat_keep(RAD, lat_cells)[None, None, :], slope_pair, 0.0)
        data_grad = adjoint(slope_pair[0], slope_pair[1], lon_cells, lat_cells)
        partial_value = jnp.sum(jnp.where(slot_hits, surface[None], 0.0), axis=1)
        partial_value = partial_value.reshape(owner_cols + 1, lat_cells // OWN, OWN).sum(axis=2)
        incoming = from_behind(partial_value[owner_cols:], "lon", 1)
        owner_sums = partial_value[:owner_cols].at[0].add(incoming[0])
        misfit = 2.0 * ALT_WEIGHT * (owner_sums / (OWN * OWN) - altimetry) / (OWN * OWN)
        following = from_behind(misfit[:1], "lon", -1)
        misfit_all = jnp.repeat(jnp.concatenate([misfit, following], axis=0), OWN, axis=1)
        alt_grad = jnp.take_along_axis(misfit_all, local_bin, axis=0)
        surface = surface - STEP_SIZE * (data_grad + alt_grad)
    return surface


def solution(mesh):
    return jax.shard_map(
        per_device,
        mesh=mesh,
        in_specs=(
            P("lon", "lat"),
            P("lon", "lat"),
            P(None, "lon", "lat"),
            P(None, "lon", "lat"),
            P(None, "lon", "lat"),
            P(),
            P("lon", "lat"),
            P("lon", "lat"),
        ),
        out_specs=P("lon", "lat"),
        check_vma=False,
    )
```

profile of v0, /device:TPU:1, one launch (start us, length us, event | category | flops | bytes accessed | tf_op | source)
XLA Modules:
  0.0 704.1 jit_solution(16185784560711770659)
XLA Ops:
  3.3 7.3 %collective-permute-start.1 = (f32[16,256]{1,0:T(8,128)S(1)}, f32[16,256]{1,0:T(8,128)S(1)}, u32[]{:S(2)}, u32[]{:S(2)}) collective-permute-start(f32[16,256]{1,0:T(8,128)S(1)} %get-tuple-element.1023), channel_id=1, source_target_pairs={{4,0},{8,4},{12,8},{16,12},{20,16},{24,20},{28,24},{32,28},{36,32}... | collective-permute-start | bytes 49160 | tf_op jit(solution)/shard_map/ppermute | solution.py:28
  12.9 77.3 %psum.7 = s32[12]{0:T(128)S(1)} all-reduce(s32[12]{0:T(128)S(1)} %bitcast.167), channel_id=1, replica_groups=mesh['lon'=64,'lat'=4] {'lon','lat'}, use_global_device_ids=true, to_apply=%region_0.0 | all-reduce | flops 12 | bytes 96 | tf_op jit(solution)/shard_map/psum | solution.py:130
  97.3 71.8 %while.57 = (s32[]{:T(128)}, f32[64,256]{1,0:T(8,128)S(1)}, f32[64,256]{1,0:T(8,128)S(1)}, f32[12,64,256]{2,1,0:T(8,128)S(1)}, f32[12,4]{0,1:T(4,128)S(1)}, /*in...) while((s32[]{:T(128)}, f32[64,256]{1,0:T(8,128)S(1)}, ...), condition=%wide.region_2.3_spmd.clone, body=%wide.region_1.2_spmd.clone.sunk | while | flops 737286 | bytes 688407 | solution.py:124
  99.9 3.4 select_add_fusion.9
  105.9 3.4 select_add_fusion.9
  111.9 3.4 select_add_fusion.9
  123.8 3.4 select_add_fusion.9
  129.8 3.4 select_add_fusion.9
  135.8 3.4 select_add_fusion.9
  141.8 3.4 select_add_fusion.9
  147.8 3.4 select_add_fusion.9
  153.8 3.4 select_add_fusion.9
  159.7 3.4 select_add_fusion.9
  170.7 5.3 collective-permute-start.9
  182.4 105.2 %gather_fusion = f32[16384]{0:T(1024)S(1)} fusion(f32[17,256]{0,1:T(8,128)S(1)} %bitcast.135, s32[16384]{0:T(1024)S(1)} %bitcast.137), kind=kCustom, calls=%fused_computation.clone | custom fusion | bytes 262144 | tf_op jit(solution)/shard_map/jit(take_along_axis)/gather | solution.py:154
  291.7 5.0 collective-permute-done.10
  296.8 3.7 collective-permute-start.13
  306.9 72.7 %while.58 = (s32[]{:T(128)}, f32[64,256]{1,0:T(8,128)S(1)}, f32[64,256]{1,0:T(8,128)S(1)}, f32[12,64,256]{2,1,0:T(8,128)S(1)}, f32[12,4]{0,1:T(4,128)S(1)}, /*in...) while((s32[]{:T(128)}, f32[64,256]{1,0:T(8,128)S(1)}, ...), condition=%wide.region_6.8_spmd.clone, body=%wide.region_5.7_spmd.clone.sunk | while | flops 737286 | bytes 688407 | solution.py:124
  309.4 3.5 select_add_fusion.10
  315.5 3.5 select_add_fusion.10
  321.6 3.5 select_add_fusion.10
  327.6 3.5 select_add_fusion.10
  333.7 3.5 select_add_fusion.10
  339.7 3.5 select_add_fusion.10
  345.8 3.5 select_add_fusion.10
  351.9 3.5 select_add_fusion.10
  357.9 3.5 select_add_fusion.10
  364.0 3.5 select_add_fusion.10
  370.0 3.5 select_add_fusion.10
  376.1 3.5 select_add_fusion.10
  381.2 4.3 collective-permute-start.19
  390.8 105.2 %gather_fusion.1 = f32[16384]{0:T(1024)S(1)} fusion(f32[17,256]{0,1:T(8,128)S(1)} %bitcast.136, s32[16384]{0:T(1024)S(1)} %bitcast.138), kind=kCustom, calls=%fused_computation.1.clone | custom fusion | bytes 262144 | tf_op jit(solution)/shard_map/jit(take_along_axis)/gather | solution.py:154
  500.0 5.9 collective-permute-done.20
  514.3 70.7 %while.59 = (s32[]{:T(128)}, f32[64,256]{1,0:T(8,128)S(1)}, f32[64,256]{1,0:T(8,128)S(1)}, f32[12,64,256]{2,1,0:T(8,128)S(1)}, f32[12,4]{0,1:T(4,128)S(1)}, /*in...) while((s32[]{:T(128)}, f32[64,256]{1,0:T(8,128)S(1)}, ...), condition=%wide.region_10.12_spmd.clone, body=%wide.region_9.11_spmd.clone.sunk | while | flops 737286 | bytes 688407 | solution.py:124
  516.8 3.4 select_add_fusion.11
  522.7 3.4 select_add_fusion.11
  528.6 3.4 select_add_fusion.11
  534.4 3.4 select_add_fusion.11
  540.3 3.4 select_add_fusion.11
  546.2 3.4 select_add_fusion.11
  552.1 3.4 select_add_fusion.11
  558.0 3.4 select_add_fusion.11
  563.9 3.4 select_add_fusion.11
  569.8 3.4 select_add_fusion.11
  575.7 3.4 select_add_fusion.11
  581.6 3.4 select_add_fusion.11
  586.5 4.3 collective-permute-start.29
  597.0 105.2 %gather_fusion.2 = f32[16384]{0:T(1024)S(1)} fusion(f32[17,256]{0,1:T(8,128)S(1)} %bitcast.134, s32[16384]{0:T(1024)S(1)} %bitcast.139), kind=kCustom, calls=%fused_computation.2.clone | custom fusion | bytes 262144 | tf_op jit(solution)/shard_map/jit(take_along_axis)/gather | solution.py:154
  (224 shorter events, 89.6 us)
Async XLA Ops:
  0.0 12.9 %copy-start.5 = (s32[12,1,1]{0,2,1:T(1,128)S(1)}, s32[12,1,1]{0,2,1:T(1,128)}, u32[]{:S(2)}) copy-start(s32[12,1,1]{0,2,1:T(1,128)} %param.26) | copy-start | bytes 148
  0.0 90.2 %copy-start.2 = (s32[12,64,256]{2,1,0:T(8,128)S(1)}, s32[12,64,256]{2,1,0:T(8,128)}, u32[]{:S(2)}) copy-start(s32[12,64,256]{2,1,0:T(8,128)} %param.25) | copy-start | bytes 2359300
  0.8 90.2 %collective-permute-start = (f32[16,256]{1,0:T(8,128)S(1)}, f32[16,256]{1,0:T(8,128)S(1)}, u32[]{:S(2)}, u32[]{:S(2)}) collective-permute-start(f32[16,256]{1,0:T(8,128)S(1)} %get-tuple-element.1024), channel_id=1, source_target_pairs={{0,4},{4,8},{8,12},{12,16},{16,20},{20,24},{24,28},{28,32},{32,36}... | collective-permute-start | bytes 49160 | tf_op jit(solution)/shard_map/ppermute | solution.py:26
  3.3 87.8 %collective-permute-start.1 = (f32[16,256]{1,0:T(8,128)S(1)}, f32[16,256]{1,0:T(8,128)S(1)}, u32[]{:S(2)}, u32[]{:S(2)}) collective-permute-start(f32[16,256]{1,0:T(8,128)S(1)} %get-tuple-element.1023), channel_id=1, source_target_pairs={{4,0},{8,4},{12,8},{16,12},{20,16},{24,20},{28,24},{32,28},{36,32}... | collective-permute-start | bytes 49160 | tf_op jit(solution)/shard_map/ppermute | solution.py:28
  12.8 81.7 %collective-permute-start.8 = (f32[1,64]{0,1:T(8,128)S(1)}, f32[1,64]{0,1:T(8,128)S(1)}, u32[]{:S(2)}, u32[]{:S(2)}) collective-permute-start(f32[1,64]{0,1:T(8,128)S(1)} %slice.403), channel_id=1, source_target_pairs={{0,4},{4,8},{8,12},{12,16},{16,20},{20,24},{24,28},{28,32},{32,36}... | collective-permute-start | bytes 776 | tf_op jit(solution)/shard_map/ppermute | solution.py:38
  90.2 0.7 copy-start.4
  90.2 0.9 copy-start.1
  91.2 5.0 collective-permute-start.3
  92.2 4.1 collective-permute-start.2
  94.4 2.8 copy-start
  94.5 2.8 copy-start.3
  169.1 6.9 collective-permute-start.5
  170.3 7.0 collective-permute-start.4
  170.7 11.6 %collective-permute-start.9 = (f32[1,64]{0,1:T(8,128)S(1)}, f32[1,64]{0,1:T(8,128)S(1)}, u32[]{:S(2)}, u32[]{:S(2)}) collective-permute-start(f32[1,64]{0,1:T(8,128)S(1)} %bitcast.165), channel_id=1, source_target_pairs={{0,252},{4,0},{8,4},{12,8},{16,12},{20,16},{24,20},{28,24},{32,28}... | collective-permute-start | bytes 776 | tf_op jit(solution)/shard_map/ppermute | solution.py:38
  177.4 110.3 %collective-permute-start.7 = (f32[2,96,16]{2,1,0:T(8,128)S(1)}, f32[2,96,16]{2,1,0:T(8,128)S(1)}, u32[]{:S(2)}, u32[]{:S(2)}) collective-permute-start(f32[2,96,16]{2,1,0:T(8,128)S(1)} %get-tuple-element.1006), channel_id=1, source_target_pairs={{1,0},{2,1},{3,2},{0,3},{5,4},{6,5},{7,6},{4,7},{9,8},{10,9},{11,1... | collective-permute-start | bytes 36872 | tf_op jit(solution)/shard_map/ppermute | solution.py:28
  179.6 108.1 %collective-permute-start.6 = (f32[2,96,16]{2,1,0:T(8,128)S(1)}, f32[2,96,16]{2,1,0:T(8,128)S(1)}, u32[]{:S(2)}, u32[]{:S(2)}) collective-permute-start(f32[2,96,16]{2,1,0:T(8,128)S(1)} %get-tuple-element.1005), channel_id=1, source_target_pairs={{0,1},{1,2},{2,3},{3,0},{4,5},{5,6},{6,7},{7,4},{8,9},{9,10},{10,1... | collective-permute-start | bytes 36872 | tf_op jit(solution)/shard_map/ppermute | solution.py:26
  288.9 2.8 collective-permute-start.11
  289.8 6.9 collective-permute-start.10
  291.0 12.3 %collective-permute-start.18 = (f32[1,64]{0,1:T(8,128)S(1)}, f32[1,64]{0,1:T(8,128)S(1)}, u32[]{:S(2)}, u32[]{:S(2)}) collective-permute-start(f32[1,64]{0,1:T(8,128)S(1)} %slice.417), channel_id=1, source_target_pairs={{0,4},{4,8},{8,12},{12,16},{16,20},{20,24},{24,28},{28,32},{32,36}... | collective-permute-start | bytes 776 | tf_op jit(solution)/shard_map/ppermute | solution.py:38
  296.8 8.9 %collective-permute-start.13 = (f32[96,16]{1,0:T(8,128)S(1)}, f32[96,16]{1,0:T(8,128)S(1)}, u32[]{:S(2)}, u32[]{:S(2)}) collective-permute-start(f32[96,16]{1,0:T(8,128)S(1)} %get-tuple-element.1016), channel_id=1, source_target_pairs={{1,0},{2,1},{3,2},{0,3},{5,4},{6,5},{7,6},{4,7},{9,8},{10,9},{11,1... | collective-permute-start | bytes 18440 | tf_op jit(solution)/shard_map/ppermute | solution.py:28
  300.6 5.2 collective-permute-start.12
  379.6 5.9 collective-permute-start.15
  379.7 7.1 %collective-permute-start.14 = (f32[2,16,256]{2,1,0:T(8,128)S(1)}, f32[2,16,256]{2,1,0:T(8,128)S(1)}, u32[]{:S(2)}, u32[]{:S(2)}) collective-permute-start(f32[2,16,256]{2,1,0:T(8,128)S(1)} %get-tuple-element.1009), channel_id=1, source_target_pairs={{0,4},{4,8},{8,12},{12,16},{16,20},{20,24},{24,28},{28,32},{32,36}... | collective-permute-start | bytes 98312 | tf_op jit(solution)/shard_map/ppermute | solution.py:26
  381.2 9.6 %collective-permute-start.19 = (f32[1,64]{0,1:T(8,128)S(1)}, f32[1,64]{0,1:T(8,128)S(1)}, u32[]{:S(2)}, u32[]{:S(2)}) collective-permute-start(f32[1,64]{0,1:T(8,128)S(1)} %bitcast.166), channel_id=1, source_target_pairs={{0,252},{4,0},{8,4},{12,8},{16,12},{20,16},{24,20},{28,24},{32,28}... | collective-permute-start | bytes 776 | tf_op jit(solution)/shard_map/ppermute | solution.py:38
  386.9 109.2 %collective-permute-start.17 = (f32[2,96,16]{2,1,0:T(8,128)S(1)}, f32[2,96,16]{2,1,0:T(8,128)S(1)}, u32[]{:S(2)}, u32[]{:S(2)}) collective-permute-start(f32[2,96,16]{2,1,0:T(8,128)S(1)} %get-tuple-element.1004), channel_id=1, source_target_pairs={{1,0},{2,1},{3,2},{0,3},{5,4},{6,5},{7,6},{4,7},{9,8},{10,9},{11,1... | collective-permute-start | bytes 36872 | tf_op jit(solution)/shard_map/ppermute | solution.py:28
  388.5 107.6 %collective-permute-start.16 = (f32[2,96,16]{2,1,0:T(8,128)S(1)}, f32[2,96,16]{2,1,0:T(8,128)S(1)}, u32[]{:S(2)}, u32[]{:S(2)}) collective-permute-start(f32[2,96,16]{2,1,0:T(8,128)S(1)} %get-tuple-element.1003), channel_id=1, source_target_pairs={{0,1},{1,2},{2,3},{3,0},{4,5},{5,6},{6,7},{7,4},{8,9},{9,10},{10,1... | collective-permute-start | bytes 36872 | tf_op jit(solution)/shard_map/ppermute | solution.py:26
  497.3 2.7 collective-permute-start.21
  499.1 6.8 collective-permute-start.20
  499.5 12.0 %collective-permute-start.28 = (f32[1,64]{0,1:T(8,128)S(1)}, f32[1,64]{0,1:T(8,128)S(1)}, u32[]{:S(2)}, u32[]{:S(2)}) collective-permute-start(f32[1,64]{0,1:T(8,128)S(1)} %slice.431), channel_id=1, source_target_pairs={{0,4},{4,8},{8,12},{12,16},{16,20},{20,24},{24,28},{28,32},{32,36}... | collective-permute-start | bytes 776 | tf_op jit(solution)/shard_map/ppermute | solution.py:38
  506.0 7.2 %collective-permute-start.23 = (f32[96,16]{1,0:T(8,128)S(1)}, f32[96,16]{1,0:T(8,128)S(1)}, u32[]{:S(2)}, u32[]{:S(2)}) collective-permute-start(f32[96,16]{1,0:T(8,128)S(1)} %get-tuple-element.1014), channel_id=1, source_target_pairs={{1,0},{2,1},{3,2},{0,3},{5,4},{6,5},{7,6},{4,7},{9,8},{10,9},{11,1... | collective-permute-start | bytes 18440 | tf_op jit(solution)/shard_map/ppermute | solution.py:28
  509.3 3.9 collective-permute-start.22
  585.0 5.9 collective-permute-start.25
  585.1 7.1 %collective-permute-start.24 = (f32[2,16,256]{2,1,0:T(8,128)S(1)}, f32[2,16,256]{2,1,0:T(8,128)S(1)}, u32[]{:S(2)}, u32[]{:S(2)}) collective-permute-start(f32[2,16,256]{2,1,0:T(8,128)S(1)} %get-tuple-element.1007), channel_id=1, source_target_pairs={{0,4},{4,8},{8,12},{12,16},{16,20},{20,24},{24,28},{28,32},{32,36}... | collective-permute-start | bytes 98312 | tf_op jit(solution)/shard_map/ppermute | solution.py:26
  586.5 10.4 %collective-permute-start.29 = (f32[1,64]{0,1:T(8,128)S(1)}, f32[1,64]{0,1:T(8,128)S(1)}, u32[]{:S(2)}, u32[]{:S(2)}) collective-permute-start(f32[1,64]{0,1:T(8,128)S(1)} %bitcast.164), channel_id=1, source_target_pairs={{0,252},{4,0},{8,4},{12,8},{16,12},{20,16},{24,20},{28,24},{32,28}... | collective-permute-start | bytes 776 | tf_op jit(solution)/shard_map/ppermute | solution.py:38
  592.2 110.0 %collective-permute-start.27 = (f32[2,96,16]{2,1,0:T(8,128)S(1)}, f32[2,96,16]{2,1,0:T(8,128)S(1)}, u32[]{:S(2)}, u32[]{:S(2)}) collective-permute-start(f32[2,96,16]{2,1,0:T(8,128)S(1)} %get-tuple-element.1002), channel_id=1, source_target_pairs={{1,0},{2,1},{3,2},{0,3},{5,4},{6,5},{7,6},{4,7},{9,8},{10,9},{11,1... | collective-permute-start | bytes 36872 | tf_op jit(solution)/shard_map/ppermute | solution.py:28
  594.7 107.6 %collective-permute-start.26 = (f32[2,96,16]{2,1,0:T(8,128)S(1)}, f32[2,96,16]{2,1,0:T(8,128)S(1)}, u32[]{:S(2)}, u32[]{:S(2)}) collective-permute-start(f32[2,96,16]{2,1,0:T(8,128)S(1)} %get-tuple-element.1001), channel_id=1, source_target_pairs={{0,1},{1,2},{2,3},{3,0},{4,5},{5,6},{6,7},{7,4},{8,9},{9,10},{10,1... | collective-permute-start | bytes 36872 | tf_op jit(solution)/shard_map/ppermute | solution.py:26
where the time goes:
time: 709 us; the launch traced here: 704 us
  local copies, waits for them, and re-layouts  342 us (48%)
  other arithmetic  126 us (18%)
  blocking collectives  77.3 us (11%)
  loops' own time  69 us (10%)
  starting transfers between devices  60.8 us (9%)
  waiting for transfers between devices  21.1 us (3%)
    gather x6, local copies, waits for them, and re-layouts, per_device(): alt_grad = jnp.take_along_axis(misfit_all, local_bin, axis=0)  316 us
    add x36, other arithmetic, accumulate(): grad_lat + residual_scale * (-sun_row[1] * lit_slope - norm_slope * slope...  123 us
    psum x1, blocking collectives, per_device(): lax.psum(lit_count.reshape(IMAGES), ('lon', 'lat')).astype(jnp.float32)  77.3 us
    another operation x3, loops' own time, gradients(): return lax.fori_loop(0, IMAGES, accumulate, (zeros_field, zeros_field))  69 us
    ppermute x12, starting transfers between devices, padded(): lax.ppermute(head, axis, [((i + 1) % count, i) for i in range(count)])  25.7 us
    slice x36, local copies, waits for them, and re-layouts, accumulate(): view_cos = sun_row[3]  20.9 us
    ppermute x12, starting transfers between devices, padded(): lax.ppermute(tail, axis, [(i, (i + 1) % count) for i in range(count)])  20.9 us
    ppermute x12, waiting for transfers between devices, padded(): lax.ppermute(tail, axis, [(i, (i + 1) % count) for i in range(count)])  14.8 us
  transfers between devices with their start and end apart: 30, of which 10 were waited for; matrix products, arithmetic and copies ran while one was open for 46% of the time, Pallas kernels for 0%

commit v1 on v0

v1 whole, which is shorter than its diff:
```python
import functools

import jax
import jax.numpy as jnp
import numpy as np
from jax import lax
from jax.experimental import pallas as pl
from jax.experimental.pallas import tpu as pltpu
from jax.sharding import PartitionSpec as P

IMAGES = 12
RAD = 16
OWN = 4
ITERS = 3
STEP_SIZE = 0.05
ALT_WEIGHT = 64.0
DATA_GAIN = 160.0
LUNAR_MIX = 0.6
SHARPNESS = 20.0

LANES = 128
STRIP = 32
EXT = STRIP + 2 * RAD
TILES = 5
FIELDS = 2 * IMAGES + 3
ALBEDO = 2 * IMAGES
HEIGHT = ALBEDO + 1
AUX = HEIGHT + 1
BINS = 16
DENOM = float(RAD * (RAD + 1) * (2 * RAD + 1)) / 3.0
TAP_SCALE = 1.0 / (DENOM * (2 * RAD + 1))
F32 = jnp.float32
BF16 = jnp.bfloat16
VMEM = pl.BlockSpec(memory_space=pltpu.VMEM)
SMEM = pl.BlockSpec(memory_space=pltpu.SMEM)
PARAMS = pltpu.CompilerParams(vmem_limit_bytes=24 * 2**20)


def band(offset, derivative):
    inside = np.abs(offset) <= RAD
    return np.where(inside, offset if derivative else 1, 0).astype(np.float32)


def constants():
    own = np.arange(STRIP)
    ext = np.arange(EXT) - RAD
    reach = ext[None, :] - own[:, None]
    rows = [band(reach, True), band(reach, False)]
    bins = np.arange(BINS)
    for shift in range(OWN):
        group = (ext[None, :] + shift) // OWN
        rows.append((group == bins[:, None]).astype(np.float32))
    down = np.concatenate(rows, axis=0)
    forward = np.concatenate([down] * 3, axis=1)
    back = own[None, :] - ext[:, None]
    spread = np.zeros((EXT, OWN * BINS), np.float32)
    for shift in range(OWN):
        hit = ((own[:, None] + shift) // OWN) == bins[None, :]
        spread[RAD : RAD + STRIP, shift * BINS : (shift + 1) * BINS] = hit
    filters = np.concatenate([band(back, True), band(back, False)], axis=1)
    backward = np.concatenate([filters, filters, spread, spread], axis=1)
    lane = np.arange(LANES)
    side = np.where(lane < LANES // 2, lane + LANES, lane - LANES)
    source = np.concatenate([lane, side])
    across = source[:, None] - lane[None, :]
    quads = (lane[:, None] // OWN == lane[None, :] // OWN).astype(np.float32)
    return [
        jnp.asarray(m, BF16)
        for m in (forward, backward, band(across, False), band(across, True), quads)
    ]


def pieces(value, count):
    out = []
    for _ in range(count - 1):
        part = value.astype(BF16)
        value = value - part.astype(F32)
        out.append(part)
    out.append(value.astype(BF16))
    return out


def dot(left, right):
    return jnp.dot(left, right, preferred_element_type=F32)


def with_sides(tiles):
    low = lax.broadcasted_iota(jnp.int32, tiles[0].shape, 1) < LANES // 2
    zero = jnp.zeros_like(tiles[0])
    rows = []
    for j, tile in enumerate(tiles):
        after = tiles[j + 1] if j + 1 < len(tiles) else zero
        before = tiles[j - 1] if j > 0 else zero
        rows.append(jnp.concatenate([tile, jnp.where(low, after, before)], axis=1))
    return jnp.concatenate(rows, axis=0)


def filter_lat(tiles, taps, count):
    total = None
    for part in pieces(with_sides(tiles), count):
        term = dot(part, taps)
        total = term if total is None else total + term
    return total


def place():
    lat = lax.axis_index("lat")
    return lat // 2, lat % 2


def own_tile(half, core, t):
    return half + 2 * core + t


def pack_kernel(height, albedo, images, lit_mask, owner, altimetry, expand, kept, sent):
    half, core = place()
    lon = lax.axis_index("lon")
    bins = owner[0:OWN, :] - lon * BINS
    shift = jnp.sum(bins, axis=0, keepdims=True).astype(F32)
    heights = dot(jnp.concatenate(pieces(altimetry[...], 3), axis=1), expand[...])
    for ref, rows_of in ((kept, core), (sent, 1 - core)):
        start = pl.multiple_of(rows_of * STRIP, STRIP)
        aux_rows = jnp.where(rows_of == 0, heights[0:8], heights[8:16])
        for t in range(2):
            rows, cols = pl.ds(start, STRIP), pl.ds(t * LANES, LANES)
            for k in range(IMAGES):
                ref[k, t] = images[k, rows, cols].astype(F32)
                ref[IMAGES + k, t] = lit_mask[k, rows, cols].astype(F32)
            ref[ALBEDO, t] = albedo[rows, cols]
            ref[HEIGHT, t] = height[rows, cols]
            lanes = slice(t * LANES, (t + 1) * LANES)
            ref[AUX, t, 0:8] = aux_rows[:, lanes]
            ref[AUX, t, 8:16] = jnp.broadcast_to(shift[:, lanes], (8, LANES))
            ref[AUX, t, 16:32] = jnp.zeros((16, LANES), F32)


def route(core, up, down, inter, intra):
    inter[...] = jnp.where(core == 0, up, down)
    intra[...] = jnp.where(core == 0, down, up)


def begin_kernel(kept, received, halo, z, aux, inter, intra):
    half, core = place()
    zero = jnp.zeros((TILES, RAD, LANES), F32)
    z[:, 0:RAD] = zero
    z[:, RAD + STRIP : EXT] = zero
    for t in range(2):
        for ref, at in ((kept, own_tile(half, core, t)), (received, own_tile(half, 1 - core, t))):
            z[at, RAD : RAD + STRIP] = ref[HEIGHT, t]
            aux[at] = ref[AUX, t, 0:BINS]
    far = (TILES - 1) * (1 - half)
    z[far, RAD : RAD + STRIP] = halo[HEIGHT]
    aux[far] = halo[AUX, 0:BINS]
    alt = jnp.concatenate([aux[:, 0:8], jnp.zeros((TILES, 8, LANES), F32)], axis=1)
    up = jnp.concatenate([alt, z[:, RAD : 2 * RAD]], axis=1)
    route(core, up, z[:, STRIP:EXT], inter, intra)


def image_sums(coef, observed, lit, albedo, slope_lon, slope_lat):
    inverse = lax.rsqrt(1.0 + slope_lon * slope_lon + slope_lat * slope_lat)
    flat_part = (1.0 - LUNAR_MIX) * inverse
    flat_shade = flat_part * (albedo * (1.0 / SHARPNESS))
    mix_shade = albedo * LUNAR_MIX
    sum_lon = sum_lat = sum_norm = None
    for k in range(IMAGES):
        steep = coef[k, 2] - coef[k, 0] * slope_lon - coef[k, 1] * slope_lat
        decay = jnp.exp(-jnp.abs(steep))
        whole = 1.0 + decay
        part = jnp.maximum(steep, 0.0) + jnp.log(whole)
        ratio = 1.0 / (part + coef[k, 3])
        gate = jnp.where(steep >= 0.0, 1.0, decay) / whole
        rendered = part * (mix_shade * ratio + flat_shade)
        residual = lit(k) * (rendered - observed(k))
        pull = residual * ((coef[k, 4] * (ratio * ratio) + flat_part) * gate)
        add_lon, add_lat = coef[k, 5] * pull, coef[k, 6] * pull
        add_norm = (coef[k, 7] * residual) * part
        if k == 0:
            sum_lon, sum_lat, sum_norm = add_lon, add_lat, add_norm
        else:
            sum_lon, sum_lat, sum_norm = sum_lon + add_lon, sum_lat + add_lat, sum_norm + add_norm
    bend = (1.0 - LUNAR_MIX) / SHARPNESS * (inverse * inverse * inverse) * sum_norm
    return albedo * (sum_lon - slope_lon * bend), albedo * (sum_lat - slope_lat * bend)


def step_kernel(first, *refs):
    (coef, kept, received, halo, z, inter, intra, aux, alt_in, forward, backward) = refs[:11]
    smooth, slope, quads = refs[11:14]
    z_out, inter_out, intra_out = refs[14:17]
    refs = refs[17:]
    if first:
        alt_out, refs = refs[0], refs[1:]
    slope_lon, slope_lat, grad_lon, grad_lat = refs
    half, core = place()
    tiles = range(TILES)
    above = jnp.where(core == 0, inter[...], intra[...])
    below = jnp.where(core == 0, intra[...], inter[...])
    if first:
        alt = jnp.concatenate([aux[:, 0:8], below[:, 0:8]], axis=1)
        alt_out[...] = alt
        below = jnp.concatenate([jnp.zeros((TILES, RAD, LANES), F32), below[:, RAD:]], axis=1)
    else:
        alt = alt_in[...]
    surface = [z[j] + jnp.concatenate([above[j], below[j]], axis=0) for j in tiles]
    stacked = jnp.concatenate(
        [jnp.concatenate(pieces(surface[j], 3), axis=0) for j in tiles], axis=1
    )
    down = dot(forward[...], stacked)

    def part(row, count, j):
        return down[row : row + count, j * LANES : (j + 1) * LANES]

    slope_lon[...] = TAP_SCALE * filter_lat([part(0, STRIP, j) for j in tiles], smooth[...], 3)
    slope_lat[...] = TAP_SCALE * filter_lat([part(STRIP, STRIP, j) for j in tiles], slope[...], 3)

    shifts = [jnp.concatenate([aux[j, 8:16]] * 2, axis=0) for j in tiles]
    sums = []
    for j in tiles:
        chosen = part(2 * STRIP, BINS, j)
        for s in range(1, OWN):
            chosen = jnp.where(shifts[j] == float(s), part(2 * STRIP + s * BINS, BINS, j), chosen)
        sums.append(chosen)
    owner_sum = None
    for p in pieces(jnp.concatenate(sums, axis=0), 3):
        term = dot(p, quads[...])
        owner_sum = term if owner_sum is None else owner_sum + term

    gain = STEP_SIZE * 2.0 * ALT_WEIGHT / (OWN * OWN)
    misfits = []
    for j in tiles:
        pull = gain * alt[j] - (gain / (OWN * OWN)) * owner_sum[j * BINS : (j + 1) * BINS]
        misfits.append(
            jnp.concatenate([jnp.where(shifts[j] == float(s), pull, 0.0) for s in range(OWN)], axis=0)
        )

    def image_tile(ref, at, index):
        rows = pl.ds(pl.multiple_of(at * STRIP, STRIP), STRIP)
        g_lon, g_lat = image_sums(
            coef,
            lambda k: ref[(k, *index)],
            lambda k: ref[(IMAGES + k, *index)],
            ref[(ALBEDO, *index)],
            slope_lon[rows],
            slope_lat[rows],
        )
        grad_lon[rows] = g_lon
        grad_lat[rows] = g_lat

    for t in range(2):
        image_tile(kept, own_tile(half, core, t), (t,))
        image_tile(received, own_tile(half, 1 - core, t), (t,))
    image_tile(halo, (TILES - 1) * (1 - half), ())

    def field(ref):
        return [ref[j * STRIP : (j + 1) * STRIP] for j in tiles]

    scale = STEP_SIZE * TAP_SCALE
    from_lon = scale * filter_lat(field(grad_lon), smooth[...], 2)
    from_lat = scale * filter_lat(field(grad_lat), slope[...], 2)
    columns = []
    for j in tiles:
        rows = slice(j * STRIP, (j + 1) * STRIP)
        data = pieces(jnp.concatenate([from_lon[rows], from_lat[rows]], axis=0), 2)
        columns.append(jnp.concatenate(data + pieces(misfits[j], 2), axis=0))
    spread = dot(backward[...], jnp.concatenate(columns, axis=1))
    for j in tiles:
        change = spread[:, j * LANES : (j + 1) * LANES]
        z_out[j, 0:RAD] = change[0:RAD]
        z_out[j, RAD : RAD + STRIP] = change[RAD : RAD + STRIP] + surface[j][RAD : RAD + STRIP]
        z_out[j, RAD + STRIP : EXT] = change[RAD + STRIP : EXT]
    route(core, z_out[:, 0:STRIP], z_out[:, STRIP:EXT], inter_out, intra_out)


def end_kernel(z, inter, intra, kept, sent):
    half, core = place()
    for ref, side in ((kept, core), (sent, 1 - core)):
        for t in range(2):
            at = own_tile(half, side, t)
            above = jnp.where(core == 0, inter[at], intra[at])
            below = jnp.where(core == 0, intra[at], inter[at])
            cols = slice(t * LANES, (t + 1) * LANES)
            ref[0:RAD, cols] = z[at, RAD : 2 * RAD] + above[RAD:]
            ref[RAD:STRIP, cols] = z[at, 2 * RAD : RAD + STRIP] + below[0:RAD]


def f32(*shape):
    return jax.ShapeDtypeStruct(shape, F32)


def per_device(height, albedo, images, lit_mask, lit_count, geometry, owner_column, altimetry):
    lon_count, lat_count = lax.axis_size("lon"), lax.axis_size("lat")
    axes = ("lon", "lat")
    devices = lon_count * lat_count
    sites = [(a, b) for a in range(lon_count) for b in range(lat_count)]

    def index(a, b):
        return (a % lon_count) * lat_count + b

    across_cores = [(index(a, b), index(a, b ^ 1)) for a, b in sites]
    across_halves = [(index(a, b), index(a, b ^ 2)) for a, b in sites]
    across_strips = [(index(a, b), index(a + 2 * (b % 2) - 1, b ^ 1)) for a, b in sites]

    def exchange(inter, intra):
        return lax.ppermute(inter, axes, across_strips), lax.ppermute(intra, axes, across_cores)

    counts = jnp.broadcast_to(
        jnp.pad(lit_count.reshape(1, 1, IMAGES).astype(F32), ((0, 0), (0, 0), (0, LANES - IMAGES))),
        (devices, 1, LANES),
    )
    totals = jnp.sum(lax.all_to_all(counts, axes, 0, 0), axis=(0, 1))[:IMAGES]
    cells_all = float(height.size * devices)
    weight = 2.0 * DATA_GAIN * cells_all / totals
    sun_lon, sun_lat, sun_up, view = (geometry[:, i] for i in range(4))
    coef = jnp.stack(
        [
            SHARPNESS * sun_lon,
            SHARPNESS * sun_lat,
            SHARPNESS * sun_up,
            SHARPNESS * view,
            (LUNAR_MIX * SHARPNESS * SHARPNESS) * view,
            -weight * sun_lon,
            -weight * sun_lat,
            weight,
        ],
        axis=1,
    )

    expand = np.arange(altimetry.shape[1])[:, None] == np.arange(2 * LANES)[None, :] // OWN
    expand = jnp.asarray(np.concatenate([expand] * 3, axis=0), BF16)
    kept, sent = pl.pallas_call(
        pack_kernel,
        out_shape=(f32(FIELDS, 2, STRIP, LANES),) * 2,
        in_specs=[VMEM] * 7,
        out_specs=(VMEM,) * 2,
        compiler_params=PARAMS,
    )(height, albedo, images, lit_mask, owner_column[:8], altimetry, expand)
    received = lax.ppermute(sent, axes, across_cores)
    half, core = place()
    near = lax.dynamic_index_in_dim(
        jnp.where(half == core, received, kept), 1 - half, axis=1, keepdims=False
    )
    halo = lax.ppermute(near, axes, across_halves)
    z, aux, inter, intra = pl.pallas_call(
        begin_kernel,
        out_shape=(
            f32(TILES, EXT, LANES),
            f32(TILES, BINS, LANES),
            f32(TILES, STRIP, LANES),
            f32(TILES, STRIP, LANES),
        ),
        in_specs=[VMEM] * 3,
        out_specs=(VMEM,) * 4,
        compiler_params=PARAMS,
    )(kept, received, halo)
    inter, intra = exchange(inter, intra)
    tables = constants()
    alt = aux
    for iteration in range(ITERS):
        first = iteration == 0
        shapes = [f32(TILES, EXT, LANES), f32(TILES, STRIP, LANES), f32(TILES, STRIP, LANES)]
        if first:
            shapes.append(f32(TILES, BINS, LANES))
        out = pl.pallas_call(
            functools.partial(step_kernel, first),
            out_shape=tuple(shapes),
            in_specs=[SMEM] + [VMEM] * 13,
            out_specs=(VMEM,) * len(shapes),
            scratch_shapes=[pltpu.VMEM((TILES * STRIP, LANES), F32)] * 4,
            compiler_params=PARAMS,
        )(coef, kept, received, halo, z, inter, intra, aux, alt, *tables)
        z, inter, intra = out[:3]
        if first:
            alt = out[3]
        inter, intra = exchange(inter, intra)
    mine, other = pl.pallas_call(
        end_kernel,
        out_shape=(f32(STRIP, 2 * LANES),) * 2,
        in_specs=[VMEM] * 3,
        out_specs=(VMEM,) * 2,
        compiler_params=PARAMS,
    )(z, inter, intra)
    other = lax.ppermute(other, axes, across_cores)
    upper = jnp.where(core == 0, mine, other)
    lower = jnp.where(core == 0, other, mine)
    return jnp.concatenate([upper, lower], axis=0)


def solution(mesh):
    return jax.shard_map(
        per_device,
        mesh=mesh,
        in_specs=(
            P("lon", "lat"),
            P("lon", "lat"),
            P(None, "lon", "lat"),
            P(None, "lon", "lat"),
            P(None, "lon", "lat"),
            P(),
            P("lon", "lat"),
            P("lon", "lat"),
        ),
        out_specs=P("lon", "lat"),
        check_vma=False,
    )
```

time: 709 us -> 82.5 us (0.12)
  local copies, waits for them, and re-layouts: 342 us -> 7.7 us
  other arithmetic: 126 us -> 0.79 us
  blocking collectives: 77.3 us -> 0 us
  loops' own time: 69 us -> 0 us
  starting transfers between devices: 60.8 us -> 50.6 us
  Pallas kernels: 0 us -> 8.77 us
  waiting for transfers between devices: 21.1 us -> 14 us
    gather x6 -> x0, local copies, waits for them, and re-layouts: 316 us -> none  [per_device(): alt_grad = jnp.take_along_axis(misfit_all, local_bin, axis=0)]
    add x39 -> x0, other arithmetic: 123 us -> none  [the longest x36 123 us: accumulate(): grad_lat + residual_scale * (-sun_row[1] * lit_slope - norm_slope * slope...]
    psum x1 -> x0, blocking collectives: 77.3 us -> none  [per_device(): lax.psum(lit_count.reshape(IMAGES), ('lon', 'lat')).astype(jnp.float32)]
    another operation x3 -> x0, loops' own time: 69 us -> none  [gradients(): return lax.fori_loop(0, IMAGES, accumulate, (zeros_field, zeros_field))]
    ppermute x30 -> x11, starting transfers between devices: 60.8 us -> 37.6 us  [the longest x4 26 us: exchange(): lax.ppermute(intra, axes, across_cores)]
    slice x48 -> x2, local copies, waits for them, and re-layouts: 22.4 us -> 0.72 us  [the longest x1 0.71 us: per_device(): owner_column[:8]]
    ppermute x30 -> x11, waiting for transfers between devices: 21.1 us -> 5.24 us  [the longest x4 3.29 us: exchange(): lax.ppermute(intra, axes, across_cores)]
    all_to_all x0 -> x1, starting transfers between devices: none -> 13 us  [per_device(): totals = jnp.sum(lax.all_to_all(counts, axes, 0, 0), axis=(0, 1))[:IMAGES]]
  transfers between devices with their start and end apart: 30 -> 12, of which waited for: 10 -> 7; matrix products, arithmetic and copies ran while one was open for 46% -> 2% of each run, Pallas kernels for 0% -> 0%
where the time goes in v1:
time: 82.5 us; the launch traced here: 82 us
  starting transfers between devices  50.6 us (61%)
  waiting for transfers between devices  14 us (17%)
  Pallas kernels  8.77 us (11%)
  local copies, waits for them, and re-layouts  7.7 us (9%)
    ppermute x4, starting transfers between devices, exchange(): lax.ppermute(intra, axes, across_cores)  26 us
    all_to_all x1, starting transfers between devices, per_device(): totals = jnp.sum(lax.all_to_all(counts, axes, 0, 0), axis=(0, 1))[:IMAGES]  13 us
    all_to_all x1, waiting for transfers between devices, per_device(): totals = jnp.sum(lax.all_to_all(counts, axes, 0, 0), axis=(0, 1))[:IMAGES]  8.72 us
    pallas_call x3, Pallas kernels, per_device(): pl.pallas_call(functools.partial(step_kernel, first), out_shape=tuple(sha...  8.54 us
    unnamed x30, local copies, waits for them, and re-layouts  5.89 us
    ppermute x4, starting transfers between devices, exchange(): lax.ppermute(inter, axes, across_strips)  3.93 us
    ppermute x1, starting transfers between devices, per_device(): received = lax.ppermute(sent, axes, across_cores)  3.31 us
    ppermute x4, waiting for transfers between devices, exchange(): lax.ppermute(intra, axes, across_cores)  3.29 us
  transfers between devices with their start and end apart: 12, of which 7 were waited for; matrix products, arithmetic and copies ran while one was open for 2% of the time, Pallas kernels for 0%

profile of v1, /device:TPU:1, one launch (start us, length us, event | category | flops | bytes accessed | tf_op | source)
XLA Modules:
  0.0 82.0 jit_solution(2078498410471913474)
XLA Ops:
  0.0 0.7 slice.23.owner
  0.7 1.1 %copy-done = s32[12,64,256]{2,1,0:T(8,128)S(1)} copy-done((s32[12,64,256]{2,1,0:T(8,128)S(1)}, s32[12,64,256]{2,1,0:T(8,128)}, u32[]{:S(2)}) %copy-start) | copy-done | bytes 786456
  1.9 1.0 %copy-done.4 = bf16[12,64,256]{2,1,0:T(8,128)(2,1)S(1)} copy-done((bf16[12,64,256]{2,1,0:T(8,128)(2,1)S(1)}, bf16[12,64,256]{2,1,0:T(8,128)(2,1)}, u32[]{:S(2)}) %copy-start.4) | copy-done | bytes 393240
  2.8 0.9 %copy-done.7 = bf16[192,256]{1,0:T(8,128)(2,1)S(1)} copy-done((bf16[192,256]{1,0:T(8,128)(2,1)S(1)}, bf16[192,256]{1,0:T(8,128)(2,1)}, u32[]{:S(2)}) %copy-start.7) | copy-done | bytes 98328
  3.7 0.8 %copy-done.8 = f32[64,256]{1,0:T(8,128)S(1)} copy-done((f32[64,256]{1,0:T(8,128)S(1)}, f32[64,256]{1,0:T(8,128)}, u32[]{:S(2)}) %copy-start.8) | copy-done | bytes 65560
  4.6 0.8 %copy-done.9 = f32[64,256]{1,0:T(8,128)S(1)} copy-done((f32[64,256]{1,0:T(8,128)S(1)}, f32[64,256]{1,0:T(8,128)}, u32[]{:S(2)}) %copy-start.9) | copy-done | bytes 65560
  5.4 0.2 shard_map.136
  5.6 3.3 %collective-permute-start = (f32[27,2,32,128]{3,2,1,0:T(8,128)S(1)}, f32[27,2,32,128]{3,2,1,0:T(8,128)S(1)}, u32[]{:S(2)}, u32[]{:S(2)}) collective-permute-start(f32[27,2,32,128]{3,2,1,0:T(8,128)S(1)} %get-tuple-element.24), channel_id=1, source_target_pairs={{0,1},{1,0},{2,3},{3,2},{4,5},{5,4},{6,7},{7,6},{8,9},{9,8},{10,11... | collective-permute-start | bytes 2654216 | tf_op jit(solution)/shard_map/ppermute | solution.py:336
  8.9 0.7 broadcast_in_dim.8
  9.7 13.0 %all-to-all-start = ((f32[256,1,128]{2,1,0:T(1,128)}), f32[256,1,128]{2,1,0:T(1,128)S(1)}, u32[]{:S(2)}, u32[]{:S(2)}) async-start(f32[256,1,128]{2,1,0:T(1,128)} %broadcast_in_dim.8), calls=%async_computation | async-start | bytes 262144 | tf_op jit(solution)/shard_map/all_to_all | solution.py:309
  22.7 0.0 copy-start.11
  22.7 0.7 copy-done.11
  23.4 0.1 copy.47
  23.5 0.1 copy.46
  23.6 0.1 copy.45
  23.7 0.1 copy.44
  23.8 0.0 collective-permute-done.received.refs_2_
  23.8 0.1 fusion
  23.8 3.0 %collective-permute-start.1 = (f32[27,32,128]{2,1,0:T(8,128)S(1)}, f32[27,32,128]{2,1,0:T(8,128)S(1)}, u32[]{:S(2)}, u32[]{:S(2)}) collective-permute-start(f32[27,32,128]{2,1,0:T(8,128)S(1)} %fusion), channel_id=1, source_target_pairs={{0,2},{1,3},{2,0},{3,1},{4,6},{5,7},{6,4},{7,5},{8,10},{9,11},{10,... | collective-permute-start | bytes 1327112 | tf_op jit(solution)/shard_map/ppermute | solution.py:341
  26.8 8.7 %all-to-all-done = f32[256,1,128]{2,1,0:T(1,128)S(1)} async-done(((f32[256,1,128]{2,1,0:T(1,128)}), f32[256,1,128]{2,1,0:T(1,128)S(1)}, u32[]{:S(2)}, u32[]{:S(2)}) %all-to-all-start) | async-done | bytes 131104 | tf_op jit(solution)/shard_map/all_to_all | solution.py:309
  35.6 1.1 %collective-permute-done.1.halo.refs_3_ = f32[27,32,128]{2,1,0:T(8,128)S(1)} collective-permute-done((f32[27,32,128]{2,1,0:T(8,128)S(1)}, f32[27,32,128]{2,1,0:T(8,128)S(1)}, u32[]{:S(2)}, u32[]{:S(2)}) %collective-permute-start.1) | collective-permute-done | bytes 442400 | tf_op jit(solution)/shard_map/ppermute | solution.py:341
  36.7 0.0 copy-start.1
  36.7 3.7 %collective-permute-start.2 = (f32[5,32,128]{2,1,0:T(8,128)S(1)}, f32[5,32,128]{2,1,0:T(8,128)S(1)}, u32[]{:S(2)}, u32[]{:S(2)}) collective-permute-start(f32[5,32,128]{2,1,0:T(8,128)S(1)} %get-tuple-element.26), channel_id=1, source_target_pairs={{0,253},{1,4},{2,255},{3,6},{4,1},{5,8},{6,3},{7,10},{8,5},{9,12},... | collective-permute-start | bytes 245768 | tf_op jit(solution)/shard_map/ppermute | solution.py:303
  40.4 4.6 %collective-permute-start.3 = (f32[5,32,128]{2,1,0:T(8,128)S(1)}, f32[5,32,128]{2,1,0:T(8,128)S(1)}, u32[]{:S(2)}, u32[]{:S(2)}) collective-permute-start(f32[5,32,128]{2,1,0:T(8,128)S(1)} %get-tuple-element.27), channel_id=1, source_target_pairs={{0,1},{1,0},{2,3},{3,2},{4,5},{5,4},{6,7},{7,6},{8,9},{9,8},{10,11... | collective-permute-start | bytes 245768 | tf_op jit(solution)/shard_map/ppermute | solution.py:303
  45.0 0.1 copy.41
  45.1 0.1 copy.42
  45.2 0.1 copy.43
  45.3 0.1 stack.20.refs_0_
  45.4 0.0 collective-permute-done.2.refs_5_
  45.4 0.5 collective-permute-done.3.refs_6_
  46.0 0.1 copy-done.5
  46.1 2.8 %shard_map.138 = (f32[5,64,128]{2,1,0:T(8,128)S(1)}, f32[5,32,128]{2,1,0:T(8,128)S(1)}, f32[5,32,128]{2,1,0:T(8,128)S(1)}, f32[5,16,128]{2,1,0:T(8,128)S(1)}) custom-call(f32[12,8]{1,0:T(8,128)S(1)} %stack.20.refs_0_, f32[27,2,32,128]{3,2,1,0:T(8,128)S(1)} %get-tuple-element.23.kept.refs_1_, f32[27,2,32,128]{3,2,1,0:T(8,128)S(1)} %collective-permute-done.received.refs_2_, ...), custom_call_target="tpu_custom_call" | custom-call | tf_op jit(solution)/shard_map/pallas_call | solution.py:362
  48.9 0.1 collective-permute-start.4
  49.0 7.1 %collective-permute-start.5 = (f32[5,32,128]{2,1,0:T(8,128)S(1)}, f32[5,32,128]{2,1,0:T(8,128)S(1)}, u32[]{:S(2)}, u32[]{:S(2)}) collective-permute-start(f32[5,32,128]{2,1,0:T(8,128)S(1)} %get-tuple-element.31), channel_id=1, source_target_pairs={{0,1},{1,0},{2,3},{3,2},{4,5},{5,4},{6,7},{7,6},{8,9},{9,8},{10,11... | collective-permute-start | bytes 245768 | tf_op jit(solution)/shard_map/ppermute | solution.py:303
  56.1 0.0 collective-permute-done.4.refs_5_
  56.1 0.9 %collective-permute-done.5.refs_6_ = f32[5,32,128]{2,1,0:T(8,128)S(1)} collective-permute-done((f32[5,32,128]{2,1,0:T(8,128)S(1)}, f32[5,32,128]{2,1,0:T(8,128)S(1)}, u32[]{:S(2)}, u32[]{:S(2)}) %collective-permute-start.5) | collective-permute-done | bytes 81952 | tf_op jit(solution)/shard_map/ppermute | solution.py:303
  57.0 2.8 %shard_map.139 = (f32[5,64,128]{2,1,0:T(8,128)S(1)}, f32[5,32,128]{2,1,0:T(8,128)S(1)}, f32[5,32,128]{2,1,0:T(8,128)S(1)}) custom-call(f32[12,8]{1,0:T(8,128)S(1)} %stack.20.refs_0_, f32[27,2,32,128]{3,2,1,0:T(8,128)S(1)} %get-tuple-element.23.kept.refs_1_, f32[27,2,32,128]{3,2,1,0:T(8,128)S(1)} %collective-permute-done.received.refs_2_, ...), custom_call_target="tpu_custom_call" | custom-call | tf_op jit(solution)/shard_map/pallas_call | solution.py:362
  59.9 0.1 collective-permute-start.6
  60.0 7.2 %collective-permute-start.7 = (f32[5,32,128]{2,1,0:T(8,128)S(1)}, f32[5,32,128]{2,1,0:T(8,128)S(1)}, u32[]{:S(2)}, u32[]{:S(2)}) collective-permute-start(f32[5,32,128]{2,1,0:T(8,128)S(1)} %get-tuple-element.35), channel_id=1, source_target_pairs={{0,1},{1,0},{2,3},{3,2},{4,5},{5,4},{6,7},{7,6},{8,9},{9,8},{10,11... | collective-permute-start | bytes 245768 | tf_op jit(solution)/shard_map/ppermute | solution.py:303
  67.2 0.9 %collective-permute-done.7.refs_6_ = f32[5,32,128]{2,1,0:T(8,128)S(1)} collective-permute-done((f32[5,32,128]{2,1,0:T(8,128)S(1)}, f32[5,32,128]{2,1,0:T(8,128)S(1)}, u32[]{:S(2)}, u32[]{:S(2)}) %collective-permute-start.7) | collective-permute-done | bytes 81952 | tf_op jit(solution)/shard_map/ppermute | solution.py:303
  68.1 2.8 %shard_map.140 = (f32[5,64,128]{2,1,0:T(8,128)S(1)}, f32[5,32,128]{2,1,0:T(8,128)S(1)}, f32[5,32,128]{2,1,0:T(8,128)S(1)}) custom-call(f32[12,8]{1,0:T(8,128)S(1)} %stack.20.refs_0_, f32[27,2,32,128]{3,2,1,0:T(8,128)S(1)} %get-tuple-element.23.kept.refs_1_, f32[27,2,32,128]{3,2,1,0:T(8,128)S(1)} %collective-permute-done.received.refs_2_, ...), custom_call_target="tpu_custom_call" | custom-call | tf_op jit(solution)/shard_map/pallas_call | solution.py:362
  70.9 0.1 collective-permute-start.8
  71.0 7.2 %collective-permute-start.9 = (f32[5,32,128]{2,1,0:T(8,128)S(1)}, f32[5,32,128]{2,1,0:T(8,128)S(1)}, u32[]{:S(2)}, u32[]{:S(2)}) collective-permute-start(f32[5,32,128]{2,1,0:T(8,128)S(1)} %get-tuple-element.38), channel_id=1, source_target_pairs={{0,1},{1,0},{2,3},{3,2},{4,5},{5,4},{6,7},{7,6},{8,9},{9,8},{10,11... | collective-permute-start | bytes 245768 | tf_op jit(solution)/shard_map/ppermute | solution.py:303
  78.2 0.0 collective-permute-done.8.inter
  78.2 0.9 %collective-permute-done.9.intra = f32[5,32,128]{2,1,0:T(8,128)S(1)} collective-permute-done((f32[5,32,128]{2,1,0:T(8,128)S(1)}, f32[5,32,128]{2,1,0:T(8,128)S(1)}, u32[]{:S(2)}, u32[]{:S(2)}) %collective-permute-start.9) | collective-permute-done | bytes 81952 | tf_op jit(solution)/shard_map/ppermute | solution.py:303
  79.1 1.4 %collective-permute-start.10 = (f32[32,256]{1,0:T(8,128)S(1)}, f32[32,256]{1,0:T(8,128)S(1)}, u32[]{:S(2)}, u32[]{:S(2)}) collective-permute-start(f32[32,256]{1,0:T(8,128)S(1)} %get-tuple-element.40), channel_id=1, source_target_pairs={{0,1},{1,0},{2,3},{3,2},{4,5},{5,4},{6,7},{7,6},{8,9},{9,8},{10,11... | collective-permute-start | bytes 98312 | tf_op jit(solution)/shard_map/ppermute | solution.py:381
  80.5 0.9 %collective-permute-done.10 = f32[32,256]{1,0:T(8,128)S(1)} collective-permute-done((f32[32,256]{1,0:T(8,128)S(1)}, f32[32,256]{1,0:T(8,128)S(1)}, u32[]{:S(2)}, u32[]{:S(2)}) %collective-permute-start.10) | collective-permute-done | bytes 32800 | tf_op jit(solution)/shard_map/ppermute | solution.py:381
  81.4 0.6 pad_maximum_fusion
  (30 shorter events, 0.2 us)
Async XLA Ops:
  0.0 0.7 copy-start.10
  0.7 1.1 %copy-start = (s32[12,64,256]{2,1,0:T(8,128)S(1)}, s32[12,64,256]{2,1,0:T(8,128)}, u32[]{:S(2)}) copy-start(s32[12,64,256]{2,1,0:T(8,128)} %lit_mask.1) | copy-start | bytes 2359300
  1.9 1.0 %copy-start.4 = (bf16[12,64,256]{2,1,0:T(8,128)(2,1)S(1)}, bf16[12,64,256]{2,1,0:T(8,128)(2,1)}, u32[]{:S(2)}) copy-start(bf16[12,64,256]{2,1,0:T(8,128)(2,1)} %images.1) | copy-start | bytes 1179652
  2.8 0.9 %copy-start.7 = (bf16[192,256]{1,0:T(8,128)(2,1)S(1)}, bf16[192,256]{1,0:T(8,128)(2,1)}, u32[]{:S(2)}) copy-start(bf16[192,256]{1,0:T(8,128)(2,1)} %constant.57.clone.expand) | copy-start | bytes 294916
  3.7 0.8 %copy-start.8 = (f32[64,256]{1,0:T(8,128)S(1)}, f32[64,256]{1,0:T(8,128)}, u32[]{:S(2)}) copy-start(f32[64,256]{1,0:T(8,128)} %height.1) | copy-start | bytes 196612
  4.6 0.8 %copy-start.9 = (f32[64,256]{1,0:T(8,128)S(1)}, f32[64,256]{1,0:T(8,128)}, u32[]{:S(2)}) copy-start(f32[64,256]{1,0:T(8,128)} %albedo.1) | copy-start | bytes 196612
  5.6 3.3 %copy-start.12 = (s32[12,1,1]{0,2,1:T(1,128)S(1)}, s32[12,1,1]{0,2,1:T(1,128)}, u32[]{:S(2)}) copy-start(s32[12,1,1]{0,2,1:T(1,128)} %param.18) | copy-start | bytes 148
  5.6 18.2 %collective-permute-start = (f32[27,2,32,128]{3,2,1,0:T(8,128)S(1)}, f32[27,2,32,128]{3,2,1,0:T(8,128)S(1)}, u32[]{:S(2)}, u32[]{:S(2)}) collective-permute-start(f32[27,2,32,128]{3,2,1,0:T(8,128)S(1)} %get-tuple-element.24), channel_id=1, source_target_pairs={{0,1},{1,0},{2,3},{3,2},{4,5},{5,4},{6,7},{7,6},{8,9},{9,8},{10,11... | collective-permute-start | bytes 2654216 | tf_op jit(solution)/shard_map/ppermute | solution.py:336
  9.7 25.9 %all-to-all-start = ((f32[256,1,128]{2,1,0:T(1,128)}), f32[256,1,128]{2,1,0:T(1,128)S(1)}, u32[]{:S(2)}, u32[]{:S(2)}) async-start(f32[256,1,128]{2,1,0:T(1,128)} %broadcast_in_dim.8), calls=%async_computation | async-start | bytes 262144 | tf_op jit(solution)/shard_map/all_to_all | solution.py:309
  22.7 0.7 copy-start.11
  23.8 12.8 %collective-permute-start.1 = (f32[27,32,128]{2,1,0:T(8,128)S(1)}, f32[27,32,128]{2,1,0:T(8,128)S(1)}, u32[]{:S(2)}, u32[]{:S(2)}) collective-permute-start(f32[27,32,128]{2,1,0:T(8,128)S(1)} %fusion), channel_id=1, source_target_pairs={{0,2},{1,3},{2,0},{3,1},{4,6},{5,7},{6,4},{7,5},{8,10},{9,11},{10,... | collective-permute-start | bytes 1327112 | tf_op jit(solution)/shard_map/ppermute | solution.py:341
  36.7 9.3 %copy-start.2 = (bf16[256,128]{1,0:T(8,128)(2,1)S(1)}, bf16[256,128]{1,0:T(8,128)(2,1)}, u32[]{:S(2)}) copy-start(bf16[256,128]{1,0:T(8,128)(2,1)} %constant.60.clone.refs_11_) | copy-start | bytes 196612
  36.7 9.3 %copy-start.3 = (bf16[128,192]{1,0:T(8,128)(2,1)S(1)}, bf16[128,192]{1,0:T(8,128)(2,1)}, u32[]{:S(2)}) copy-start(bf16[128,192]{1,0:T(8,128)(2,1)} %constant.58.clone.refs_9_) | copy-start | bytes 147460
  36.7 9.3 %copy-start.6 = (bf16[64,256]{1,0:T(8,128)(2,1)S(1)}, bf16[64,256]{1,0:T(8,128)(2,1)}, u32[]{:S(2)}) copy-start(bf16[64,256]{1,0:T(8,128)(2,1)} %constant.59.clone.refs_10_) | copy-start | bytes 98308
  36.7 9.2 %copy-start.1 = (bf16[256,128]{1,0:T(8,128)(2,1)S(1)}, bf16[256,128]{1,0:T(8,128)(2,1)}, u32[]{:S(2)}) copy-start(bf16[256,128]{1,0:T(8,128)(2,1)} %constant.61.clone.refs_12_) | copy-start | bytes 196612
  36.7 8.7 %collective-permute-start.2 = (f32[5,32,128]{2,1,0:T(8,128)S(1)}, f32[5,32,128]{2,1,0:T(8,128)S(1)}, u32[]{:S(2)}, u32[]{:S(2)}) collective-permute-start(f32[5,32,128]{2,1,0:T(8,128)S(1)} %get-tuple-element.26), channel_id=1, source_target_pairs={{0,253},{1,4},{2,255},{3,6},{4,1},{5,8},{6,3},{7,10},{8,5},{9,12},... | collective-permute-start | bytes 245768 | tf_op jit(solution)/shard_map/ppermute | solution.py:303
  40.4 5.6 %collective-permute-start.3 = (f32[5,32,128]{2,1,0:T(8,128)S(1)}, f32[5,32,128]{2,1,0:T(8,128)S(1)}, u32[]{:S(2)}, u32[]{:S(2)}) collective-permute-start(f32[5,32,128]{2,1,0:T(8,128)S(1)} %get-tuple-element.27), channel_id=1, source_target_pairs={{0,1},{1,0},{2,3},{3,2},{4,5},{5,4},{6,7},{7,6},{8,9},{9,8},{10,11... | collective-permute-start | bytes 245768 | tf_op jit(solution)/shard_map/ppermute | solution.py:303
  45.3 0.8 copy-start.5
  48.9 7.2 %collective-permute-start.4 = (f32[5,32,128]{2,1,0:T(8,128)S(1)}, f32[5,32,128]{2,1,0:T(8,128)S(1)}, u32[]{:S(2)}, u32[]{:S(2)}) collective-permute-start(f32[5,32,128]{2,1,0:T(8,128)S(1)} %get-tuple-element.30), channel_id=1, source_target_pairs={{0,253},{1,4},{2,255},{3,6},{4,1},{5,8},{6,3},{7,10},{8,5},{9,12},... | collective-permute-start | bytes 245768 | tf_op jit(solution)/shard_map/ppermute | solution.py:303
  49.0 8.0 %collective-permute-start.5 = (f32[5,32,128]{2,1,0:T(8,128)S(1)}, f32[5,32,128]{2,1,0:T(8,128)S(1)}, u32[]{:S(2)}, u32[]{:S(2)}) collective-permute-start(f32[5,32,128]{2,1,0:T(8,128)S(1)} %get-tuple-element.31), channel_id=1, source_target_pairs={{0,1},{1,0},{2,3},{3,2},{4,5},{5,4},{6,7},{7,6},{8,9},{9,8},{10,11... | collective-permute-start | bytes 245768 | tf_op jit(solution)/shard_map/ppermute | solution.py:303
  59.9 7.3 %collective-permute-start.6 = (f32[5,32,128]{2,1,0:T(8,128)S(1)}, f32[5,32,128]{2,1,0:T(8,128)S(1)}, u32[]{:S(2)}, u32[]{:S(2)}) collective-permute-start(f32[5,32,128]{2,1,0:T(8,128)S(1)} %get-tuple-element.34), channel_id=1, source_target_pairs={{0,253},{1,4},{2,255},{3,6},{4,1},{5,8},{6,3},{7,10},{8,5},{9,12},... | collective-permute-start | bytes 245768 | tf_op jit(solution)/shard_map/ppermute | solution.py:303
  60.0 8.1 %collective-permute-start.7 = (f32[5,32,128]{2,1,0:T(8,128)S(1)}, f32[5,32,128]{2,1,0:T(8,128)S(1)}, u32[]{:S(2)}, u32[]{:S(2)}) collective-permute-start(f32[5,32,128]{2,1,0:T(8,128)S(1)} %get-tuple-element.35), channel_id=1, source_target_pairs={{0,1},{1,0},{2,3},{3,2},{4,5},{5,4},{6,7},{7,6},{8,9},{9,8},{10,11... | collective-permute-start | bytes 245768 | tf_op jit(solution)/shard_map/ppermute | solution.py:303
  70.9 7.3 %collective-permute-start.8 = (f32[5,32,128]{2,1,0:T(8,128)S(1)}, f32[5,32,128]{2,1,0:T(8,128)S(1)}, u32[]{:S(2)}, u32[]{:S(2)}) collective-permute-start(f32[5,32,128]{2,1,0:T(8,128)S(1)} %get-tuple-element.37), channel_id=1, source_target_pairs={{0,253},{1,4},{2,255},{3,6},{4,1},{5,8},{6,3},{7,10},{8,5},{9,12},... | collective-permute-start | bytes 245768 | tf_op jit(solution)/shard_map/ppermute | solution.py:303
  71.0 8.1 %collective-permute-start.9 = (f32[5,32,128]{2,1,0:T(8,128)S(1)}, f32[5,32,128]{2,1,0:T(8,128)S(1)}, u32[]{:S(2)}, u32[]{:S(2)}) collective-permute-start(f32[5,32,128]{2,1,0:T(8,128)S(1)} %get-tuple-element.38), channel_id=1, source_target_pairs={{0,1},{1,0},{2,3},{3,2},{4,5},{5,4},{6,7},{7,6},{8,9},{9,8},{10,11... | collective-permute-start | bytes 245768 | tf_op jit(solution)/shard_map/ppermute | solution.py:303
  79.1 2.3 %collective-permute-start.10 = (f32[32,256]{1,0:T(8,128)S(1)}, f32[32,256]{1,0:T(8,128)S(1)}, u32[]{:S(2)}, u32[]{:S(2)}) collective-permute-start(f32[32,256]{1,0:T(8,128)S(1)} %get-tuple-element.40), channel_id=1, source_target_pairs={{0,1},{1,0},{2,3},{3,2},{4,5},{5,4},{6,7},{7,6},{8,9},{9,8},{10,11... | collective-permute-start | bytes 98312 | tf_op jit(solution)/shard_map/ppermute | solution.py:381

commit v2 on v1

--- a/solution.py
+++ b/solution.py
@@ -12,6 +12,8 @@
 RAD = 16
 OWN = 4
 ITERS = 3
+ROWS = 4096
+COLUMNS = 1024
 STEP_SIZE = 0.05
 ALT_WEIGHT = 64.0
 DATA_GAIN = 160.0
@@ -34,6 +36,7 @@
 VMEM = pl.BlockSpec(memory_space=pltpu.VMEM)
 SMEM = pl.BlockSpec(memory_space=pltpu.SMEM)
 PARAMS = pltpu.CompilerParams(vmem_limit_bytes=24 * 2**20)
+LARGE = pltpu.CompilerParams(vmem_limit_bytes=58 * 2**20)
 
 
 def band(offset, derivative):
@@ -112,13 +115,38 @@
     return half + 2 * core + t
 
 
-def pack_kernel(height, albedo, images, lit_mask, owner, altimetry, expand, kept, sent):
-    half, core = place()
+def pack_kernel(
+    images_hbm, mask_hbm, height_hbm, albedo_hbm, owner_hbm, altimetry_hbm, count_hbm, expand_hbm,
+    kept, sent,
+    images, lit_mask, height, albedo, owner, altimetry, count, expand, sems,
+):
+    copies = [
+        pltpu.make_async_copy(source, target, sems.at[i])
+        for i, (source, target) in enumerate(
+            (
+                (images_hbm, images),
+                (mask_hbm, lit_mask),
+                (height_hbm, height),
+                (albedo_hbm, albedo),
+                (owner_hbm.at[pl.ds(0, 8)], owner),
+                (altimetry_hbm, altimetry),
+                (count_hbm, count),
+                (expand_hbm, expand),
+            )
+        )
+    ]
+    for copy in copies:
+        copy.start()
+    core = place()[1]
     lon = lax.axis_index("lon")
+    for copy in copies:
+        copy.wait()
     bins = owner[0:OWN, :] - lon * BINS
     shift = jnp.sum(bins, axis=0, keepdims=True).astype(F32)
     heights = dot(jnp.concatenate(pieces(altimetry[...], 3), axis=1), expand[...])
-    for ref, rows_of in ((kept, core), (sent, 1 - core)):
+    lit = jnp.concatenate([count[...].astype(F32), jnp.zeros((1, LANES - IMAGES), F32)], axis=1)
+    lit = jnp.broadcast_to(lit, (8, LANES))
+    for ref, rows_of in ((sent, 1 - core), (kept, core)):
         start = pl.multiple_of(rows_of * STRIP, STRIP)
         aux_rows = jnp.where(rows_of == 0, heights[0:8], heights[8:16])
         for t in range(2):
@@ -131,7 +159,25 @@
             lanes = slice(t * LANES, (t + 1) * LANES)
             ref[AUX, t, 0:8] = aux_rows[:, lanes]
             ref[AUX, t, 8:16] = jnp.broadcast_to(shift[:, lanes], (8, LANES))
-            ref[AUX, t, 16:32] = jnp.zeros((16, LANES), F32)
+            ref[AUX, t, 16:24] = lit
+            ref[AUX, t, 24:32] = jnp.zeros((8, LANES), F32)
+
+
+def near_kernel(kept, received, near_small, near):
+    half, core = place()
+    t = 1 - half
+    from_kept = half != core
+    for i, field in enumerate((HEIGHT, AUX)):
+        near_small[i] = jnp.where(from_kept, kept[field, t], received[field, t])
+    near_small[1, 16:24] = kept[AUX, 0, 16:24] + received[AUX, 0, 16:24]
+
+    @pl.when(from_kept)
+    def _():
+        near[...] = kept[0:HEIGHT, t]
+
+    @pl.when(jnp.logical_not(from_kept))
+    def _():
+        near[...] = received[0:HEIGHT, t]
 
 
 def route(core, up, down, inter, intra):
@@ -139,7 +185,7 @@
     intra[...] = jnp.where(core == 0, down, up)
 
 
-def begin_kernel(kept, received, halo, z, aux, inter, intra):
+def begin_kernel(kept, received, halo_small, z, aux, inter, intra, counts):
     half, core = place()
     zero = jnp.zeros((TILES, RAD, LANES), F32)
     z[:, 0:RAD] = zero
@@ -149,14 +195,27 @@
             z[at, RAD : RAD + STRIP] = ref[HEIGHT, t]
             aux[at] = ref[AUX, t, 0:BINS]
     far = (TILES - 1) * (1 - half)
-    z[far, RAD : RAD + STRIP] = halo[HEIGHT]
-    aux[far] = halo[AUX, 0:BINS]
+    z[far, RAD : RAD + STRIP] = halo_small[0]
+    aux[far] = halo_small[1, 0:BINS]
+    total = kept[AUX, 0, 16:17] + received[AUX, 0, 16:17] + halo_small[1, 16:17]
+    counts[...] = jnp.broadcast_to(total[None], counts.shape)
     alt = jnp.concatenate([aux[:, 0:8], jnp.zeros((TILES, 8, LANES), F32)], axis=1)
     up = jnp.concatenate([alt, z[:, RAD : 2 * RAD]], axis=1)
     route(core, up, z[:, STRIP:EXT], inter, intra)
 
 
-def image_sums(coef, observed, lit, albedo, slope_lon, slope_lat):
+def image_weights(counts):
+    total = jnp.sum(counts[...], axis=0)
+    weight = 2.0 * DATA_GAIN * float(ROWS * COLUMNS) / total
+    image = lax.broadcasted_iota(jnp.int32, (BINS, LANES), 0)
+    lane = lax.broadcasted_iota(jnp.int32, (BINS, LANES), 1)
+    diagonal = jnp.where((image == lane) & (image < IMAGES), weight, 0.0)
+    ones = jnp.ones((LANES, LANES), BF16)
+    first, second, third = pieces(diagonal, 3)
+    return dot(first, ones) + dot(second, ones) + dot(third, ones)
+
+
+def image_sums(coef, weight, observed, lit, albedo, slope_lon, slope_lat):
     inverse = lax.rsqrt(1.0 + slope_lon * slope_lon + slope_lat * slope_lat)
     flat_part = (1.0 - LUNAR_MIX) * inverse
     flat_shade = flat_part * (albedo * (1.0 / SHARPNESS))
@@ -170,10 +229,10 @@
         ratio = 1.0 / (part + coef[k, 3])
         gate = jnp.where(steep >= 0.0, 1.0, decay) / whole
         rendered = part * (mix_shade * ratio + flat_shade)
-        residual = lit(k) * (rendered - observed(k))
+        residual = (weight[k : k + 1] * lit(k)) * (rendered - observed(k))
         pull = residual * ((coef[k, 4] * (ratio * ratio) + flat_part) * gate)
         add_lon, add_lat = coef[k, 5] * pull, coef[k, 6] * pull
-        add_norm = (coef[k, 7] * residual) * part
+        add_norm = residual * part
         if k == 0:
             sum_lon, sum_lat, sum_norm = add_lon, add_lat, add_norm
         else:
@@ -183,12 +242,16 @@
 
 
 def step_kernel(first, *refs):
-    (coef, kept, received, halo, z, inter, intra, aux, alt_in, forward, backward) = refs[:11]
-    smooth, slope, quads = refs[11:14]
-    z_out, inter_out, intra_out = refs[14:17]
-    refs = refs[17:]
+    coef, kept, received, halo, z, inter, intra, aux, alt_in, weight_in = refs[:10]
+    forward, backward, smooth, slope, quads = refs[10:15]
+    z_out, inter_out, intra_out = refs[15:18]
+    refs = refs[18:]
     if first:
-        alt_out, refs = refs[0], refs[1:]
+        alt_out, weight_out, refs = refs[0], refs[1], refs[2:]
+        weight = image_weights(weight_in)
+        weight_out[...] = weight
+    else:
+        weight = weight_in[...]
     slope_lon, slope_lat, grad_lon, grad_lat = refs
     half, core = place()
     tiles = range(TILES)
@@ -236,6 +299,7 @@
         rows = pl.ds(pl.multiple_of(at * STRIP, STRIP), STRIP)
         g_lon, g_lat = image_sums(
             coef,
+            weight,
             lambda k: ref[(k, *index)],
             lambda k: ref[(IMAGES + k, *index)],
             ref[(ALBEDO, *index)],
@@ -282,6 +346,12 @@
             ref[RAD:STRIP, cols] = z[at, 2 * RAD : RAD + STRIP] + below[0:RAD]
 
 
+def place_kernel(mine, other, out):
+    core = place()[1]
+    out[pl.ds(pl.multiple_of(core * STRIP, STRIP), STRIP)] = mine[...]
+    out[pl.ds(pl.multiple_of((1 - core) * STRIP, STRIP), STRIP)] = other[...]
+
+
 def f32(*shape):
     return jax.ShapeDtypeStruct(shape, F32)
 
@@ -289,7 +359,6 @@
 def per_device(height, albedo, images, lit_mask, lit_count, geometry, owner_column, altimetry):
     lon_count, lat_count = lax.axis_size("lon"), lax.axis_size("lat")
     axes = ("lon", "lat")
-    devices = lon_count * lat_count
     sites = [(a, b) for a in range(lon_count) for b in range(lat_count)]
 
     def index(a, b):
@@ -302,13 +371,6 @@
     def exchange(inter, intra):
         return lax.ppermute(inter, axes, across_strips), lax.ppermute(intra, axes, across_cores)
 
-    counts = jnp.broadcast_to(
-        jnp.pad(lit_count.reshape(1, 1, IMAGES).astype(F32), ((0, 0), (0, 0), (0, LANES - IMAGES))),
-        (devices, 1, LANES),
-    )
-    totals = jnp.sum(lax.all_to_all(counts, axes, 0, 0), axis=(0, 1))[:IMAGES]
-    cells_all = float(height.size * devices)
-    weight = 2.0 * DATA_GAIN * cells_all / totals
     sun_lon, sun_lat, sun_up, view = (geometry[:, i] for i in range(4))
     coef = jnp.stack(
         [
@@ -317,40 +379,52 @@
             SHARPNESS * sun_up,
             SHARPNESS * view,
             (LUNAR_MIX * SHARPNESS * SHARPNESS) * view,
-            -weight * sun_lon,
-            -weight * sun_lat,
-            weight,
+            -sun_lon,
+            -sun_lat,
         ],
         axis=1,
     )
 
     expand = np.arange(altimetry.shape[1])[:, None] == np.arange(2 * LANES)[None, :] // OWN
     expand = jnp.asarray(np.concatenate([expand] * 3, axis=0), BF16)
+    count = lit_count.reshape(1, IMAGES)
+    inputs = (images, lit_mask, height, albedo, owner_column, altimetry, count, expand)
+    held = [
+        pltpu.VMEM((8,) + a.shape[1:] if a is owner_column else a.shape, a.dtype) for a in inputs
+    ]
     kept, sent = pl.pallas_call(
         pack_kernel,
         out_shape=(f32(FIELDS, 2, STRIP, LANES),) * 2,
-        in_specs=[VMEM] * 7,
+        in_specs=[pl.BlockSpec(memory_space=pltpu.HBM)] * len(inputs),
+        out_specs=(VMEM,) * 2,
+        scratch_shapes=held + [pltpu.SemaphoreType.DMA((len(inputs),))],
+        compiler_params=LARGE,
+    )(*inputs)
+    received = lax.ppermute(sent, axes, across_cores)
+    near_small, near = pl.pallas_call(
+        near_kernel,
+        out_shape=(f32(2, STRIP, LANES), f32(HEIGHT, STRIP, LANES)),
+        in_specs=[VMEM] * 2,
         out_specs=(VMEM,) * 2,
         compiler_params=PARAMS,
-    )(height, albedo, images, lit_mask, owner_column[:8], altimetry, expand)
-    received = lax.ppermute(sent, axes, across_cores)
-    half, core = place()
-    near = lax.dynamic_index_in_dim(
-        jnp.where(half == core, received, kept), 1 - half, axis=1, keepdims=False
-    )
+    )(kept, received)
+    halo_small = lax.ppermute(near_small, axes, across_halves)
+    halo_small, near = lax.optimization_barrier((halo_small, near))
     halo = lax.ppermute(near, axes, across_halves)
-    z, aux, inter, intra = pl.pallas_call(
+    z, aux, inter, intra, counts = pl.pallas_call(
         begin_kernel,
         out_shape=(
             f32(TILES, EXT, LANES),
             f32(TILES, BINS, LANES),
             f32(TILES, STRIP, LANES),
             f32(TILES, STRIP, LANES),
+            f32(lon_count, 1, LANES),
         ),
         in_specs=[VMEM] * 3,
-        out_specs=(VMEM,) * 4,
+        out_specs=(VMEM,) * 5,
         compiler_params=PARAMS,
-    )(kept, received, halo)
+    )(kept, received, halo_small)
+    weight = lax.all_to_all(counts, "lon", 0, 0)
     inter, intra = exchange(inter, intra)
     tables = constants()
     alt = aux
@@ -358,18 +432,18 @@
         first = iteration == 0
         shapes = [f32(TILES, EXT, LANES), f32(TILES, STRIP, LANES), f32(TILES, STRIP, LANES)]
         if first:
-            shapes.append(f32(TILES, BINS, LANES))
+            shapes += [f32(TILES, BINS, LANES), f32(BINS, LANES)]
         out = pl.pallas_call(
             functools.partial(step_kernel, first),
             out_shape=tuple(shapes),
-            in_specs=[SMEM] + [VMEM] * 13,
+            in_specs=[SMEM] + [VMEM] * 14,
             out_specs=(VMEM,) * len(shapes),
             scratch_shapes=[pltpu.VMEM((TILES * STRIP, LANES), F32)] * 4,
             compiler_params=PARAMS,
-        )(coef, kept, received, halo, z, inter, intra, aux, alt, *tables)
+        )(coef, kept, received, halo, z, inter, intra, aux, alt, weight, *tables)
         z, inter, intra = out[:3]
         if first:
-            alt = out[3]
+            alt, weight = out[3:]
         inter, intra = exchange(inter, intra)
     mine, other = pl.pallas_call(
         end_kernel,
@@ -379,9 +453,13 @@
         compiler_params=PARAMS,
     )(z, inter, intra)
     other = lax.ppermute(other, axes, across_cores)
-    upper = jnp.where(core == 0, mine, other)
-    lower = jnp.where(core == 0, other, mine)
-    return jnp.concatenate([upper, lower], axis=0)
+    return pl.pallas_call(
+        place_kernel,
+        out_shape=f32(2 * STRIP, 2 * LANES),
+        in_specs=[VMEM] * 2,
+        out_specs=VMEM,
+        compiler_params=PARAMS,
+    )(mine, other)
 
 
 def solution(mesh):

time: 82.5 us -> 76.3 us (0.925)
  starting transfers between devices: 50.6 us -> 42.4 us
  local copies, waits for them, and re-layouts: 7.7 us -> 1.66 us
  waiting for transfers between devices: 14 us -> 19 us
  Pallas kernels: 8.77 us -> 12.8 us
    ppermute x4, starting transfers between devices: 26 us -> 16.4 us  [exchange(): lax.ppermute(intra, axes, across_cores)]
    all_to_all x1, starting transfers between devices: 13 us -> 5.97 us  [per_device(): weight = lax.all_to_all(counts, 'lon', 0, 0)]
    ppermute x1, starting transfers between devices: 1.39 us -> 7.15 us  [per_device(): other = lax.ppermute(other, axes, across_cores)]
    unnamed x30 -> x20, local copies, waits for them, and re-layouts: 5.89 us -> 1.58 us
    ppermute x4, starting transfers between devices: 3.93 us -> 7.48 us  [exchange(): lax.ppermute(inter, axes, across_strips)]
    ppermute x0 -> x1, waiting for transfers between devices: none -> 3.07 us  [per_device(): halo_small = lax.ppermute(near_small, axes, across_halves)]
    pallas_call x1, Pallas kernels: 0.19 us -> 2.84 us  [per_device(): pl.pallas_call(pack_kernel, out_shape=(f32(FIELDS, 2, STRIP, LANES),) * 2...]
    ppermute x4, waiting for transfers between devices: 0.01 us -> 2.13 us  [exchange(): lax.ppermute(inter, axes, across_strips)]
  transfers between devices with their start and end apart: 12 -> 13, of which waited for: 7 -> 7; matrix products, arithmetic and copies ran while one was open for 2% -> 1% of each run, Pallas kernels for 0% -> 1%
where the time goes in v2:
time: 76.3 us; the launch traced here: 76.1 us
  starting transfers between devices  42.4 us (56%)
  waiting for transfers between devices  19 us (25%)
  Pallas kernels  12.8 us (17%)
  local copies, waits for them, and re-layouts  1.66 us (2%)
    ppermute x4, starting transfers between devices, exchange(): lax.ppermute(intra, axes, across_cores)  16.4 us
    all_to_all x1, waiting for transfers between devices, per_device(): weight = lax.all_to_all(counts, 'lon', 0, 0)  9.08 us
    pallas_call x3, Pallas kernels, per_device(): pl.pallas_call(functools.partial(step_kernel, first), out_shape=tuple(sha...  8.68 us
    ppermute x4, starting transfers between devices, exchange(): lax.ppermute(inter, axes, across_strips)  7.48 us
    ppermute x1, starting transfers between devices, per_device(): other = lax.ppermute(other, axes, across_cores)  7.15 us
    all_to_all x1, starting transfers between devices, per_device(): weight = lax.all_to_all(counts, 'lon', 0, 0)  5.97 us
    ppermute x1, starting transfers between devices, per_device(): received = lax.ppermute(sent, axes, across_cores)  3.33 us
    ppermute x1, waiting for transfers between devices, per_device(): halo_small = lax.ppermute(near_small, axes, across_halves)  3.07 us
  transfers between devices with their start and end apart: 13, of which 7 were waited for; matrix products, arithmetic and copies ran while one was open for 1% of the time, Pallas kernels for 1%

profile of v2, /device:TPU:1, one launch (start us, length us, event | category | flops | bytes accessed | tf_op | source)
XLA Modules:
  0.0 76.1 jit_solution(5859413810374781870)
XLA Ops:
  0.0 0.0 copy-start.7
  0.0 2.8 %shard_map.136 = (f32[27,2,32,128]{3,2,1,0:T(8,128)}, f32[27,2,32,128]{3,2,1,0:T(8,128)}) custom-call(bf16[12,64,256]{2,1,0:T(8,128)(2,1)} %images_hbm.1, s32[12,64,256]{2,1,0:T(8,128)} %mask_hbm.1, f32[64,256]{1,0:T(8,128)} %height_hbm.1, f32[64,256]{1,0:T(8,128)} %albedo_hbm.1, s32[64,256]{1,0:T(8,128)} %owner_hbm.1, f32[16,64]{1,0:T(8,128)} %altimetry_hbm.1, ...), custom_call_target="tpu_custom_call" | custom-call | tf_op jit(solution)/shard_map/pallas_call | solution.py:395
  2.8 3.3 %collective-permute-start = (f32[27,2,32,128]{3,2,1,0:T(8,128)}, f32[27,2,32,128]{3,2,1,0:T(8,128)S(1)}, u32[]{:S(2)}, u32[]{:S(2)}) collective-permute-start(f32[27,2,32,128]{3,2,1,0:T(8,128)} %get-tuple-element.30), channel_id=1, source_target_pairs={{0,1},{1,0},{2,3},{3,2},{4,5},{5,4},{6,7},{7,6},{8,9},{9,8},{10,11... | collective-permute-start | bytes 2654216 | tf_op jit(solution)/shard_map/ppermute | solution.py:403
  6.2 0.0 copy-done.7
  6.2 0.1 copy.22
  6.3 0.1 copy.20
  6.4 2.1 %collective-permute-done.received.refs_2_ = f32[27,2,32,128]{3,2,1,0:T(8,128)S(1)} collective-permute-done((f32[27,2,32,128]{3,2,1,0:T(8,128)}, f32[27,2,32,128]{3,2,1,0:T(8,128)S(1)}, u32[]{:S(2)}, u32[]{:S(2)}) %collective-permute-start) | collective-permute-done | bytes 884768 | tf_op jit(solution)/shard_map/ppermute | solution.py:403
  8.4 0.0 copy-start
  8.4 1.2 %copy-done = f32[27,2,32,128]{3,2,1,0:T(8,128)S(1)} copy-done((f32[27,2,32,128]{3,2,1,0:T(8,128)S(1)}, f32[27,2,32,128]{3,2,1,0:T(8,128)}, u32[]{:S(2)}) %copy-start) | copy-done | bytes 884760
  9.6 1.1 %collective-permute-start.1 = (f32[2,32,128]{2,1,0:T(8,128)S(1)}, f32[2,32,128]{2,1,0:T(8,128)S(1)}, u32[]{:S(2)}, u32[]{:S(2)}) collective-permute-start(f32[2,32,128]{2,1,0:T(8,128)S(1)} %get-tuple-element.31), channel_id=1, source_target_pairs={{0,2},{1,3},{2,0},{3,1},{4,6},{5,7},{6,4},{7,5},{8,10},{9,11},{10,... | collective-permute-start | bytes 98312 | tf_op jit(solution)/shard_map/ppermute | solution.py:411
  10.7 0.1 copy.19
  10.8 0.1 copy.21
  10.9 3.1 %collective-permute-done.1.halo_small = f32[2,32,128]{2,1,0:T(8,128)S(1)} collective-permute-done((f32[2,32,128]{2,1,0:T(8,128)S(1)}, f32[2,32,128]{2,1,0:T(8,128)S(1)}, u32[]{:S(2)}, u32[]{:S(2)}) %collective-permute-start.1) | collective-permute-done | bytes 32800 | tf_op jit(solution)/shard_map/ppermute | solution.py:411
  14.0 1.0 %collective-permute-start.2 = (f32[25,32,128]{2,1,0:T(8,128)S(1)}, f32[25,32,128]{2,1,0:T(8,128)S(1)}, u32[]{:S(2)}, u32[]{:S(2)}) collective-permute-start(f32[25,32,128]{2,1,0:T(8,128)S(1)} %get-tuple-element.33), channel_id=1, source_target_pairs={{0,2},{1,3},{2,0},{3,1},{4,6},{5,7},{6,4},{7,5},{8,10},{9,11},{10,... | collective-permute-start | bytes 1228808 | tf_op jit(solution)/shard_map/ppermute | solution.py:413
  15.0 0.0 copy-done.1
  15.0 0.0 copy-start.6
  15.0 0.6 shard_map.138
  15.7 3.3 %collective-permute-start.3 = (f32[5,32,128]{2,1,0:T(8,128)S(1)}, f32[5,32,128]{2,1,0:T(8,128)S(1)}, u32[]{:S(2)}, u32[]{:S(2)}) collective-permute-start(f32[5,32,128]{2,1,0:T(8,128)S(1)} %get-tuple-element.36), channel_id=1, source_target_pairs={{0,253},{1,4},{2,255},{3,6},{4,1},{5,8},{6,3},{7,10},{8,5},{9,12},... | collective-permute-start | bytes 245768 | tf_op jit(solution)/shard_map/ppermute | solution.py:372
  19.0 5.1 %collective-permute-start.4 = (f32[5,32,128]{2,1,0:T(8,128)S(1)}, f32[5,32,128]{2,1,0:T(8,128)S(1)}, u32[]{:S(2)}, u32[]{:S(2)}) collective-permute-start(f32[5,32,128]{2,1,0:T(8,128)S(1)} %get-tuple-element.37), channel_id=1, source_target_pairs={{0,1},{1,0},{2,3},{3,2},{4,5},{5,4},{6,7},{7,6},{8,9},{9,8},{10,11... | collective-permute-start | bytes 245768 | tf_op jit(solution)/shard_map/ppermute | solution.py:372
  24.1 6.0 %all-to-all-start = ((f32[64,1,128]{2,1,0:T(1,128)}), f32[64,1,128]{2,1,0:T(1,128)S(1)}, u32[]{:S(2)}, u32[]{:S(2)}) async-start(f32[64,1,128]{2,1,0:T(1,128)} %get-tuple-element.39), calls=%async_computation | async-start | bytes 65536 | tf_op jit(solution)/shard_map/all_to_all | solution.py:427
  30.1 0.1 stack.2.refs_0_
  30.2 9.1 %all-to-all-done.refs_9_ = f32[64,1,128]{2,1,0:T(1,128)S(1)} async-done(((f32[64,1,128]{2,1,0:T(1,128)}), f32[64,1,128]{2,1,0:T(1,128)S(1)}, u32[]{:S(2)}, u32[]{:S(2)}) %all-to-all-start) | async-done | bytes 32800 | tf_op jit(solution)/shard_map/all_to_all | solution.py:427
  39.3 0.0 collective-permute-done.3.refs_5_
  39.3 0.0 collective-permute-done.4.refs_6_
  39.3 0.0 collective-permute-done.2.refs_3_
  39.3 0.0 copy-done.4
  39.3 0.0 copy-done.5
  39.3 0.0 copy-done.6
  39.3 0.0 copy-done.2
  39.3 0.0 copy-done.3
  39.4 3.0 %shard_map.139 = (f32[5,64,128]{2,1,0:T(8,128)S(1)}, f32[5,32,128]{2,1,0:T(8,128)S(1)}, f32[5,32,128]{2,1,0:T(8,128)S(1)}, f32[5,16,128]{2,1,0:T(8,128)S(1)}, f32[16,128]{1,0:T(8,128)S(1)}) custom-call(f32[12,7]{1,0:T(8,128)S(1)} %stack.2.refs_0_, f32[27,2,32,128]{3,2,1,0:T(8,128)S(1)} %copy-done.1, ...), custom_call_target="tpu_custom_call" | custom-call | tf_op jit(solution)/shard_map/pallas_call | solution.py:436
  42.4 2.2 %collective-permute-start.5 = (f32[5,32,128]{2,1,0:T(8,128)S(1)}, f32[5,32,128]{2,1,0:T(8,128)S(1)}, u32[]{:S(2)}, u32[]{:S(2)}) collective-permute-start(f32[5,32,128]{2,1,0:T(8,128)S(1)} %get-tuple-element.41), channel_id=1, source_target_pairs={{0,253},{1,4},{2,255},{3,6},{4,1},{5,8},{6,3},{7,10},{8,5},{9,12},... | collective-permute-start | bytes 245768 | tf_op jit(solution)/shard_map/ppermute | solution.py:372
  44.6 0.0 collective-permute-start.6
  44.6 2.1 %collective-permute-done.5.refs_5_ = f32[5,32,128]{2,1,0:T(8,128)S(1)} collective-permute-done((f32[5,32,128]{2,1,0:T(8,128)S(1)}, f32[5,32,128]{2,1,0:T(8,128)S(1)}, u32[]{:S(2)}, u32[]{:S(2)}) %collective-permute-start.5) | collective-permute-done | bytes 81952 | tf_op jit(solution)/shard_map/ppermute | solution.py:372
  46.7 0.0 collective-permute-done.6.refs_6_
  46.7 2.8 %shard_map.140 = (f32[5,64,128]{2,1,0:T(8,128)S(1)}, f32[5,32,128]{2,1,0:T(8,128)S(1)}, f32[5,32,128]{2,1,0:T(8,128)S(1)}) custom-call(f32[12,7]{1,0:T(8,128)S(1)} %stack.2.refs_0_, f32[27,2,32,128]{3,2,1,0:T(8,128)S(1)} %copy-done.1, f32[27,2,32,128]{3,2,1,0:T(8,128)S(1)} %collective-permute-done.received.refs_2_, ...), custom_call_target="tpu_custom_call" | custom-call | tf_op jit(solution)/shard_map/pallas_call | solution.py:436
  49.6 1.8 %collective-permute-start.7 = (f32[5,32,128]{2,1,0:T(8,128)S(1)}, f32[5,32,128]{2,1,0:T(8,128)S(1)}, u32[]{:S(2)}, u32[]{:S(2)}) collective-permute-start(f32[5,32,128]{2,1,0:T(8,128)S(1)} %get-tuple-element.46), channel_id=1, source_target_pairs={{0,253},{1,4},{2,255},{3,6},{4,1},{5,8},{6,3},{7,10},{8,5},{9,12},... | collective-permute-start | bytes 245768 | tf_op jit(solution)/shard_map/ppermute | solution.py:372
  51.4 4.3 %collective-permute-start.8 = (f32[5,32,128]{2,1,0:T(8,128)S(1)}, f32[5,32,128]{2,1,0:T(8,128)S(1)}, u32[]{:S(2)}, u32[]{:S(2)}) collective-permute-start(f32[5,32,128]{2,1,0:T(8,128)S(1)} %get-tuple-element.47), channel_id=1, source_target_pairs={{0,1},{1,0},{2,3},{3,2},{4,5},{5,4},{6,7},{7,6},{8,9},{9,8},{10,11... | collective-permute-start | bytes 245768 | tf_op jit(solution)/shard_map/ppermute | solution.py:372
  55.7 0.0 collective-permute-done.7.refs_5_
  55.7 0.9 %collective-permute-done.8.refs_6_ = f32[5,32,128]{2,1,0:T(8,128)S(1)} collective-permute-done((f32[5,32,128]{2,1,0:T(8,128)S(1)}, f32[5,32,128]{2,1,0:T(8,128)S(1)}, u32[]{:S(2)}, u32[]{:S(2)}) %collective-permute-start.8) | collective-permute-done | bytes 81952 | tf_op jit(solution)/shard_map/ppermute | solution.py:372
  56.6 2.8 %shard_map.141 = (f32[5,64,128]{2,1,0:T(8,128)S(1)}, f32[5,32,128]{2,1,0:T(8,128)S(1)}, f32[5,32,128]{2,1,0:T(8,128)S(1)}) custom-call(f32[12,7]{1,0:T(8,128)S(1)} %stack.2.refs_0_, f32[27,2,32,128]{3,2,1,0:T(8,128)S(1)} %copy-done.1, f32[27,2,32,128]{3,2,1,0:T(8,128)S(1)} %collective-permute-done.received.refs_2_, ...), custom_call_target="tpu_custom_call" | custom-call | tf_op jit(solution)/shard_map/pallas_call | solution.py:436
  59.5 0.1 collective-permute-start.9
  59.6 7.0 %collective-permute-start.10 = (f32[5,32,128]{2,1,0:T(8,128)S(1)}, f32[5,32,128]{2,1,0:T(8,128)S(1)}, u32[]{:S(2)}, u32[]{:S(2)}) collective-permute-start(f32[5,32,128]{2,1,0:T(8,128)S(1)} %get-tuple-element.50), channel_id=1, source_target_pairs={{0,1},{1,0},{2,3},{3,2},{4,5},{5,4},{6,7},{7,6},{8,9},{9,8},{10,11... | collective-permute-start | bytes 245768 | tf_op jit(solution)/shard_map/ppermute | solution.py:372
  66.5 0.0 collective-permute-done.9.inter
  66.5 0.9 %collective-permute-done.10.intra = f32[5,32,128]{2,1,0:T(8,128)S(1)} collective-permute-done((f32[5,32,128]{2,1,0:T(8,128)S(1)}, f32[5,32,128]{2,1,0:T(8,128)S(1)}, u32[]{:S(2)}, u32[]{:S(2)}) %collective-permute-start.10) | collective-permute-done | bytes 81952 | tf_op jit(solution)/shard_map/ppermute | solution.py:372
  67.5 7.2 %collective-permute-start.11 = (f32[32,256]{1,0:T(8,128)S(1)}, f32[32,256]{1,0:T(8,128)S(1)}, u32[]{:S(2)}, u32[]{:S(2)}) collective-permute-start(f32[32,256]{1,0:T(8,128)S(1)} %get-tuple-element.52), channel_id=1, source_target_pairs={{0,1},{1,0},{2,3},{3,2},{4,5},{5,4},{6,7},{7,6},{8,9},{9,8},{10,11... | collective-permute-start | bytes 98312 | tf_op jit(solution)/shard_map/ppermute | solution.py:455
  74.6 0.9 %collective-permute-done.11.other = f32[32,256]{1,0:T(8,128)S(1)} collective-permute-done((f32[32,256]{1,0:T(8,128)S(1)}, f32[32,256]{1,0:T(8,128)S(1)}, u32[]{:S(2)}, u32[]{:S(2)}) %collective-permute-start.11) | collective-permute-done | bytes 32800 | tf_op jit(solution)/shard_map/ppermute | solution.py:455
  75.5 0.6 shard_map.143
  (11 shorter events, 0.1 us)
Async XLA Ops:
  0.0 6.2 %copy-start.7 = (f32[12,4]{0,1:T(4,128)S(1)}, f32[12,4]{0,1:T(4,128)}, u32[]{:S(2)}) copy-start(f32[12,4]{0,1:T(4,128)} %param.19) | copy-start | bytes 580
  2.8 5.6 %collective-permute-start = (f32[27,2,32,128]{3,2,1,0:T(8,128)}, f32[27,2,32,128]{3,2,1,0:T(8,128)S(1)}, u32[]{:S(2)}, u32[]{:S(2)}) collective-permute-start(f32[27,2,32,128]{3,2,1,0:T(8,128)} %get-tuple-element.30), channel_id=1, source_target_pairs={{0,1},{1,0},{2,3},{3,2},{4,5},{5,4},{6,7},{7,6},{8,9},{9,8},{10,11... | collective-permute-start | bytes 2654216 | tf_op jit(solution)/shard_map/ppermute | solution.py:403
  8.4 1.2 %copy-start = (f32[27,2,32,128]{3,2,1,0:T(8,128)S(1)}, f32[27,2,32,128]{3,2,1,0:T(8,128)}, u32[]{:S(2)}) copy-start(f32[27,2,32,128]{3,2,1,0:T(8,128)} %get-tuple-element.29.kept.refs_1_) | copy-start | bytes 2654212
  9.6 5.4 %copy-start.1 = (f32[27,2,32,128]{3,2,1,0:T(8,128)S(1)}, f32[27,2,32,128]{3,2,1,0:T(8,128)}, u32[]{:S(2)}) copy-start(f32[27,2,32,128]{3,2,1,0:T(8,128)} %get-tuple-element.29.kept.refs_1_) | copy-start | bytes 2654212
  9.6 4.4 %collective-permute-start.1 = (f32[2,32,128]{2,1,0:T(8,128)S(1)}, f32[2,32,128]{2,1,0:T(8,128)S(1)}, u32[]{:S(2)}, u32[]{:S(2)}) collective-permute-start(f32[2,32,128]{2,1,0:T(8,128)S(1)} %get-tuple-element.31), channel_id=1, source_target_pairs={{0,2},{1,3},{2,0},{3,1},{4,6},{5,7},{6,4},{7,5},{8,10},{9,11},{10,... | collective-permute-start | bytes 98312 | tf_op jit(solution)/shard_map/ppermute | solution.py:411
  14.0 25.3 %collective-permute-start.2 = (f32[25,32,128]{2,1,0:T(8,128)S(1)}, f32[25,32,128]{2,1,0:T(8,128)S(1)}, u32[]{:S(2)}, u32[]{:S(2)}) collective-permute-start(f32[25,32,128]{2,1,0:T(8,128)S(1)} %get-tuple-element.33), channel_id=1, source_target_pairs={{0,2},{1,3},{2,0},{3,1},{4,6},{5,7},{6,4},{7,5},{8,10},{9,11},{10,... | collective-permute-start | bytes 1228808 | tf_op jit(solution)/shard_map/ppermute | solution.py:413
  15.0 24.3 %copy-start.4 = (bf16[256,128]{1,0:T(8,128)(2,1)S(1)}, bf16[256,128]{1,0:T(8,128)(2,1)}, u32[]{:S(2)}) copy-start(bf16[256,128]{1,0:T(8,128)(2,1)} %constant.20.clone.refs_13_) | copy-start | bytes 196612
  15.0 24.3 %copy-start.5 = (bf16[64,256]{1,0:T(8,128)(2,1)S(1)}, bf16[64,256]{1,0:T(8,128)(2,1)}, u32[]{:S(2)}) copy-start(bf16[64,256]{1,0:T(8,128)(2,1)} %constant.18.clone.refs_11_) | copy-start | bytes 98308
  15.0 24.3 %copy-start.6 = (bf16[128,128]{1,0:T(8,128)(2,1)S(1)}, bf16[128,128]{1,0:T(8,128)(2,1)}, u32[]{:S(2)}) copy-start(bf16[128,128]{1,0:T(8,128)(2,1)} %constant.21.clone.refs_14_) | copy-start | bytes 98308
  15.7 23.6 %collective-permute-start.3 = (f32[5,32,128]{2,1,0:T(8,128)S(1)}, f32[5,32,128]{2,1,0:T(8,128)S(1)}, u32[]{:S(2)}, u32[]{:S(2)}) collective-permute-start(f32[5,32,128]{2,1,0:T(8,128)S(1)} %get-tuple-element.36), channel_id=1, source_target_pairs={{0,253},{1,4},{2,255},{3,6},{4,1},{5,8},{6,3},{7,10},{8,5},{9,12},... | collective-permute-start | bytes 245768 | tf_op jit(solution)/shard_map/ppermute | solution.py:372
  19.0 20.3 %collective-permute-start.4 = (f32[5,32,128]{2,1,0:T(8,128)S(1)}, f32[5,32,128]{2,1,0:T(8,128)S(1)}, u32[]{:S(2)}, u32[]{:S(2)}) collective-permute-start(f32[5,32,128]{2,1,0:T(8,128)S(1)} %get-tuple-element.37), channel_id=1, source_target_pairs={{0,1},{1,0},{2,3},{3,2},{4,5},{5,4},{6,7},{7,6},{8,9},{9,8},{10,11... | collective-permute-start | bytes 245768 | tf_op jit(solution)/shard_map/ppermute | solution.py:372
  24.1 15.2 %copy-start.2 = (bf16[128,192]{1,0:T(8,128)(2,1)S(1)}, bf16[128,192]{1,0:T(8,128)(2,1)}, u32[]{:S(2)}) copy-start(bf16[128,192]{1,0:T(8,128)(2,1)} %constant.17.clone.refs_10_) | copy-start | bytes 147460
  24.1 15.2 %copy-start.3 = (bf16[256,128]{1,0:T(8,128)(2,1)S(1)}, bf16[256,128]{1,0:T(8,128)(2,1)}, u32[]{:S(2)}) copy-start(bf16[256,128]{1,0:T(8,128)(2,1)} %constant.19.clone.refs_12_) | copy-start | bytes 196612
  24.1 15.2 %all-to-all-start = ((f32[64,1,128]{2,1,0:T(1,128)}), f32[64,1,128]{2,1,0:T(1,128)S(1)}, u32[]{:S(2)}, u32[]{:S(2)}) async-start(f32[64,1,128]{2,1,0:T(1,128)} %get-tuple-element.39), calls=%async_computation | async-start | bytes 65536 | tf_op jit(solution)/shard_map/all_to_all | solution.py:427
  42.4 4.4 %collective-permute-start.5 = (f32[5,32,128]{2,1,0:T(8,128)S(1)}, f32[5,32,128]{2,1,0:T(8,128)S(1)}, u32[]{:S(2)}, u32[]{:S(2)}) collective-permute-start(f32[5,32,128]{2,1,0:T(8,128)S(1)} %get-tuple-element.41), channel_id=1, source_target_pairs={{0,253},{1,4},{2,255},{3,6},{4,1},{5,8},{6,3},{7,10},{8,5},{9,12},... | collective-permute-start | bytes 245768 | tf_op jit(solution)/shard_map/ppermute | solution.py:372
  44.6 2.1 %collective-permute-start.6 = (f32[5,32,128]{2,1,0:T(8,128)S(1)}, f32[5,32,128]{2,1,0:T(8,128)S(1)}, u32[]{:S(2)}, u32[]{:S(2)}) collective-permute-start(f32[5,32,128]{2,1,0:T(8,128)S(1)} %get-tuple-element.42), channel_id=1, source_target_pairs={{0,1},{1,0},{2,3},{3,2},{4,5},{5,4},{6,7},{7,6},{8,9},{9,8},{10,11... | collective-permute-start | bytes 245768 | tf_op jit(solution)/shard_map/ppermute | solution.py:372
  49.6 6.1 %collective-permute-start.7 = (f32[5,32,128]{2,1,0:T(8,128)S(1)}, f32[5,32,128]{2,1,0:T(8,128)S(1)}, u32[]{:S(2)}, u32[]{:S(2)}) collective-permute-start(f32[5,32,128]{2,1,0:T(8,128)S(1)} %get-tuple-element.46), channel_id=1, source_target_pairs={{0,253},{1,4},{2,255},{3,6},{4,1},{5,8},{6,3},{7,10},{8,5},{9,12},... | collective-permute-start | bytes 245768 | tf_op jit(solution)/shard_map/ppermute | solution.py:372
  51.4 5.2 %collective-permute-start.8 = (f32[5,32,128]{2,1,0:T(8,128)S(1)}, f32[5,32,128]{2,1,0:T(8,128)S(1)}, u32[]{:S(2)}, u32[]{:S(2)}) collective-permute-start(f32[5,32,128]{2,1,0:T(8,128)S(1)} %get-tuple-element.47), channel_id=1, source_target_pairs={{0,1},{1,0},{2,3},{3,2},{4,5},{5,4},{6,7},{7,6},{8,9},{9,8},{10,11... | collective-permute-start | bytes 245768 | tf_op jit(solution)/shard_map/ppermute | solution.py:372
  59.5 7.1 %collective-permute-start.9 = (f32[5,32,128]{2,1,0:T(8,128)S(1)}, f32[5,32,128]{2,1,0:T(8,128)S(1)}, u32[]{:S(2)}, u32[]{:S(2)}) collective-permute-start(f32[5,32,128]{2,1,0:T(8,128)S(1)} %get-tuple-element.49), channel_id=1, source_target_pairs={{0,253},{1,4},{2,255},{3,6},{4,1},{5,8},{6,3},{7,10},{8,5},{9,12},... | collective-permute-start | bytes 245768 | tf_op jit(solution)/shard_map/ppermute | solution.py:372
  59.6 7.9 %collective-permute-start.10 = (f32[5,32,128]{2,1,0:T(8,128)S(1)}, f32[5,32,128]{2,1,0:T(8,128)S(1)}, u32[]{:S(2)}, u32[]{:S(2)}) collective-permute-start(f32[5,32,128]{2,1,0:T(8,128)S(1)} %get-tuple-element.50), channel_id=1, source_target_pairs={{0,1},{1,0},{2,3},{3,2},{4,5},{5,4},{6,7},{7,6},{8,9},{9,8},{10,11... | collective-permute-start | bytes 245768 | tf_op jit(solution)/shard_map/ppermute | solution.py:372
  67.5 8.0 %collective-permute-start.11 = (f32[32,256]{1,0:T(8,128)S(1)}, f32[32,256]{1,0:T(8,128)S(1)}, u32[]{:S(2)}, u32[]{:S(2)}) collective-permute-start(f32[32,256]{1,0:T(8,128)S(1)} %get-tuple-element.52), channel_id=1, source_target_pairs={{0,1},{1,0},{2,3},{3,2},{4,5},{5,4},{6,7},{7,6},{8,9},{9,8},{10,11... | collective-permute-start | bytes 98312 | tf_op jit(solution)/shard_map/ppermute | solution.py:455

commit v3 on v2

v3 whole, which is shorter than its diff:
```python
import jax
import jax.numpy as jnp
import numpy as np
from jax import lax
from jax.experimental import pallas as pl
from jax.experimental.pallas import tpu as pltpu
from jax.sharding import PartitionSpec as P

IMAGES = 12
RAD = 16
OWN = 4
ITERS = 3
ROWS = 4096
COLUMNS = 1024
STEP_SIZE = 0.05
ALT_WEIGHT = 64.0
DATA_GAIN = 160.0
LUNAR_MIX = 0.6
SHARPNESS = 20.0

LANES = 128
STRIP = 32
EXT = STRIP + 2 * RAD
TILES = 5
FIELDS = 2 * IMAGES + 3
ALBEDO = 2 * IMAGES
HEIGHT = ALBEDO + 1
AUX = HEIGHT + 1
BINS = 16
DENOM = float(RAD * (RAD + 1) * (2 * RAD + 1)) / 3.0
TAP_SCALE = 1.0 / (DENOM * (2 * RAD + 1))
F32 = jnp.float32
BF16 = jnp.bfloat16
VMEM = pl.BlockSpec(memory_space=pltpu.VMEM)
SMEM = pl.BlockSpec(memory_space=pltpu.SMEM)
PARAMS = pltpu.CompilerParams(vmem_limit_bytes=24 * 2**20)
LARGE = pltpu.CompilerParams(vmem_limit_bytes=58 * 2**20)


def band(offset, derivative):
    inside = np.abs(offset) <= RAD
    return np.where(inside, offset if derivative else 1, 0).astype(np.float32)


def constants():
    own = np.arange(STRIP)
    ext = np.arange(EXT) - RAD
    reach = ext[None, :] - own[:, None]
    rows = [band(reach, True), band(reach, False)]
    bins = np.arange(BINS)
    for shift in range(OWN):
        group = (ext[None, :] + shift) // OWN
        rows.append((group == bins[:, None]).astype(np.float32))
    down = np.concatenate(rows, axis=0)
    forward = np.concatenate([down] * 3, axis=1)
    back = own[None, :] - ext[:, None]
    spread = np.zeros((EXT, OWN * BINS), np.float32)
    for shift in range(OWN):
        hit = ((own[:, None] + shift) // OWN) == bins[None, :]
        spread[RAD : RAD + STRIP, shift * BINS : (shift + 1) * BINS] = hit
    filters = np.concatenate([band(back, True), band(back, False)], axis=1)
    backward = np.concatenate([filters, filters, spread, spread], axis=1)
    lane = np.arange(LANES)
    side = np.where(lane < LANES // 2, lane + LANES, lane - LANES)
    source = np.concatenate([lane, side])
    across = source[:, None] - lane[None, :]
    quads = (lane[:, None] // OWN == lane[None, :] // OWN).astype(np.float32)
    return [
        jnp.asarray(m, BF16)
        for m in (forward, backward, band(across, False), band(across, True), quads)
    ]


def pieces(value, count):
    out = []
    for _ in range(count - 1):
        part = value.astype(BF16)
        value = value - part.astype(F32)
        out.append(part)
    out.append(value.astype(BF16))
    return out


def dot(left, right):
    return jnp.dot(left, right, preferred_element_type=F32)


def with_sides(tiles):
    low = lax.broadcasted_iota(jnp.int32, tiles[0].shape, 1) < LANES // 2
    zero = jnp.zeros_like(tiles[0])
    rows = []
    for j, tile in enumerate(tiles):
        after = tiles[j + 1] if j + 1 < len(tiles) else zero
        before = tiles[j - 1] if j > 0 else zero
        rows.append(jnp.concatenate([tile, jnp.where(low, after, before)], axis=1))
    return jnp.concatenate(rows, axis=0)


def filter_lat(tiles, taps, count):
    total = None
    for part in pieces(with_sides(tiles), count):
        term = dot(part, taps)
        total = term if total is None else total + term
    return total


def place():
    lat = lax.axis_index("lat")
    return lat // 2, lat % 2


def own_tile(half, core, t):
    return half + 2 * core + t


def aux_fields(ref, rows_of, owner, altimetry, count, expand):
    bins = owner[0:OWN, :] - lax.axis_index("lon") * BINS
    shift = jnp.sum(bins, axis=0, keepdims=True).astype(F32)
    heights = dot(jnp.concatenate(pieces(altimetry[...], 3), axis=1), expand[...])
    heights = jnp.where(rows_of == 0, heights[0:8], heights[8:16])
    lit = jnp.concatenate([count[...].astype(F32), jnp.zeros((1, LANES - IMAGES), F32)], axis=1)
    for t in range(2):
        lanes = slice(t * LANES, (t + 1) * LANES)
        ref[AUX, t, 0:8] = heights[:, lanes]
        ref[AUX, t, 8:16] = jnp.broadcast_to(shift[:, lanes], (8, LANES))
        ref[AUX, t, 16:24] = jnp.broadcast_to(lit, (8, LANES))
        ref[AUX, t, 24:32] = jnp.zeros((8, LANES), F32)


def send_kernel(
    images_hbm, mask_hbm, height_hbm, albedo_hbm, owner_hbm, altimetry_hbm, count_hbm, expand_hbm,
    sent,
    images, lit_mask, height, albedo, owner, altimetry, count, expand, sems,
):
    other = 1 - place()[1]
    rows = pl.ds(pl.multiple_of(other * STRIP, STRIP), STRIP)
    copies = [
        pltpu.make_async_copy(source, target, sems.at[i])
        for i, (source, target) in enumerate(
            (
                (images_hbm.at[:, rows], images),
                (mask_hbm.at[:, rows], lit_mask),
                (height_hbm.at[rows], height),
                (albedo_hbm.at[rows], albedo),
                (owner_hbm.at[pl.ds(0, 8)], owner),
                (altimetry_hbm, altimetry),
                (count_hbm, count),
                (expand_hbm, expand),
            )
        )
    ]
    for copy in copies:
        copy.start()
    for copy in copies:
        copy.wait()
    aux_fields(sent, other, owner, altimetry, count, expand)
    for t in range(2):
        cols = pl.ds(t * LANES, LANES)
        for k in range(IMAGES):
            sent[k, t] = images[k, :, cols].astype(F32)
            sent[IMAGES + k, t] = lit_mask[k, :, cols].astype(F32)
        sent[ALBEDO, t] = albedo[:, cols]
        sent[HEIGHT, t] = height[:, cols]


def keep_kernel(images, lit_mask, height, albedo, owner, altimetry, count, expand, sent, kept):
    core = place()[1]
    rows = pl.ds(pl.multiple_of(core * STRIP, STRIP), STRIP)
    aux_fields(kept, core, owner, altimetry, count, expand)
    for t in range(2):
        cols = pl.ds(t * LANES, LANES)
        for k in range(IMAGES):
            kept[k, t] = images[k, rows, cols].astype(F32)
            kept[IMAGES + k, t] = lit_mask[k, rows, cols].astype(F32)
        kept[ALBEDO, t] = albedo[rows, cols]
        kept[HEIGHT, t] = height[rows, cols]


def near_small_kernel(kept, received, near_small):
    half, core = place()
    for i, field in enumerate((HEIGHT, AUX)):
        near_small[i] = jnp.where(half != core, kept[field, 1 - half], received[field, 1 - half])


def near_kernel(kept, received, near_small, near):
    half, core = place()

    @pl.when(half != core)
    def _():
        near[...] = kept[0:HEIGHT, 1 - half]

    @pl.when(half == core)
    def _():
        near[...] = received[0:HEIGHT, 1 - half]


def count_kernel(kept, received, near, counts):
    total = kept[0, 0, 16:17] + received[0, 0, 16:17]
    counts[...] = jnp.broadcast_to(total[None], counts.shape)


def route(core, up, down, inter, intra):
    inter[...] = jnp.where(core == 0, up, down)
    intra[...] = jnp.where(core == 0, down, up)


def begin_kernel(kept, received, halo_small, z, aux, inter, intra):
    half, core = place()
    zero = jnp.zeros((TILES, RAD, LANES), F32)
    z[:, 0:RAD] = zero
    z[:, RAD + STRIP : EXT] = zero
    for t in range(2):
        for ref, at in ((kept, own_tile(half, core, t)), (received, own_tile(half, 1 - core, t))):
            z[at, RAD : RAD + STRIP] = ref[HEIGHT, t]
            aux[at] = ref[AUX, t, 0:BINS]
    far = (TILES - 1) * (1 - half)
    z[far, RAD : RAD + STRIP] = halo_small[0]
    aux[far] = halo_small[1, 0:BINS]
    alt = jnp.concatenate([aux[:, 0:8], jnp.zeros((TILES, 8, LANES), F32)], axis=1)
    up = jnp.concatenate([alt, z[:, RAD : 2 * RAD]], axis=1)
    route(core, up, z[:, STRIP:EXT], inter, intra)


def image_weights(counts):
    total = jnp.sum(counts[...], axis=0)
    weight = 2.0 * DATA_GAIN * float(ROWS * COLUMNS) / total
    image = lax.broadcasted_iota(jnp.int32, (BINS, LANES), 0)
    lane = lax.broadcasted_iota(jnp.int32, (BINS, LANES), 1)
    diagonal = jnp.where((image == lane) & (image < IMAGES), weight, 0.0)
    ones = jnp.ones((LANES, LANES), BF16)
    first, second, third = pieces(diagonal, 3)
    return dot(first, ones) + dot(second, ones) + dot(third, ones)


def inverse_of(value):
    guess = pl.reciprocal(value, approx=True)
    return guess * (2.0 - value * guess)


def image_term(coef, k, observed, lit, flat_part, flat_shade, mix_shade, slope_lon, slope_lat):
    steep = coef[k, 2] - coef[k, 0] * slope_lon - coef[k, 1] * slope_lat
    decay = jnp.exp(-jnp.abs(steep))
    whole = 1.0 + decay
    part = jnp.maximum(steep, 0.0) + jnp.log(whole)
    level = part + coef[k, 3]
    both = inverse_of(whole * level)
    ratio = both * whole
    gate = jnp.where(steep >= 0.0, 1.0, decay) * (both * level)
    residual = lit * (part * (mix_shade * ratio + flat_shade) - observed)
    pull = residual * ((coef[k, 4] * (ratio * ratio) + flat_part) * gate)
    return pull, residual * part


def shades(albedo, slope_lon, slope_lat):
    inverse = lax.rsqrt(1.0 + slope_lon * slope_lon + slope_lat * slope_lat)
    flat_part = (1.0 - LUNAR_MIX) * inverse
    return inverse, (flat_part, flat_part * (albedo * (1.0 / SHARPNESS)), albedo * LUNAR_MIX)


def gradients(albedo, inverse, slope_lon, slope_lat, sums):
    sum_lon, sum_lat, sum_norm = sums
    bend = (1.0 - LUNAR_MIX) / SHARPNESS * (inverse * inverse * inverse) * sum_norm
    return albedo * (sum_lon - slope_lon * bend), albedo * (sum_lat - slope_lat * bend)


def add_image(sums, coef, k, pull, norm):
    terms = (coef[k, 5] * pull, coef[k, 6] * pull, norm)
    return terms if sums is None else tuple(a + b for a, b in zip(sums, terms))


def tile_rows(at):
    return pl.ds(pl.multiple_of(at * STRIP, STRIP), STRIP)


def image_tiles(kept, received, halo):
    half, core = place()
    for t in range(2):
        yield kept, (t,), tile_rows(own_tile(half, core, t))
        yield received, (t,), tile_rows(own_tile(half, 1 - core, t))
    yield halo, (), tile_rows((TILES - 1) * (1 - half))


def shift_rows(aux, j):
    return jnp.concatenate([aux[j, 8:16]] * 2, axis=0)


def slopes_and_misfit(surface, aux, alt, tables, slope_lon, slope_lat):
    forward, backward, smooth, slope, quads = tables
    tiles = range(TILES)
    stacked = jnp.concatenate(
        [jnp.concatenate(pieces(surface[j], 3), axis=0) for j in tiles], axis=1
    )
    down = dot(forward[...], stacked)

    def part(row, count, j):
        return down[row : row + count, j * LANES : (j + 1) * LANES]

    slope_lon[...] = TAP_SCALE * filter_lat([part(0, STRIP, j) for j in tiles], smooth[...], 3)
    slope_lat[...] = TAP_SCALE * filter_lat([part(STRIP, STRIP, j) for j in tiles], slope[...], 3)
    sums = []
    for j in tiles:
        shift = shift_rows(aux, j)
        chosen = part(2 * STRIP, BINS, j)
        for s in range(1, OWN):
            chosen = jnp.where(shift == float(s), part(2 * STRIP + s * BINS, BINS, j), chosen)
        sums.append(chosen)
    owner_sum = None
    for p in pieces(jnp.concatenate(sums, axis=0), 3):
        term = dot(p, quads[...])
        owner_sum = term if owner_sum is None else owner_sum + term
    gain = STEP_SIZE * 2.0 * ALT_WEIGHT / (OWN * OWN)
    rows = [slice(j * BINS, (j + 1) * BINS) for j in tiles]
    return [gain * alt[j] - (gain / (OWN * OWN)) * owner_sum[rows[j]] for j in tiles]


def contribute(surface, aux, misfit, grad_lon, grad_lat, tables, z_out, inter_out, intra_out):
    forward, backward, smooth, slope, quads = tables
    tiles = range(TILES)

    def field(ref):
        return [ref[j * STRIP : (j + 1) * STRIP] for j in tiles]

    scale = STEP_SIZE * TAP_SCALE
    from_lon = scale * filter_lat(field(grad_lon), smooth[...], 2)
    from_lat = scale * filter_lat(field(grad_lat), slope[...], 2)
    columns = []
    for j in tiles:
        rows = slice(j * STRIP, (j + 1) * STRIP)
        data = pieces(jnp.concatenate([from_lon[rows], from_lat[rows]], axis=0), 2)
        shift = shift_rows(aux, j)
        pull = [jnp.where(shift == float(s), misfit[j], 0.0) for s in range(OWN)]
        columns.append(jnp.concatenate(data + pieces(jnp.concatenate(pull, axis=0), 2), axis=0))
    spread = dot(backward[...], jnp.concatenate(columns, axis=1))
    for j in tiles:
        change = spread[:, j * LANES : (j + 1) * LANES]
        z_out[j, 0:RAD] = change[0:RAD]
        z_out[j, RAD : RAD + STRIP] = change[RAD : RAD + STRIP] + surface[j][RAD : RAD + STRIP]
        z_out[j, RAD + STRIP : EXT] = change[RAD + STRIP : EXT]
    core = place()[1]
    route(core, z_out[:, 0:STRIP], z_out[:, STRIP:EXT], inter_out, intra_out)


def arrived(inter, intra):
    core = place()[1]
    return (
        jnp.where(core == 0, inter[...], intra[...]),
        jnp.where(core == 0, intra[...], inter[...]),
    )


def surface_step(
    coef, weight, kept, received, halo, surface, aux, alt, tables, z_out, inter_out, intra_out, fields
):
    slope_lon, slope_lat, grad_lon, grad_lat = fields
    misfit = slopes_and_misfit(surface, aux, alt, tables, slope_lon, slope_lat)
    for ref, index, rows in image_tiles(kept, received, halo):
        albedo, lon, lat = ref[(ALBEDO, *index)], slope_lon[rows], slope_lat[rows]
        inverse, shade = shades(albedo, lon, lat)
        sums = None
        for k in range(IMAGES):
            lit = weight[k : k + 1] * ref[(IMAGES + k, *index)]
            pull, norm = image_term(coef, k, ref[(k, *index)], lit, *shade, lon, lat)
            sums = add_image(sums, coef, k, pull, norm)
        grad_lon[rows], grad_lat[rows] = gradients(albedo, inverse, lon, lat, sums)
    contribute(surface, aux, misfit, grad_lon, grad_lat, tables, z_out, inter_out, intra_out)


def first_kernel(coef, counts, kept, received, halo, z, inter, intra, aux, *refs):
    tables, (z_out, inter_out, intra_out, alt_out, weight_out), fields = refs[:5], refs[5:10], refs[10:]
    weight = image_weights(counts)
    weight_out[...] = weight
    above, below = arrived(inter, intra)
    alt = jnp.concatenate([aux[:, 0:8], below[:, 0:8]], axis=1)
    alt_out[...] = alt
    below = jnp.concatenate([jnp.zeros((TILES, RAD, LANES), F32), below[:, RAD:]], axis=1)
    surface = [z[j] + jnp.concatenate([above[j], below[j]], axis=0) for j in range(TILES)]
    surface_step(
        coef, weight, kept, received, halo, surface, aux, alt, tables, z_out, inter_out, intra_out, fields
    )


def step_kernel(coef, weight, kept, received, halo, z, inter, intra, aux, alt, *refs):
    tables, (z_out, inter_out, intra_out), fields = refs[:5], refs[5:8], refs[8:]
    above, below = arrived(inter, intra)
    surface = [z[j] + jnp.concatenate([above[j], below[j]], axis=0) for j in range(TILES)]
    surface_step(
        coef, weight[...], kept, received, halo, surface, aux, alt, tables, z_out, inter_out, intra_out, fields
    )


def end_kernel(z, inter, intra, kept, sent):
    half, core = place()
    for ref, side in ((kept, core), (sent, 1 - core)):
        for t in range(2):
            at = own_tile(half, side, t)
            above = jnp.where(core == 0, inter[at], intra[at])
            below = jnp.where(core == 0, intra[at], inter[at])
            cols = slice(t * LANES, (t + 1) * LANES)
            ref[0:RAD, cols] = z[at, RAD : 2 * RAD] + above[RAD:]
            ref[RAD:STRIP, cols] = z[at, 2 * RAD : RAD + STRIP] + below[0:RAD]


def place_kernel(mine, other, out):
    core = place()[1]
    out[pl.ds(pl.multiple_of(core * STRIP, STRIP), STRIP)] = mine[...]
    out[pl.ds(pl.multiple_of((1 - core) * STRIP, STRIP), STRIP)] = other[...]


def f32(*shape):
    return jax.ShapeDtypeStruct(shape, F32)


def call(kernel, out_shape, *args, scratch=()):
    scalars = kernel in (first_kernel, step_kernel)
    return pl.pallas_call(
        kernel,
        out_shape=out_shape,
        in_specs=[SMEM if scalars and i == 0 else VMEM for i in range(len(args))],
        out_specs=jax.tree.map(lambda _: VMEM, out_shape),
        scratch_shapes=list(scratch),
        compiler_params=PARAMS,
    )(*args)


def per_device(height, albedo, images, lit_mask, lit_count, geometry, owner_column, altimetry):
    lon_count, lat_count = lax.axis_size("lon"), lax.axis_size("lat")
    axes = ("lon", "lat")
    sites = [(a, b) for a in range(lon_count) for b in range(lat_count)]

    def index(a, b):
        return (a % lon_count) * lat_count + b

    across_cores = [(index(a, b), index(a, b ^ 1)) for a, b in sites]
    across_halves = [(index(a, b), index(a, b ^ 2)) for a, b in sites]
    across_strips = [(index(a, b), index(a + 2 * (b % 2) - 1, b ^ 1)) for a, b in sites]

    def exchange(inter, intra):
        return lax.ppermute(inter, axes, across_strips), lax.ppermute(intra, axes, across_cores)

    sun_lon, sun_lat, sun_up, view = (geometry[:, i] for i in range(4))
    coef = jnp.stack(
        [
            SHARPNESS * sun_lon,
            SHARPNESS * sun_lat,
            SHARPNESS * sun_up,
            SHARPNESS * view,
            (LUNAR_MIX * SHARPNESS * SHARPNESS) * view,
            -sun_lon,
            -sun_lat,
        ],
        axis=1,
    )

    expand = np.arange(altimetry.shape[1])[:, None] == np.arange(2 * LANES)[None, :] // OWN
    expand = jnp.asarray(np.concatenate([expand] * 3, axis=0), BF16)
    count = lit_count.reshape(1, IMAGES)
    inputs = (images, lit_mask, height, albedo, owner_column, altimetry, count, expand)
    cut = [(IMAGES, STRIP, 2 * LANES)] * 2 + [(STRIP, 2 * LANES)] * 2 + [(8, 2 * LANES)]
    cut += [a.shape for a in inputs[len(cut) :]]
    fields = f32(FIELDS, 2, STRIP, LANES)
    sent = pl.pallas_call(
        send_kernel,
        out_shape=fields,
        in_specs=[pl.BlockSpec(memory_space=pltpu.HBM)] * len(inputs),
        out_specs=VMEM,
        scratch_shapes=[pltpu.VMEM(shape, a.dtype) for shape, a in zip(cut, inputs)]
        + [pltpu.SemaphoreType.DMA((len(inputs),))],
        compiler_params=LARGE,
    )(*inputs)
    received = lax.ppermute(sent, axes, across_cores)
    kept = call(keep_kernel, fields, *inputs, sent[:1, :1, :8])
    near_small = call(near_small_kernel, f32(2, STRIP, LANES), kept, received)
    halo_small = lax.ppermute(near_small, axes, across_halves)
    near = call(near_kernel, f32(HEIGHT, STRIP, LANES), kept, received, near_small)
    halo = lax.ppermute(near, axes, across_halves)
    counts = call(
        count_kernel, f32(len(sites) // 2, 1, LANES), kept[AUX:], received[AUX:], near[:1, :8]
    )
    same_core = [[index(a, b) for a, b in sites if b % 2 == core] for core in range(2)]
    counts = lax.all_to_all(counts, axes, 0, 0, axis_index_groups=same_core)
    message = f32(TILES, STRIP, LANES)
    window = f32(TILES, EXT, LANES)
    rows_of_bins = f32(TILES, BINS, LANES)
    z, aux, inter, intra = call(
        begin_kernel, (window, rows_of_bins, message, message), kept, received, halo_small
    )
    inter, intra = exchange(inter, intra)
    tables = constants()
    scratch = [pltpu.VMEM((TILES * STRIP, LANES), F32)] * 4
    z, inter, intra, alt, weight = call(
        first_kernel,
        (window, message, message, rows_of_bins, f32(BINS, LANES)),
        coef, counts, kept, received, halo, z, inter, intra, aux, *tables,
        scratch=scratch,
    )
    for _ in range(ITERS - 1):
        inter, intra = exchange(inter, intra)
        z, inter, intra = call(
            step_kernel,
            (window, message, message),
            coef, weight, kept, received, halo, z, inter, intra, aux, alt, *tables,
            scratch=scratch,
        )
    inter, intra = exchange(inter, intra)
    half_out = f32(STRIP, 2 * LANES)
    mine, other = call(end_kernel, (half_out, half_out), z, inter, intra)
    other = lax.ppermute(other, axes, across_cores)
    return call(place_kernel, f32(2 * STRIP, 2 * LANES), mine, other)


def solution(mesh):
    return jax.shard_map(
        per_device,
        mesh=mesh,
        in_specs=(
            P("lon", "lat"),
            P("lon", "lat"),
            P(None, "lon", "lat"),
            P(None, "lon", "lat"),
            P(None, "lon", "lat"),
            P(),
            P("lon", "lat"),
            P("lon", "lat"),
        ),
        out_specs=P("lon", "lat"),
        check_vma=False,
    )
```

time: 76.3 us -> 74.2 us (0.972)
  waiting for transfers between devices: 19 us -> 8.23 us
  starting transfers between devices: 42.4 us -> 50.4 us
    all_to_all x1, starting transfers between devices: 5.97 us -> 13.8 us  [per_device(): counts = lax.all_to_all(counts, axes, 0, 0, axis_index_groups=same_core)]
    all_to_all x1, waiting for transfers between devices: 9.08 us -> 3.24 us  [per_device(): counts = lax.all_to_all(counts, axes, 0, 0, axis_index_groups=same_core)]
    ppermute x1, waiting for transfers between devices: 3.07 us -> 0.01 us  [per_device(): halo_small = lax.ppermute(near_small, axes, across_halves)]
    ppermute x1, waiting for transfers between devices: 2.06 us -> 0.53 us  [per_device(): received = lax.ppermute(sent, axes, across_cores)]
    ppermute x4, starting transfers between devices: 16.4 us -> 17.9 us  [exchange(): lax.ppermute(intra, axes, across_cores)]
    ppermute x1, starting transfers between devices: 7.15 us -> 5.67 us  [per_device(): other = lax.ppermute(other, axes, across_cores)]
    ppermute x4, waiting for transfers between devices: 2.13 us -> 0.87 us  [exchange(): lax.ppermute(inter, axes, across_strips)]
    ppermute x1, starting transfers between devices: 1 us -> 2.03 us  [per_device(): halo = lax.ppermute(near, axes, across_halves)]
  transfers between devices with their start and end apart: 13 -> 13, of which waited for: 7 -> 8; matrix products, arithmetic and copies ran while one was open for 1% -> 2% of each run, Pallas kernels for 1% -> 1%
where the time goes in v3:
time: 74.2 us; the launch traced here: 73.9 us
  starting transfers between devices  50.4 us (68%)
  Pallas kernels  13.4 us (18%)
  waiting for transfers between devices  8.23 us (11%)
  local copies, waits for them, and re-layouts  1.75 us (2%)
    ppermute x4, starting transfers between devices, exchange(): lax.ppermute(intra, axes, across_cores)  17.9 us
    all_to_all x1, starting transfers between devices, per_device(): counts = lax.all_to_all(counts, axes, 0, 0, axis_index_groups=same_core)  13.8 us
    pallas_call x10, Pallas kernels, call(): pl.pallas_call(kernel, out_shape=out_shape, in_specs=[SMEM if scalars and...  10.9 us
    ppermute x4, starting transfers between devices, exchange(): lax.ppermute(inter, axes, across_strips)  6.67 us
    ppermute x1, starting transfers between devices, per_device(): other = lax.ppermute(other, axes, across_cores)  5.67 us
    ppermute x1, starting transfers between devices, per_device(): received = lax.ppermute(sent, axes, across_cores)  3.32 us
    all_to_all x1, waiting for transfers between devices, per_device(): counts = lax.all_to_all(counts, axes, 0, 0, axis_index_groups=same_core)  3.24 us
    ppermute x4, waiting for transfers between devices, exchange(): lax.ppermute(intra, axes, across_cores)  2.72 us
  transfers between devices with their start and end apart: 13, of which 8 were waited for; matrix products, arithmetic and copies ran while one was open for 2% of the time, Pallas kernels for 1%

profile of v3, /device:TPU:1, one launch (start us, length us, event | category | flops | bytes accessed | tf_op | source)
XLA Modules:
  0.0 73.9 jit_solution(16369921205795202329)
XLA Ops:
  0.0 0.0 copy-start.8
  0.0 2.4 %shard_map.136 = f32[27,2,32,128]{3,2,1,0:T(8,128)} custom-call(bf16[12,64,256]{2,1,0:T(8,128)(2,1)} %images.1, s32[12,64,256]{2,1,0:T(8,128)} %lit_mask.1, f32[64,256]{1,0:T(8,128)} %height.1, f32[64,256]{1,0:T(8,128)} %albedo.1, s32[64,256]{1,0:T(8,128)} %owner.1, f32[16,64]{1,0:T(8,128)} %altimetry.1, s32[1,12]{1,0:T(1,128)} %bitcast.1, ...), custom_call_target="tpu_custom_call" | custom-call | tf_op jit(solution)/shard_map/pallas_call | solution.py:461
  2.5 0.0 copy-start.13
  2.5 3.3 %collective-permute-start = (f32[27,2,32,128]{3,2,1,0:T(8,128)}, f32[27,2,32,128]{3,2,1,0:T(8,128)S(1)}, u32[]{:S(2)}, u32[]{:S(2)}) collective-permute-start(f32[27,2,32,128]{3,2,1,0:T(8,128)} %shard_map.136), channel_id=1, source_target_pairs={{0,1},{1,0},{2,3},{3,2},{4,5},{5,4},{6,7},{7,6},{8,9},{9,8},{10,11... | collective-permute-start | bytes 2654216 | tf_op jit(solution)/shard_map/ppermute | solution.py:470
  5.8 0.7 slice.32.sent
  6.5 0.1 copy.19
  6.6 0.1 copy.22
  6.7 0.1 copy.20
  6.8 0.0 copy-done.5
  6.8 0.5 copy-done.11
  7.3 0.1 copy-done.12
  7.4 0.2 shard_map.137.kept
  7.5 0.5 collective-permute-done.received
  8.1 1.0 %collective-permute-start.2 = (f32[2,32,128]{2,1,0:T(8,128)S(1)}, f32[2,32,128]{2,1,0:T(8,128)S(1)}, u32[]{:S(2)}, u32[]{:S(2)}) collective-permute-start(f32[2,32,128]{2,1,0:T(8,128)S(1)} %shard_map.138.near_small), channel_id=1, source_target_pairs={{0,2},{1,3},{2,0},{3,1},{4,6},{5,7},{6,4},{7,5},{8,10},{9,11},{10,... | collective-permute-start | bytes 98312 | tf_op jit(solution)/shard_map/ppermute | solution.py:473
  9.1 2.0 %collective-permute-start.1 = (f32[25,32,128]{2,1,0:T(8,128)S(1)}, f32[25,32,128]{2,1,0:T(8,128)S(1)}, u32[]{:S(2)}, u32[]{:S(2)}) collective-permute-start(f32[25,32,128]{2,1,0:T(8,128)S(1)} %shard_map.139), channel_id=1, source_target_pairs={{0,2},{1,3},{2,0},{3,1},{4,6},{5,7},{6,4},{7,5},{8,10},{9,11},{10,... | collective-permute-start | bytes 1228808 | tf_op jit(solution)/shard_map/ppermute | solution.py:475
  11.2 0.1 copy.21
  11.3 0.7 shard_map.140
  11.9 13.8 %all-to-all-start = ((f32[128,1,128]{2,1,0:T(1,128)}), f32[128,1,128]{2,1,0:T(1,128)S(1)}, u32[]{:S(2)}, u32[]{:S(2)}) async-start(f32[128,1,128]{2,1,0:T(1,128)} %shard_map.140), calls=%async_computation | async-start | bytes 131072 | tf_op jit(solution)/shard_map/all_to_all | solution.py:480
  25.7 0.0 collective-permute-done.2.halo_small
  25.8 0.0 copy-start.3
  25.8 0.0 copy-start.4
  25.8 0.0 copy-start.7
  25.8 0.0 copy-start.2
  25.8 2.0 %collective-permute-start.3 = (f32[5,32,128]{2,1,0:T(8,128)S(1)}, f32[5,32,128]{2,1,0:T(8,128)S(1)}, u32[]{:S(2)}, u32[]{:S(2)}) collective-permute-start(f32[5,32,128]{2,1,0:T(8,128)S(1)} %get-tuple-element.23), channel_id=1, source_target_pairs={{0,253},{1,4},{2,255},{3,6},{4,1},{5,8},{6,3},{7,10},{8,5},{9,12},... | collective-permute-start | bytes 245768 | tf_op jit(solution)/shard_map/ppermute | solution.py:438
  27.9 4.0 %collective-permute-start.4 = (f32[5,32,128]{2,1,0:T(8,128)S(1)}, f32[5,32,128]{2,1,0:T(8,128)S(1)}, u32[]{:S(2)}, u32[]{:S(2)}) collective-permute-start(f32[5,32,128]{2,1,0:T(8,128)S(1)} %get-tuple-element.24), channel_id=1, source_target_pairs={{0,1},{1,0},{2,3},{3,2},{4,5},{5,4},{6,7},{7,6},{8,9},{9,8},{10,11... | collective-permute-start | bytes 245768 | tf_op jit(solution)/shard_map/ppermute | solution.py:438
  31.9 0.1 stack.2.coef
  32.0 0.0 collective-permute-done.3.inter
  32.0 0.8 %collective-permute-done.4.intra = f32[5,32,128]{2,1,0:T(8,128)S(1)} collective-permute-done((f32[5,32,128]{2,1,0:T(8,128)S(1)}, f32[5,32,128]{2,1,0:T(8,128)S(1)}, u32[]{:S(2)}, u32[]{:S(2)}) %collective-permute-start.4) | collective-permute-done | bytes 81952 | tf_op jit(solution)/shard_map/ppermute | solution.py:438
  32.8 3.2 %all-to-all-done.counts = f32[128,1,128]{2,1,0:T(1,128)S(1)} async-done(((f32[128,1,128]{2,1,0:T(1,128)}), f32[128,1,128]{2,1,0:T(1,128)S(1)}, u32[]{:S(2)}, u32[]{:S(2)}) %all-to-all-start) | async-done | bytes 65568 | tf_op jit(solution)/shard_map/all_to_all | solution.py:480
  36.0 0.0 collective-permute-done.1.halo
  36.1 3.3 %shard_map.142 = (f32[5,64,128]{2,1,0:T(8,128)S(1)}, f32[5,32,128]{2,1,0:T(8,128)S(1)}, f32[5,32,128]{2,1,0:T(8,128)S(1)}, f32[5,16,128]{2,1,0:T(8,128)S(1)}, f32[16,128]{1,0:T(8,128)S(1)}) custom-call(f32[12,7]{1,0:T(8,128)S(1)} %stack.2.coef, f32[128,1,128]{2,1,0:T(1,128)S(1)} %all-to-all-done.counts, f32[27,2,32,128]{3,2,1,0:T(8,128)S(1)} %shard_map.137.kept, ...), custom_call_target="tpu_custom_call" | custom-call | tf_op jit(solution)/shard_map/pallas_call | solution.py:415
  39.4 2.8 %collective-permute-start.5 = (f32[5,32,128]{2,1,0:T(8,128)S(1)}, f32[5,32,128]{2,1,0:T(8,128)S(1)}, u32[]{:S(2)}, u32[]{:S(2)}) collective-permute-start(f32[5,32,128]{2,1,0:T(8,128)S(1)} %get-tuple-element.28), channel_id=1, source_target_pairs={{0,253},{1,4},{2,255},{3,6},{4,1},{5,8},{6,3},{7,10},{8,5},{9,12},... | collective-permute-start | bytes 245768 | tf_op jit(solution)/shard_map/ppermute | solution.py:438
  42.1 1.3 %collective-permute-start.6 = (f32[5,32,128]{2,1,0:T(8,128)S(1)}, f32[5,32,128]{2,1,0:T(8,128)S(1)}, u32[]{:S(2)}, u32[]{:S(2)}) collective-permute-start(f32[5,32,128]{2,1,0:T(8,128)S(1)} %get-tuple-element.29), channel_id=1, source_target_pairs={{0,1},{1,0},{2,3},{3,2},{4,5},{5,4},{6,7},{7,6},{8,9},{9,8},{10,11... | collective-permute-start | bytes 245768 | tf_op jit(solution)/shard_map/ppermute | solution.py:438
  43.4 0.9 %collective-permute-done.5.inter = f32[5,32,128]{2,1,0:T(8,128)S(1)} collective-permute-done((f32[5,32,128]{2,1,0:T(8,128)S(1)}, f32[5,32,128]{2,1,0:T(8,128)S(1)}, u32[]{:S(2)}, u32[]{:S(2)}) %collective-permute-start.5) | collective-permute-done | bytes 81952 | tf_op jit(solution)/shard_map/ppermute | solution.py:438
  44.3 0.1 collective-permute-done.6.intra
  44.3 3.0 %shard_map.143 = (f32[5,64,128]{2,1,0:T(8,128)S(1)}, f32[5,32,128]{2,1,0:T(8,128)S(1)}, f32[5,32,128]{2,1,0:T(8,128)S(1)}) custom-call(f32[12,7]{1,0:T(8,128)S(1)} %stack.2.coef, f32[16,128]{1,0:T(8,128)S(1)} %get-tuple-element.26.weight, f32[27,2,32,128]{3,2,1,0:T(8,128)S(1)} %shard_map.137.kept, f32[27,2,32,128]{3,2,1,0:T(8,128)S(1)} %collective-permute-done.received, ...), custom_call_target="tpu_custom_call" | custom-call | tf_op jit(solution)/shard_map/pallas_call | solution.py:415
  47.4 1.8 %collective-permute-start.7 = (f32[5,32,128]{2,1,0:T(8,128)S(1)}, f32[5,32,128]{2,1,0:T(8,128)S(1)}, u32[]{:S(2)}, u32[]{:S(2)}) collective-permute-start(f32[5,32,128]{2,1,0:T(8,128)S(1)} %get-tuple-element.32), channel_id=1, source_target_pairs={{0,253},{1,4},{2,255},{3,6},{4,1},{5,8},{6,3},{7,10},{8,5},{9,12},... | collective-permute-start | bytes 245768 | tf_op jit(solution)/shard_map/ppermute | solution.py:438
  49.1 5.5 %collective-permute-start.8 = (f32[5,32,128]{2,1,0:T(8,128)S(1)}, f32[5,32,128]{2,1,0:T(8,128)S(1)}, u32[]{:S(2)}, u32[]{:S(2)}) collective-permute-start(f32[5,32,128]{2,1,0:T(8,128)S(1)} %get-tuple-element.33), channel_id=1, source_target_pairs={{0,1},{1,0},{2,3},{3,2},{4,5},{5,4},{6,7},{7,6},{8,9},{9,8},{10,11... | collective-permute-start | bytes 245768 | tf_op jit(solution)/shard_map/ppermute | solution.py:438
  54.6 0.0 collective-permute-done.7.inter
  54.6 0.9 %collective-permute-done.8.intra = f32[5,32,128]{2,1,0:T(8,128)S(1)} collective-permute-done((f32[5,32,128]{2,1,0:T(8,128)S(1)}, f32[5,32,128]{2,1,0:T(8,128)S(1)}, u32[]{:S(2)}, u32[]{:S(2)}) %collective-permute-start.8) | collective-permute-done | bytes 81952 | tf_op jit(solution)/shard_map/ppermute | solution.py:438
  55.5 3.0 %shard_map.144 = (f32[5,64,128]{2,1,0:T(8,128)S(1)}, f32[5,32,128]{2,1,0:T(8,128)S(1)}, f32[5,32,128]{2,1,0:T(8,128)S(1)}) custom-call(f32[12,7]{1,0:T(8,128)S(1)} %stack.2.coef, f32[16,128]{1,0:T(8,128)S(1)} %get-tuple-element.26.weight, f32[27,2,32,128]{3,2,1,0:T(8,128)S(1)} %shard_map.137.kept, f32[27,2,32,128]{3,2,1,0:T(8,128)S(1)} %collective-permute-done.received, ...), custom_call_target="tpu_custom_call" | custom-call | tf_op jit(solution)/shard_map/pallas_call | solution.py:415
  58.6 0.1 collective-permute-start.9
  58.7 7.2 %collective-permute-start.10 = (f32[5,32,128]{2,1,0:T(8,128)S(1)}, f32[5,32,128]{2,1,0:T(8,128)S(1)}, u32[]{:S(2)}, u32[]{:S(2)}) collective-permute-start(f32[5,32,128]{2,1,0:T(8,128)S(1)} %get-tuple-element.36), channel_id=1, source_target_pairs={{0,1},{1,0},{2,3},{3,2},{4,5},{5,4},{6,7},{7,6},{8,9},{9,8},{10,11... | collective-permute-start | bytes 245768 | tf_op jit(solution)/shard_map/ppermute | solution.py:438
  65.8 0.0 collective-permute-done.9.inter
  65.8 0.9 %collective-permute-done.10.intra = f32[5,32,128]{2,1,0:T(8,128)S(1)} collective-permute-done((f32[5,32,128]{2,1,0:T(8,128)S(1)}, f32[5,32,128]{2,1,0:T(8,128)S(1)}, u32[]{:S(2)}, u32[]{:S(2)}) %collective-permute-start.10) | collective-permute-done | bytes 81952 | tf_op jit(solution)/shard_map/ppermute | solution.py:438
  66.8 5.7 %collective-permute-start.11 = (f32[32,256]{1,0:T(8,128)S(1)}, f32[32,256]{1,0:T(8,128)S(1)}, u32[]{:S(2)}, u32[]{:S(2)}) collective-permute-start(f32[32,256]{1,0:T(8,128)S(1)} %get-tuple-element.38), channel_id=1, source_target_pairs={{0,1},{1,0},{2,3},{3,2},{4,5},{5,4},{6,7},{7,6},{8,9},{9,8},{10,11... | collective-permute-start | bytes 98312 | tf_op jit(solution)/shard_map/ppermute | solution.py:507
  72.4 0.9 %collective-permute-done.11.other = f32[32,256]{1,0:T(8,128)S(1)} collective-permute-done((f32[32,256]{1,0:T(8,128)S(1)}, f32[32,256]{1,0:T(8,128)S(1)}, u32[]{:S(2)}, u32[]{:S(2)}) %collective-permute-start.11) | collective-permute-done | bytes 32800 | tf_op jit(solution)/shard_map/ppermute | solution.py:507
  73.3 0.6 shard_map.146
  (30 shorter events, 0.1 us)
Async XLA Ops:
  0.0 6.8 %copy-start = (s32[12,64,256]{2,1,0:T(8,128)S(1)}, s32[12,64,256]{2,1,0:T(8,128)}, u32[]{:S(2)}) copy-start(s32[12,64,256]{2,1,0:T(8,128)} %lit_mask.1) | copy-start | bytes 2359300
  0.0 6.8 %copy-start.1 = (bf16[12,64,256]{2,1,0:T(8,128)(2,1)S(1)}, bf16[12,64,256]{2,1,0:T(8,128)(2,1)}, u32[]{:S(2)}) copy-start(bf16[12,64,256]{2,1,0:T(8,128)(2,1)} %images.1) | copy-start | bytes 1179652
  0.0 6.8 %copy-start.5 = (bf16[192,256]{1,0:T(8,128)(2,1)S(1)}, bf16[192,256]{1,0:T(8,128)(2,1)}, u32[]{:S(2)}) copy-start(bf16[192,256]{1,0:T(8,128)(2,1)} %constant.16.clone.expand_hbm.expand) | copy-start | bytes 294916
  0.0 6.8 %copy-start.8 = (f32[64,256]{1,0:T(8,128)S(1)}, f32[64,256]{1,0:T(8,128)}, u32[]{:S(2)}) copy-start(f32[64,256]{1,0:T(8,128)} %height.1) | copy-start | bytes 196612
  0.0 6.8 %copy-start.9 = (f32[64,256]{1,0:T(8,128)S(1)}, f32[64,256]{1,0:T(8,128)}, u32[]{:S(2)}) copy-start(f32[64,256]{1,0:T(8,128)} %albedo.1) | copy-start | bytes 196612
  0.0 6.8 %copy-start.10 = (s32[64,256]{1,0:T(8,128)S(1)}, s32[64,256]{1,0:T(8,128)}, u32[]{:S(2)}) copy-start(s32[64,256]{1,0:T(8,128)} %owner.1) | copy-start | bytes 196612
  2.5 4.0 %copy-start.13 = (f32[12,4]{0,1:T(4,128)S(1)}, f32[12,4]{0,1:T(4,128)}, u32[]{:S(2)}) copy-start(f32[12,4]{0,1:T(4,128)} %param.19) | copy-start | bytes 580
  2.5 5.6 %collective-permute-start = (f32[27,2,32,128]{3,2,1,0:T(8,128)}, f32[27,2,32,128]{3,2,1,0:T(8,128)S(1)}, u32[]{:S(2)}, u32[]{:S(2)}) collective-permute-start(f32[27,2,32,128]{3,2,1,0:T(8,128)} %shard_map.136), channel_id=1, source_target_pairs={{0,1},{1,0},{2,3},{3,2},{4,5},{5,4},{6,7},{7,6},{8,9},{9,8},{10,11... | collective-permute-start | bytes 2654216 | tf_op jit(solution)/shard_map/ppermute | solution.py:470
  6.6 0.7 copy-start.11
  6.7 0.7 copy-start.12
  8.1 17.7 %collective-permute-start.2 = (f32[2,32,128]{2,1,0:T(8,128)S(1)}, f32[2,32,128]{2,1,0:T(8,128)S(1)}, u32[]{:S(2)}, u32[]{:S(2)}) collective-permute-start(f32[2,32,128]{2,1,0:T(8,128)S(1)} %shard_map.138.near_small), channel_id=1, source_target_pairs={{0,2},{1,3},{2,0},{3,1},{4,6},{5,7},{6,4},{7,5},{8,10},{9,11},{10,... | collective-permute-start | bytes 98312 | tf_op jit(solution)/shard_map/ppermute | solution.py:473
  9.1 26.9 %collective-permute-start.1 = (f32[25,32,128]{2,1,0:T(8,128)S(1)}, f32[25,32,128]{2,1,0:T(8,128)S(1)}, u32[]{:S(2)}, u32[]{:S(2)}) collective-permute-start(f32[25,32,128]{2,1,0:T(8,128)S(1)} %shard_map.139), channel_id=1, source_target_pairs={{0,2},{1,3},{2,0},{3,1},{4,6},{5,7},{6,4},{7,5},{8,10},{9,11},{10,... | collective-permute-start | bytes 1228808 | tf_op jit(solution)/shard_map/ppermute | solution.py:475
  11.9 24.1 %all-to-all-start = ((f32[128,1,128]{2,1,0:T(1,128)}), f32[128,1,128]{2,1,0:T(1,128)S(1)}, u32[]{:S(2)}, u32[]{:S(2)}) async-start(f32[128,1,128]{2,1,0:T(1,128)} %shard_map.140), calls=%async_computation | async-start | bytes 131072 | tf_op jit(solution)/shard_map/all_to_all | solution.py:480
  25.8 10.3 %copy-start.3 = (bf16[256,128]{1,0:T(8,128)(2,1)S(1)}, bf16[256,128]{1,0:T(8,128)(2,1)}, u32[]{:S(2)}) copy-start(bf16[256,128]{1,0:T(8,128)(2,1)} %constant.19.clone.refs_2_) | copy-start | bytes 196612
  25.8 10.3 %copy-start.4 = (bf16[256,128]{1,0:T(8,128)(2,1)S(1)}, bf16[256,128]{1,0:T(8,128)(2,1)}, u32[]{:S(2)}) copy-start(bf16[256,128]{1,0:T(8,128)(2,1)} %constant.20.clone.refs_3_) | copy-start | bytes 196612
  25.8 10.3 %copy-start.7 = (bf16[128,128]{1,0:T(8,128)(2,1)S(1)}, bf16[128,128]{1,0:T(8,128)(2,1)}, u32[]{:S(2)}) copy-start(bf16[128,128]{1,0:T(8,128)(2,1)} %constant.21.clone.refs_4_) | copy-start | bytes 98308
  25.8 10.2 %copy-start.2 = (bf16[128,192]{1,0:T(8,128)(2,1)S(1)}, bf16[128,192]{1,0:T(8,128)(2,1)}, u32[]{:S(2)}) copy-start(bf16[128,192]{1,0:T(8,128)(2,1)} %constant.17.clone.refs_0_) | copy-start | bytes 147460
  25.8 6.1 %collective-permute-start.3 = (f32[5,32,128]{2,1,0:T(8,128)S(1)}, f32[5,32,128]{2,1,0:T(8,128)S(1)}, u32[]{:S(2)}, u32[]{:S(2)}) collective-permute-start(f32[5,32,128]{2,1,0:T(8,128)S(1)} %get-tuple-element.23), channel_id=1, source_target_pairs={{0,253},{1,4},{2,255},{3,6},{4,1},{5,8},{6,3},{7,10},{8,5},{9,12},... | collective-permute-start | bytes 245768 | tf_op jit(solution)/shard_map/ppermute | solution.py:438
  27.9 4.9 %collective-permute-start.4 = (f32[5,32,128]{2,1,0:T(8,128)S(1)}, f32[5,32,128]{2,1,0:T(8,128)S(1)}, u32[]{:S(2)}, u32[]{:S(2)}) collective-permute-start(f32[5,32,128]{2,1,0:T(8,128)S(1)} %get-tuple-element.24), channel_id=1, source_target_pairs={{0,1},{1,0},{2,3},{3,2},{4,5},{5,4},{6,7},{7,6},{8,9},{9,8},{10,11... | collective-permute-start | bytes 245768 | tf_op jit(solution)/shard_map/ppermute | solution.py:438
  31.9 4.2 %copy-start.6 = (bf16[64,256]{1,0:T(8,128)(2,1)S(1)}, bf16[64,256]{1,0:T(8,128)(2,1)}, u32[]{:S(2)}) copy-start(bf16[64,256]{1,0:T(8,128)(2,1)} %constant.18.clone.refs_1_) | copy-start | bytes 98308
  39.4 4.9 %collective-permute-start.5 = (f32[5,32,128]{2,1,0:T(8,128)S(1)}, f32[5,32,128]{2,1,0:T(8,128)S(1)}, u32[]{:S(2)}, u32[]{:S(2)}) collective-permute-start(f32[5,32,128]{2,1,0:T(8,128)S(1)} %get-tuple-element.28), channel_id=1, source_target_pairs={{0,253},{1,4},{2,255},{3,6},{4,1},{5,8},{6,3},{7,10},{8,5},{9,12},... | collective-permute-start | bytes 245768 | tf_op jit(solution)/shard_map/ppermute | solution.py:438
  42.1 2.2 %collective-permute-start.6 = (f32[5,32,128]{2,1,0:T(8,128)S(1)}, f32[5,32,128]{2,1,0:T(8,128)S(1)}, u32[]{:S(2)}, u32[]{:S(2)}) collective-permute-start(f32[5,32,128]{2,1,0:T(8,128)S(1)} %get-tuple-element.29), channel_id=1, source_target_pairs={{0,1},{1,0},{2,3},{3,2},{4,5},{5,4},{6,7},{7,6},{8,9},{9,8},{10,11... | collective-permute-start | bytes 245768 | tf_op jit(solution)/shard_map/ppermute | solution.py:438
  47.4 7.3 %collective-permute-start.7 = (f32[5,32,128]{2,1,0:T(8,128)S(1)}, f32[5,32,128]{2,1,0:T(8,128)S(1)}, u32[]{:S(2)}, u32[]{:S(2)}) collective-permute-start(f32[5,32,128]{2,1,0:T(8,128)S(1)} %get-tuple-element.32), channel_id=1, source_target_pairs={{0,253},{1,4},{2,255},{3,6},{4,1},{5,8},{6,3},{7,10},{8,5},{9,12},... | collective-permute-start | bytes 245768 | tf_op jit(solution)/shard_map/ppermute | solution.py:438
  49.1 6.4 %collective-permute-start.8 = (f32[5,32,128]{2,1,0:T(8,128)S(1)}, f32[5,32,128]{2,1,0:T(8,128)S(1)}, u32[]{:S(2)}, u32[]{:S(2)}) collective-permute-start(f32[5,32,128]{2,1,0:T(8,128)S(1)} %get-tuple-element.33), channel_id=1, source_target_pairs={{0,1},{1,0},{2,3},{3,2},{4,5},{5,4},{6,7},{7,6},{8,9},{9,8},{10,11... | collective-permute-start | bytes 245768 | tf_op jit(solution)/shard_map/ppermute | solution.py:438
  58.6 7.3 %collective-permute-start.9 = (f32[5,32,128]{2,1,0:T(8,128)S(1)}, f32[5,32,128]{2,1,0:T(8,128)S(1)}, u32[]{:S(2)}, u32[]{:S(2)}) collective-permute-start(f32[5,32,128]{2,1,0:T(8,128)S(1)} %get-tuple-element.35), channel_id=1, source_target_pairs={{0,253},{1,4},{2,255},{3,6},{4,1},{5,8},{6,3},{7,10},{8,5},{9,12},... | collective-permute-start | bytes 245768 | tf_op jit(solution)/shard_map/ppermute | solution.py:438
  58.7 8.1 %collective-permute-start.10 = (f32[5,32,128]{2,1,0:T(8,128)S(1)}, f32[5,32,128]{2,1,0:T(8,128)S(1)}, u32[]{:S(2)}, u32[]{:S(2)}) collective-permute-start(f32[5,32,128]{2,1,0:T(8,128)S(1)} %get-tuple-element.36), channel_id=1, source_target_pairs={{0,1},{1,0},{2,3},{3,2},{4,5},{5,4},{6,7},{7,6},{8,9},{9,8},{10,11... | collective-permute-start | bytes 245768 | tf_op jit(solution)/shard_map/ppermute | solution.py:438
  66.8 6.5 %collective-permute-start.11 = (f32[32,256]{1,0:T(8,128)S(1)}, f32[32,256]{1,0:T(8,128)S(1)}, u32[]{:S(2)}, u32[]{:S(2)}) collective-permute-start(f32[32,256]{1,0:T(8,128)S(1)} %get-tuple-element.38), channel_id=1, source_target_pairs={{0,1},{1,0},{2,3},{3,2},{4,5},{5,4},{6,7},{7,6},{8,9},{9,8},{10,11... | collective-permute-start | bytes 98312 | tf_op jit(solution)/shard_map/ppermute | solution.py:507

commit v4 on v3

--- a/solution.py
+++ b/solution.py
@@ -27,6 +27,7 @@
 HEIGHT = ALBEDO + 1
 AUX = HEIGHT + 1
 BINS = 16
+LINE = 8
 DENOM = float(RAD * (RAD + 1) * (2 * RAD + 1)) / 3.0
 TAP_SCALE = 1.0 / (DENOM * (2 * RAD + 1))
 F32 = jnp.float32
@@ -163,7 +164,7 @@
         sent[HEIGHT, t] = height[:, cols]
 
 
-def keep_kernel(images, lit_mask, height, albedo, owner, altimetry, count, expand, sent, kept):
+def keep_kernel(images, lit_mask, height, albedo, owner, altimetry, count, expand, kept):
     core = place()[1]
     rows = pl.ds(pl.multiple_of(core * STRIP, STRIP), STRIP)
     aux_fields(kept, core, owner, altimetry, count, expand)
@@ -194,9 +195,13 @@
         near[...] = received[0:HEIGHT, 1 - half]
 
 
-def count_kernel(kept, received, near, counts):
-    total = kept[0, 0, 16:17] + received[0, 0, 16:17]
+def count_kernel(kept, received, near_small, counts):
+    total = kept[AUX, 0, 16:17] + received[AUX, 0, 16:17]
     counts[...] = jnp.broadcast_to(total[None], counts.shape)
+
+
+def line_kernel(line, inter, counts):
+    counts[...] = jnp.broadcast_to(jnp.sum(line[...], axis=0, keepdims=True), counts.shape)
 
 
 def route(core, up, down, inter, intra):
@@ -232,20 +237,13 @@
     return dot(first, ones) + dot(second, ones) + dot(third, ones)
 
 
-def inverse_of(value):
-    guess = pl.reciprocal(value, approx=True)
-    return guess * (2.0 - value * guess)
-
-
 def image_term(coef, k, observed, lit, flat_part, flat_shade, mix_shade, slope_lon, slope_lat):
     steep = coef[k, 2] - coef[k, 0] * slope_lon - coef[k, 1] * slope_lat
     decay = jnp.exp(-jnp.abs(steep))
     whole = 1.0 + decay
     part = jnp.maximum(steep, 0.0) + jnp.log(whole)
-    level = part + coef[k, 3]
-    both = inverse_of(whole * level)
-    ratio = both * whole
-    gate = jnp.where(steep >= 0.0, 1.0, decay) * (both * level)
+    ratio = 1.0 / (part + coef[k, 3])
+    gate = jnp.where(steep >= 0.0, 1.0, decay) / whole
     residual = lit * (part * (mix_shade * ratio + flat_shade) - observed)
     pull = residual * ((coef[k, 4] * (ratio * ratio) + flat_part) * gate)
     return pull, residual * part
@@ -467,23 +465,33 @@
         + [pltpu.SemaphoreType.DMA((len(inputs),))],
         compiler_params=LARGE,
     )(*inputs)
+    sent, count = lax.optimization_barrier((sent, count))
     received = lax.ppermute(sent, axes, across_cores)
-    kept = call(keep_kernel, fields, *inputs, sent[:1, :1, :8])
+    kept = call(keep_kernel, fields, *inputs[:-2], count, expand)
     near_small = call(near_small_kernel, f32(2, STRIP, LANES), kept, received)
     halo_small = lax.ppermute(near_small, axes, across_halves)
+    line = call(count_kernel, f32(LINE, 1, LANES), kept, received, near_small)
+    in_line = [
+        [index(first + a, b) for a in range(LINE)]
+        for first in range(0, lon_count, LINE)
+        for b in range(lat_count)
+    ]
+    across_lines = [
+        [index(first + a, b + core) for first in range(0, lon_count, LINE) for b in range(0, lat_count, 2)]
+        for a in range(LINE)
+        for core in range(2)
+    ]
+    line = lax.all_to_all(line, axes, 0, 0, axis_index_groups=in_line)
     near = call(near_kernel, f32(HEIGHT, STRIP, LANES), kept, received, near_small)
     halo = lax.ppermute(near, axes, across_halves)
-    counts = call(
-        count_kernel, f32(len(sites) // 2, 1, LANES), kept[AUX:], received[AUX:], near[:1, :8]
-    )
-    same_core = [[index(a, b) for a, b in sites if b % 2 == core] for core in range(2)]
-    counts = lax.all_to_all(counts, axes, 0, 0, axis_index_groups=same_core)
     message = f32(TILES, STRIP, LANES)
     window = f32(TILES, EXT, LANES)
     rows_of_bins = f32(TILES, BINS, LANES)
     z, aux, inter, intra = call(
         begin_kernel, (window, rows_of_bins, message, message), kept, received, halo_small
     )
+    counts = call(line_kernel, f32(len(across_lines[0]), 1, LANES), line, inter)
+    counts = lax.all_to_all(counts, axes, 0, 0, axis_index_groups=across_lines)
     inter, intra = exchange(inter, intra)
     tables = constants()
     scratch = [pltpu.VMEM((TILES * STRIP, LANES), F32)] * 4

time: 74.2 us -> 74.9 us (level)
  waiting for transfers between devices: 8.23 us -> 12.9 us
  starting transfers between devices: 50.4 us -> 47.4 us
    ppermute x4, starting transfers between devices: 17.9 us -> 13.7 us  [exchange(): lax.ppermute(intra, axes, across_cores)]
    all_to_all x1 -> x2, waiting for transfers between devices: 3.24 us -> 6.84 us  [the longest x1 3.81 us: per_device(): counts = lax.all_to_all(counts, axes, 0, 0, axis_index_groups=across_lines)]
    ppermute x4, starting transfers between devices: 6.67 us -> 8.63 us  [exchange(): lax.ppermute(inter, axes, across_strips)]
    ppermute x1, starting transfers between devices: 2.03 us -> 0.31 us  [per_device(): halo = lax.ppermute(near, axes, across_halves)]
    ppermute x1, starting transfers between devices: 5.67 us -> 7.15 us  [per_device(): other = lax.ppermute(other, axes, across_cores)]
    ppermute x4, waiting for transfers between devices: 0.87 us -> 2.13 us  [exchange(): lax.ppermute(inter, axes, across_strips)]
    ppermute x4, waiting for transfers between devices: 2.72 us -> 1.85 us  [exchange(): lax.ppermute(intra, axes, across_cores)]
    all_to_all x1 -> x2, starting transfers between devices: 13.8 us -> 13.2 us  [the longest x1 8.19 us: per_device(): line = lax.all_to_all(line, axes, 0, 0, axis_index_groups=in_line)]
  transfers between devices with their start and end apart: 13 -> 14, of which waited for: 8 -> 7; matrix products, arithmetic and copies ran while one was open for 2% -> 1% of each run, Pallas kernels for 1% -> 2%
where the time goes in v4:
time: 74.9 us; the launch traced here: 74.7 us
  starting transfers between devices  47.4 us (63%)
  Pallas kernels  13.2 us (18%)
  waiting for transfers between devices  12.9 us (17%)
  local copies, waits for them, and re-layouts  1.04 us (1%)
    ppermute x4, starting transfers between devices, exchange(): lax.ppermute(intra, axes, across_cores)  13.7 us
    pallas_call x11, Pallas kernels, call(): pl.pallas_call(kernel, out_shape=out_shape, in_specs=[SMEM if scalars and...  10.7 us
    ppermute x4, starting transfers between devices, exchange(): lax.ppermute(inter, axes, across_strips)  8.63 us
    all_to_all x1, starting transfers between devices, per_device(): line = lax.all_to_all(line, axes, 0, 0, axis_index_groups=in_line)  8.19 us
    ppermute x1, starting transfers between devices, per_device(): other = lax.ppermute(other, axes, across_cores)  7.15 us
    all_to_all x1, starting transfers between devices, per_device(): counts = lax.all_to_all(counts, axes, 0, 0, axis_index_groups=across_lines)  5 us
    all_to_all x1, waiting for transfers between devices, per_device(): counts = lax.all_to_all(counts, axes, 0, 0, axis_index_groups=across_lines)  3.81 us
    ppermute x1, starting transfers between devices, per_device(): received = lax.ppermute(sent, axes, across_cores)  3.31 us
  transfers between devices with their start and end apart: 14, of which 7 were waited for; matrix products, arithmetic and copies ran while one was open for 1% of the time, Pallas kernels for 2%

profile of v4, /device:TPU:1, one launch (start us, length us, event | category | flops | bytes accessed | tf_op | source)
XLA Modules:
  0.0 74.7 jit_solution(4125861905949576634)
XLA Ops:
  0.0 0.0 copy-start.5
  0.0 0.0 copy-start.8
  0.1 2.4 %shard_map.136 = f32[27,2,32,128]{3,2,1,0:T(8,128)} custom-call(bf16[12,64,256]{2,1,0:T(8,128)(2,1)} %images.1, s32[12,64,256]{2,1,0:T(8,128)} %lit_mask.1, f32[64,256]{1,0:T(8,128)} %height.1, f32[64,256]{1,0:T(8,128)} %albedo.1, s32[64,256]{1,0:T(8,128)} %owner.1, f32[16,64]{1,0:T(8,128)} %altimetry.1, s32[1,12]{1,0:T(1,128)} %bitcast.1, ...), custom_call_target="tpu_custom_call" | custom-call | tf_op jit(solution)/shard_map/pallas_call | solution.py:459
  2.5 3.3 %collective-permute-start = (f32[27,2,32,128]{3,2,1,0:T(8,128)}, f32[27,2,32,128]{3,2,1,0:T(8,128)S(1)}, u32[]{:S(2)}, u32[]{:S(2)}) collective-permute-start(f32[27,2,32,128]{3,2,1,0:T(8,128)} %shard_map.136), channel_id=1, source_target_pairs={{0,1},{1,0},{2,3},{3,2},{4,5},{5,4},{6,7},{7,6},{8,9},{9,8},{10,11... | collective-permute-start | bytes 2654216 | tf_op jit(solution)/shard_map/ppermute | solution.py:469
  5.8 0.0 copy-done.13
  5.8 0.1 copy.22
  5.9 0.1 copy.20
  6.0 0.1 copy.19
  6.1 0.0 copy-done.1
  6.1 0.0 copy-done.8
  6.2 0.5 copy-done.11
  6.6 0.1 copy-done.12
  6.7 0.2 shard_map.137.kept
  6.9 1.2 %collective-permute-done.received = f32[27,2,32,128]{3,2,1,0:T(8,128)S(1)} collective-permute-done((f32[27,2,32,128]{3,2,1,0:T(8,128)}, f32[27,2,32,128]{3,2,1,0:T(8,128)S(1)}, u32[]{:S(2)}, u32[]{:S(2)}) %collective-permute-start) | collective-permute-done | bytes 884768 | tf_op jit(solution)/shard_map/ppermute | solution.py:469
  8.1 1.0 %collective-permute-start.1 = (f32[2,32,128]{2,1,0:T(8,128)S(1)}, f32[2,32,128]{2,1,0:T(8,128)S(1)}, u32[]{:S(2)}, u32[]{:S(2)}) collective-permute-start(f32[2,32,128]{2,1,0:T(8,128)S(1)} %shard_map.138.near_small), channel_id=1, source_target_pairs={{0,2},{1,3},{2,0},{3,1},{4,6},{5,7},{6,4},{7,5},{8,10},{9,11},{10,... | collective-permute-start | bytes 98312 | tf_op jit(solution)/shard_map/ppermute | solution.py:472
  9.1 0.6 shard_map.139
  9.7 8.2 %all-to-all-start = ((f32[8,1,128]{2,1,0:T(1,128)}), f32[8,1,128]{2,1,0:T(1,128)S(1)}, u32[]{:S(2)}, u32[]{:S(2)}) async-start(f32[8,1,128]{2,1,0:T(1,128)} %shard_map.139), calls=%async_computation | async-start | bytes 8192 | tf_op jit(solution)/shard_map/all_to_all | solution.py:484
  17.9 0.3 collective-permute-start.2
  18.2 0.1 copy.21
  18.3 0.0 collective-permute-done.1.halo_small
  18.4 2.9 %collective-permute-start.3 = (f32[5,32,128]{2,1,0:T(8,128)S(1)}, f32[5,32,128]{2,1,0:T(8,128)S(1)}, u32[]{:S(2)}, u32[]{:S(2)}) collective-permute-start(f32[5,32,128]{2,1,0:T(8,128)S(1)} %get-tuple-element.26.inter), channel_id=1, source_target_pairs={{0,253},{1,4},{2,255},{3,6},{4,1},{5,8},{6,3},{7,10},{8,5},{9,12},... | collective-permute-start | bytes 245768 | tf_op jit(solution)/shard_map/ppermute | solution.py:436
  21.3 3.0 %all-to-all-done.line = f32[8,1,128]{2,1,0:T(1,128)S(1)} async-done(((f32[8,1,128]{2,1,0:T(1,128)}), f32[8,1,128]{2,1,0:T(1,128)S(1)}, u32[]{:S(2)}, u32[]{:S(2)}) %all-to-all-start) | async-done | bytes 4128 | tf_op jit(solution)/shard_map/all_to_all | solution.py:484
  24.4 0.6 shard_map.141
  25.0 5.0 %all-to-all-start.1 = ((f32[16,1,128]{2,1,0:T(1,128)}), f32[16,1,128]{2,1,0:T(1,128)S(1)}, u32[]{:S(2)}, u32[]{:S(2)}) async-start(f32[16,1,128]{2,1,0:T(1,128)} %shard_map.141), calls=%async_computation.1 | async-start | bytes 16384 | tf_op jit(solution)/shard_map/all_to_all | solution.py:494
  30.0 2.4 %collective-permute-start.4 = (f32[5,32,128]{2,1,0:T(8,128)S(1)}, f32[5,32,128]{2,1,0:T(8,128)S(1)}, u32[]{:S(2)}, u32[]{:S(2)}) collective-permute-start(f32[5,32,128]{2,1,0:T(8,128)S(1)} %get-tuple-element.28), channel_id=1, source_target_pairs={{0,1},{1,0},{2,3},{3,2},{4,5},{5,4},{6,7},{7,6},{8,9},{9,8},{10,11... | collective-permute-start | bytes 245768 | tf_op jit(solution)/shard_map/ppermute | solution.py:436
  32.4 0.1 stack.2.coef
  32.5 3.8 %all-to-all-done.1.counts = f32[16,1,128]{2,1,0:T(1,128)S(1)} async-done(((f32[16,1,128]{2,1,0:T(1,128)}), f32[16,1,128]{2,1,0:T(1,128)S(1)}, u32[]{:S(2)}, u32[]{:S(2)}) %all-to-all-start.1) | async-done | bytes 8224 | tf_op jit(solution)/shard_map/all_to_all | solution.py:494
  36.3 0.0 collective-permute-done.4.intra
  36.3 0.0 collective-permute-done.3.inter
  36.3 0.0 collective-permute-done.2.halo
  36.4 2.9 %shard_map.143 = (f32[5,64,128]{2,1,0:T(8,128)S(1)}, f32[5,32,128]{2,1,0:T(8,128)S(1)}, f32[5,32,128]{2,1,0:T(8,128)S(1)}, f32[5,16,128]{2,1,0:T(8,128)S(1)}, f32[16,128]{1,0:T(8,128)S(1)}) custom-call(f32[12,7]{1,0:T(8,128)S(1)} %stack.2.coef, f32[16,1,128]{2,1,0:T(1,128)S(1)} %all-to-all-done.1.counts, f32[27,2,32,128]{3,2,1,0:T(8,128)S(1)} %shard_map.137.kept, ...), custom_call_target="tpu_custom_call" | custom-call | tf_op jit(solution)/shard_map/pallas_call | solution.py:413
  39.3 3.8 %collective-permute-start.5 = (f32[5,32,128]{2,1,0:T(8,128)S(1)}, f32[5,32,128]{2,1,0:T(8,128)S(1)}, u32[]{:S(2)}, u32[]{:S(2)}) collective-permute-start(f32[5,32,128]{2,1,0:T(8,128)S(1)} %get-tuple-element.32), channel_id=1, source_target_pairs={{0,253},{1,4},{2,255},{3,6},{4,1},{5,8},{6,3},{7,10},{8,5},{9,12},... | collective-permute-start | bytes 245768 | tf_op jit(solution)/shard_map/ppermute | solution.py:436
  43.1 0.0 collective-permute-start.6
  43.1 2.1 %collective-permute-done.5.inter = f32[5,32,128]{2,1,0:T(8,128)S(1)} collective-permute-done((f32[5,32,128]{2,1,0:T(8,128)S(1)}, f32[5,32,128]{2,1,0:T(8,128)S(1)}, u32[]{:S(2)}, u32[]{:S(2)}) %collective-permute-start.5) | collective-permute-done | bytes 81952 | tf_op jit(solution)/shard_map/ppermute | solution.py:436
  45.2 0.0 collective-permute-done.6.intra
  45.2 2.8 %shard_map.144 = (f32[5,64,128]{2,1,0:T(8,128)S(1)}, f32[5,32,128]{2,1,0:T(8,128)S(1)}, f32[5,32,128]{2,1,0:T(8,128)S(1)}) custom-call(f32[12,7]{1,0:T(8,128)S(1)} %stack.2.coef, f32[16,128]{1,0:T(8,128)S(1)} %get-tuple-element.30.weight, f32[27,2,32,128]{3,2,1,0:T(8,128)S(1)} %shard_map.137.kept, f32[27,2,32,128]{3,2,1,0:T(8,128)S(1)} %collective-permute-done.received, ...), custom_call_target="tpu_custom_call" | custom-call | tf_op jit(solution)/shard_map/pallas_call | solution.py:413
  48.1 1.8 %collective-permute-start.7 = (f32[5,32,128]{2,1,0:T(8,128)S(1)}, f32[5,32,128]{2,1,0:T(8,128)S(1)}, u32[]{:S(2)}, u32[]{:S(2)}) collective-permute-start(f32[5,32,128]{2,1,0:T(8,128)S(1)} %get-tuple-element.36), channel_id=1, source_target_pairs={{0,253},{1,4},{2,255},{3,6},{4,1},{5,8},{6,3},{7,10},{8,5},{9,12},... | collective-permute-start | bytes 245768 | tf_op jit(solution)/shard_map/ppermute | solution.py:436
  49.9 4.3 %collective-permute-start.8 = (f32[5,32,128]{2,1,0:T(8,128)S(1)}, f32[5,32,128]{2,1,0:T(8,128)S(1)}, u32[]{:S(2)}, u32[]{:S(2)}) collective-permute-start(f32[5,32,128]{2,1,0:T(8,128)S(1)} %get-tuple-element.37), channel_id=1, source_target_pairs={{0,1},{1,0},{2,3},{3,2},{4,5},{5,4},{6,7},{7,6},{8,9},{9,8},{10,11... | collective-permute-start | bytes 245768 | tf_op jit(solution)/shard_map/ppermute | solution.py:436
  54.2 0.0 collective-permute-done.7.inter
  54.2 0.9 %collective-permute-done.8.intra = f32[5,32,128]{2,1,0:T(8,128)S(1)} collective-permute-done((f32[5,32,128]{2,1,0:T(8,128)S(1)}, f32[5,32,128]{2,1,0:T(8,128)S(1)}, u32[]{:S(2)}, u32[]{:S(2)}) %collective-permute-start.8) | collective-permute-done | bytes 81952 | tf_op jit(solution)/shard_map/ppermute | solution.py:436
  55.2 2.8 %shard_map.145 = (f32[5,64,128]{2,1,0:T(8,128)S(1)}, f32[5,32,128]{2,1,0:T(8,128)S(1)}, f32[5,32,128]{2,1,0:T(8,128)S(1)}) custom-call(f32[12,7]{1,0:T(8,128)S(1)} %stack.2.coef, f32[16,128]{1,0:T(8,128)S(1)} %get-tuple-element.30.weight, f32[27,2,32,128]{3,2,1,0:T(8,128)S(1)} %shard_map.137.kept, f32[27,2,32,128]{3,2,1,0:T(8,128)S(1)} %collective-permute-done.received, ...), custom_call_target="tpu_custom_call" | custom-call | tf_op jit(solution)/shard_map/pallas_call | solution.py:413
  58.0 0.1 collective-permute-start.9
  58.1 7.0 %collective-permute-start.10 = (f32[5,32,128]{2,1,0:T(8,128)S(1)}, f32[5,32,128]{2,1,0:T(8,128)S(1)}, u32[]{:S(2)}, u32[]{:S(2)}) collective-permute-start(f32[5,32,128]{2,1,0:T(8,128)S(1)} %get-tuple-element.40), channel_id=1, source_target_pairs={{0,1},{1,0},{2,3},{3,2},{4,5},{5,4},{6,7},{7,6},{8,9},{9,8},{10,11... | collective-permute-start | bytes 245768 | tf_op jit(solution)/shard_map/ppermute | solution.py:436
  65.1 0.0 collective-permute-done.9.inter
  65.1 0.9 %collective-permute-done.10.intra = f32[5,32,128]{2,1,0:T(8,128)S(1)} collective-permute-done((f32[5,32,128]{2,1,0:T(8,128)S(1)}, f32[5,32,128]{2,1,0:T(8,128)S(1)}, u32[]{:S(2)}, u32[]{:S(2)}) %collective-permute-start.10) | collective-permute-done | bytes 81952 | tf_op jit(solution)/shard_map/ppermute | solution.py:436
  66.0 7.2 %collective-permute-start.11 = (f32[32,256]{1,0:T(8,128)S(1)}, f32[32,256]{1,0:T(8,128)S(1)}, u32[]{:S(2)}, u32[]{:S(2)}) collective-permute-start(f32[32,256]{1,0:T(8,128)S(1)} %get-tuple-element.42), channel_id=1, source_target_pairs={{0,1},{1,0},{2,3},{3,2},{4,5},{5,4},{6,7},{7,6},{8,9},{9,8},{10,11... | collective-permute-start | bytes 98312 | tf_op jit(solution)/shard_map/ppermute | solution.py:515
  73.2 0.9 %collective-permute-done.11.other = f32[32,256]{1,0:T(8,128)S(1)} collective-permute-done((f32[32,256]{1,0:T(8,128)S(1)}, f32[32,256]{1,0:T(8,128)S(1)}, u32[]{:S(2)}, u32[]{:S(2)}) %collective-permute-start.11) | collective-permute-done | bytes 32800 | tf_op jit(solution)/shard_map/ppermute | solution.py:515
  74.0 0.6 shard_map.147
  (29 shorter events, 0.1 us)
Async XLA Ops:
  0.0 5.8 %copy-start.13 = (f32[12,4]{0,1:T(4,128)S(1)}, f32[12,4]{0,1:T(4,128)}, u32[]{:S(2)}) copy-start(f32[12,4]{0,1:T(4,128)} %param.19) | copy-start | bytes 580
  0.0 6.1 %copy-start = (s32[12,64,256]{2,1,0:T(8,128)S(1)}, s32[12,64,256]{2,1,0:T(8,128)}, u32[]{:S(2)}) copy-start(s32[12,64,256]{2,1,0:T(8,128)} %lit_mask.1) | copy-start | bytes 2359300
  0.0 6.1 %copy-start.1 = (bf16[12,64,256]{2,1,0:T(8,128)(2,1)S(1)}, bf16[12,64,256]{2,1,0:T(8,128)(2,1)}, u32[]{:S(2)}) copy-start(bf16[12,64,256]{2,1,0:T(8,128)(2,1)} %images.1) | copy-start | bytes 1179652
  0.0 6.1 %copy-start.5 = (bf16[192,256]{1,0:T(8,128)(2,1)S(1)}, bf16[192,256]{1,0:T(8,128)(2,1)}, u32[]{:S(2)}) copy-start(bf16[192,256]{1,0:T(8,128)(2,1)} %constant.16.clone.expand_hbm.expand) | copy-start | bytes 294916
  0.0 6.1 %copy-start.8 = (f32[64,256]{1,0:T(8,128)S(1)}, f32[64,256]{1,0:T(8,128)}, u32[]{:S(2)}) copy-start(f32[64,256]{1,0:T(8,128)} %height.1) | copy-start | bytes 196612
  0.0 6.1 %copy-start.9 = (f32[64,256]{1,0:T(8,128)S(1)}, f32[64,256]{1,0:T(8,128)}, u32[]{:S(2)}) copy-start(f32[64,256]{1,0:T(8,128)} %albedo.1) | copy-start | bytes 196612
  0.0 6.1 %copy-start.10 = (s32[64,256]{1,0:T(8,128)S(1)}, s32[64,256]{1,0:T(8,128)}, u32[]{:S(2)}) copy-start(s32[64,256]{1,0:T(8,128)} %owner.1) | copy-start | bytes 196612
  2.5 5.6 %collective-permute-start = (f32[27,2,32,128]{3,2,1,0:T(8,128)}, f32[27,2,32,128]{3,2,1,0:T(8,128)S(1)}, u32[]{:S(2)}, u32[]{:S(2)}) collective-permute-start(f32[27,2,32,128]{3,2,1,0:T(8,128)} %shard_map.136), channel_id=1, source_target_pairs={{0,1},{1,0},{2,3},{3,2},{4,5},{5,4},{6,7},{7,6},{8,9},{9,8},{10,11... | collective-permute-start | bytes 2654216 | tf_op jit(solution)/shard_map/ppermute | solution.py:469
  5.9 0.7 copy-start.11
  6.0 0.7 copy-start.12
  8.1 10.3 %collective-permute-start.1 = (f32[2,32,128]{2,1,0:T(8,128)S(1)}, f32[2,32,128]{2,1,0:T(8,128)S(1)}, u32[]{:S(2)}, u32[]{:S(2)}) collective-permute-start(f32[2,32,128]{2,1,0:T(8,128)S(1)} %shard_map.138.near_small), channel_id=1, source_target_pairs={{0,2},{1,3},{2,0},{3,1},{4,6},{5,7},{6,4},{7,5},{8,10},{9,11},{10,... | collective-permute-start | bytes 98312 | tf_op jit(solution)/shard_map/ppermute | solution.py:472
  9.7 14.6 %all-to-all-start = ((f32[8,1,128]{2,1,0:T(1,128)}), f32[8,1,128]{2,1,0:T(1,128)S(1)}, u32[]{:S(2)}, u32[]{:S(2)}) async-start(f32[8,1,128]{2,1,0:T(1,128)} %shard_map.139), calls=%async_computation | async-start | bytes 8192 | tf_op jit(solution)/shard_map/all_to_all | solution.py:484
  17.9 18.4 %collective-permute-start.2 = (f32[25,32,128]{2,1,0:T(8,128)S(1)}, f32[25,32,128]{2,1,0:T(8,128)S(1)}, u32[]{:S(2)}, u32[]{:S(2)}) collective-permute-start(f32[25,32,128]{2,1,0:T(8,128)S(1)} %shard_map.142), channel_id=1, source_target_pairs={{0,2},{1,3},{2,0},{3,1},{4,6},{5,7},{6,4},{7,5},{8,10},{9,11},{10,... | collective-permute-start | bytes 1228808 | tf_op jit(solution)/shard_map/ppermute | solution.py:486
  18.3 18.0 %copy-start.6 = (bf16[128,128]{1,0:T(8,128)(2,1)S(1)}, bf16[128,128]{1,0:T(8,128)(2,1)}, u32[]{:S(2)}) copy-start(bf16[128,128]{1,0:T(8,128)(2,1)} %constant.21.clone.refs_4_) | copy-start | bytes 98308
  18.3 18.0 %copy-start.7 = (bf16[64,256]{1,0:T(8,128)(2,1)S(1)}, bf16[64,256]{1,0:T(8,128)(2,1)}, u32[]{:S(2)}) copy-start(bf16[64,256]{1,0:T(8,128)(2,1)} %constant.18.clone.refs_1_) | copy-start | bytes 98308
  18.4 17.9 %collective-permute-start.3 = (f32[5,32,128]{2,1,0:T(8,128)S(1)}, f32[5,32,128]{2,1,0:T(8,128)S(1)}, u32[]{:S(2)}, u32[]{:S(2)}) collective-permute-start(f32[5,32,128]{2,1,0:T(8,128)S(1)} %get-tuple-element.26.inter), channel_id=1, source_target_pairs={{0,253},{1,4},{2,255},{3,6},{4,1},{5,8},{6,3},{7,10},{8,5},{9,12},... | collective-permute-start | bytes 245768 | tf_op jit(solution)/shard_map/ppermute | solution.py:436
  24.3 12.0 %copy-start.3 = (bf16[256,128]{1,0:T(8,128)(2,1)S(1)}, bf16[256,128]{1,0:T(8,128)(2,1)}, u32[]{:S(2)}) copy-start(bf16[256,128]{1,0:T(8,128)(2,1)} %constant.19.clone.refs_2_) | copy-start | bytes 196612
  24.4 12.0 %copy-start.4 = (bf16[128,192]{1,0:T(8,128)(2,1)S(1)}, bf16[128,192]{1,0:T(8,128)(2,1)}, u32[]{:S(2)}) copy-start(bf16[128,192]{1,0:T(8,128)(2,1)} %constant.17.clone.refs_0_) | copy-start | bytes 147460
  25.0 11.4 %copy-start.2 = (bf16[256,128]{1,0:T(8,128)(2,1)S(1)}, bf16[256,128]{1,0:T(8,128)(2,1)}, u32[]{:S(2)}) copy-start(bf16[256,128]{1,0:T(8,128)(2,1)} %constant.20.clone.refs_3_) | copy-start | bytes 196612
  25.0 11.4 %all-to-all-start.1 = ((f32[16,1,128]{2,1,0:T(1,128)}), f32[16,1,128]{2,1,0:T(1,128)S(1)}, u32[]{:S(2)}, u32[]{:S(2)}) async-start(f32[16,1,128]{2,1,0:T(1,128)} %shard_map.141), calls=%async_computation.1 | async-start | bytes 16384 | tf_op jit(solution)/shard_map/all_to_all | solution.py:494
  30.0 6.4 %collective-permute-start.4 = (f32[5,32,128]{2,1,0:T(8,128)S(1)}, f32[5,32,128]{2,1,0:T(8,128)S(1)}, u32[]{:S(2)}, u32[]{:S(2)}) collective-permute-start(f32[5,32,128]{2,1,0:T(8,128)S(1)} %get-tuple-element.28), channel_id=1, source_target_pairs={{0,1},{1,0},{2,3},{3,2},{4,5},{5,4},{6,7},{7,6},{8,9},{9,8},{10,11... | collective-permute-start | bytes 245768 | tf_op jit(solution)/shard_map/ppermute | solution.py:436
  39.3 5.9 %collective-permute-start.5 = (f32[5,32,128]{2,1,0:T(8,128)S(1)}, f32[5,32,128]{2,1,0:T(8,128)S(1)}, u32[]{:S(2)}, u32[]{:S(2)}) collective-permute-start(f32[5,32,128]{2,1,0:T(8,128)S(1)} %get-tuple-element.32), channel_id=1, source_target_pairs={{0,253},{1,4},{2,255},{3,6},{4,1},{5,8},{6,3},{7,10},{8,5},{9,12},... | collective-permute-start | bytes 245768 | tf_op jit(solution)/shard_map/ppermute | solution.py:436
  43.1 2.1 %collective-permute-start.6 = (f32[5,32,128]{2,1,0:T(8,128)S(1)}, f32[5,32,128]{2,1,0:T(8,128)S(1)}, u32[]{:S(2)}, u32[]{:S(2)}) collective-permute-start(f32[5,32,128]{2,1,0:T(8,128)S(1)} %get-tuple-element.33), channel_id=1, source_target_pairs={{0,1},{1,0},{2,3},{3,2},{4,5},{5,4},{6,7},{7,6},{8,9},{9,8},{10,11... | collective-permute-start | bytes 245768 | tf_op jit(solution)/shard_map/ppermute | solution.py:436
  48.1 6.2 %collective-permute-start.7 = (f32[5,32,128]{2,1,0:T(8,128)S(1)}, f32[5,32,128]{2,1,0:T(8,128)S(1)}, u32[]{:S(2)}, u32[]{:S(2)}) collective-permute-start(f32[5,32,128]{2,1,0:T(8,128)S(1)} %get-tuple-element.36), channel_id=1, source_target_pairs={{0,253},{1,4},{2,255},{3,6},{4,1},{5,8},{6,3},{7,10},{8,5},{9,12},... | collective-permute-start | bytes 245768 | tf_op jit(solution)/shard_map/ppermute | solution.py:436
  49.9 5.2 %collective-permute-start.8 = (f32[5,32,128]{2,1,0:T(8,128)S(1)}, f32[5,32,128]{2,1,0:T(8,128)S(1)}, u32[]{:S(2)}, u32[]{:S(2)}) collective-permute-start(f32[5,32,128]{2,1,0:T(8,128)S(1)} %get-tuple-element.37), channel_id=1, source_target_pairs={{0,1},{1,0},{2,3},{3,2},{4,5},{5,4},{6,7},{7,6},{8,9},{9,8},{10,11... | collective-permute-start | bytes 245768 | tf_op jit(solution)/shard_map/ppermute | solution.py:436
  58.0 7.1 %collective-permute-start.9 = (f32[5,32,128]{2,1,0:T(8,128)S(1)}, f32[5,32,128]{2,1,0:T(8,128)S(1)}, u32[]{:S(2)}, u32[]{:S(2)}) collective-permute-start(f32[5,32,128]{2,1,0:T(8,128)S(1)} %get-tuple-element.39), channel_id=1, source_target_pairs={{0,253},{1,4},{2,255},{3,6},{4,1},{5,8},{6,3},{7,10},{8,5},{9,12},... | collective-permute-start | bytes 245768 | tf_op jit(solution)/shard_map/ppermute | solution.py:436
  58.1 7.9 %collective-permute-start.10 = (f32[5,32,128]{2,1,0:T(8,128)S(1)}, f32[5,32,128]{2,1,0:T(8,128)S(1)}, u32[]{:S(2)}, u32[]{:S(2)}) collective-permute-start(f32[5,32,128]{2,1,0:T(8,128)S(1)} %get-tuple-element.40), channel_id=1, source_target_pairs={{0,1},{1,0},{2,3},{3,2},{4,5},{5,4},{6,7},{7,6},{8,9},{9,8},{10,11... | collective-permute-start | bytes 245768 | tf_op jit(solution)/shard_map/ppermute | solution.py:436
  66.0 8.0 %collective-permute-start.11 = (f32[32,256]{1,0:T(8,128)S(1)}, f32[32,256]{1,0:T(8,128)S(1)}, u32[]{:S(2)}, u32[]{:S(2)}) collective-permute-start(f32[32,256]{1,0:T(8,128)S(1)} %get-tuple-element.42), channel_id=1, source_target_pairs={{0,1},{1,0},{2,3},{3,2},{4,5},{5,4},{6,7},{7,6},{8,9},{9,8},{10,11... | collective-permute-start | bytes 98312 | tf_op jit(solution)/shard_map/ppermute | solution.py:515

commit v5 on v4

--- a/solution.py
+++ b/solution.py
@@ -27,7 +27,6 @@
 HEIGHT = ALBEDO + 1
 AUX = HEIGHT + 1
 BINS = 16
-LINE = 8
 DENOM = float(RAD * (RAD + 1) * (2 * RAD + 1)) / 3.0
 TAP_SCALE = 1.0 / (DENOM * (2 * RAD + 1))
 F32 = jnp.float32
@@ -181,6 +180,7 @@
     half, core = place()
     for i, field in enumerate((HEIGHT, AUX)):
         near_small[i] = jnp.where(half != core, kept[field, 1 - half], received[field, 1 - half])
+    near_small[1, 16:24] = kept[AUX, 0, 16:24] + received[AUX, 0, 16:24]
 
 
 def near_kernel(kept, received, near_small, near):
@@ -195,13 +195,9 @@
         near[...] = received[0:HEIGHT, 1 - half]
 
 
-def count_kernel(kept, received, near_small, counts):
-    total = kept[AUX, 0, 16:17] + received[AUX, 0, 16:17]
+def count_kernel(halo_small, near_small, near, counts):
+    total = halo_small[1, 16:17] + near_small[1, 16:17]
     counts[...] = jnp.broadcast_to(total[None], counts.shape)
-
-
-def line_kernel(line, inter, counts):
-    counts[...] = jnp.broadcast_to(jnp.sum(line[...], axis=0, keepdims=True), counts.shape)
 
 
 def route(core, up, down, inter, intra):
@@ -470,28 +466,17 @@
     kept = call(keep_kernel, fields, *inputs[:-2], count, expand)
     near_small = call(near_small_kernel, f32(2, STRIP, LANES), kept, received)
     halo_small = lax.ppermute(near_small, axes, across_halves)
-    line = call(count_kernel, f32(LINE, 1, LANES), kept, received, near_small)
-    in_line = [
-        [index(first + a, b) for a in range(LINE)]
-        for first in range(0, lon_count, LINE)
-        for b in range(lat_count)
-    ]
-    across_lines = [
-        [index(first + a, b + core) for first in range(0, lon_count, LINE) for b in range(0, lat_count, 2)]
-        for a in range(LINE)
-        for core in range(2)
-    ]
-    line = lax.all_to_all(line, axes, 0, 0, axis_index_groups=in_line)
     near = call(near_kernel, f32(HEIGHT, STRIP, LANES), kept, received, near_small)
     halo = lax.ppermute(near, axes, across_halves)
+    counts = call(count_kernel, f32(lon_count, 1, LANES), halo_small, near_small, near[:1, :8])
+    counts, halo_small = lax.optimization_barrier((counts, halo_small))
+    counts = lax.all_to_all(counts, "lon", 0, 0)
     message = f32(TILES, STRIP, LANES)
     window = f32(TILES, EXT, LANES)
     rows_of_bins = f32(TILES, BINS, LANES)
     z, aux, inter, intra = call(
         begin_kernel, (window, rows_of_bins, message, message), kept, received, halo_small
     )
-    counts = call(line_kernel, f32(len(across_lines[0]), 1, LANES), line, inter)
-    counts = lax.all_to_all(counts, axes, 0, 0, axis_index_groups=across_lines)
     inter, intra = exchange(inter, intra)
     tables = constants()
     scratch = [pltpu.VMEM((TILES * STRIP, LANES), F32)] * 4

time: 74.9 us -> 71.3 us (0.952)
  waiting for transfers between devices: 12.9 us -> 8.9 us
  starting transfers between devices: 47.4 us -> 48.3 us
    ppermute x4, starting transfers between devices: 13.7 us -> 17.9 us  [exchange(): lax.ppermute(intra, axes, across_cores)]
    all_to_all x2 -> x1, waiting for transfers between devices: 6.84 us -> 2.97 us  [per_device(): counts = lax.all_to_all(counts, 'lon', 0, 0)]
    all_to_all x2 -> x1, starting transfers between devices: 13.2 us -> 11 us  [per_device(): counts = lax.all_to_all(counts, 'lon', 0, 0)]
    ppermute x1, starting transfers between devices: 7.15 us -> 5.24 us  [per_device(): other = lax.ppermute(other, axes, across_cores)]
    ppermute x4, waiting for transfers between devices: 2.13 us -> 0.32 us  [exchange(): lax.ppermute(inter, axes, across_strips)]
    ppermute x1, starting transfers between devices: 0.31 us -> 2.03 us  [per_device(): halo = lax.ppermute(near, axes, across_halves)]
    ppermute x1, waiting for transfers between devices: 0.01 us -> 1.08 us  [per_device(): halo_small = lax.ppermute(near_small, axes, across_halves)]
    ppermute x4, starting transfers between devices: 8.63 us -> 7.71 us  [exchange(): lax.ppermute(inter, axes, across_strips)]
  transfers between devices with their start and end apart: 14 -> 13, of which waited for: 7 -> 8; matrix products, arithmetic and copies ran while one was open for 1% -> 1% of each run, Pallas kernels for 2% -> 1%
where the time goes in v5:
time: 71.3 us; the launch traced here: 71.1 us
  starting transfers between devices  48.3 us (68%)
  Pallas kernels  12.6 us (18%)
  waiting for transfers between devices  8.9 us (12%)
  local copies, waits for them, and re-layouts  1.05 us (1%)
    ppermute x4, starting transfers between devices, exchange(): lax.ppermute(intra, axes, across_cores)  17.9 us
    all_to_all x1, starting transfers between devices, per_device(): counts = lax.all_to_all(counts, 'lon', 0, 0)  11 us
    pallas_call x10, Pallas kernels, call(): pl.pallas_call(kernel, out_shape=out_shape, in_specs=[SMEM if scalars and...  10.2 us
    ppermute x4, starting transfers between devices, exchange(): lax.ppermute(inter, axes, across_strips)  7.71 us
    ppermute x1, starting transfers between devices, per_device(): other = lax.ppermute(other, axes, across_cores)  5.24 us
    ppermute x1, starting transfers between devices, per_device(): received = lax.ppermute(sent, axes, across_cores)  3.31 us
    all_to_all x1, waiting for transfers between devices, per_device(): counts = lax.all_to_all(counts, 'lon', 0, 0)  2.97 us
    ppermute x4, waiting for transfers between devices, exchange(): lax.ppermute(intra, axes, across_cores)  2.45 us
  transfers between devices with their start and end apart: 13, of which 8 were waited for; matrix products, arithmetic and copies ran while one was open for 1% of the time, Pallas kernels for 1%

profile of v5, /device:TPU:1, one launch (start us, length us, event | category | flops | bytes accessed | tf_op | source)
XLA Modules:
  0.0 71.1 jit_solution(3204034521426248620)
XLA Ops:
  0.0 0.0 copy-start.5
  0.0 0.0 copy-start.8
  0.0 0.0 copy-start.9
  0.0 0.0 copy-start.10
  0.1 2.4 %shard_map.136 = f32[27,2,32,128]{3,2,1,0:T(8,128)} custom-call(bf16[12,64,256]{2,1,0:T(8,128)(2,1)} %images.1, s32[12,64,256]{2,1,0:T(8,128)} %lit_mask.1, f32[64,256]{1,0:T(8,128)} %height.1, f32[64,256]{1,0:T(8,128)} %albedo.1, s32[64,256]{1,0:T(8,128)} %owner.1, f32[16,64]{1,0:T(8,128)} %altimetry.1, s32[1,12]{1,0:T(1,128)} %bitcast.1, ...), custom_call_target="tpu_custom_call" | custom-call | tf_op jit(solution)/shard_map/pallas_call | solution.py:455
  2.5 3.3 %collective-permute-start = (f32[27,2,32,128]{3,2,1,0:T(8,128)}, f32[27,2,32,128]{3,2,1,0:T(8,128)S(1)}, u32[]{:S(2)}, u32[]{:S(2)}) collective-permute-start(f32[27,2,32,128]{3,2,1,0:T(8,128)} %shard_map.136), channel_id=1, source_target_pairs={{0,1},{1,0},{2,3},{3,2},{4,5},{5,4},{6,7},{7,6},{8,9},{9,8},{10,11... | collective-permute-start | bytes 2654216 | tf_op jit(solution)/shard_map/ppermute | solution.py:465
  5.8 0.1 copy.19
  5.9 0.1 copy.22
  6.0 0.1 copy.20
  6.1 0.5 copy-done.11
  6.6 0.1 copy-done.12
  6.7 0.2 shard_map.137.kept
  6.9 1.2 %collective-permute-done.received = f32[27,2,32,128]{3,2,1,0:T(8,128)S(1)} collective-permute-done((f32[27,2,32,128]{3,2,1,0:T(8,128)}, f32[27,2,32,128]{3,2,1,0:T(8,128)S(1)}, u32[]{:S(2)}, u32[]{:S(2)}) %collective-permute-start) | collective-permute-done | bytes 884768 | tf_op jit(solution)/shard_map/ppermute | solution.py:465
  8.1 1.1 %collective-permute-start.1 = (f32[2,32,128]{2,1,0:T(8,128)S(1)}, f32[2,32,128]{2,1,0:T(8,128)S(1)}, u32[]{:S(2)}, u32[]{:S(2)}) collective-permute-start(f32[2,32,128]{2,1,0:T(8,128)S(1)} %shard_map.138.near_small), channel_id=1, source_target_pairs={{0,2},{1,3},{2,0},{3,1},{4,6},{5,7},{6,4},{7,5},{8,10},{9,11},{10,... | collective-permute-start | bytes 98312 | tf_op jit(solution)/shard_map/ppermute | solution.py:468
  9.2 2.0 %collective-permute-start.2 = (f32[25,32,128]{2,1,0:T(8,128)S(1)}, f32[25,32,128]{2,1,0:T(8,128)S(1)}, u32[]{:S(2)}, u32[]{:S(2)}) collective-permute-start(f32[25,32,128]{2,1,0:T(8,128)S(1)} %shard_map.139), channel_id=1, source_target_pairs={{0,2},{1,3},{2,0},{3,1},{4,6},{5,7},{6,4},{7,5},{8,10},{9,11},{10,... | collective-permute-start | bytes 1228808 | tf_op jit(solution)/shard_map/ppermute | solution.py:470
  11.2 0.1 copy.21
  11.3 1.1 %collective-permute-done.1.halo_small = f32[2,32,128]{2,1,0:T(8,128)S(1)} collective-permute-done((f32[2,32,128]{2,1,0:T(8,128)S(1)}, f32[2,32,128]{2,1,0:T(8,128)S(1)}, u32[]{:S(2)}, u32[]{:S(2)}) %collective-permute-start.1) | collective-permute-done | bytes 32800 | tf_op jit(solution)/shard_map/ppermute | solution.py:468
  12.4 0.6 shard_map.140
  13.0 11.0 %all-to-all-start = ((f32[64,1,128]{2,1,0:T(1,128)}), f32[64,1,128]{2,1,0:T(1,128)S(1)}, u32[]{:S(2)}, u32[]{:S(2)}) async-start(f32[64,1,128]{2,1,0:T(1,128)} %shard_map.140), calls=%async_computation | async-start | bytes 65536 | tf_op jit(solution)/shard_map/all_to_all | solution.py:473
  24.1 0.0 copy-start.3
  24.1 0.0 copy-start.4
  24.1 0.0 copy-start.7
  24.2 0.0 copy-start.2
  24.2 3.1 %collective-permute-start.3 = (f32[5,32,128]{2,1,0:T(8,128)S(1)}, f32[5,32,128]{2,1,0:T(8,128)S(1)}, u32[]{:S(2)}, u32[]{:S(2)}) collective-permute-start(f32[5,32,128]{2,1,0:T(8,128)S(1)} %get-tuple-element.31), channel_id=1, source_target_pairs={{0,253},{1,4},{2,255},{3,6},{4,1},{5,8},{6,3},{7,10},{8,5},{9,12},... | collective-permute-start | bytes 245768 | tf_op jit(solution)/shard_map/ppermute | solution.py:432
  27.3 2.9 %collective-permute-start.4 = (f32[5,32,128]{2,1,0:T(8,128)S(1)}, f32[5,32,128]{2,1,0:T(8,128)S(1)}, u32[]{:S(2)}, u32[]{:S(2)}) collective-permute-start(f32[5,32,128]{2,1,0:T(8,128)S(1)} %get-tuple-element.32), channel_id=1, source_target_pairs={{0,1},{1,0},{2,3},{3,2},{4,5},{5,4},{6,7},{7,6},{8,9},{9,8},{10,11... | collective-permute-start | bytes 245768 | tf_op jit(solution)/shard_map/ppermute | solution.py:432
  30.2 0.1 stack.2.coef
  30.3 3.0 %all-to-all-done.counts = f32[64,1,128]{2,1,0:T(1,128)S(1)} async-done(((f32[64,1,128]{2,1,0:T(1,128)}), f32[64,1,128]{2,1,0:T(1,128)S(1)}, u32[]{:S(2)}, u32[]{:S(2)}) %all-to-all-start) | async-done | bytes 32800 | tf_op jit(solution)/shard_map/all_to_all | solution.py:473
  33.2 0.0 collective-permute-done.3.inter
  33.3 0.0 collective-permute-done.4.intra
  33.3 0.0 collective-permute-done.2.halo
  33.3 3.0 %shard_map.142 = (f32[5,64,128]{2,1,0:T(8,128)S(1)}, f32[5,32,128]{2,1,0:T(8,128)S(1)}, f32[5,32,128]{2,1,0:T(8,128)S(1)}, f32[5,16,128]{2,1,0:T(8,128)S(1)}, f32[16,128]{1,0:T(8,128)S(1)}) custom-call(f32[12,7]{1,0:T(8,128)S(1)} %stack.2.coef, f32[64,1,128]{2,1,0:T(1,128)S(1)} %all-to-all-done.counts, f32[27,2,32,128]{3,2,1,0:T(8,128)S(1)} %shard_map.137.kept, ...), custom_call_target="tpu_custom_call" | custom-call | tf_op jit(solution)/shard_map/pallas_call | solution.py:409
  36.3 3.3 %collective-permute-start.5 = (f32[5,32,128]{2,1,0:T(8,128)S(1)}, f32[5,32,128]{2,1,0:T(8,128)S(1)}, u32[]{:S(2)}, u32[]{:S(2)}) collective-permute-start(f32[5,32,128]{2,1,0:T(8,128)S(1)} %get-tuple-element.36), channel_id=1, source_target_pairs={{0,253},{1,4},{2,255},{3,6},{4,1},{5,8},{6,3},{7,10},{8,5},{9,12},... | collective-permute-start | bytes 245768 | tf_op jit(solution)/shard_map/ppermute | solution.py:432
  39.6 1.8 %collective-permute-start.6 = (f32[5,32,128]{2,1,0:T(8,128)S(1)}, f32[5,32,128]{2,1,0:T(8,128)S(1)}, u32[]{:S(2)}, u32[]{:S(2)}) collective-permute-start(f32[5,32,128]{2,1,0:T(8,128)S(1)} %get-tuple-element.37), channel_id=1, source_target_pairs={{0,1},{1,0},{2,3},{3,2},{4,5},{5,4},{6,7},{7,6},{8,9},{9,8},{10,11... | collective-permute-start | bytes 245768 | tf_op jit(solution)/shard_map/ppermute | solution.py:432
  41.4 0.3 collective-permute-done.5.inter
  41.7 0.6 collective-permute-done.6.intra
  42.4 2.8 %shard_map.143 = (f32[5,64,128]{2,1,0:T(8,128)S(1)}, f32[5,32,128]{2,1,0:T(8,128)S(1)}, f32[5,32,128]{2,1,0:T(8,128)S(1)}) custom-call(f32[12,7]{1,0:T(8,128)S(1)} %stack.2.coef, f32[16,128]{1,0:T(8,128)S(1)} %get-tuple-element.34.weight, f32[27,2,32,128]{3,2,1,0:T(8,128)S(1)} %shard_map.137.kept, f32[27,2,32,128]{3,2,1,0:T(8,128)S(1)} %collective-permute-done.received, ...), custom_call_target="tpu_custom_call" | custom-call | tf_op jit(solution)/shard_map/pallas_call | solution.py:409
  45.2 1.2 %collective-permute-start.7 = (f32[5,32,128]{2,1,0:T(8,128)S(1)}, f32[5,32,128]{2,1,0:T(8,128)S(1)}, u32[]{:S(2)}, u32[]{:S(2)}) collective-permute-start(f32[5,32,128]{2,1,0:T(8,128)S(1)} %get-tuple-element.40), channel_id=1, source_target_pairs={{0,253},{1,4},{2,255},{3,6},{4,1},{5,8},{6,3},{7,10},{8,5},{9,12},... | collective-permute-start | bytes 245768 | tf_op jit(solution)/shard_map/ppermute | solution.py:432
  46.4 6.0 %collective-permute-start.8 = (f32[5,32,128]{2,1,0:T(8,128)S(1)}, f32[5,32,128]{2,1,0:T(8,128)S(1)}, u32[]{:S(2)}, u32[]{:S(2)}) collective-permute-start(f32[5,32,128]{2,1,0:T(8,128)S(1)} %get-tuple-element.41), channel_id=1, source_target_pairs={{0,1},{1,0},{2,3},{3,2},{4,5},{5,4},{6,7},{7,6},{8,9},{9,8},{10,11... | collective-permute-start | bytes 245768 | tf_op jit(solution)/shard_map/ppermute | solution.py:432
  52.4 0.0 collective-permute-done.7.inter
  52.4 0.9 %collective-permute-done.8.intra = f32[5,32,128]{2,1,0:T(8,128)S(1)} collective-permute-done((f32[5,32,128]{2,1,0:T(8,128)S(1)}, f32[5,32,128]{2,1,0:T(8,128)S(1)}, u32[]{:S(2)}, u32[]{:S(2)}) %collective-permute-start.8) | collective-permute-done | bytes 81952 | tf_op jit(solution)/shard_map/ppermute | solution.py:432
  53.4 2.8 %shard_map.144 = (f32[5,64,128]{2,1,0:T(8,128)S(1)}, f32[5,32,128]{2,1,0:T(8,128)S(1)}, f32[5,32,128]{2,1,0:T(8,128)S(1)}) custom-call(f32[12,7]{1,0:T(8,128)S(1)} %stack.2.coef, f32[16,128]{1,0:T(8,128)S(1)} %get-tuple-element.34.weight, f32[27,2,32,128]{3,2,1,0:T(8,128)S(1)} %shard_map.137.kept, f32[27,2,32,128]{3,2,1,0:T(8,128)S(1)} %collective-permute-done.received, ...), custom_call_target="tpu_custom_call" | custom-call | tf_op jit(solution)/shard_map/pallas_call | solution.py:409
  56.2 0.1 collective-permute-start.9
  56.3 7.2 %collective-permute-start.10 = (f32[5,32,128]{2,1,0:T(8,128)S(1)}, f32[5,32,128]{2,1,0:T(8,128)S(1)}, u32[]{:S(2)}, u32[]{:S(2)}) collective-permute-start(f32[5,32,128]{2,1,0:T(8,128)S(1)} %get-tuple-element.44), channel_id=1, source_target_pairs={{0,1},{1,0},{2,3},{3,2},{4,5},{5,4},{6,7},{7,6},{8,9},{9,8},{10,11... | collective-permute-start | bytes 245768 | tf_op jit(solution)/shard_map/ppermute | solution.py:432
  63.5 0.0 collective-permute-done.9.inter
  63.5 0.9 %collective-permute-done.10.intra = f32[5,32,128]{2,1,0:T(8,128)S(1)} collective-permute-done((f32[5,32,128]{2,1,0:T(8,128)S(1)}, f32[5,32,128]{2,1,0:T(8,128)S(1)}, u32[]{:S(2)}, u32[]{:S(2)}) %collective-permute-start.10) | collective-permute-done | bytes 81952 | tf_op jit(solution)/shard_map/ppermute | solution.py:432
  64.4 5.2 %collective-permute-start.11 = (f32[32,256]{1,0:T(8,128)S(1)}, f32[32,256]{1,0:T(8,128)S(1)}, u32[]{:S(2)}, u32[]{:S(2)}) collective-permute-start(f32[32,256]{1,0:T(8,128)S(1)} %get-tuple-element.46), channel_id=1, source_target_pairs={{0,1},{1,0},{2,3},{3,2},{4,5},{5,4},{6,7},{7,6},{8,9},{9,8},{10,11... | collective-permute-start | bytes 98312 | tf_op jit(solution)/shard_map/ppermute | solution.py:500
  69.6 0.9 %collective-permute-done.11.other = f32[32,256]{1,0:T(8,128)S(1)} collective-permute-done((f32[32,256]{1,0:T(8,128)S(1)}, f32[32,256]{1,0:T(8,128)S(1)}, u32[]{:S(2)}, u32[]{:S(2)}) %collective-permute-start.11) | collective-permute-done | bytes 32800 | tf_op jit(solution)/shard_map/ppermute | solution.py:500
  70.5 0.6 shard_map.146
  (27 shorter events, 0.1 us)
Async XLA Ops:
  0.0 5.8 %copy-start.13 = (f32[12,4]{0,1:T(4,128)S(1)}, f32[12,4]{0,1:T(4,128)}, u32[]{:S(2)}) copy-start(f32[12,4]{0,1:T(4,128)} %param.19) | copy-start | bytes 580
  0.0 6.1 %copy-start = (s32[12,64,256]{2,1,0:T(8,128)S(1)}, s32[12,64,256]{2,1,0:T(8,128)}, u32[]{:S(2)}) copy-start(s32[12,64,256]{2,1,0:T(8,128)} %lit_mask.1) | copy-start | bytes 2359300
  0.0 6.1 %copy-start.1 = (bf16[12,64,256]{2,1,0:T(8,128)(2,1)S(1)}, bf16[12,64,256]{2,1,0:T(8,128)(2,1)}, u32[]{:S(2)}) copy-start(bf16[12,64,256]{2,1,0:T(8,128)(2,1)} %images.1) | copy-start | bytes 1179652
  0.0 6.1 %copy-start.5 = (bf16[192,256]{1,0:T(8,128)(2,1)S(1)}, bf16[192,256]{1,0:T(8,128)(2,1)}, u32[]{:S(2)}) copy-start(bf16[192,256]{1,0:T(8,128)(2,1)} %constant.16.clone.expand_hbm.expand) | copy-start | bytes 294916
  0.0 6.1 %copy-start.8 = (f32[64,256]{1,0:T(8,128)S(1)}, f32[64,256]{1,0:T(8,128)}, u32[]{:S(2)}) copy-start(f32[64,256]{1,0:T(8,128)} %height.1) | copy-start | bytes 196612
  0.0 6.1 %copy-start.9 = (f32[64,256]{1,0:T(8,128)S(1)}, f32[64,256]{1,0:T(8,128)}, u32[]{:S(2)}) copy-start(f32[64,256]{1,0:T(8,128)} %albedo.1) | copy-start | bytes 196612
  0.0 6.1 %copy-start.10 = (s32[64,256]{1,0:T(8,128)S(1)}, s32[64,256]{1,0:T(8,128)}, u32[]{:S(2)}) copy-start(s32[64,256]{1,0:T(8,128)} %owner.1) | copy-start | bytes 196612
  2.5 5.6 %collective-permute-start = (f32[27,2,32,128]{3,2,1,0:T(8,128)}, f32[27,2,32,128]{3,2,1,0:T(8,128)S(1)}, u32[]{:S(2)}, u32[]{:S(2)}) collective-permute-start(f32[27,2,32,128]{3,2,1,0:T(8,128)} %shard_map.136), channel_id=1, source_target_pairs={{0,1},{1,0},{2,3},{3,2},{4,5},{5,4},{6,7},{7,6},{8,9},{9,8},{10,11... | collective-permute-start | bytes 2654216 | tf_op jit(solution)/shard_map/ppermute | solution.py:465
  5.9 0.7 copy-start.11
  6.0 0.7 copy-start.12
  8.1 4.3 %collective-permute-start.1 = (f32[2,32,128]{2,1,0:T(8,128)S(1)}, f32[2,32,128]{2,1,0:T(8,128)S(1)}, u32[]{:S(2)}, u32[]{:S(2)}) collective-permute-start(f32[2,32,128]{2,1,0:T(8,128)S(1)} %shard_map.138.near_small), channel_id=1, source_target_pairs={{0,2},{1,3},{2,0},{3,1},{4,6},{5,7},{6,4},{7,5},{8,10},{9,11},{10,... | collective-permute-start | bytes 98312 | tf_op jit(solution)/shard_map/ppermute | solution.py:468
  9.2 24.1 %collective-permute-start.2 = (f32[25,32,128]{2,1,0:T(8,128)S(1)}, f32[25,32,128]{2,1,0:T(8,128)S(1)}, u32[]{:S(2)}, u32[]{:S(2)}) collective-permute-start(f32[25,32,128]{2,1,0:T(8,128)S(1)} %shard_map.139), channel_id=1, source_target_pairs={{0,2},{1,3},{2,0},{3,1},{4,6},{5,7},{6,4},{7,5},{8,10},{9,11},{10,... | collective-permute-start | bytes 1228808 | tf_op jit(solution)/shard_map/ppermute | solution.py:470
  13.0 20.2 %all-to-all-start = ((f32[64,1,128]{2,1,0:T(1,128)}), f32[64,1,128]{2,1,0:T(1,128)S(1)}, u32[]{:S(2)}, u32[]{:S(2)}) async-start(f32[64,1,128]{2,1,0:T(1,128)} %shard_map.140), calls=%async_computation | async-start | bytes 65536 | tf_op jit(solution)/shard_map/all_to_all | solution.py:473
  24.1 9.2 %copy-start.3 = (bf16[256,128]{1,0:T(8,128)(2,1)S(1)}, bf16[256,128]{1,0:T(8,128)(2,1)}, u32[]{:S(2)}) copy-start(bf16[256,128]{1,0:T(8,128)(2,1)} %constant.19.clone.refs_2_) | copy-start | bytes 196612
  24.1 9.2 %copy-start.4 = (bf16[256,128]{1,0:T(8,128)(2,1)S(1)}, bf16[256,128]{1,0:T(8,128)(2,1)}, u32[]{:S(2)}) copy-start(bf16[256,128]{1,0:T(8,128)(2,1)} %constant.20.clone.refs_3_) | copy-start | bytes 196612
  24.1 9.2 %copy-start.7 = (bf16[128,128]{1,0:T(8,128)(2,1)S(1)}, bf16[128,128]{1,0:T(8,128)(2,1)}, u32[]{:S(2)}) copy-start(bf16[128,128]{1,0:T(8,128)(2,1)} %constant.21.clone.refs_4_) | copy-start | bytes 98308
  24.2 9.1 %copy-start.2 = (bf16[128,192]{1,0:T(8,128)(2,1)S(1)}, bf16[128,192]{1,0:T(8,128)(2,1)}, u32[]{:S(2)}) copy-start(bf16[128,192]{1,0:T(8,128)(2,1)} %constant.17.clone.refs_0_) | copy-start | bytes 147460
  24.2 9.1 %collective-permute-start.3 = (f32[5,32,128]{2,1,0:T(8,128)S(1)}, f32[5,32,128]{2,1,0:T(8,128)S(1)}, u32[]{:S(2)}, u32[]{:S(2)}) collective-permute-start(f32[5,32,128]{2,1,0:T(8,128)S(1)} %get-tuple-element.31), channel_id=1, source_target_pairs={{0,253},{1,4},{2,255},{3,6},{4,1},{5,8},{6,3},{7,10},{8,5},{9,12},... | collective-permute-start | bytes 245768 | tf_op jit(solution)/shard_map/ppermute | solution.py:432
  27.3 6.0 %collective-permute-start.4 = (f32[5,32,128]{2,1,0:T(8,128)S(1)}, f32[5,32,128]{2,1,0:T(8,128)S(1)}, u32[]{:S(2)}, u32[]{:S(2)}) collective-permute-start(f32[5,32,128]{2,1,0:T(8,128)S(1)} %get-tuple-element.32), channel_id=1, source_target_pairs={{0,1},{1,0},{2,3},{3,2},{4,5},{5,4},{6,7},{7,6},{8,9},{9,8},{10,11... | collective-permute-start | bytes 245768 | tf_op jit(solution)/shard_map/ppermute | solution.py:432
  30.2 3.1 %copy-start.6 = (bf16[64,256]{1,0:T(8,128)(2,1)S(1)}, bf16[64,256]{1,0:T(8,128)(2,1)}, u32[]{:S(2)}) copy-start(bf16[64,256]{1,0:T(8,128)(2,1)} %constant.18.clone.refs_1_) | copy-start | bytes 98308
  36.3 5.4 %collective-permute-start.5 = (f32[5,32,128]{2,1,0:T(8,128)S(1)}, f32[5,32,128]{2,1,0:T(8,128)S(1)}, u32[]{:S(2)}, u32[]{:S(2)}) collective-permute-start(f32[5,32,128]{2,1,0:T(8,128)S(1)} %get-tuple-element.36), channel_id=1, source_target_pairs={{0,253},{1,4},{2,255},{3,6},{4,1},{5,8},{6,3},{7,10},{8,5},{9,12},... | collective-permute-start | bytes 245768 | tf_op jit(solution)/shard_map/ppermute | solution.py:432
  39.6 2.7 %collective-permute-start.6 = (f32[5,32,128]{2,1,0:T(8,128)S(1)}, f32[5,32,128]{2,1,0:T(8,128)S(1)}, u32[]{:S(2)}, u32[]{:S(2)}) collective-permute-start(f32[5,32,128]{2,1,0:T(8,128)S(1)} %get-tuple-element.37), channel_id=1, source_target_pairs={{0,1},{1,0},{2,3},{3,2},{4,5},{5,4},{6,7},{7,6},{8,9},{9,8},{10,11... | collective-permute-start | bytes 245768 | tf_op jit(solution)/shard_map/ppermute | solution.py:432
  45.2 7.3 %collective-permute-start.7 = (f32[5,32,128]{2,1,0:T(8,128)S(1)}, f32[5,32,128]{2,1,0:T(8,128)S(1)}, u32[]{:S(2)}, u32[]{:S(2)}) collective-permute-start(f32[5,32,128]{2,1,0:T(8,128)S(1)} %get-tuple-element.40), channel_id=1, source_target_pairs={{0,253},{1,4},{2,255},{3,6},{4,1},{5,8},{6,3},{7,10},{8,5},{9,12},... | collective-permute-start | bytes 245768 | tf_op jit(solution)/shard_map/ppermute | solution.py:432
  46.4 7.0 %collective-permute-start.8 = (f32[5,32,128]{2,1,0:T(8,128)S(1)}, f32[5,32,128]{2,1,0:T(8,128)S(1)}, u32[]{:S(2)}, u32[]{:S(2)}) collective-permute-start(f32[5,32,128]{2,1,0:T(8,128)S(1)} %get-tuple-element.41), channel_id=1, source_target_pairs={{0,1},{1,0},{2,3},{3,2},{4,5},{5,4},{6,7},{7,6},{8,9},{9,8},{10,11... | collective-permute-start | bytes 245768 | tf_op jit(solution)/shard_map/ppermute | solution.py:432
  56.2 7.3 %collective-permute-start.9 = (f32[5,32,128]{2,1,0:T(8,128)S(1)}, f32[5,32,128]{2,1,0:T(8,128)S(1)}, u32[]{:S(2)}, u32[]{:S(2)}) collective-permute-start(f32[5,32,128]{2,1,0:T(8,128)S(1)} %get-tuple-element.43), channel_id=1, source_target_pairs={{0,253},{1,4},{2,255},{3,6},{4,1},{5,8},{6,3},{7,10},{8,5},{9,12},... | collective-permute-start | bytes 245768 | tf_op jit(solution)/shard_map/ppermute | solution.py:432
  56.3 8.1 %collective-permute-start.10 = (f32[5,32,128]{2,1,0:T(8,128)S(1)}, f32[5,32,128]{2,1,0:T(8,128)S(1)}, u32[]{:S(2)}, u32[]{:S(2)}) collective-permute-start(f32[5,32,128]{2,1,0:T(8,128)S(1)} %get-tuple-element.44), channel_id=1, source_target_pairs={{0,1},{1,0},{2,3},{3,2},{4,5},{5,4},{6,7},{7,6},{8,9},{9,8},{10,11... | collective-permute-start | bytes 245768 | tf_op jit(solution)/shard_map/ppermute | solution.py:432
  64.4 6.1 %collective-permute-start.11 = (f32[32,256]{1,0:T(8,128)S(1)}, f32[32,256]{1,0:T(8,128)S(1)}, u32[]{:S(2)}, u32[]{:S(2)}) collective-permute-start(f32[32,256]{1,0:T(8,128)S(1)} %get-tuple-element.46), channel_id=1, source_target_pairs={{0,1},{1,0},{2,3},{3,2},{4,5},{5,4},{6,7},{7,6},{8,9},{9,8},{10,11... | collective-permute-start | bytes 98312 | tf_op jit(solution)/shard_map/ppermute | solution.py:500

commit v6 on v5

--- a/solution.py
+++ b/solution.py
@@ -32,7 +32,6 @@
 F32 = jnp.float32
 BF16 = jnp.bfloat16
 VMEM = pl.BlockSpec(memory_space=pltpu.VMEM)
-SMEM = pl.BlockSpec(memory_space=pltpu.SMEM)
 PARAMS = pltpu.CompilerParams(vmem_limit_bytes=24 * 2**20)
 LARGE = pltpu.CompilerParams(vmem_limit_bytes=58 * 2**20)
 
@@ -234,14 +233,14 @@
 
 
 def image_term(coef, k, observed, lit, flat_part, flat_shade, mix_shade, slope_lon, slope_lat):
-    steep = coef[k, 2] - coef[k, 0] * slope_lon - coef[k, 1] * slope_lat
+    steep = coef[2, k : k + 1] - coef[0, k : k + 1] * slope_lon - coef[1, k : k + 1] * slope_lat
     decay = jnp.exp(-jnp.abs(steep))
     whole = 1.0 + decay
     part = jnp.maximum(steep, 0.0) + jnp.log(whole)
-    ratio = 1.0 / (part + coef[k, 3])
+    ratio = 1.0 / (part + coef[3, k : k + 1])
     gate = jnp.where(steep >= 0.0, 1.0, decay) / whole
     residual = lit * (part * (mix_shade * ratio + flat_shade) - observed)
-    pull = residual * ((coef[k, 4] * (ratio * ratio) + flat_part) * gate)
+    pull = residual * ((coef[4, k : k + 1] * (ratio * ratio) + flat_part) * gate)
     return pull, residual * part
 
 
@@ -258,7 +257,7 @@
 
 
 def add_image(sums, coef, k, pull, norm):
-    terms = (coef[k, 5] * pull, coef[k, 6] * pull, norm)
+    terms = (coef[5, k : k + 1] * pull, coef[6, k : k + 1] * pull, norm)
     return terms if sums is None else tuple(a + b for a, b in zip(sums, terms))
 
 
@@ -307,7 +306,7 @@
     return [gain * alt[j] - (gain / (OWN * OWN)) * owner_sum[rows[j]] for j in tiles]
 
 
-def contribute(surface, aux, misfit, grad_lon, grad_lat, tables, z_out, inter_out, intra_out):
+def contribute(surface, aux, misfit, grad_lon, grad_lat, tables, z_out):
     forward, backward, smooth, slope, quads = tables
     tiles = range(TILES)
 
@@ -330,8 +329,6 @@
         z_out[j, 0:RAD] = change[0:RAD]
         z_out[j, RAD : RAD + STRIP] = change[RAD : RAD + STRIP] + surface[j][RAD : RAD + STRIP]
         z_out[j, RAD + STRIP : EXT] = change[RAD + STRIP : EXT]
-    core = place()[1]
-    route(core, z_out[:, 0:STRIP], z_out[:, STRIP:EXT], inter_out, intra_out)
 
 
 def arrived(inter, intra):
@@ -343,7 +340,7 @@
 
 
 def surface_step(
-    coef, weight, kept, received, halo, surface, aux, alt, tables, z_out, inter_out, intra_out, fields
+    coef, weight, kept, received, halo, surface, aux, alt, tables, z_out, fields
 ):
     slope_lon, slope_lat, grad_lon, grad_lat = fields
     misfit = slopes_and_misfit(surface, aux, alt, tables, slope_lon, slope_lat)
@@ -356,7 +353,7 @@
             pull, norm = image_term(coef, k, ref[(k, *index)], lit, *shade, lon, lat)
             sums = add_image(sums, coef, k, pull, norm)
         grad_lon[rows], grad_lat[rows] = gradients(albedo, inverse, lon, lat, sums)
-    contribute(surface, aux, misfit, grad_lon, grad_lat, tables, z_out, inter_out, intra_out)
+    contribute(surface, aux, misfit, grad_lon, grad_lat, tables, z_out)
 
 
 def first_kernel(coef, counts, kept, received, halo, z, inter, intra, aux, *refs):
@@ -369,8 +366,9 @@
     below = jnp.concatenate([jnp.zeros((TILES, RAD, LANES), F32), below[:, RAD:]], axis=1)
     surface = [z[j] + jnp.concatenate([above[j], below[j]], axis=0) for j in range(TILES)]
     surface_step(
-        coef, weight, kept, received, halo, surface, aux, alt, tables, z_out, inter_out, intra_out, fields
-    )
+        coef, weight, kept, received, halo, surface, aux, alt, tables, z_out, fields
+    )
+    route(place()[1], z_out[:, 0:STRIP], z_out[:, STRIP:EXT], inter_out, intra_out)
 
 
 def step_kernel(coef, weight, kept, received, halo, z, inter, intra, aux, alt, *refs):
@@ -378,26 +376,45 @@
     above, below = arrived(inter, intra)
     surface = [z[j] + jnp.concatenate([above[j], below[j]], axis=0) for j in range(TILES)]
     surface_step(
-        coef, weight[...], kept, received, halo, surface, aux, alt, tables, z_out, inter_out, intra_out, fields
-    )
-
-
-def end_kernel(z, inter, intra, kept, sent):
+        coef, weight[...], kept, received, halo, surface, aux, alt, tables, z_out, fields
+    )
+    route(place()[1], z_out[:, 0:STRIP], z_out[:, STRIP:EXT], inter_out, intra_out)
+
+
+def last_kernel(coef, weight, kept, received, halo, z, inter, intra, aux, alt, *refs):
+    tables, (mine, inter_out, intra_out, z_out), fields = refs[:5], refs[5:9], refs[9:]
+    above, below = arrived(inter, intra)
+    surface = [z[j] + jnp.concatenate([above[j], below[j]], axis=0) for j in range(TILES)]
+    surface_step(
+        coef, weight[...], kept, received, halo, surface, aux, alt, tables, z_out, fields
+    )
     half, core = place()
-    for ref, side in ((kept, core), (sent, 1 - core)):
-        for t in range(2):
-            at = own_tile(half, side, t)
-            above = jnp.where(core == 0, inter[at], intra[at])
-            below = jnp.where(core == 0, intra[at], inter[at])
-            cols = slice(t * LANES, (t + 1) * LANES)
-            ref[0:RAD, cols] = z[at, RAD : 2 * RAD] + above[RAD:]
-            ref[RAD:STRIP, cols] = z[at, 2 * RAD : RAD + STRIP] + below[0:RAD]
-
-
-def place_kernel(mine, other, out):
+    for t in range(2):
+        mine[t] = z_out[own_tile(half, core, t)]
+        intra_out[t] = z_out[own_tile(half, 1 - core, t)]
+    for t in range(TILES - 1):
+        inter_out[t] = jnp.where(core == 0, z_out[half + t, 0:RAD], z_out[half + t, EXT - RAD : EXT])
+
+
+def forward_kernel(inter, forward):
     core = place()[1]
-    out[pl.ds(pl.multiple_of(core * STRIP, STRIP), STRIP)] = mine[...]
-    out[pl.ds(pl.multiple_of((1 - core) * STRIP, STRIP), STRIP)] = other[...]
+    for t in range(2):
+        forward[t] = inter[2 * (1 - core) + t]
+
+
+def place_kernel(mine, intra, inter, forward, out):
+    core = place()[1]
+    for t in range(2):
+        upper = jnp.where(core == 0, mine[t], intra[t])
+        lower = jnp.where(core == 0, intra[t], mine[t])
+        direct = inter[2 * core + t]
+        top = jnp.where(core == 0, direct, forward[t])
+        bottom = jnp.where(core == 0, forward[t], direct)
+        cols = slice(t * LANES, (t + 1) * LANES)
+        out[0:RAD, cols] = upper[RAD : 2 * RAD] + top
+        out[RAD : 2 * RAD, cols] = upper[2 * RAD : 3 * RAD] + lower[0:RAD]
+        out[2 * RAD : 3 * RAD, cols] = lower[RAD : 2 * RAD] + upper[3 * RAD : EXT]
+        out[3 * RAD : EXT, cols] = lower[2 * RAD : 3 * RAD] + bottom
 
 
 def f32(*shape):
@@ -405,11 +422,10 @@
 
 
 def call(kernel, out_shape, *args, scratch=()):
-    scalars = kernel in (first_kernel, step_kernel)
     return pl.pallas_call(
         kernel,
         out_shape=out_shape,
-        in_specs=[SMEM if scalars and i == 0 else VMEM for i in range(len(args))],
+        in_specs=[VMEM] * len(args),
         out_specs=jax.tree.map(lambda _: VMEM, out_shape),
         scratch_shapes=list(scratch),
         compiler_params=PARAMS,
@@ -432,19 +448,16 @@
         return lax.ppermute(inter, axes, across_strips), lax.ppermute(intra, axes, across_cores)
 
     sun_lon, sun_lat, sun_up, view = (geometry[:, i] for i in range(4))
-    coef = jnp.stack(
-        [
-            SHARPNESS * sun_lon,
-            SHARPNESS * sun_lat,
-            SHARPNESS * sun_up,
-            SHARPNESS * view,
-            (LUNAR_MIX * SHARPNESS * SHARPNESS) * view,
-            -sun_lon,
-            -sun_lat,
-        ],
-        axis=1,
-    )
-
+    rows = [
+        SHARPNESS * sun_lon,
+        SHARPNESS * sun_lat,
+        SHARPNESS * sun_up,
+        SHARPNESS * view,
+        (LUNAR_MIX * SHARPNESS * SHARPNESS) * view,
+        -sun_lon,
+        -sun_lat,
+    ]
+    coef = jnp.stack([jnp.broadcast_to(row[:, None], (IMAGES, LANES)) for row in rows])
     expand = np.arange(altimetry.shape[1])[:, None] == np.arange(2 * LANES)[None, :] // OWN
     expand = jnp.asarray(np.concatenate([expand] * 3, axis=0), BF16)
     count = lit_count.reshape(1, IMAGES)
@@ -486,7 +499,7 @@
         coef, counts, kept, received, halo, z, inter, intra, aux, *tables,
         scratch=scratch,
     )
-    for _ in range(ITERS - 1):
+    for _ in range(ITERS - 2):
         inter, intra = exchange(inter, intra)
         z, inter, intra = call(
             step_kernel,
@@ -495,10 +508,16 @@
             scratch=scratch,
         )
     inter, intra = exchange(inter, intra)
-    half_out = f32(STRIP, 2 * LANES)
-    mine, other = call(end_kernel, (half_out, half_out), z, inter, intra)
-    other = lax.ppermute(other, axes, across_cores)
-    return call(place_kernel, f32(2 * STRIP, 2 * LANES), mine, other)
+    mine, inter, intra = call(
+        last_kernel,
+        (f32(2, EXT, LANES), f32(TILES - 1, RAD, LANES), f32(2, EXT, LANES)),
+        coef, weight, kept, received, halo, z, inter, intra, aux, alt, *tables,
+        scratch=[pltpu.VMEM((TILES, EXT, LANES), F32)] + scratch,
+    )
+    inter, intra = exchange(inter, intra)
+    passed = call(forward_kernel, f32(2, RAD, LANES), inter)
+    passed = lax.ppermute(passed, axes, across_cores)
+    return call(place_kernel, f32(2 * STRIP, 2 * LANES), mine, intra, inter, passed)
 
 
 def solution(mesh):

time: 71.3 us -> 68.9 us (0.966)
  starting transfers between devices: 48.3 us -> 45.4 us
  waiting for transfers between devices: 8.9 us -> 11.2 us
  Pallas kernels: 12.6 us -> 10.7 us
    ppermute x4, waiting for transfers between devices: 0.32 us -> 3.64 us  [exchange(): lax.ppermute(inter, axes, across_strips)]
    pallas_call x10, Pallas kernels: 10.2 us -> 8.23 us  [call(): pl.pallas_call(kernel, out_shape=out_shape, in_specs=[VMEM] * len(args),...]
    ppermute x4, starting transfers between devices: 17.9 us -> 16 us  [exchange(): lax.ppermute(intra, axes, across_cores)]
    ppermute x1, starting transfers between devices: 5.24 us -> 4.32 us  [per_device(): passed = lax.ppermute(passed, axes, across_cores)]
    ppermute x4, waiting for transfers between devices: 2.45 us -> 1.55 us  [exchange(): lax.ppermute(intra, axes, across_cores)]
where the time goes in v6:
time: 68.9 us; the launch traced here: 68.6 us
  starting transfers between devices  45.4 us (66%)
  waiting for transfers between devices  11.2 us (16%)
  Pallas kernels  10.7 us (16%)
  local copies, waits for them, and re-layouts  1.09 us (2%)
    ppermute x4, starting transfers between devices, exchange(): lax.ppermute(intra, axes, across_cores)  16 us
    all_to_all x1, starting transfers between devices, per_device(): counts = lax.all_to_all(counts, 'lon', 0, 0)  11 us
    pallas_call x10, Pallas kernels, call(): pl.pallas_call(kernel, out_shape=out_shape, in_specs=[VMEM] * len(args),...  8.23 us
    ppermute x4, starting transfers between devices, exchange(): lax.ppermute(inter, axes, across_strips)  7.6 us
    ppermute x1, starting transfers between devices, per_device(): passed = lax.ppermute(passed, axes, across_cores)  4.32 us
    ppermute x4, waiting for transfers between devices, exchange(): lax.ppermute(inter, axes, across_strips)  3.64 us
    ppermute x1, starting transfers between devices, per_device(): received = lax.ppermute(sent, axes, across_cores)  3.31 us
    all_to_all x1, waiting for transfers between devices, per_device(): counts = lax.all_to_all(counts, 'lon', 0, 0)  2.97 us
  transfers between devices with their start and end apart: 13, of which 8 were waited for; matrix products, arithmetic and copies ran while one was open for 1% of the time, Pallas kernels for 1%

profile of v6, /device:TPU:1, one launch (start us, length us, event | category | flops | bytes accessed | tf_op | source)
XLA Modules:
  0.0 68.6 jit_solution(10887727520269656395)
XLA Ops:
  0.0 0.0 copy-start.5
  0.1 2.5 %shard_map.136 = f32[27,2,32,128]{3,2,1,0:T(8,128)} custom-call(bf16[12,64,256]{2,1,0:T(8,128)(2,1)} %images.1, s32[12,64,256]{2,1,0:T(8,128)} %lit_mask.1, f32[64,256]{1,0:T(8,128)} %height.1, f32[64,256]{1,0:T(8,128)} %albedo.1, s32[64,256]{1,0:T(8,128)} %owner.1, f32[16,64]{1,0:T(8,128)} %altimetry.1, s32[1,12]{1,0:T(1,128)} %bitcast.15, ...), custom_call_target="tpu_custom_call" | custom-call | tf_op jit(solution)/shard_map/pallas_call | solution.py:468
  2.5 0.0 copy-start.11
  2.5 3.3 %collective-permute-start = (f32[27,2,32,128]{3,2,1,0:T(8,128)}, f32[27,2,32,128]{3,2,1,0:T(8,128)S(1)}, u32[]{:S(2)}, u32[]{:S(2)}) collective-permute-start(f32[27,2,32,128]{3,2,1,0:T(8,128)} %shard_map.136), channel_id=1, source_target_pairs={{0,1},{1,0},{2,3},{3,2},{4,5},{5,4},{6,7},{7,6},{8,9},{9,8},{10,11... | collective-permute-start | bytes 2654216 | tf_op jit(solution)/shard_map/ppermute | solution.py:478
  5.8 0.0 copy-start.12
  5.9 0.1 constant_dynamic-update-slice_fusion.6
  6.0 0.5 copy-done.12
  6.5 0.2 shard_map.137.kept
  6.7 0.1 constant_dynamic-update-slice_fusion.5
  6.8 0.1 constant_dynamic-update-slice_fusion.4
  6.8 0.1 constant_dynamic-update-slice_fusion.3
  6.9 0.1 constant_dynamic-update-slice_fusion.2
  7.0 1.1 %collective-permute-done.received = f32[27,2,32,128]{3,2,1,0:T(8,128)S(1)} collective-permute-done((f32[27,2,32,128]{3,2,1,0:T(8,128)}, f32[27,2,32,128]{3,2,1,0:T(8,128)S(1)}, u32[]{:S(2)}, u32[]{:S(2)}) %collective-permute-start) | collective-permute-done | bytes 884768 | tf_op jit(solution)/shard_map/ppermute | solution.py:478
  8.1 1.1 %collective-permute-start.1 = (f32[2,32,128]{2,1,0:T(8,128)S(1)}, f32[2,32,128]{2,1,0:T(8,128)S(1)}, u32[]{:S(2)}, u32[]{:S(2)}) collective-permute-start(f32[2,32,128]{2,1,0:T(8,128)S(1)} %shard_map.138.near_small), channel_id=1, source_target_pairs={{0,2},{1,3},{2,0},{3,1},{4,6},{5,7},{6,4},{7,5},{8,10},{9,11},{10,... | collective-permute-start | bytes 98312 | tf_op jit(solution)/shard_map/ppermute | solution.py:481
  9.2 2.0 %collective-permute-start.2 = (f32[25,32,128]{2,1,0:T(8,128)S(1)}, f32[25,32,128]{2,1,0:T(8,128)S(1)}, u32[]{:S(2)}, u32[]{:S(2)}) collective-permute-start(f32[25,32,128]{2,1,0:T(8,128)S(1)} %shard_map.139), channel_id=1, source_target_pairs={{0,2},{1,3},{2,0},{3,1},{4,6},{5,7},{6,4},{7,5},{8,10},{9,11},{10,... | collective-permute-start | bytes 1228808 | tf_op jit(solution)/shard_map/ppermute | solution.py:483
  11.2 0.1 constant_dynamic-update-slice_fusion.1
  11.3 1.1 %collective-permute-done.1.halo_small = f32[2,32,128]{2,1,0:T(8,128)S(1)} collective-permute-done((f32[2,32,128]{2,1,0:T(8,128)S(1)}, f32[2,32,128]{2,1,0:T(8,128)S(1)}, u32[]{:S(2)}, u32[]{:S(2)}) %collective-permute-start.1) | collective-permute-done | bytes 32800 | tf_op jit(solution)/shard_map/ppermute | solution.py:481
  12.4 0.6 shard_map.140
  13.1 11.0 %all-to-all-start = ((f32[64,1,128]{2,1,0:T(1,128)}), f32[64,1,128]{2,1,0:T(1,128)S(1)}, u32[]{:S(2)}, u32[]{:S(2)}) async-start(f32[64,1,128]{2,1,0:T(1,128)} %shard_map.140), calls=%async_computation | async-start | bytes 65536 | tf_op jit(solution)/shard_map/all_to_all | solution.py:486
  24.1 0.0 copy-start.2
  24.1 0.0 copy-start.3
  24.1 0.0 copy-start.4
  24.1 0.0 copy-start.6
  24.2 0.0 copy-start.7
  24.2 3.1 %collective-permute-start.3 = (f32[5,32,128]{2,1,0:T(8,128)S(1)}, f32[5,32,128]{2,1,0:T(8,128)S(1)}, u32[]{:S(2)}, u32[]{:S(2)}) collective-permute-start(f32[5,32,128]{2,1,0:T(8,128)S(1)} %get-tuple-element.29), channel_id=1, source_target_pairs={{0,253},{1,4},{2,255},{3,6},{4,1},{5,8},{6,3},{7,10},{8,5},{9,12},... | collective-permute-start | bytes 245768 | tf_op jit(solution)/shard_map/ppermute | solution.py:448
  27.3 2.9 %collective-permute-start.4 = (f32[5,32,128]{2,1,0:T(8,128)S(1)}, f32[5,32,128]{2,1,0:T(8,128)S(1)}, u32[]{:S(2)}, u32[]{:S(2)}) collective-permute-start(f32[5,32,128]{2,1,0:T(8,128)S(1)} %get-tuple-element.30), channel_id=1, source_target_pairs={{0,1},{1,0},{2,3},{3,2},{4,5},{5,4},{6,7},{7,6},{8,9},{9,8},{10,11... | collective-permute-start | bytes 245768 | tf_op jit(solution)/shard_map/ppermute | solution.py:448
  30.2 0.1 constant_dynamic-update-slice_fusion.coef
  30.3 3.0 %all-to-all-done.counts = f32[64,1,128]{2,1,0:T(1,128)S(1)} async-done(((f32[64,1,128]{2,1,0:T(1,128)}), f32[64,1,128]{2,1,0:T(1,128)S(1)}, u32[]{:S(2)}, u32[]{:S(2)}) %all-to-all-start) | async-done | bytes 32800 | tf_op jit(solution)/shard_map/all_to_all | solution.py:486
  33.3 0.0 collective-permute-done.3.inter
  33.3 0.0 collective-permute-done.4.intra
  33.3 0.0 collective-permute-done.2.halo
  33.3 2.3 %shard_map.142 = (f32[5,64,128]{2,1,0:T(8,128)S(1)}, f32[5,32,128]{2,1,0:T(8,128)S(1)}, f32[5,32,128]{2,1,0:T(8,128)S(1)}, f32[5,16,128]{2,1,0:T(8,128)S(1)}, f32[16,128]{1,0:T(8,128)S(1)}) custom-call(f32[7,12,128]{2,1,0:T(8,128)S(1)} %constant_dynamic-update-slice_fusion.coef, f32[64,1,128]{2,1,0:T(1,128)S(1)} %all-to-all-done.counts, ...), custom_call_target="tpu_custom_call" | custom-call | tf_op jit(solution)/shard_map/pallas_call | solution.py:425
  35.7 3.3 %collective-permute-start.5 = (f32[5,32,128]{2,1,0:T(8,128)S(1)}, f32[5,32,128]{2,1,0:T(8,128)S(1)}, u32[]{:S(2)}, u32[]{:S(2)}) collective-permute-start(f32[5,32,128]{2,1,0:T(8,128)S(1)} %get-tuple-element.34), channel_id=1, source_target_pairs={{0,253},{1,4},{2,255},{3,6},{4,1},{5,8},{6,3},{7,10},{8,5},{9,12},... | collective-permute-start | bytes 245768 | tf_op jit(solution)/shard_map/ppermute | solution.py:448
  39.0 1.8 %collective-permute-start.6 = (f32[5,32,128]{2,1,0:T(8,128)S(1)}, f32[5,32,128]{2,1,0:T(8,128)S(1)}, u32[]{:S(2)}, u32[]{:S(2)}) collective-permute-start(f32[5,32,128]{2,1,0:T(8,128)S(1)} %get-tuple-element.35), channel_id=1, source_target_pairs={{0,1},{1,0},{2,3},{3,2},{4,5},{5,4},{6,7},{7,6},{8,9},{9,8},{10,11... | collective-permute-start | bytes 245768 | tf_op jit(solution)/shard_map/ppermute | solution.py:448
  40.8 0.3 collective-permute-done.5.inter
  41.1 0.6 collective-permute-done.6.intra
  41.7 2.2 %shard_map.143 = (f32[5,64,128]{2,1,0:T(8,128)S(1)}, f32[5,32,128]{2,1,0:T(8,128)S(1)}, f32[5,32,128]{2,1,0:T(8,128)S(1)}) custom-call(f32[7,12,128]{2,1,0:T(8,128)S(1)} %constant_dynamic-update-slice_fusion.coef, f32[16,128]{1,0:T(8,128)S(1)} %get-tuple-element.32.weight, f32[27,2,32,128]{3,2,1,0:T(8,128)S(1)} %shard_map.137.kept, ...), custom_call_target="tpu_custom_call" | custom-call | tf_op jit(solution)/shard_map/pallas_call | solution.py:425
  43.9 1.2 %collective-permute-start.7 = (f32[5,32,128]{2,1,0:T(8,128)S(1)}, f32[5,32,128]{2,1,0:T(8,128)S(1)}, u32[]{:S(2)}, u32[]{:S(2)}) collective-permute-start(f32[5,32,128]{2,1,0:T(8,128)S(1)} %get-tuple-element.38), channel_id=1, source_target_pairs={{0,253},{1,4},{2,255},{3,6},{4,1},{5,8},{6,3},{7,10},{8,5},{9,12},... | collective-permute-start | bytes 245768 | tf_op jit(solution)/shard_map/ppermute | solution.py:448
  45.1 6.1 %collective-permute-start.8 = (f32[5,32,128]{2,1,0:T(8,128)S(1)}, f32[5,32,128]{2,1,0:T(8,128)S(1)}, u32[]{:S(2)}, u32[]{:S(2)}) collective-permute-start(f32[5,32,128]{2,1,0:T(8,128)S(1)} %get-tuple-element.39), channel_id=1, source_target_pairs={{0,1},{1,0},{2,3},{3,2},{4,5},{5,4},{6,7},{7,6},{8,9},{9,8},{10,11... | collective-permute-start | bytes 245768 | tf_op jit(solution)/shard_map/ppermute | solution.py:448
  51.2 0.0 collective-permute-done.7.inter
  51.2 0.9 %collective-permute-done.8.intra = f32[5,32,128]{2,1,0:T(8,128)S(1)} collective-permute-done((f32[5,32,128]{2,1,0:T(8,128)S(1)}, f32[5,32,128]{2,1,0:T(8,128)S(1)}, u32[]{:S(2)}, u32[]{:S(2)}) %collective-permute-start.8) | collective-permute-done | bytes 81952 | tf_op jit(solution)/shard_map/ppermute | solution.py:448
  52.1 2.2 %shard_map.144 = (f32[2,64,128]{2,1,0:T(8,128)S(1)}, f32[4,16,128]{2,1,0:T(8,128)S(1)}, f32[2,64,128]{2,1,0:T(8,128)S(1)}) custom-call(f32[7,12,128]{2,1,0:T(8,128)S(1)} %constant_dynamic-update-slice_fusion.coef, f32[16,128]{1,0:T(8,128)S(1)} %get-tuple-element.32.weight, f32[27,2,32,128]{3,2,1,0:T(8,128)S(1)} %shard_map.137.kept, ...), custom_call_target="tpu_custom_call" | custom-call | tf_op jit(solution)/shard_map/pallas_call | solution.py:425
  54.3 5.2 %collective-permute-start.9 = (f32[2,64,128]{2,1,0:T(8,128)S(1)}, f32[2,64,128]{2,1,0:T(8,128)S(1)}, u32[]{:S(2)}, u32[]{:S(2)}) collective-permute-start(f32[2,64,128]{2,1,0:T(8,128)S(1)} %get-tuple-element.41), channel_id=1, source_target_pairs={{0,1},{1,0},{2,3},{3,2},{4,5},{5,4},{6,7},{7,6},{8,9},{9,8},{10,11... | collective-permute-start | bytes 196616 | tf_op jit(solution)/shard_map/ppermute | solution.py:448
  59.5 0.0 collective-permute-start.10
  59.5 3.3 %collective-permute-done.10.inter = f32[4,16,128]{2,1,0:T(8,128)S(1)} collective-permute-done((f32[4,16,128]{2,1,0:T(8,128)S(1)}, f32[4,16,128]{2,1,0:T(8,128)S(1)}, u32[]{:S(2)}, u32[]{:S(2)}) %collective-permute-start.10) | collective-permute-done | bytes 32800 | tf_op jit(solution)/shard_map/ppermute | solution.py:448
  62.8 4.3 %collective-permute-start.11 = (f32[2,16,128]{2,1,0:T(8,128)S(1)}, f32[2,16,128]{2,1,0:T(8,128)S(1)}, u32[]{:S(2)}, u32[]{:S(2)}) collective-permute-start(f32[2,16,128]{2,1,0:T(8,128)S(1)} %shard_map.145), channel_id=1, source_target_pairs={{0,1},{1,0},{2,3},{3,2},{4,5},{5,4},{6,7},{7,6},{8,9},{9,8},{10,11... | collective-permute-start | bytes 49160 | tf_op jit(solution)/shard_map/ppermute | solution.py:519
  67.2 0.8 %collective-permute-done.11.forward = f32[2,16,128]{2,1,0:T(8,128)S(1)} collective-permute-done((f32[2,16,128]{2,1,0:T(8,128)S(1)}, f32[2,16,128]{2,1,0:T(8,128)S(1)}, u32[]{:S(2)}, u32[]{:S(2)}) %collective-permute-start.11) | collective-permute-done | bytes 16416 | tf_op jit(solution)/shard_map/ppermute | solution.py:519
  68.0 0.6 shard_map.146
  (26 shorter events, 0.1 us)
Async XLA Ops:
  0.0 5.8 %copy-start.13 = (f32[12,4]{0,1:T(4,128)S(1)}, f32[12,4]{0,1:T(4,128)}, u32[]{:S(2)}) copy-start(f32[12,4]{0,1:T(4,128)} %param.19) | copy-start | bytes 580
  0.0 5.9 %copy-start = (s32[12,64,256]{2,1,0:T(8,128)S(1)}, s32[12,64,256]{2,1,0:T(8,128)}, u32[]{:S(2)}) copy-start(s32[12,64,256]{2,1,0:T(8,128)} %lit_mask.1) | copy-start | bytes 2359300
  0.0 5.9 %copy-start.1 = (bf16[12,64,256]{2,1,0:T(8,128)(2,1)S(1)}, bf16[12,64,256]{2,1,0:T(8,128)(2,1)}, u32[]{:S(2)}) copy-start(bf16[12,64,256]{2,1,0:T(8,128)(2,1)} %images.1) | copy-start | bytes 1179652
  0.0 5.9 %copy-start.5 = (bf16[192,256]{1,0:T(8,128)(2,1)S(1)}, bf16[192,256]{1,0:T(8,128)(2,1)}, u32[]{:S(2)}) copy-start(bf16[192,256]{1,0:T(8,128)(2,1)} %constant.16.clone.expand_hbm.expand) | copy-start | bytes 294916
  0.0 5.9 %copy-start.8 = (f32[64,256]{1,0:T(8,128)S(1)}, f32[64,256]{1,0:T(8,128)}, u32[]{:S(2)}) copy-start(f32[64,256]{1,0:T(8,128)} %height.1) | copy-start | bytes 196612
  0.0 5.9 %copy-start.9 = (f32[64,256]{1,0:T(8,128)S(1)}, f32[64,256]{1,0:T(8,128)}, u32[]{:S(2)}) copy-start(f32[64,256]{1,0:T(8,128)} %albedo.1) | copy-start | bytes 196612
  0.0 5.9 %copy-start.10 = (s32[64,256]{1,0:T(8,128)S(1)}, s32[64,256]{1,0:T(8,128)}, u32[]{:S(2)}) copy-start(s32[64,256]{1,0:T(8,128)} %owner.1) | copy-start | bytes 196612
  2.5 3.5 %copy-start.11 = (f32[16,64]{1,0:T(8,128)S(1)}, f32[16,64]{1,0:T(8,128)}, u32[]{:S(2)}) copy-start(f32[16,64]{1,0:T(8,128)} %altimetry.1) | copy-start | bytes 12292
  2.5 5.6 %collective-permute-start = (f32[27,2,32,128]{3,2,1,0:T(8,128)}, f32[27,2,32,128]{3,2,1,0:T(8,128)S(1)}, u32[]{:S(2)}, u32[]{:S(2)}) collective-permute-start(f32[27,2,32,128]{3,2,1,0:T(8,128)} %shard_map.136), channel_id=1, source_target_pairs={{0,1},{1,0},{2,3},{3,2},{4,5},{5,4},{6,7},{7,6},{8,9},{9,8},{10,11... | collective-permute-start | bytes 2654216 | tf_op jit(solution)/shard_map/ppermute | solution.py:478
  5.8 0.7 copy-start.12
  8.1 4.3 %collective-permute-start.1 = (f32[2,32,128]{2,1,0:T(8,128)S(1)}, f32[2,32,128]{2,1,0:T(8,128)S(1)}, u32[]{:S(2)}, u32[]{:S(2)}) collective-permute-start(f32[2,32,128]{2,1,0:T(8,128)S(1)} %shard_map.138.near_small), channel_id=1, source_target_pairs={{0,2},{1,3},{2,0},{3,1},{4,6},{5,7},{6,4},{7,5},{8,10},{9,11},{10,... | collective-permute-start | bytes 98312 | tf_op jit(solution)/shard_map/ppermute | solution.py:481
  9.2 24.1 %collective-permute-start.2 = (f32[25,32,128]{2,1,0:T(8,128)S(1)}, f32[25,32,128]{2,1,0:T(8,128)S(1)}, u32[]{:S(2)}, u32[]{:S(2)}) collective-permute-start(f32[25,32,128]{2,1,0:T(8,128)S(1)} %shard_map.139), channel_id=1, source_target_pairs={{0,2},{1,3},{2,0},{3,1},{4,6},{5,7},{6,4},{7,5},{8,10},{9,11},{10,... | collective-permute-start | bytes 1228808 | tf_op jit(solution)/shard_map/ppermute | solution.py:483
  13.1 20.2 %all-to-all-start = ((f32[64,1,128]{2,1,0:T(1,128)}), f32[64,1,128]{2,1,0:T(1,128)S(1)}, u32[]{:S(2)}, u32[]{:S(2)}) async-start(f32[64,1,128]{2,1,0:T(1,128)} %shard_map.140), calls=%async_computation | async-start | bytes 65536 | tf_op jit(solution)/shard_map/all_to_all | solution.py:486
  24.1 9.2 %copy-start.2 = (bf16[128,192]{1,0:T(8,128)(2,1)S(1)}, bf16[128,192]{1,0:T(8,128)(2,1)}, u32[]{:S(2)}) copy-start(bf16[128,192]{1,0:T(8,128)(2,1)} %constant.17.clone.refs_0_) | copy-start | bytes 147460
  24.1 9.2 %copy-start.3 = (bf16[256,128]{1,0:T(8,128)(2,1)S(1)}, bf16[256,128]{1,0:T(8,128)(2,1)}, u32[]{:S(2)}) copy-start(bf16[256,128]{1,0:T(8,128)(2,1)} %constant.19.clone.refs_2_) | copy-start | bytes 196612
  24.1 9.2 %copy-start.4 = (bf16[256,128]{1,0:T(8,128)(2,1)S(1)}, bf16[256,128]{1,0:T(8,128)(2,1)}, u32[]{:S(2)}) copy-start(bf16[256,128]{1,0:T(8,128)(2,1)} %constant.20.clone.refs_3_) | copy-start | bytes 196612
  24.1 9.2 %copy-start.6 = (bf16[64,256]{1,0:T(8,128)(2,1)S(1)}, bf16[64,256]{1,0:T(8,128)(2,1)}, u32[]{:S(2)}) copy-start(bf16[64,256]{1,0:T(8,128)(2,1)} %constant.18.clone.refs_1_) | copy-start | bytes 98308
  24.2 9.2 %copy-start.7 = (bf16[128,128]{1,0:T(8,128)(2,1)S(1)}, bf16[128,128]{1,0:T(8,128)(2,1)}, u32[]{:S(2)}) copy-start(bf16[128,128]{1,0:T(8,128)(2,1)} %constant.21.clone.refs_4_) | copy-start | bytes 98308
  24.2 9.1 %collective-permute-start.3 = (f32[5,32,128]{2,1,0:T(8,128)S(1)}, f32[5,32,128]{2,1,0:T(8,128)S(1)}, u32[]{:S(2)}, u32[]{:S(2)}) collective-permute-start(f32[5,32,128]{2,1,0:T(8,128)S(1)} %get-tuple-element.29), channel_id=1, source_target_pairs={{0,253},{1,4},{2,255},{3,6},{4,1},{5,8},{6,3},{7,10},{8,5},{9,12},... | collective-permute-start | bytes 245768 | tf_op jit(solution)/shard_map/ppermute | solution.py:448
  27.3 6.0 %collective-permute-start.4 = (f32[5,32,128]{2,1,0:T(8,128)S(1)}, f32[5,32,128]{2,1,0:T(8,128)S(1)}, u32[]{:S(2)}, u32[]{:S(2)}) collective-permute-start(f32[5,32,128]{2,1,0:T(8,128)S(1)} %get-tuple-element.30), channel_id=1, source_target_pairs={{0,1},{1,0},{2,3},{3,2},{4,5},{5,4},{6,7},{7,6},{8,9},{9,8},{10,11... | collective-permute-start | bytes 245768 | tf_op jit(solution)/shard_map/ppermute | solution.py:448
  35.7 5.4 %collective-permute-start.5 = (f32[5,32,128]{2,1,0:T(8,128)S(1)}, f32[5,32,128]{2,1,0:T(8,128)S(1)}, u32[]{:S(2)}, u32[]{:S(2)}) collective-permute-start(f32[5,32,128]{2,1,0:T(8,128)S(1)} %get-tuple-element.34), channel_id=1, source_target_pairs={{0,253},{1,4},{2,255},{3,6},{4,1},{5,8},{6,3},{7,10},{8,5},{9,12},... | collective-permute-start | bytes 245768 | tf_op jit(solution)/shard_map/ppermute | solution.py:448
  39.0 2.8 %collective-permute-start.6 = (f32[5,32,128]{2,1,0:T(8,128)S(1)}, f32[5,32,128]{2,1,0:T(8,128)S(1)}, u32[]{:S(2)}, u32[]{:S(2)}) collective-permute-start(f32[5,32,128]{2,1,0:T(8,128)S(1)} %get-tuple-element.35), channel_id=1, source_target_pairs={{0,1},{1,0},{2,3},{3,2},{4,5},{5,4},{6,7},{7,6},{8,9},{9,8},{10,11... | collective-permute-start | bytes 245768 | tf_op jit(solution)/shard_map/ppermute | solution.py:448
  43.9 7.3 %collective-permute-start.7 = (f32[5,32,128]{2,1,0:T(8,128)S(1)}, f32[5,32,128]{2,1,0:T(8,128)S(1)}, u32[]{:S(2)}, u32[]{:S(2)}) collective-permute-start(f32[5,32,128]{2,1,0:T(8,128)S(1)} %get-tuple-element.38), channel_id=1, source_target_pairs={{0,253},{1,4},{2,255},{3,6},{4,1},{5,8},{6,3},{7,10},{8,5},{9,12},... | collective-permute-start | bytes 245768 | tf_op jit(solution)/shard_map/ppermute | solution.py:448
  45.1 7.0 %collective-permute-start.8 = (f32[5,32,128]{2,1,0:T(8,128)S(1)}, f32[5,32,128]{2,1,0:T(8,128)S(1)}, u32[]{:S(2)}, u32[]{:S(2)}) collective-permute-start(f32[5,32,128]{2,1,0:T(8,128)S(1)} %get-tuple-element.39), channel_id=1, source_target_pairs={{0,1},{1,0},{2,3},{3,2},{4,5},{5,4},{6,7},{7,6},{8,9},{9,8},{10,11... | collective-permute-start | bytes 245768 | tf_op jit(solution)/shard_map/ppermute | solution.py:448
  54.3 13.7 %collective-permute-start.9 = (f32[2,64,128]{2,1,0:T(8,128)S(1)}, f32[2,64,128]{2,1,0:T(8,128)S(1)}, u32[]{:S(2)}, u32[]{:S(2)}) collective-permute-start(f32[2,64,128]{2,1,0:T(8,128)S(1)} %get-tuple-element.41), channel_id=1, source_target_pairs={{0,1},{1,0},{2,3},{3,2},{4,5},{5,4},{6,7},{7,6},{8,9},{9,8},{10,11... | collective-permute-start | bytes 196616 | tf_op jit(solution)/shard_map/ppermute | solution.py:448
  59.5 3.3 %collective-permute-start.10 = (f32[4,16,128]{2,1,0:T(8,128)S(1)}, f32[4,16,128]{2,1,0:T(8,128)S(1)}, u32[]{:S(2)}, u32[]{:S(2)}) collective-permute-start(f32[4,16,128]{2,1,0:T(8,128)S(1)} %get-tuple-element.42), channel_id=1, source_target_pairs={{0,253},{1,4},{2,255},{3,6},{4,1},{5,8},{6,3},{7,10},{8,5},{9,12},... | collective-permute-start | bytes 98312 | tf_op jit(solution)/shard_map/ppermute | solution.py:448
  62.8 5.2 %collective-permute-start.11 = (f32[2,16,128]{2,1,0:T(8,128)S(1)}, f32[2,16,128]{2,1,0:T(8,128)S(1)}, u32[]{:S(2)}, u32[]{:S(2)}) collective-permute-start(f32[2,16,128]{2,1,0:T(8,128)S(1)} %shard_map.145), channel_id=1, source_target_pairs={{0,1},{1,0},{2,3},{3,2},{4,5},{5,4},{6,7},{7,6},{8,9},{9,8},{10,11... | collective-permute-start | bytes 49160 | tf_op jit(solution)/shard_map/ppermute | solution.py:519

commit v7 on v6

--- a/solution.py
+++ b/solution.py
@@ -27,6 +27,7 @@
 HEIGHT = ALBEDO + 1
 AUX = HEIGHT + 1
 BINS = 16
+EDGE = 24
 DENOM = float(RAD * (RAD + 1) * (2 * RAD + 1)) / 3.0
 TAP_SCALE = 1.0 / (DENOM * (2 * RAD + 1))
 F32 = jnp.float32
@@ -340,10 +341,11 @@
 
 
 def surface_step(
-    coef, weight, kept, received, halo, surface, aux, alt, tables, z_out, fields
+    coef, weight, kept, received, halo, surface, aux, alt, tables, z_out, fields, misfit=None
 ):
     slope_lon, slope_lat, grad_lon, grad_lat = fields
-    misfit = slopes_and_misfit(surface, aux, alt, tables, slope_lon, slope_lat)
+    if misfit is None:
+        misfit = slopes_and_misfit(surface, aux, alt, tables, slope_lon, slope_lat)
     for ref, index, rows in image_tiles(kept, received, halo):
         albedo, lon, lat = ref[(ALBEDO, *index)], slope_lon[rows], slope_lat[rows]
         inverse, shade = shades(albedo, lon, lat)
@@ -356,17 +358,25 @@
     contribute(surface, aux, misfit, grad_lon, grad_lat, tables, z_out)
 
 
-def first_kernel(coef, counts, kept, received, halo, z, inter, intra, aux, *refs):
-    tables, (z_out, inter_out, intra_out, alt_out, weight_out), fields = refs[:5], refs[5:10], refs[10:]
-    weight = image_weights(counts)
-    weight_out[...] = weight
+def slope_kernel(z, inter, intra, aux, *refs):
+    tables, (surface_out, alt_out, misfit_out, slope_lon, slope_lat) = refs[:5], refs[5:]
     above, below = arrived(inter, intra)
     alt = jnp.concatenate([aux[:, 0:8], below[:, 0:8]], axis=1)
     alt_out[...] = alt
     below = jnp.concatenate([jnp.zeros((TILES, RAD, LANES), F32), below[:, RAD:]], axis=1)
     surface = [z[j] + jnp.concatenate([above[j], below[j]], axis=0) for j in range(TILES)]
+    for j, misfit in enumerate(slopes_and_misfit(surface, aux, alt, tables, slope_lon, slope_lat)):
+        surface_out[j] = surface[j]
+        misfit_out[j] = misfit
+
+
+def first_kernel(coef, counts, kept, received, halo, surface, aux, misfit, slope_lon, slope_lat, *refs):
+    tables, (z_out, inter_out, intra_out, weight_out), fields = refs[:5], refs[5:9], refs[9:]
+    weight = image_weights(counts)
+    weight_out[...] = weight
     surface_step(
-        coef, weight, kept, received, halo, surface, aux, alt, tables, z_out, fields
+        coef, weight, kept, received, halo, surface, aux, None, tables, z_out,
+        (slope_lon, slope_lat, *fields), misfit,
     )
     route(place()[1], z_out[:, 0:STRIP], z_out[:, STRIP:EXT], inter_out, intra_out)
 
@@ -382,24 +392,30 @@
 
 
 def last_kernel(coef, weight, kept, received, halo, z, inter, intra, aux, alt, *refs):
-    tables, (mine, inter_out, intra_out, z_out), fields = refs[:5], refs[5:9], refs[9:]
+    tables, (inter_out, mine, intra_out, z_out), fields = refs[:5], refs[5:9], refs[9:]
     above, below = arrived(inter, intra)
     surface = [z[j] + jnp.concatenate([above[j], below[j]], axis=0) for j in range(TILES)]
     surface_step(
         coef, weight[...], kept, received, halo, surface, aux, alt, tables, z_out, fields
     )
     half, core = place()
-    for t in range(2):
-        mine[t] = z_out[own_tile(half, core, t)]
-        intra_out[t] = z_out[own_tile(half, 1 - core, t)]
     for t in range(TILES - 1):
-        inter_out[t] = jnp.where(core == 0, z_out[half + t, 0:RAD], z_out[half + t, EXT - RAD : EXT])
+        at = half + t
+        inter_out[t] = jnp.where(core == 0, z_out[at, 0:EDGE], z_out[at, EXT - EDGE : EXT])
+    for ref, side in ((mine, core), (intra_out, 1 - core)):
+        for t in range(2):
+            at = own_tile(half, side, t)
+            ref[t] = jnp.where(core == 0, z_out[at, RAD:EXT], z_out[at, 0 : EXT - RAD])
+
+
+def edge(inter, t, core):
+    return jnp.where(core == 0, inter[t, EDGE - RAD : EDGE], inter[t, 0:RAD])
 
 
 def forward_kernel(inter, forward):
     core = place()[1]
     for t in range(2):
-        forward[t] = inter[2 * (1 - core) + t]
+        forward[t] = edge(inter, 2 * (1 - core) + t, core)
 
 
 def place_kernel(mine, intra, inter, forward, out):
@@ -407,13 +423,13 @@
     for t in range(2):
         upper = jnp.where(core == 0, mine[t], intra[t])
         lower = jnp.where(core == 0, intra[t], mine[t])
-        direct = inter[2 * core + t]
+        direct = edge(inter, 2 * core + t, core)
         top = jnp.where(core == 0, direct, forward[t])
         bottom = jnp.where(core == 0, forward[t], direct)
         cols = slice(t * LANES, (t + 1) * LANES)
-        out[0:RAD, cols] = upper[RAD : 2 * RAD] + top
-        out[RAD : 2 * RAD, cols] = upper[2 * RAD : 3 * RAD] + lower[0:RAD]
-        out[2 * RAD : 3 * RAD, cols] = lower[RAD : 2 * RAD] + upper[3 * RAD : EXT]
+        out[0:RAD, cols] = upper[0:RAD] + top
+        out[RAD : 2 * RAD, cols] = upper[RAD : 2 * RAD] + lower[0:RAD]
+        out[2 * RAD : 3 * RAD, cols] = lower[RAD : 2 * RAD] + upper[2 * RAD : 3 * RAD]
         out[3 * RAD : EXT, cols] = lower[2 * RAD : 3 * RAD] + bottom
 
 
@@ -493,11 +509,17 @@
     inter, intra = exchange(inter, intra)
     tables = constants()
     scratch = [pltpu.VMEM((TILES * STRIP, LANES), F32)] * 4
-    z, inter, intra, alt, weight = call(
+    flat = f32(TILES * STRIP, LANES)
+    surface, alt, misfit, *slopes = call(
+        slope_kernel,
+        (window, rows_of_bins, rows_of_bins, flat, flat),
+        z, inter, intra, aux, *tables,
+    )
+    z, inter, intra, weight = call(
         first_kernel,
-        (window, message, message, rows_of_bins, f32(BINS, LANES)),
-        coef, counts, kept, received, halo, z, inter, intra, aux, *tables,
-        scratch=scratch,
+        (window, message, message, f32(BINS, LANES)),
+        coef, counts, kept, received, halo, surface, aux, misfit, *slopes, *tables,
+        scratch=scratch[:2],
     )
     for _ in range(ITERS - 2):
         inter, intra = exchange(inter, intra)
@@ -508,9 +530,10 @@
             scratch=scratch,
         )
     inter, intra = exchange(inter, intra)
-    mine, inter, intra = call(
+    part = f32(2, EXT - RAD, LANES)
+    inter, mine, intra = call(
         last_kernel,
-        (f32(2, EXT, LANES), f32(TILES - 1, RAD, LANES), f32(2, EXT, LANES)),
+        (f32(TILES - 1, EDGE, LANES), part, part),
         coef, weight, kept, received, halo, z, inter, intra, aux, alt, *tables,
         scratch=[pltpu.VMEM((TILES, EXT, LANES), F32)] + scratch,
     )

time: 68.9 us -> 68.4 us (level)
  waiting for transfers between devices: 11.2 us -> 7.38 us
  starting transfers between devices: 45.4 us -> 48.8 us
    ppermute x4, waiting for transfers between devices: 3.64 us -> 0.01 us  [exchange(): lax.ppermute(inter, axes, across_strips)]
    ppermute x4, starting transfers between devices: 16 us -> 19.1 us  [exchange(): lax.ppermute(intra, axes, across_cores)]
    all_to_all x1, waiting for transfers between devices: 2.97 us -> 1.61 us  [per_device(): counts = lax.all_to_all(counts, 'lon', 0, 0)]
    ppermute x4, waiting for transfers between devices: 1.55 us -> 2.69 us  [exchange(): lax.ppermute(intra, axes, across_cores)]
    ppermute x1, starting transfers between devices: 4.32 us -> 5.14 us  [per_device(): passed = lax.ppermute(passed, axes, across_cores)]
    pallas_call x10 -> x11, Pallas kernels: 8.23 us -> 8.26 us  [call(): pl.pallas_call(kernel, out_shape=out_shape, in_specs=[VMEM] * len(args),...]
  transfers between devices with their start and end apart: 13 -> 13, of which waited for: 8 -> 7; matrix products, arithmetic and copies ran while one was open for 1% -> 1% of each run, Pallas kernels for 1% -> 2%
where the time goes in v7:
time: 68.4 us; the launch traced here: 68.2 us
  starting transfers between devices  48.8 us (71%)
  Pallas kernels  10.7 us (16%)
  waiting for transfers between devices  7.38 us (11%)
  local copies, waits for them, and re-layouts  1.09 us (2%)
    ppermute x4, starting transfers between devices, exchange(): lax.ppermute(intra, axes, across_cores)  19.1 us
    all_to_all x1, starting transfers between devices, per_device(): counts = lax.all_to_all(counts, 'lon', 0, 0)  11 us
    pallas_call x11, Pallas kernels, call(): pl.pallas_call(kernel, out_shape=out_shape, in_specs=[VMEM] * len(args),...  8.26 us
    ppermute x4, starting transfers between devices, exchange(): lax.ppermute(inter, axes, across_strips)  7.13 us
    ppermute x1, starting transfers between devices, per_device(): passed = lax.ppermute(passed, axes, across_cores)  5.14 us
    ppermute x1, starting transfers between devices, per_device(): received = lax.ppermute(sent, axes, across_cores)  3.31 us
    ppermute x4, waiting for transfers between devices, exchange(): lax.ppermute(intra, axes, across_cores)  2.69 us
    pallas_call x1, Pallas kernels, per_device(): pl.pallas_call(send_kernel, out_shape=fields, in_specs=[pl.BlockSpec(memo...  2.43 us
  transfers between devices with their start and end apart: 13, of which 7 were waited for; matrix products, arithmetic and copies ran while one was open for 1% of the time, Pallas kernels for 2%

profile of v7, /device:TPU:1, one launch (start us, length us, event | category | flops | bytes accessed | tf_op | source)
XLA Modules:
  0.0 68.2 jit_solution(631371049104768756)
XLA Ops:
  0.0 0.0 copy-start.7
  0.1 2.4 %shard_map.136 = f32[27,2,32,128]{3,2,1,0:T(8,128)} custom-call(bf16[12,64,256]{2,1,0:T(8,128)(2,1)} %images.1, s32[12,64,256]{2,1,0:T(8,128)} %lit_mask.1, f32[64,256]{1,0:T(8,128)} %height.1, f32[64,256]{1,0:T(8,128)} %albedo.1, s32[64,256]{1,0:T(8,128)} %owner.1, f32[16,64]{1,0:T(8,128)} %altimetry.1, s32[1,12]{1,0:T(1,128)} %bitcast.15, ...), custom_call_target="tpu_custom_call" | custom-call | tf_op jit(solution)/shard_map/pallas_call | solution.py:484
  2.5 0.0 copy-start.11
  2.5 3.3 %collective-permute-start = (f32[27,2,32,128]{3,2,1,0:T(8,128)}, f32[27,2,32,128]{3,2,1,0:T(8,128)S(1)}, u32[]{:S(2)}, u32[]{:S(2)}) collective-permute-start(f32[27,2,32,128]{3,2,1,0:T(8,128)} %shard_map.136), channel_id=1, source_target_pairs={{0,1},{1,0},{2,3},{3,2},{4,5},{5,4},{6,7},{7,6},{8,9},{9,8},{10,11... | collective-permute-start | bytes 2654216 | tf_op jit(solution)/shard_map/ppermute | solution.py:494
  5.8 0.0 copy-start.12
  5.8 0.1 constant_dynamic-update-slice_fusion.6
  6.0 0.5 copy-done.12
  6.5 0.2 shard_map.137.kept
  6.7 0.1 constant_dynamic-update-slice_fusion.5
  6.7 0.1 constant_dynamic-update-slice_fusion.4
  6.8 0.1 constant_dynamic-update-slice_fusion.3
  6.9 0.1 constant_dynamic-update-slice_fusion.2
  7.0 1.1 %collective-permute-done.received = f32[27,2,32,128]{3,2,1,0:T(8,128)S(1)} collective-permute-done((f32[27,2,32,128]{3,2,1,0:T(8,128)}, f32[27,2,32,128]{3,2,1,0:T(8,128)S(1)}, u32[]{:S(2)}, u32[]{:S(2)}) %collective-permute-start) | collective-permute-done | bytes 884768 | tf_op jit(solution)/shard_map/ppermute | solution.py:494
  8.1 1.1 %collective-permute-start.1 = (f32[2,32,128]{2,1,0:T(8,128)S(1)}, f32[2,32,128]{2,1,0:T(8,128)S(1)}, u32[]{:S(2)}, u32[]{:S(2)}) collective-permute-start(f32[2,32,128]{2,1,0:T(8,128)S(1)} %shard_map.138.near_small), channel_id=1, source_target_pairs={{0,2},{1,3},{2,0},{3,1},{4,6},{5,7},{6,4},{7,5},{8,10},{9,11},{10,... | collective-permute-start | bytes 98312 | tf_op jit(solution)/shard_map/ppermute | solution.py:497
  9.2 2.0 %collective-permute-start.2 = (f32[25,32,128]{2,1,0:T(8,128)S(1)}, f32[25,32,128]{2,1,0:T(8,128)S(1)}, u32[]{:S(2)}, u32[]{:S(2)}) collective-permute-start(f32[25,32,128]{2,1,0:T(8,128)S(1)} %shard_map.139), channel_id=1, source_target_pairs={{0,2},{1,3},{2,0},{3,1},{4,6},{5,7},{6,4},{7,5},{8,10},{9,11},{10,... | collective-permute-start | bytes 1228808 | tf_op jit(solution)/shard_map/ppermute | solution.py:499
  11.2 0.1 constant_dynamic-update-slice_fusion.1
  11.3 1.1 %collective-permute-done.1.halo_small = f32[2,32,128]{2,1,0:T(8,128)S(1)} collective-permute-done((f32[2,32,128]{2,1,0:T(8,128)S(1)}, f32[2,32,128]{2,1,0:T(8,128)S(1)}, u32[]{:S(2)}, u32[]{:S(2)}) %collective-permute-start.1) | collective-permute-done | bytes 32800 | tf_op jit(solution)/shard_map/ppermute | solution.py:497
  12.4 0.6 shard_map.140
  13.0 11.0 %all-to-all-start = ((f32[64,1,128]{2,1,0:T(1,128)}), f32[64,1,128]{2,1,0:T(1,128)S(1)}, u32[]{:S(2)}, u32[]{:S(2)}) async-start(f32[64,1,128]{2,1,0:T(1,128)} %shard_map.140), calls=%async_computation | async-start | bytes 65536 | tf_op jit(solution)/shard_map/all_to_all | solution.py:502
  24.1 0.0 copy-start.2
  24.1 0.0 copy-start.3
  24.1 0.0 copy-start.4
  24.1 0.0 copy-start.5
  24.1 0.0 copy-start.6
  24.2 3.1 %collective-permute-start.3 = (f32[5,32,128]{2,1,0:T(8,128)S(1)}, f32[5,32,128]{2,1,0:T(8,128)S(1)}, u32[]{:S(2)}, u32[]{:S(2)}) collective-permute-start(f32[5,32,128]{2,1,0:T(8,128)S(1)} %get-tuple-element.33), channel_id=1, source_target_pairs={{0,253},{1,4},{2,255},{3,6},{4,1},{5,8},{6,3},{7,10},{8,5},{9,12},... | collective-permute-start | bytes 245768 | tf_op jit(solution)/shard_map/ppermute | solution.py:464
  27.3 2.9 %collective-permute-start.4 = (f32[5,32,128]{2,1,0:T(8,128)S(1)}, f32[5,32,128]{2,1,0:T(8,128)S(1)}, u32[]{:S(2)}, u32[]{:S(2)}) collective-permute-start(f32[5,32,128]{2,1,0:T(8,128)S(1)} %get-tuple-element.34), channel_id=1, source_target_pairs={{0,1},{1,0},{2,3},{3,2},{4,5},{5,4},{6,7},{7,6},{8,9},{9,8},{10,11... | collective-permute-start | bytes 245768 | tf_op jit(solution)/shard_map/ppermute | solution.py:464
  30.2 0.1 constant_dynamic-update-slice_fusion.coef
  30.3 0.0 collective-permute-done.3.inter
  30.3 0.8 %collective-permute-done.4.intra = f32[5,32,128]{2,1,0:T(8,128)S(1)} collective-permute-done((f32[5,32,128]{2,1,0:T(8,128)S(1)}, f32[5,32,128]{2,1,0:T(8,128)S(1)}, u32[]{:S(2)}, u32[]{:S(2)}) %collective-permute-start.4) | collective-permute-done | bytes 81952 | tf_op jit(solution)/shard_map/ppermute | solution.py:464
  31.2 0.5 shard_map.142
  31.6 1.6 %all-to-all-done.counts = f32[64,1,128]{2,1,0:T(1,128)S(1)} async-done(((f32[64,1,128]{2,1,0:T(1,128)}), f32[64,1,128]{2,1,0:T(1,128)S(1)}, u32[]{:S(2)}, u32[]{:S(2)}) %all-to-all-start) | async-done | bytes 32800 | tf_op jit(solution)/shard_map/all_to_all | solution.py:502
  33.3 0.0 collective-permute-done.2.halo
  33.3 1.9 %shard_map.143 = (f32[5,64,128]{2,1,0:T(8,128)S(1)}, f32[5,32,128]{2,1,0:T(8,128)S(1)}, f32[5,32,128]{2,1,0:T(8,128)S(1)}, f32[16,128]{1,0:T(8,128)S(1)}) custom-call(f32[7,12,128]{2,1,0:T(8,128)S(1)} %constant_dynamic-update-slice_fusion.coef, f32[64,1,128]{2,1,0:T(1,128)S(1)} %all-to-all-done.counts, f32[27,2,32,128]{3,2,1,0:T(8,128)S(1)} %shard_map.137.kept, ...), custom_call_target="tpu_custom_call" | custom-call | tf_op jit(solution)/shard_map/pallas_call | solution.py:441
  35.2 3.3 %collective-permute-start.5 = (f32[5,32,128]{2,1,0:T(8,128)S(1)}, f32[5,32,128]{2,1,0:T(8,128)S(1)}, u32[]{:S(2)}, u32[]{:S(2)}) collective-permute-start(f32[5,32,128]{2,1,0:T(8,128)S(1)} %get-tuple-element.42), channel_id=1, source_target_pairs={{0,253},{1,4},{2,255},{3,6},{4,1},{5,8},{6,3},{7,10},{8,5},{9,12},... | collective-permute-start | bytes 245768 | tf_op jit(solution)/shard_map/ppermute | solution.py:464
  38.5 2.4 %collective-permute-start.6 = (f32[5,32,128]{2,1,0:T(8,128)S(1)}, f32[5,32,128]{2,1,0:T(8,128)S(1)}, u32[]{:S(2)}, u32[]{:S(2)}) collective-permute-start(f32[5,32,128]{2,1,0:T(8,128)S(1)} %get-tuple-element.43), channel_id=1, source_target_pairs={{0,1},{1,0},{2,3},{3,2},{4,5},{5,4},{6,7},{7,6},{8,9},{9,8},{10,11... | collective-permute-start | bytes 245768 | tf_op jit(solution)/shard_map/ppermute | solution.py:464
  40.9 0.9 %collective-permute-done.6.intra = f32[5,32,128]{2,1,0:T(8,128)S(1)} collective-permute-done((f32[5,32,128]{2,1,0:T(8,128)S(1)}, f32[5,32,128]{2,1,0:T(8,128)S(1)}, u32[]{:S(2)}, u32[]{:S(2)}) %collective-permute-start.6) | collective-permute-done | bytes 81952 | tf_op jit(solution)/shard_map/ppermute | solution.py:464
  41.8 2.2 %shard_map.144 = (f32[5,64,128]{2,1,0:T(8,128)S(1)}, f32[5,32,128]{2,1,0:T(8,128)S(1)}, f32[5,32,128]{2,1,0:T(8,128)S(1)}) custom-call(f32[7,12,128]{2,1,0:T(8,128)S(1)} %constant_dynamic-update-slice_fusion.coef, f32[16,128]{1,0:T(8,128)S(1)} %get-tuple-element.40.weight, f32[27,2,32,128]{3,2,1,0:T(8,128)S(1)} %shard_map.137.kept, ...), custom_call_target="tpu_custom_call" | custom-call | tf_op jit(solution)/shard_map/pallas_call | solution.py:441
  43.9 0.6 collective-permute-start.7
  44.6 6.6 %collective-permute-start.8 = (f32[5,32,128]{2,1,0:T(8,128)S(1)}, f32[5,32,128]{2,1,0:T(8,128)S(1)}, u32[]{:S(2)}, u32[]{:S(2)}) collective-permute-start(f32[5,32,128]{2,1,0:T(8,128)S(1)} %get-tuple-element.47), channel_id=1, source_target_pairs={{0,1},{1,0},{2,3},{3,2},{4,5},{5,4},{6,7},{7,6},{8,9},{9,8},{10,11... | collective-permute-start | bytes 245768 | tf_op jit(solution)/shard_map/ppermute | solution.py:464
  51.2 0.0 collective-permute-done.7.inter
  51.2 0.9 %collective-permute-done.8.intra = f32[5,32,128]{2,1,0:T(8,128)S(1)} collective-permute-done((f32[5,32,128]{2,1,0:T(8,128)S(1)}, f32[5,32,128]{2,1,0:T(8,128)S(1)}, u32[]{:S(2)}, u32[]{:S(2)}) %collective-permute-start.8) | collective-permute-done | bytes 81952 | tf_op jit(solution)/shard_map/ppermute | solution.py:464
  52.1 2.2 %shard_map.145 = (f32[4,24,128]{2,1,0:T(8,128)S(1)}, f32[2,48,128]{2,1,0:T(8,128)S(1)}, f32[2,48,128]{2,1,0:T(8,128)S(1)}) custom-call(f32[7,12,128]{2,1,0:T(8,128)S(1)} %constant_dynamic-update-slice_fusion.coef, f32[16,128]{1,0:T(8,128)S(1)} %get-tuple-element.40.weight, f32[27,2,32,128]{3,2,1,0:T(8,128)S(1)} %shard_map.137.kept, ...), custom_call_target="tpu_custom_call" | custom-call | tf_op jit(solution)/shard_map/pallas_call | solution.py:441
  54.3 0.1 collective-permute-start.10
  54.4 7.2 %collective-permute-start.9 = (f32[2,48,128]{2,1,0:T(8,128)S(1)}, f32[2,48,128]{2,1,0:T(8,128)S(1)}, u32[]{:S(2)}, u32[]{:S(2)}) collective-permute-start(f32[2,48,128]{2,1,0:T(8,128)S(1)} %get-tuple-element.49), channel_id=1, source_target_pairs={{0,1},{1,0},{2,3},{3,2},{4,5},{5,4},{6,7},{7,6},{8,9},{9,8},{10,11... | collective-permute-start | bytes 147464 | tf_op jit(solution)/shard_map/ppermute | solution.py:464
  61.6 0.0 collective-permute-done.10.inter
  61.6 5.1 %collective-permute-start.11 = (f32[2,16,128]{2,1,0:T(8,128)S(1)}, f32[2,16,128]{2,1,0:T(8,128)S(1)}, u32[]{:S(2)}, u32[]{:S(2)}) collective-permute-start(f32[2,16,128]{2,1,0:T(8,128)S(1)} %shard_map.146), channel_id=1, source_target_pairs={{0,1},{1,0},{2,3},{3,2},{4,5},{5,4},{6,7},{7,6},{8,9},{9,8},{10,11... | collective-permute-start | bytes 49160 | tf_op jit(solution)/shard_map/ppermute | solution.py:542
  66.7 0.8 %collective-permute-done.11.forward = f32[2,16,128]{2,1,0:T(8,128)S(1)} collective-permute-done((f32[2,16,128]{2,1,0:T(8,128)S(1)}, f32[2,16,128]{2,1,0:T(8,128)S(1)}, u32[]{:S(2)}, u32[]{:S(2)}) %collective-permute-start.11) | collective-permute-done | bytes 16416 | tf_op jit(solution)/shard_map/ppermute | solution.py:542
  67.5 0.6 shard_map.147
  (27 shorter events, 0.1 us)
Async XLA Ops:
  0.0 5.8 %copy-start.13 = (f32[12,4]{0,1:T(4,128)S(1)}, f32[12,4]{0,1:T(4,128)}, u32[]{:S(2)}) copy-start(f32[12,4]{0,1:T(4,128)} %param.19) | copy-start | bytes 580
  0.0 5.9 %copy-start = (s32[12,64,256]{2,1,0:T(8,128)S(1)}, s32[12,64,256]{2,1,0:T(8,128)}, u32[]{:S(2)}) copy-start(s32[12,64,256]{2,1,0:T(8,128)} %lit_mask.1) | copy-start | bytes 2359300
  0.0 5.9 %copy-start.1 = (bf16[12,64,256]{2,1,0:T(8,128)(2,1)S(1)}, bf16[12,64,256]{2,1,0:T(8,128)(2,1)}, u32[]{:S(2)}) copy-start(bf16[12,64,256]{2,1,0:T(8,128)(2,1)} %images.1) | copy-start | bytes 1179652
  0.0 5.9 %copy-start.7 = (bf16[192,256]{1,0:T(8,128)(2,1)S(1)}, bf16[192,256]{1,0:T(8,128)(2,1)}, u32[]{:S(2)}) copy-start(bf16[192,256]{1,0:T(8,128)(2,1)} %constant.16.clone.expand_hbm.expand) | copy-start | bytes 294916
  0.0 5.9 %copy-start.8 = (f32[64,256]{1,0:T(8,128)S(1)}, f32[64,256]{1,0:T(8,128)}, u32[]{:S(2)}) copy-start(f32[64,256]{1,0:T(8,128)} %height.1) | copy-start | bytes 196612
  0.0 5.9 %copy-start.9 = (f32[64,256]{1,0:T(8,128)S(1)}, f32[64,256]{1,0:T(8,128)}, u32[]{:S(2)}) copy-start(f32[64,256]{1,0:T(8,128)} %albedo.1) | copy-start | bytes 196612
  0.0 5.9 %copy-start.10 = (s32[64,256]{1,0:T(8,128)S(1)}, s32[64,256]{1,0:T(8,128)}, u32[]{:S(2)}) copy-start(s32[64,256]{1,0:T(8,128)} %owner.1) | copy-start | bytes 196612
  2.5 3.5 %copy-start.11 = (f32[16,64]{1,0:T(8,128)S(1)}, f32[16,64]{1,0:T(8,128)}, u32[]{:S(2)}) copy-start(f32[16,64]{1,0:T(8,128)} %altimetry.1) | copy-start | bytes 12292
  2.5 5.6 %collective-permute-start = (f32[27,2,32,128]{3,2,1,0:T(8,128)}, f32[27,2,32,128]{3,2,1,0:T(8,128)S(1)}, u32[]{:S(2)}, u32[]{:S(2)}) collective-permute-start(f32[27,2,32,128]{3,2,1,0:T(8,128)} %shard_map.136), channel_id=1, source_target_pairs={{0,1},{1,0},{2,3},{3,2},{4,5},{5,4},{6,7},{7,6},{8,9},{9,8},{10,11... | collective-permute-start | bytes 2654216 | tf_op jit(solution)/shard_map/ppermute | solution.py:494
  5.8 0.7 copy-start.12
  8.1 4.3 %collective-permute-start.1 = (f32[2,32,128]{2,1,0:T(8,128)S(1)}, f32[2,32,128]{2,1,0:T(8,128)S(1)}, u32[]{:S(2)}, u32[]{:S(2)}) collective-permute-start(f32[2,32,128]{2,1,0:T(8,128)S(1)} %shard_map.138.near_small), channel_id=1, source_target_pairs={{0,2},{1,3},{2,0},{3,1},{4,6},{5,7},{6,4},{7,5},{8,10},{9,11},{10,... | collective-permute-start | bytes 98312 | tf_op jit(solution)/shard_map/ppermute | solution.py:497
  9.2 24.1 %collective-permute-start.2 = (f32[25,32,128]{2,1,0:T(8,128)S(1)}, f32[25,32,128]{2,1,0:T(8,128)S(1)}, u32[]{:S(2)}, u32[]{:S(2)}) collective-permute-start(f32[25,32,128]{2,1,0:T(8,128)S(1)} %shard_map.139), channel_id=1, source_target_pairs={{0,2},{1,3},{2,0},{3,1},{4,6},{5,7},{6,4},{7,5},{8,10},{9,11},{10,... | collective-permute-start | bytes 1228808 | tf_op jit(solution)/shard_map/ppermute | solution.py:499
  13.0 20.2 %all-to-all-start = ((f32[64,1,128]{2,1,0:T(1,128)}), f32[64,1,128]{2,1,0:T(1,128)S(1)}, u32[]{:S(2)}, u32[]{:S(2)}) async-start(f32[64,1,128]{2,1,0:T(1,128)} %shard_map.140), calls=%async_computation | async-start | bytes 65536 | tf_op jit(solution)/shard_map/all_to_all | solution.py:502
  24.1 7.1 %copy-start.2 = (bf16[128,192]{1,0:T(8,128)(2,1)S(1)}, bf16[128,192]{1,0:T(8,128)(2,1)}, u32[]{:S(2)}) copy-start(bf16[128,192]{1,0:T(8,128)(2,1)} %constant.17.clone.refs_0_) | copy-start | bytes 147460
  24.1 7.0 %copy-start.3 = (bf16[256,128]{1,0:T(8,128)(2,1)S(1)}, bf16[256,128]{1,0:T(8,128)(2,1)}, u32[]{:S(2)}) copy-start(bf16[256,128]{1,0:T(8,128)(2,1)} %constant.19.clone.refs_2_) | copy-start | bytes 196612
  24.1 7.0 %copy-start.4 = (bf16[256,128]{1,0:T(8,128)(2,1)S(1)}, bf16[256,128]{1,0:T(8,128)(2,1)}, u32[]{:S(2)}) copy-start(bf16[256,128]{1,0:T(8,128)(2,1)} %constant.20.clone.refs_3_) | copy-start | bytes 196612
  24.1 7.0 %copy-start.5 = (bf16[64,256]{1,0:T(8,128)(2,1)S(1)}, bf16[64,256]{1,0:T(8,128)(2,1)}, u32[]{:S(2)}) copy-start(bf16[64,256]{1,0:T(8,128)(2,1)} %constant.18.clone.refs_1_) | copy-start | bytes 98308
  24.1 7.0 %copy-start.6 = (bf16[128,128]{1,0:T(8,128)(2,1)S(1)}, bf16[128,128]{1,0:T(8,128)(2,1)}, u32[]{:S(2)}) copy-start(bf16[128,128]{1,0:T(8,128)(2,1)} %constant.21.clone.refs_4_) | copy-start | bytes 98308
  24.2 6.1 %collective-permute-start.3 = (f32[5,32,128]{2,1,0:T(8,128)S(1)}, f32[5,32,128]{2,1,0:T(8,128)S(1)}, u32[]{:S(2)}, u32[]{:S(2)}) collective-permute-start(f32[5,32,128]{2,1,0:T(8,128)S(1)} %get-tuple-element.33), channel_id=1, source_target_pairs={{0,253},{1,4},{2,255},{3,6},{4,1},{5,8},{6,3},{7,10},{8,5},{9,12},... | collective-permute-start | bytes 245768 | tf_op jit(solution)/shard_map/ppermute | solution.py:464
  27.3 3.8 %collective-permute-start.4 = (f32[5,32,128]{2,1,0:T(8,128)S(1)}, f32[5,32,128]{2,1,0:T(8,128)S(1)}, u32[]{:S(2)}, u32[]{:S(2)}) collective-permute-start(f32[5,32,128]{2,1,0:T(8,128)S(1)} %get-tuple-element.34), channel_id=1, source_target_pairs={{0,1},{1,0},{2,3},{3,2},{4,5},{5,4},{6,7},{7,6},{8,9},{9,8},{10,11... | collective-permute-start | bytes 245768 | tf_op jit(solution)/shard_map/ppermute | solution.py:464
  35.2 5.7 %collective-permute-start.5 = (f32[5,32,128]{2,1,0:T(8,128)S(1)}, f32[5,32,128]{2,1,0:T(8,128)S(1)}, u32[]{:S(2)}, u32[]{:S(2)}) collective-permute-start(f32[5,32,128]{2,1,0:T(8,128)S(1)} %get-tuple-element.42), channel_id=1, source_target_pairs={{0,253},{1,4},{2,255},{3,6},{4,1},{5,8},{6,3},{7,10},{8,5},{9,12},... | collective-permute-start | bytes 245768 | tf_op jit(solution)/shard_map/ppermute | solution.py:464
  38.5 3.3 %collective-permute-start.6 = (f32[5,32,128]{2,1,0:T(8,128)S(1)}, f32[5,32,128]{2,1,0:T(8,128)S(1)}, u32[]{:S(2)}, u32[]{:S(2)}) collective-permute-start(f32[5,32,128]{2,1,0:T(8,128)S(1)} %get-tuple-element.43), channel_id=1, source_target_pairs={{0,1},{1,0},{2,3},{3,2},{4,5},{5,4},{6,7},{7,6},{8,9},{9,8},{10,11... | collective-permute-start | bytes 245768 | tf_op jit(solution)/shard_map/ppermute | solution.py:464
  43.9 7.3 %collective-permute-start.7 = (f32[5,32,128]{2,1,0:T(8,128)S(1)}, f32[5,32,128]{2,1,0:T(8,128)S(1)}, u32[]{:S(2)}, u32[]{:S(2)}) collective-permute-start(f32[5,32,128]{2,1,0:T(8,128)S(1)} %get-tuple-element.46), channel_id=1, source_target_pairs={{0,253},{1,4},{2,255},{3,6},{4,1},{5,8},{6,3},{7,10},{8,5},{9,12},... | collective-permute-start | bytes 245768 | tf_op jit(solution)/shard_map/ppermute | solution.py:464
  44.6 7.5 %collective-permute-start.8 = (f32[5,32,128]{2,1,0:T(8,128)S(1)}, f32[5,32,128]{2,1,0:T(8,128)S(1)}, u32[]{:S(2)}, u32[]{:S(2)}) collective-permute-start(f32[5,32,128]{2,1,0:T(8,128)S(1)} %get-tuple-element.47), channel_id=1, source_target_pairs={{0,1},{1,0},{2,3},{3,2},{4,5},{5,4},{6,7},{7,6},{8,9},{9,8},{10,11... | collective-permute-start | bytes 245768 | tf_op jit(solution)/shard_map/ppermute | solution.py:464
  54.3 7.3 %collective-permute-start.10 = (f32[4,24,128]{2,1,0:T(8,128)S(1)}, f32[4,24,128]{2,1,0:T(8,128)S(1)}, u32[]{:S(2)}, u32[]{:S(2)}) collective-permute-start(f32[4,24,128]{2,1,0:T(8,128)S(1)} %get-tuple-element.50), channel_id=1, source_target_pairs={{0,253},{1,4},{2,255},{3,6},{4,1},{5,8},{6,3},{7,10},{8,5},{9,12},... | collective-permute-start | bytes 147464 | tf_op jit(solution)/shard_map/ppermute | solution.py:464
  54.4 12.3 %collective-permute-start.9 = (f32[2,48,128]{2,1,0:T(8,128)S(1)}, f32[2,48,128]{2,1,0:T(8,128)S(1)}, u32[]{:S(2)}, u32[]{:S(2)}) collective-permute-start(f32[2,48,128]{2,1,0:T(8,128)S(1)} %get-tuple-element.49), channel_id=1, source_target_pairs={{0,1},{1,0},{2,3},{3,2},{4,5},{5,4},{6,7},{7,6},{8,9},{9,8},{10,11... | collective-permute-start | bytes 147464 | tf_op jit(solution)/shard_map/ppermute | solution.py:464
  61.6 6.0 %collective-permute-start.11 = (f32[2,16,128]{2,1,0:T(8,128)S(1)}, f32[2,16,128]{2,1,0:T(8,128)S(1)}, u32[]{:S(2)}, u32[]{:S(2)}) collective-permute-start(f32[2,16,128]{2,1,0:T(8,128)S(1)} %shard_map.146), channel_id=1, source_target_pairs={{0,1},{1,0},{2,3},{3,2},{4,5},{5,4},{6,7},{7,6},{8,9},{9,8},{10,11... | collective-permute-start | bytes 49160 | tf_op jit(solution)/shard_map/ppermute | solution.py:542

commit v8 on v7

--- a/solution.py
+++ b/solution.py
@@ -176,27 +176,20 @@
         kept[HEIGHT, t] = height[rows, cols]
 
 
-def near_small_kernel(kept, received, near_small):
-    half, core = place()
-    for i, field in enumerate((HEIGHT, AUX)):
-        near_small[i] = jnp.where(half != core, kept[field, 1 - half], received[field, 1 - half])
-    near_small[1, 16:24] = kept[AUX, 0, 16:24] + received[AUX, 0, 16:24]
-
-
-def near_kernel(kept, received, near_small, near):
+def near_kernel(kept, received, near):
     half, core = place()
 
     @pl.when(half != core)
     def _():
-        near[...] = kept[0:HEIGHT, 1 - half]
+        near[...] = kept[:, 1 - half]
 
     @pl.when(half == core)
     def _():
-        near[...] = received[0:HEIGHT, 1 - half]
-
-
-def count_kernel(halo_small, near_small, near, counts):
-    total = halo_small[1, 16:17] + near_small[1, 16:17]
+        near[...] = received[:, 1 - half]
+
+
+def count_kernel(kept, received, near, counts):
+    total = kept[AUX, 0, 16:17] + received[AUX, 0, 16:17]
     counts[...] = jnp.broadcast_to(total[None], counts.shape)
 
 
@@ -205,7 +198,7 @@
     intra[...] = jnp.where(core == 0, down, up)
 
 
-def begin_kernel(kept, received, halo_small, z, aux, inter, intra):
+def begin_kernel(kept, received, halo, z, aux, inter, intra):
     half, core = place()
     zero = jnp.zeros((TILES, RAD, LANES), F32)
     z[:, 0:RAD] = zero
@@ -215,8 +208,8 @@
             z[at, RAD : RAD + STRIP] = ref[HEIGHT, t]
             aux[at] = ref[AUX, t, 0:BINS]
     far = (TILES - 1) * (1 - half)
-    z[far, RAD : RAD + STRIP] = halo_small[0]
-    aux[far] = halo_small[1, 0:BINS]
+    z[far, RAD : RAD + STRIP] = halo[HEIGHT]
+    aux[far] = halo[AUX, 0:BINS]
     alt = jnp.concatenate([aux[:, 0:8], jnp.zeros((TILES, 8, LANES), F32)], axis=1)
     up = jnp.concatenate([alt, z[:, RAD : 2 * RAD]], axis=1)
     route(core, up, z[:, STRIP:EXT], inter, intra)
@@ -493,18 +486,16 @@
     sent, count = lax.optimization_barrier((sent, count))
     received = lax.ppermute(sent, axes, across_cores)
     kept = call(keep_kernel, fields, *inputs[:-2], count, expand)
-    near_small = call(near_small_kernel, f32(2, STRIP, LANES), kept, received)
-    halo_small = lax.ppermute(near_small, axes, across_halves)
-    near = call(near_kernel, f32(HEIGHT, STRIP, LANES), kept, received, near_small)
+    near = call(near_kernel, f32(FIELDS, STRIP, LANES), kept, received)
     halo = lax.ppermute(near, axes, across_halves)
-    counts = call(count_kernel, f32(lon_count, 1, LANES), halo_small, near_small, near[:1, :8])
-    counts, halo_small = lax.optimization_barrier((counts, halo_small))
-    counts = lax.all_to_all(counts, "lon", 0, 0)
+    same_core = [[index(a, b) for a, b in sites if b % 2 == core] for core in range(2)]
+    counts = call(count_kernel, f32(len(same_core[0]), 1, LANES), kept, received, near)
+    counts = lax.all_to_all(counts, axes, 0, 0, axis_index_groups=same_core)
     message = f32(TILES, STRIP, LANES)
     window = f32(TILES, EXT, LANES)
     rows_of_bins = f32(TILES, BINS, LANES)
     z, aux, inter, intra = call(
-        begin_kernel, (window, rows_of_bins, message, message), kept, received, halo_small
+        begin_kernel, (window, rows_of_bins, message, message), kept, received, halo
     )
     inter, intra = exchange(inter, intra)
     tables = constants()

time: 68.4 us -> 68.2 us (level)
    all_to_all x1, starting transfers between devices: 11 us -> 13.6 us  [per_device(): counts = lax.all_to_all(counts, axes, 0, 0, axis_index_groups=same_core)]
    ppermute x4, starting transfers between devices: 7.13 us -> 5.22 us  [exchange(): lax.ppermute(inter, axes, across_strips)]
    all_to_all x1, waiting for transfers between devices: 1.61 us -> 2.79 us  [per_device(): counts = lax.all_to_all(counts, axes, 0, 0, axis_index_groups=same_core)]
    ppermute x1 -> x0, waiting for transfers between devices: 1.11 us -> none  [per_device(): halo_small = lax.ppermute(near_small, axes, across_halves)]
    ppermute x1 -> x0, starting transfers between devices: 1.07 us -> none  [per_device(): halo_small = lax.ppermute(near_small, axes, across_halves)]
    ppermute x1, starting transfers between devices: 2.03 us -> 1.1 us  [per_device(): halo = lax.ppermute(near, axes, across_halves)]
    ppermute x4, starting transfers between devices: 19.1 us -> 19.8 us  [exchange(): lax.ppermute(intra, axes, across_cores)]
    pallas_call x11 -> x10, Pallas kernels: 8.26 us -> 8.34 us  [call(): pl.pallas_call(kernel, out_shape=out_shape, in_specs=[VMEM] * len(args),...]
  transfers between devices with their start and end apart: 13 -> 12, of which waited for: 7 -> 6; matrix products, arithmetic and copies ran while one was open for 1% -> 1% of each run, Pallas kernels for 2% -> 2%
where the time goes in v8:
time: 68.2 us; the launch traced here: 68 us
  starting transfers between devices  48.4 us (71%)
  Pallas kernels  10.8 us (16%)
  waiting for transfers between devices  8.03 us (12%)
    ppermute x4, starting transfers between devices, exchange(): lax.ppermute(intra, axes, across_cores)  19.8 us
    all_to_all x1, starting transfers between devices, per_device(): counts = lax.all_to_all(counts, axes, 0, 0, axis_index_groups=same_core)  13.6 us
    pallas_call x10, Pallas kernels, call(): pl.pallas_call(kernel, out_shape=out_shape, in_specs=[VMEM] * len(args),...  8.34 us
    ppermute x1, starting transfers between devices, per_device(): passed = lax.ppermute(passed, axes, across_cores)  5.32 us
    ppermute x4, starting transfers between devices, exchange(): lax.ppermute(inter, axes, across_strips)  5.22 us
    ppermute x1, starting transfers between devices, per_device(): received = lax.ppermute(sent, axes, across_cores)  3.31 us
    all_to_all x1, waiting for transfers between devices, per_device(): counts = lax.all_to_all(counts, axes, 0, 0, axis_index_groups=same_core)  2.79 us
    ppermute x4, waiting for transfers between devices, exchange(): lax.ppermute(intra, axes, across_cores)  2.65 us
  transfers between devices with their start and end apart: 12, of which 6 were waited for; matrix products, arithmetic and copies ran while one was open for 1% of the time, Pallas kernels for 2%

profile of v8, /device:TPU:1, one launch (start us, length us, event | category | flops | bytes accessed | tf_op | source)
XLA Modules:
  0.0 68.0 jit_solution(14377974841813436884)
XLA Ops:
  0.0 0.0 copy-start.7
  0.0 0.0 copy-start.8
  0.0 0.0 copy-start.9
  0.1 2.4 %shard_map.136 = f32[27,2,32,128]{3,2,1,0:T(8,128)} custom-call(bf16[12,64,256]{2,1,0:T(8,128)(2,1)} %images.1, s32[12,64,256]{2,1,0:T(8,128)} %lit_mask.1, f32[64,256]{1,0:T(8,128)} %height.1, f32[64,256]{1,0:T(8,128)} %albedo.1, s32[64,256]{1,0:T(8,128)} %owner.1, f32[16,64]{1,0:T(8,128)} %altimetry.1, s32[1,12]{1,0:T(1,128)} %bitcast.15, ...), custom_call_target="tpu_custom_call" | custom-call | tf_op jit(solution)/shard_map/pallas_call | solution.py:477
  2.5 0.0 copy-start.12
  2.5 3.3 %collective-permute-start = (f32[27,2,32,128]{3,2,1,0:T(8,128)}, f32[27,2,32,128]{3,2,1,0:T(8,128)S(1)}, u32[]{:S(2)}, u32[]{:S(2)}) collective-permute-start(f32[27,2,32,128]{3,2,1,0:T(8,128)} %shard_map.136), channel_id=1, source_target_pairs={{0,1},{1,0},{2,3},{3,2},{4,5},{5,4},{6,7},{7,6},{8,9},{9,8},{10,11... | collective-permute-start | bytes 2654216 | tf_op jit(solution)/shard_map/ppermute | solution.py:487
  5.9 0.2 shard_map.137.kept
  6.1 0.1 constant_dynamic-update-slice_fusion.6
  6.2 0.1 constant_dynamic-update-slice_fusion.5
  6.3 0.1 constant_dynamic-update-slice_fusion.4
  6.3 0.1 constant_dynamic-update-slice_fusion.3
  6.4 1.7 %collective-permute-done.received = f32[27,2,32,128]{3,2,1,0:T(8,128)S(1)} collective-permute-done((f32[27,2,32,128]{3,2,1,0:T(8,128)}, f32[27,2,32,128]{3,2,1,0:T(8,128)S(1)}, u32[]{:S(2)}, u32[]{:S(2)}) %collective-permute-start) | collective-permute-done | bytes 884768 | tf_op jit(solution)/shard_map/ppermute | solution.py:487
  8.1 1.1 %collective-permute-start.1 = (f32[27,32,128]{2,1,0:T(8,128)S(1)}, f32[27,32,128]{2,1,0:T(8,128)S(1)}, u32[]{:S(2)}, u32[]{:S(2)}) collective-permute-start(f32[27,32,128]{2,1,0:T(8,128)S(1)} %shard_map.138.near), channel_id=1, source_target_pairs={{0,2},{1,3},{2,0},{3,1},{4,6},{5,7},{6,4},{7,5},{8,10},{9,11},{10,... | collective-permute-start | bytes 1327112 | tf_op jit(solution)/shard_map/ppermute | solution.py:490
  9.2 0.1 constant_dynamic-update-slice_fusion.2
  9.3 0.1 constant_dynamic-update-slice_fusion.1
  9.4 0.7 shard_map.139
  10.1 13.6 %all-to-all-start = ((f32[128,1,128]{2,1,0:T(1,128)}), f32[128,1,128]{2,1,0:T(1,128)S(1)}, u32[]{:S(2)}, u32[]{:S(2)}) async-start(f32[128,1,128]{2,1,0:T(1,128)} %shard_map.139), calls=%async_computation | async-start | bytes 131072 | tf_op jit(solution)/shard_map/all_to_all | solution.py:493
  23.7 0.0 copy-start.2
  23.7 0.0 copy-start.3
  23.7 0.0 copy-start.4
  23.7 0.0 collective-permute-done.1.halo
  23.7 0.0 copy-start.5
  23.8 0.0 copy-start.6
  23.8 1.8 %collective-permute-start.2 = (f32[5,32,128]{2,1,0:T(8,128)S(1)}, f32[5,32,128]{2,1,0:T(8,128)S(1)}, u32[]{:S(2)}, u32[]{:S(2)}) collective-permute-start(f32[5,32,128]{2,1,0:T(8,128)S(1)} %get-tuple-element.29), channel_id=1, source_target_pairs={{0,253},{1,4},{2,255},{3,6},{4,1},{5,8},{6,3},{7,10},{8,5},{9,12},... | collective-permute-start | bytes 245768 | tf_op jit(solution)/shard_map/ppermute | solution.py:457
  25.6 4.3 %collective-permute-start.3 = (f32[5,32,128]{2,1,0:T(8,128)S(1)}, f32[5,32,128]{2,1,0:T(8,128)S(1)}, u32[]{:S(2)}, u32[]{:S(2)}) collective-permute-start(f32[5,32,128]{2,1,0:T(8,128)S(1)} %get-tuple-element.30), channel_id=1, source_target_pairs={{0,1},{1,0},{2,3},{3,2},{4,5},{5,4},{6,7},{7,6},{8,9},{9,8},{10,11... | collective-permute-start | bytes 245768 | tf_op jit(solution)/shard_map/ppermute | solution.py:457
  29.8 0.1 constant_dynamic-update-slice_fusion.coef
  29.9 0.0 collective-permute-done.2.inter
  29.9 0.8 %collective-permute-done.3.intra = f32[5,32,128]{2,1,0:T(8,128)S(1)} collective-permute-done((f32[5,32,128]{2,1,0:T(8,128)S(1)}, f32[5,32,128]{2,1,0:T(8,128)S(1)}, u32[]{:S(2)}, u32[]{:S(2)}) %collective-permute-start.3) | collective-permute-done | bytes 81952 | tf_op jit(solution)/shard_map/ppermute | solution.py:457
  30.8 0.5 shard_map.141
  31.3 2.8 %all-to-all-done.counts = f32[128,1,128]{2,1,0:T(1,128)S(1)} async-done(((f32[128,1,128]{2,1,0:T(1,128)}), f32[128,1,128]{2,1,0:T(1,128)S(1)}, u32[]{:S(2)}, u32[]{:S(2)}) %all-to-all-start) | async-done | bytes 65568 | tf_op jit(solution)/shard_map/all_to_all | solution.py:493
  34.1 1.9 %shard_map.142 = (f32[5,64,128]{2,1,0:T(8,128)S(1)}, f32[5,32,128]{2,1,0:T(8,128)S(1)}, f32[5,32,128]{2,1,0:T(8,128)S(1)}, f32[16,128]{1,0:T(8,128)S(1)}) custom-call(f32[7,12,128]{2,1,0:T(8,128)S(1)} %constant_dynamic-update-slice_fusion.coef, f32[128,1,128]{2,1,0:T(1,128)S(1)} %all-to-all-done.counts, f32[27,2,32,128]{3,2,1,0:T(8,128)S(1)} %shard_map.137.kept, ...), custom_call_target="tpu_custom_call" | custom-call | tf_op jit(solution)/shard_map/pallas_call | solution.py:434
  36.0 2.4 %collective-permute-start.4 = (f32[5,32,128]{2,1,0:T(8,128)S(1)}, f32[5,32,128]{2,1,0:T(8,128)S(1)}, u32[]{:S(2)}, u32[]{:S(2)}) collective-permute-start(f32[5,32,128]{2,1,0:T(8,128)S(1)} %get-tuple-element.38), channel_id=1, source_target_pairs={{0,253},{1,4},{2,255},{3,6},{4,1},{5,8},{6,3},{7,10},{8,5},{9,12},... | collective-permute-start | bytes 245768 | tf_op jit(solution)/shard_map/ppermute | solution.py:457
  38.4 2.1 %collective-permute-start.5 = (f32[5,32,128]{2,1,0:T(8,128)S(1)}, f32[5,32,128]{2,1,0:T(8,128)S(1)}, u32[]{:S(2)}, u32[]{:S(2)}) collective-permute-start(f32[5,32,128]{2,1,0:T(8,128)S(1)} %get-tuple-element.39), channel_id=1, source_target_pairs={{0,1},{1,0},{2,3},{3,2},{4,5},{5,4},{6,7},{7,6},{8,9},{9,8},{10,11... | collective-permute-start | bytes 245768 | tf_op jit(solution)/shard_map/ppermute | solution.py:457
  40.5 0.1 collective-permute-done.4.inter
  40.6 0.9 %collective-permute-done.5.intra = f32[5,32,128]{2,1,0:T(8,128)S(1)} collective-permute-done((f32[5,32,128]{2,1,0:T(8,128)S(1)}, f32[5,32,128]{2,1,0:T(8,128)S(1)}, u32[]{:S(2)}, u32[]{:S(2)}) %collective-permute-start.5) | collective-permute-done | bytes 81952 | tf_op jit(solution)/shard_map/ppermute | solution.py:457
  41.4 2.2 %shard_map.143 = (f32[5,64,128]{2,1,0:T(8,128)S(1)}, f32[5,32,128]{2,1,0:T(8,128)S(1)}, f32[5,32,128]{2,1,0:T(8,128)S(1)}) custom-call(f32[7,12,128]{2,1,0:T(8,128)S(1)} %constant_dynamic-update-slice_fusion.coef, f32[16,128]{1,0:T(8,128)S(1)} %get-tuple-element.36.weight, f32[27,2,32,128]{3,2,1,0:T(8,128)S(1)} %shard_map.137.kept, ...), custom_call_target="tpu_custom_call" | custom-call | tf_op jit(solution)/shard_map/pallas_call | solution.py:434
  43.6 1.0 %collective-permute-start.6 = (f32[5,32,128]{2,1,0:T(8,128)S(1)}, f32[5,32,128]{2,1,0:T(8,128)S(1)}, u32[]{:S(2)}, u32[]{:S(2)}) collective-permute-start(f32[5,32,128]{2,1,0:T(8,128)S(1)} %get-tuple-element.42), channel_id=1, source_target_pairs={{0,253},{1,4},{2,255},{3,6},{4,1},{5,8},{6,3},{7,10},{8,5},{9,12},... | collective-permute-start | bytes 245768 | tf_op jit(solution)/shard_map/ppermute | solution.py:457
  44.5 6.3 %collective-permute-start.7 = (f32[5,32,128]{2,1,0:T(8,128)S(1)}, f32[5,32,128]{2,1,0:T(8,128)S(1)}, u32[]{:S(2)}, u32[]{:S(2)}) collective-permute-start(f32[5,32,128]{2,1,0:T(8,128)S(1)} %get-tuple-element.43), channel_id=1, source_target_pairs={{0,1},{1,0},{2,3},{3,2},{4,5},{5,4},{6,7},{7,6},{8,9},{9,8},{10,11... | collective-permute-start | bytes 245768 | tf_op jit(solution)/shard_map/ppermute | solution.py:457
  50.8 0.0 collective-permute-done.6.inter
  50.9 0.9 %collective-permute-done.7.intra = f32[5,32,128]{2,1,0:T(8,128)S(1)} collective-permute-done((f32[5,32,128]{2,1,0:T(8,128)S(1)}, f32[5,32,128]{2,1,0:T(8,128)S(1)}, u32[]{:S(2)}, u32[]{:S(2)}) %collective-permute-start.7) | collective-permute-done | bytes 81952 | tf_op jit(solution)/shard_map/ppermute | solution.py:457
  51.8 2.2 %shard_map.144 = (f32[4,24,128]{2,1,0:T(8,128)S(1)}, f32[2,48,128]{2,1,0:T(8,128)S(1)}, f32[2,48,128]{2,1,0:T(8,128)S(1)}) custom-call(f32[7,12,128]{2,1,0:T(8,128)S(1)} %constant_dynamic-update-slice_fusion.coef, f32[16,128]{1,0:T(8,128)S(1)} %get-tuple-element.36.weight, f32[27,2,32,128]{3,2,1,0:T(8,128)S(1)} %shard_map.137.kept, ...), custom_call_target="tpu_custom_call" | custom-call | tf_op jit(solution)/shard_map/pallas_call | solution.py:434
  53.9 0.1 collective-permute-start.9
  54.1 7.2 %collective-permute-start.8 = (f32[2,48,128]{2,1,0:T(8,128)S(1)}, f32[2,48,128]{2,1,0:T(8,128)S(1)}, u32[]{:S(2)}, u32[]{:S(2)}) collective-permute-start(f32[2,48,128]{2,1,0:T(8,128)S(1)} %get-tuple-element.45), channel_id=1, source_target_pairs={{0,1},{1,0},{2,3},{3,2},{4,5},{5,4},{6,7},{7,6},{8,9},{9,8},{10,11... | collective-permute-start | bytes 147464 | tf_op jit(solution)/shard_map/ppermute | solution.py:457
  61.2 0.0 collective-permute-done.9.inter
  61.2 5.3 %collective-permute-start.10 = (f32[2,16,128]{2,1,0:T(8,128)S(1)}, f32[2,16,128]{2,1,0:T(8,128)S(1)}, u32[]{:S(2)}, u32[]{:S(2)}) collective-permute-start(f32[2,16,128]{2,1,0:T(8,128)S(1)} %shard_map.145), channel_id=1, source_target_pairs={{0,1},{1,0},{2,3},{3,2},{4,5},{5,4},{6,7},{7,6},{8,9},{9,8},{10,11... | collective-permute-start | bytes 49160 | tf_op jit(solution)/shard_map/ppermute | solution.py:533
  66.5 0.0 collective-permute-done.8.intra
  66.5 0.8 %collective-permute-done.10.forward = f32[2,16,128]{2,1,0:T(8,128)S(1)} collective-permute-done((f32[2,16,128]{2,1,0:T(8,128)S(1)}, f32[2,16,128]{2,1,0:T(8,128)S(1)}, u32[]{:S(2)}, u32[]{:S(2)}) %collective-permute-start.10) | collective-permute-done | bytes 16416 | tf_op jit(solution)/shard_map/ppermute | solution.py:533
  67.4 0.6 shard_map.146
  (23 shorter events, 0.1 us)
Async XLA Ops:
  0.0 5.8 %copy-start.13 = (f32[12,4]{0,1:T(4,128)S(1)}, f32[12,4]{0,1:T(4,128)}, u32[]{:S(2)}) copy-start(f32[12,4]{0,1:T(4,128)} %param.19) | copy-start | bytes 580
  0.0 5.8 %copy-start = (s32[12,64,256]{2,1,0:T(8,128)S(1)}, s32[12,64,256]{2,1,0:T(8,128)}, u32[]{:S(2)}) copy-start(s32[12,64,256]{2,1,0:T(8,128)} %lit_mask.1) | copy-start | bytes 2359300
  0.0 5.9 %copy-start.1 = (bf16[12,64,256]{2,1,0:T(8,128)(2,1)S(1)}, bf16[12,64,256]{2,1,0:T(8,128)(2,1)}, u32[]{:S(2)}) copy-start(bf16[12,64,256]{2,1,0:T(8,128)(2,1)} %images.1) | copy-start | bytes 1179652
  0.0 5.9 %copy-start.7 = (bf16[192,256]{1,0:T(8,128)(2,1)S(1)}, bf16[192,256]{1,0:T(8,128)(2,1)}, u32[]{:S(2)}) copy-start(bf16[192,256]{1,0:T(8,128)(2,1)} %constant.16.clone.expand_hbm.expand) | copy-start | bytes 294916
  0.0 5.9 %copy-start.8 = (f32[64,256]{1,0:T(8,128)S(1)}, f32[64,256]{1,0:T(8,128)}, u32[]{:S(2)}) copy-start(f32[64,256]{1,0:T(8,128)} %height.1) | copy-start | bytes 196612
  0.0 5.9 %copy-start.9 = (f32[64,256]{1,0:T(8,128)S(1)}, f32[64,256]{1,0:T(8,128)}, u32[]{:S(2)}) copy-start(f32[64,256]{1,0:T(8,128)} %albedo.1) | copy-start | bytes 196612
  0.0 5.9 %copy-start.10 = (s32[64,256]{1,0:T(8,128)S(1)}, s32[64,256]{1,0:T(8,128)}, u32[]{:S(2)}) copy-start(s32[64,256]{1,0:T(8,128)} %owner.1) | copy-start | bytes 196612
  0.1 5.9 %copy-start.11 = (f32[16,64]{1,0:T(8,128)S(1)}, f32[16,64]{1,0:T(8,128)}, u32[]{:S(2)}) copy-start(f32[16,64]{1,0:T(8,128)} %altimetry.1) | copy-start | bytes 12292
  2.5 3.4 %copy-start.12 = (s32[12,1,1]{0,2,1:T(1,128)S(1)}, s32[12,1,1]{0,2,1:T(1,128)}, u32[]{:S(2)}) copy-start(s32[12,1,1]{0,2,1:T(1,128)} %param.18) | copy-start | bytes 148
  2.5 5.6 %collective-permute-start = (f32[27,2,32,128]{3,2,1,0:T(8,128)}, f32[27,2,32,128]{3,2,1,0:T(8,128)S(1)}, u32[]{:S(2)}, u32[]{:S(2)}) collective-permute-start(f32[27,2,32,128]{3,2,1,0:T(8,128)} %shard_map.136), channel_id=1, source_target_pairs={{0,1},{1,0},{2,3},{3,2},{4,5},{5,4},{6,7},{7,6},{8,9},{9,8},{10,11... | collective-permute-start | bytes 2654216 | tf_op jit(solution)/shard_map/ppermute | solution.py:487
  8.1 15.6 %collective-permute-start.1 = (f32[27,32,128]{2,1,0:T(8,128)S(1)}, f32[27,32,128]{2,1,0:T(8,128)S(1)}, u32[]{:S(2)}, u32[]{:S(2)}) collective-permute-start(f32[27,32,128]{2,1,0:T(8,128)S(1)} %shard_map.138.near), channel_id=1, source_target_pairs={{0,2},{1,3},{2,0},{3,1},{4,6},{5,7},{6,4},{7,5},{8,10},{9,11},{10,... | collective-permute-start | bytes 1327112 | tf_op jit(solution)/shard_map/ppermute | solution.py:490
  10.1 24.0 %all-to-all-start = ((f32[128,1,128]{2,1,0:T(1,128)}), f32[128,1,128]{2,1,0:T(1,128)S(1)}, u32[]{:S(2)}, u32[]{:S(2)}) async-start(f32[128,1,128]{2,1,0:T(1,128)} %shard_map.139), calls=%async_computation | async-start | bytes 131072 | tf_op jit(solution)/shard_map/all_to_all | solution.py:493
  23.7 7.1 %copy-start.2 = (bf16[256,128]{1,0:T(8,128)(2,1)S(1)}, bf16[256,128]{1,0:T(8,128)(2,1)}, u32[]{:S(2)}) copy-start(bf16[256,128]{1,0:T(8,128)(2,1)} %constant.20.clone.refs_3_) | copy-start | bytes 196612
  23.7 7.1 %copy-start.3 = (bf16[256,128]{1,0:T(8,128)(2,1)S(1)}, bf16[256,128]{1,0:T(8,128)(2,1)}, u32[]{:S(2)}) copy-start(bf16[256,128]{1,0:T(8,128)(2,1)} %constant.19.clone.refs_2_) | copy-start | bytes 196612
  23.7 7.0 %copy-start.4 = (bf16[128,192]{1,0:T(8,128)(2,1)S(1)}, bf16[128,192]{1,0:T(8,128)(2,1)}, u32[]{:S(2)}) copy-start(bf16[128,192]{1,0:T(8,128)(2,1)} %constant.17.clone.refs_0_) | copy-start | bytes 147460
  23.7 7.0 %copy-start.5 = (bf16[128,128]{1,0:T(8,128)(2,1)S(1)}, bf16[128,128]{1,0:T(8,128)(2,1)}, u32[]{:S(2)}) copy-start(bf16[128,128]{1,0:T(8,128)(2,1)} %constant.21.clone.refs_4_) | copy-start | bytes 98308
  23.8 7.0 %copy-start.6 = (bf16[64,256]{1,0:T(8,128)(2,1)S(1)}, bf16[64,256]{1,0:T(8,128)(2,1)}, u32[]{:S(2)}) copy-start(bf16[64,256]{1,0:T(8,128)(2,1)} %constant.18.clone.refs_1_) | copy-start | bytes 98308
  23.8 6.1 %collective-permute-start.2 = (f32[5,32,128]{2,1,0:T(8,128)S(1)}, f32[5,32,128]{2,1,0:T(8,128)S(1)}, u32[]{:S(2)}, u32[]{:S(2)}) collective-permute-start(f32[5,32,128]{2,1,0:T(8,128)S(1)} %get-tuple-element.29), channel_id=1, source_target_pairs={{0,253},{1,4},{2,255},{3,6},{4,1},{5,8},{6,3},{7,10},{8,5},{9,12},... | collective-permute-start | bytes 245768 | tf_op jit(solution)/shard_map/ppermute | solution.py:457
  25.6 5.2 %collective-permute-start.3 = (f32[5,32,128]{2,1,0:T(8,128)S(1)}, f32[5,32,128]{2,1,0:T(8,128)S(1)}, u32[]{:S(2)}, u32[]{:S(2)}) collective-permute-start(f32[5,32,128]{2,1,0:T(8,128)S(1)} %get-tuple-element.30), channel_id=1, source_target_pairs={{0,1},{1,0},{2,3},{3,2},{4,5},{5,4},{6,7},{7,6},{8,9},{9,8},{10,11... | collective-permute-start | bytes 245768 | tf_op jit(solution)/shard_map/ppermute | solution.py:457
  36.0 4.5 %collective-permute-start.4 = (f32[5,32,128]{2,1,0:T(8,128)S(1)}, f32[5,32,128]{2,1,0:T(8,128)S(1)}, u32[]{:S(2)}, u32[]{:S(2)}) collective-permute-start(f32[5,32,128]{2,1,0:T(8,128)S(1)} %get-tuple-element.38), channel_id=1, source_target_pairs={{0,253},{1,4},{2,255},{3,6},{4,1},{5,8},{6,3},{7,10},{8,5},{9,12},... | collective-permute-start | bytes 245768 | tf_op jit(solution)/shard_map/ppermute | solution.py:457
  38.4 3.0 %collective-permute-start.5 = (f32[5,32,128]{2,1,0:T(8,128)S(1)}, f32[5,32,128]{2,1,0:T(8,128)S(1)}, u32[]{:S(2)}, u32[]{:S(2)}) collective-permute-start(f32[5,32,128]{2,1,0:T(8,128)S(1)} %get-tuple-element.39), channel_id=1, source_target_pairs={{0,1},{1,0},{2,3},{3,2},{4,5},{5,4},{6,7},{7,6},{8,9},{9,8},{10,11... | collective-permute-start | bytes 245768 | tf_op jit(solution)/shard_map/ppermute | solution.py:457
  43.6 7.3 %collective-permute-start.6 = (f32[5,32,128]{2,1,0:T(8,128)S(1)}, f32[5,32,128]{2,1,0:T(8,128)S(1)}, u32[]{:S(2)}, u32[]{:S(2)}) collective-permute-start(f32[5,32,128]{2,1,0:T(8,128)S(1)} %get-tuple-element.42), channel_id=1, source_target_pairs={{0,253},{1,4},{2,255},{3,6},{4,1},{5,8},{6,3},{7,10},{8,5},{9,12},... | collective-permute-start | bytes 245768 | tf_op jit(solution)/shard_map/ppermute | solution.py:457
  44.5 7.2 %collective-permute-start.7 = (f32[5,32,128]{2,1,0:T(8,128)S(1)}, f32[5,32,128]{2,1,0:T(8,128)S(1)}, u32[]{:S(2)}, u32[]{:S(2)}) collective-permute-start(f32[5,32,128]{2,1,0:T(8,128)S(1)} %get-tuple-element.43), channel_id=1, source_target_pairs={{0,1},{1,0},{2,3},{3,2},{4,5},{5,4},{6,7},{7,6},{8,9},{9,8},{10,11... | collective-permute-start | bytes 245768 | tf_op jit(solution)/shard_map/ppermute | solution.py:457
  53.9 7.3 %collective-permute-start.9 = (f32[4,24,128]{2,1,0:T(8,128)S(1)}, f32[4,24,128]{2,1,0:T(8,128)S(1)}, u32[]{:S(2)}, u32[]{:S(2)}) collective-permute-start(f32[4,24,128]{2,1,0:T(8,128)S(1)} %get-tuple-element.46), channel_id=1, source_target_pairs={{0,253},{1,4},{2,255},{3,6},{4,1},{5,8},{6,3},{7,10},{8,5},{9,12},... | collective-permute-start | bytes 147464 | tf_op jit(solution)/shard_map/ppermute | solution.py:457
  54.1 12.5 %collective-permute-start.8 = (f32[2,48,128]{2,1,0:T(8,128)S(1)}, f32[2,48,128]{2,1,0:T(8,128)S(1)}, u32[]{:S(2)}, u32[]{:S(2)}) collective-permute-start(f32[2,48,128]{2,1,0:T(8,128)S(1)} %get-tuple-element.45), channel_id=1, source_target_pairs={{0,1},{1,0},{2,3},{3,2},{4,5},{5,4},{6,7},{7,6},{8,9},{9,8},{10,11... | collective-permute-start | bytes 147464 | tf_op jit(solution)/shard_map/ppermute | solution.py:457
  61.2 6.2 %collective-permute-start.10 = (f32[2,16,128]{2,1,0:T(8,128)S(1)}, f32[2,16,128]{2,1,0:T(8,128)S(1)}, u32[]{:S(2)}, u32[]{:S(2)}) collective-permute-start(f32[2,16,128]{2,1,0:T(8,128)S(1)} %shard_map.145), channel_id=1, source_target_pairs={{0,1},{1,0},{2,3},{3,2},{4,5},{5,4},{6,7},{7,6},{8,9},{9,8},{10,11... | collective-permute-start | bytes 49160 | tf_op jit(solution)/shard_map/ppermute | solution.py:533

commit v9 on v8

--- a/solution.py
+++ b/solution.py
@@ -129,8 +129,8 @@
 
 def send_kernel(
     images_hbm, mask_hbm, height_hbm, albedo_hbm, owner_hbm, altimetry_hbm, count_hbm, expand_hbm,
-    sent,
-    images, lit_mask, height, albedo, owner, altimetry, count, expand, sems,
+    sent_hbm,
+    images, lit_mask, height, albedo, owner, altimetry, count, expand, sent, sems, out_sems,
 ):
     other = 1 - place()[1]
     rows = pl.ds(pl.multiple_of(other * STRIP, STRIP), STRIP)
@@ -151,16 +151,27 @@
     ]
     for copy in copies:
         copy.start()
-    for copy in copies:
+    parts = [pl.ds(0, IMAGES), pl.ds(IMAGES, IMAGES), pl.ds(ALBEDO, FIELDS - ALBEDO)]
+    sends = [
+        pltpu.make_async_copy(sent.at[part], sent_hbm.at[part], out_sems.at[i])
+        for i, part in enumerate(parts)
+    ]
+    columns = [pl.ds(t * LANES, LANES) for t in range(2)]
+    for i, source in enumerate((images, lit_mask)):
+        copies[i].wait()
+        for t, cols in enumerate(columns):
+            for k in range(IMAGES):
+                sent[i * IMAGES + k, t] = source[k, :, cols].astype(F32)
+        sends[i].start()
+    for copy in copies[2:]:
         copy.wait()
     aux_fields(sent, other, owner, altimetry, count, expand)
-    for t in range(2):
-        cols = pl.ds(t * LANES, LANES)
-        for k in range(IMAGES):
-            sent[k, t] = images[k, :, cols].astype(F32)
-            sent[IMAGES + k, t] = lit_mask[k, :, cols].astype(F32)
+    for t, cols in enumerate(columns):
         sent[ALBEDO, t] = albedo[:, cols]
         sent[HEIGHT, t] = height[:, cols]
+    sends[2].start()
+    for send in sends:
+        send.wait()
 
 
 def keep_kernel(images, lit_mask, height, albedo, owner, altimetry, count, expand, kept):
@@ -478,9 +489,10 @@
         send_kernel,
         out_shape=fields,
         in_specs=[pl.BlockSpec(memory_space=pltpu.HBM)] * len(inputs),
-        out_specs=VMEM,
+        out_specs=pl.BlockSpec(memory_space=pltpu.HBM),
         scratch_shapes=[pltpu.VMEM(shape, a.dtype) for shape, a in zip(cut, inputs)]
-        + [pltpu.SemaphoreType.DMA((len(inputs),))],
+        + [pltpu.VMEM(fields.shape, F32)]
+        + [pltpu.SemaphoreType.DMA((len(inputs),)), pltpu.SemaphoreType.DMA((3,))],
         compiler_params=LARGE,
     )(*inputs)
     sent, count = lax.optimization_barrier((sent, count))

time: 68.2 us -> 67.9 us (level)
  no operation moved by 1% of the time
where the time goes in v9:
time: 67.9 us; the launch traced here: 67.7 us
  starting transfers between devices  48.4 us (71%)
  Pallas kernels  10.5 us (15%)
  waiting for transfers between devices  8.03 us (12%)
    ppermute x4, starting transfers between devices, exchange(): lax.ppermute(intra, axes, across_cores)  19.8 us
    all_to_all x1, starting transfers between devices, per_device(): counts = lax.all_to_all(counts, axes, 0, 0, axis_index_groups=same_core)  13.6 us
    pallas_call x10, Pallas kernels, call(): pl.pallas_call(kernel, out_shape=out_shape, in_specs=[VMEM] * len(args),...  8.34 us
    ppermute x1, starting transfers between devices, per_device(): passed = lax.ppermute(passed, axes, across_cores)  5.33 us
    ppermute x4, starting transfers between devices, exchange(): lax.ppermute(inter, axes, across_strips)  5.22 us
    ppermute x1, starting transfers between devices, per_device(): received = lax.ppermute(sent, axes, across_cores)  3.31 us
    all_to_all x1, waiting for transfers between devices, per_device(): counts = lax.all_to_all(counts, axes, 0, 0, axis_index_groups=same_core)  2.79 us
    ppermute x4, waiting for transfers between devices, exchange(): lax.ppermute(intra, axes, across_cores)  2.65 us
  transfers between devices with their start and end apart: 12, of which 6 were waited for; matrix products, arithmetic and copies ran while one was open for 1% of the time, Pallas kernels for 2%

profile of v9, /device:TPU:1, one launch (start us, length us, event | category | flops | bytes accessed | tf_op | source)
XLA Modules:
  0.0 67.7 jit_solution(13428074133323765142)
XLA Ops:
  0.0 0.0 copy-start.7
  0.0 0.0 copy-start.8
  0.1 2.2 %shard_map.136 = f32[27,2,32,128]{3,2,1,0:T(8,128)} custom-call(bf16[12,64,256]{2,1,0:T(8,128)(2,1)} %images.1, s32[12,64,256]{2,1,0:T(8,128)} %lit_mask.1, f32[64,256]{1,0:T(8,128)} %height.1, f32[64,256]{1,0:T(8,128)} %albedo.1, s32[64,256]{1,0:T(8,128)} %owner.1, f32[16,64]{1,0:T(8,128)} %altimetry.1, s32[1,12]{1,0:T(1,128)} %bitcast.15, ...), custom_call_target="tpu_custom_call" | custom-call | tf_op jit(solution)/shard_map/pallas_call | solution.py:488
  2.2 0.0 copy-start.12
  2.3 3.3 %collective-permute-start = (f32[27,2,32,128]{3,2,1,0:T(8,128)}, f32[27,2,32,128]{3,2,1,0:T(8,128)S(1)}, u32[]{:S(2)}, u32[]{:S(2)}) collective-permute-start(f32[27,2,32,128]{3,2,1,0:T(8,128)} %shard_map.136), channel_id=1, source_target_pairs={{0,1},{1,0},{2,3},{3,2},{4,5},{5,4},{6,7},{7,6},{8,9},{9,8},{10,11... | collective-permute-start | bytes 2654216 | tf_op jit(solution)/shard_map/ppermute | solution.py:499
  5.7 0.2 shard_map.137.kept
  5.9 0.1 constant_dynamic-update-slice_fusion.6
  5.9 0.1 constant_dynamic-update-slice_fusion.5
  6.0 0.1 constant_dynamic-update-slice_fusion.4
  6.1 0.1 constant_dynamic-update-slice_fusion.3
  6.1 1.7 %collective-permute-done.received = f32[27,2,32,128]{3,2,1,0:T(8,128)S(1)} collective-permute-done((f32[27,2,32,128]{3,2,1,0:T(8,128)}, f32[27,2,32,128]{3,2,1,0:T(8,128)S(1)}, u32[]{:S(2)}, u32[]{:S(2)}) %collective-permute-start) | collective-permute-done | bytes 884768 | tf_op jit(solution)/shard_map/ppermute | solution.py:499
  7.9 1.1 %collective-permute-start.1 = (f32[27,32,128]{2,1,0:T(8,128)S(1)}, f32[27,32,128]{2,1,0:T(8,128)S(1)}, u32[]{:S(2)}, u32[]{:S(2)}) collective-permute-start(f32[27,32,128]{2,1,0:T(8,128)S(1)} %shard_map.138.near), channel_id=1, source_target_pairs={{0,2},{1,3},{2,0},{3,1},{4,6},{5,7},{6,4},{7,5},{8,10},{9,11},{10,... | collective-permute-start | bytes 1327112 | tf_op jit(solution)/shard_map/ppermute | solution.py:502
  9.0 0.1 constant_dynamic-update-slice_fusion.2
  9.0 0.1 constant_dynamic-update-slice_fusion.1
  9.1 0.7 shard_map.139
  9.8 13.6 %all-to-all-start = ((f32[128,1,128]{2,1,0:T(1,128)}), f32[128,1,128]{2,1,0:T(1,128)S(1)}, u32[]{:S(2)}, u32[]{:S(2)}) async-start(f32[128,1,128]{2,1,0:T(1,128)} %shard_map.139), calls=%async_computation | async-start | bytes 131072 | tf_op jit(solution)/shard_map/all_to_all | solution.py:505
  23.4 0.0 copy-start.2
  23.4 0.0 copy-start.3
  23.4 0.0 copy-start.4
  23.5 0.0 collective-permute-done.1.halo
  23.5 0.0 copy-start.5
  23.5 0.0 copy-start.6
  23.5 1.8 %collective-permute-start.2 = (f32[5,32,128]{2,1,0:T(8,128)S(1)}, f32[5,32,128]{2,1,0:T(8,128)S(1)}, u32[]{:S(2)}, u32[]{:S(2)}) collective-permute-start(f32[5,32,128]{2,1,0:T(8,128)S(1)} %get-tuple-element.29), channel_id=1, source_target_pairs={{0,253},{1,4},{2,255},{3,6},{4,1},{5,8},{6,3},{7,10},{8,5},{9,12},... | collective-permute-start | bytes 245768 | tf_op jit(solution)/shard_map/ppermute | solution.py:468
  25.3 4.3 %collective-permute-start.3 = (f32[5,32,128]{2,1,0:T(8,128)S(1)}, f32[5,32,128]{2,1,0:T(8,128)S(1)}, u32[]{:S(2)}, u32[]{:S(2)}) collective-permute-start(f32[5,32,128]{2,1,0:T(8,128)S(1)} %get-tuple-element.30), channel_id=1, source_target_pairs={{0,1},{1,0},{2,3},{3,2},{4,5},{5,4},{6,7},{7,6},{8,9},{9,8},{10,11... | collective-permute-start | bytes 245768 | tf_op jit(solution)/shard_map/ppermute | solution.py:468
  29.6 0.1 constant_dynamic-update-slice_fusion.coef
  29.6 0.0 collective-permute-done.2.inter
  29.6 0.8 %collective-permute-done.3.intra = f32[5,32,128]{2,1,0:T(8,128)S(1)} collective-permute-done((f32[5,32,128]{2,1,0:T(8,128)S(1)}, f32[5,32,128]{2,1,0:T(8,128)S(1)}, u32[]{:S(2)}, u32[]{:S(2)}) %collective-permute-start.3) | collective-permute-done | bytes 81952 | tf_op jit(solution)/shard_map/ppermute | solution.py:468
  30.5 0.0 copy-done.4
  30.5 0.5 shard_map.141
  31.0 2.8 %all-to-all-done.counts = f32[128,1,128]{2,1,0:T(1,128)S(1)} async-done(((f32[128,1,128]{2,1,0:T(1,128)}), f32[128,1,128]{2,1,0:T(1,128)S(1)}, u32[]{:S(2)}, u32[]{:S(2)}) %all-to-all-start) | async-done | bytes 65568 | tf_op jit(solution)/shard_map/all_to_all | solution.py:505
  33.8 1.9 %shard_map.142 = (f32[5,64,128]{2,1,0:T(8,128)S(1)}, f32[5,32,128]{2,1,0:T(8,128)S(1)}, f32[5,32,128]{2,1,0:T(8,128)S(1)}, f32[16,128]{1,0:T(8,128)S(1)}) custom-call(f32[7,12,128]{2,1,0:T(8,128)S(1)} %constant_dynamic-update-slice_fusion.coef, f32[128,1,128]{2,1,0:T(1,128)S(1)} %all-to-all-done.counts, f32[27,2,32,128]{3,2,1,0:T(8,128)S(1)} %shard_map.137.kept, ...), custom_call_target="tpu_custom_call" | custom-call | tf_op jit(solution)/shard_map/pallas_call | solution.py:445
  35.7 2.4 %collective-permute-start.4 = (f32[5,32,128]{2,1,0:T(8,128)S(1)}, f32[5,32,128]{2,1,0:T(8,128)S(1)}, u32[]{:S(2)}, u32[]{:S(2)}) collective-permute-start(f32[5,32,128]{2,1,0:T(8,128)S(1)} %get-tuple-element.38), channel_id=1, source_target_pairs={{0,253},{1,4},{2,255},{3,6},{4,1},{5,8},{6,3},{7,10},{8,5},{9,12},... | collective-permute-start | bytes 245768 | tf_op jit(solution)/shard_map/ppermute | solution.py:468
  38.2 2.1 %collective-permute-start.5 = (f32[5,32,128]{2,1,0:T(8,128)S(1)}, f32[5,32,128]{2,1,0:T(8,128)S(1)}, u32[]{:S(2)}, u32[]{:S(2)}) collective-permute-start(f32[5,32,128]{2,1,0:T(8,128)S(1)} %get-tuple-element.39), channel_id=1, source_target_pairs={{0,1},{1,0},{2,3},{3,2},{4,5},{5,4},{6,7},{7,6},{8,9},{9,8},{10,11... | collective-permute-start | bytes 245768 | tf_op jit(solution)/shard_map/ppermute | solution.py:468
  40.2 0.0 collective-permute-done.4.inter
  40.3 0.9 %collective-permute-done.5.intra = f32[5,32,128]{2,1,0:T(8,128)S(1)} collective-permute-done((f32[5,32,128]{2,1,0:T(8,128)S(1)}, f32[5,32,128]{2,1,0:T(8,128)S(1)}, u32[]{:S(2)}, u32[]{:S(2)}) %collective-permute-start.5) | collective-permute-done | bytes 81952 | tf_op jit(solution)/shard_map/ppermute | solution.py:468
  41.2 2.2 %shard_map.143 = (f32[5,64,128]{2,1,0:T(8,128)S(1)}, f32[5,32,128]{2,1,0:T(8,128)S(1)}, f32[5,32,128]{2,1,0:T(8,128)S(1)}) custom-call(f32[7,12,128]{2,1,0:T(8,128)S(1)} %constant_dynamic-update-slice_fusion.coef, f32[16,128]{1,0:T(8,128)S(1)} %get-tuple-element.36.weight, f32[27,2,32,128]{3,2,1,0:T(8,128)S(1)} %shard_map.137.kept, ...), custom_call_target="tpu_custom_call" | custom-call | tf_op jit(solution)/shard_map/pallas_call | solution.py:445
  43.3 1.0 %collective-permute-start.6 = (f32[5,32,128]{2,1,0:T(8,128)S(1)}, f32[5,32,128]{2,1,0:T(8,128)S(1)}, u32[]{:S(2)}, u32[]{:S(2)}) collective-permute-start(f32[5,32,128]{2,1,0:T(8,128)S(1)} %get-tuple-element.42), channel_id=1, source_target_pairs={{0,253},{1,4},{2,255},{3,6},{4,1},{5,8},{6,3},{7,10},{8,5},{9,12},... | collective-permute-start | bytes 245768 | tf_op jit(solution)/shard_map/ppermute | solution.py:468
  44.3 6.3 %collective-permute-start.7 = (f32[5,32,128]{2,1,0:T(8,128)S(1)}, f32[5,32,128]{2,1,0:T(8,128)S(1)}, u32[]{:S(2)}, u32[]{:S(2)}) collective-permute-start(f32[5,32,128]{2,1,0:T(8,128)S(1)} %get-tuple-element.43), channel_id=1, source_target_pairs={{0,1},{1,0},{2,3},{3,2},{4,5},{5,4},{6,7},{7,6},{8,9},{9,8},{10,11... | collective-permute-start | bytes 245768 | tf_op jit(solution)/shard_map/ppermute | solution.py:468
  50.6 0.0 collective-permute-done.6.inter
  50.6 0.9 %collective-permute-done.7.intra = f32[5,32,128]{2,1,0:T(8,128)S(1)} collective-permute-done((f32[5,32,128]{2,1,0:T(8,128)S(1)}, f32[5,32,128]{2,1,0:T(8,128)S(1)}, u32[]{:S(2)}, u32[]{:S(2)}) %collective-permute-start.7) | collective-permute-done | bytes 81952 | tf_op jit(solution)/shard_map/ppermute | solution.py:468
  51.5 2.2 %shard_map.144 = (f32[4,24,128]{2,1,0:T(8,128)S(1)}, f32[2,48,128]{2,1,0:T(8,128)S(1)}, f32[2,48,128]{2,1,0:T(8,128)S(1)}) custom-call(f32[7,12,128]{2,1,0:T(8,128)S(1)} %constant_dynamic-update-slice_fusion.coef, f32[16,128]{1,0:T(8,128)S(1)} %get-tuple-element.36.weight, f32[27,2,32,128]{3,2,1,0:T(8,128)S(1)} %shard_map.137.kept, ...), custom_call_target="tpu_custom_call" | custom-call | tf_op jit(solution)/shard_map/pallas_call | solution.py:445
  53.7 0.1 collective-permute-start.9
  53.8 7.2 %collective-permute-start.8 = (f32[2,48,128]{2,1,0:T(8,128)S(1)}, f32[2,48,128]{2,1,0:T(8,128)S(1)}, u32[]{:S(2)}, u32[]{:S(2)}) collective-permute-start(f32[2,48,128]{2,1,0:T(8,128)S(1)} %get-tuple-element.45), channel_id=1, source_target_pairs={{0,1},{1,0},{2,3},{3,2},{4,5},{5,4},{6,7},{7,6},{8,9},{9,8},{10,11... | collective-permute-start | bytes 147464 | tf_op jit(solution)/shard_map/ppermute | solution.py:468
  60.9 0.0 collective-permute-done.9.inter
  60.9 5.3 %collective-permute-start.10 = (f32[2,16,128]{2,1,0:T(8,128)S(1)}, f32[2,16,128]{2,1,0:T(8,128)S(1)}, u32[]{:S(2)}, u32[]{:S(2)}) collective-permute-start(f32[2,16,128]{2,1,0:T(8,128)S(1)} %shard_map.145), channel_id=1, source_target_pairs={{0,1},{1,0},{2,3},{3,2},{4,5},{5,4},{6,7},{7,6},{8,9},{9,8},{10,11... | collective-permute-start | bytes 49160 | tf_op jit(solution)/shard_map/ppermute | solution.py:545
  66.3 0.0 collective-permute-done.8.intra
  66.3 0.8 %collective-permute-done.10.forward = f32[2,16,128]{2,1,0:T(8,128)S(1)} collective-permute-done((f32[2,16,128]{2,1,0:T(8,128)S(1)}, f32[2,16,128]{2,1,0:T(8,128)S(1)}, u32[]{:S(2)}, u32[]{:S(2)}) %collective-permute-start.10) | collective-permute-done | bytes 16416 | tf_op jit(solution)/shard_map/ppermute | solution.py:545
  67.1 0.6 shard_map.146
  (23 shorter events, 0.1 us)
Async XLA Ops:
  0.0 5.6 %copy-start.13 = (f32[12,4]{0,1:T(4,128)S(1)}, f32[12,4]{0,1:T(4,128)}, u32[]{:S(2)}) copy-start(f32[12,4]{0,1:T(4,128)} %param.19) | copy-start | bytes 580
  0.0 5.6 %copy-start = (s32[12,64,256]{2,1,0:T(8,128)S(1)}, s32[12,64,256]{2,1,0:T(8,128)}, u32[]{:S(2)}) copy-start(s32[12,64,256]{2,1,0:T(8,128)} %lit_mask.1) | copy-start | bytes 2359300
  0.0 5.6 %copy-start.1 = (bf16[12,64,256]{2,1,0:T(8,128)(2,1)S(1)}, bf16[12,64,256]{2,1,0:T(8,128)(2,1)}, u32[]{:S(2)}) copy-start(bf16[12,64,256]{2,1,0:T(8,128)(2,1)} %images.1) | copy-start | bytes 1179652
  0.0 5.6 %copy-start.7 = (bf16[192,256]{1,0:T(8,128)(2,1)S(1)}, bf16[192,256]{1,0:T(8,128)(2,1)}, u32[]{:S(2)}) copy-start(bf16[192,256]{1,0:T(8,128)(2,1)} %constant.16.clone.expand_hbm.expand) | copy-start | bytes 294916
  0.0 5.6 %copy-start.8 = (f32[64,256]{1,0:T(8,128)S(1)}, f32[64,256]{1,0:T(8,128)}, u32[]{:S(2)}) copy-start(f32[64,256]{1,0:T(8,128)} %height.1) | copy-start | bytes 196612
  0.0 5.6 %copy-start.9 = (f32[64,256]{1,0:T(8,128)S(1)}, f32[64,256]{1,0:T(8,128)}, u32[]{:S(2)}) copy-start(f32[64,256]{1,0:T(8,128)} %albedo.1) | copy-start | bytes 196612
  0.0 5.6 %copy-start.10 = (s32[64,256]{1,0:T(8,128)S(1)}, s32[64,256]{1,0:T(8,128)}, u32[]{:S(2)}) copy-start(s32[64,256]{1,0:T(8,128)} %owner.1) | copy-start | bytes 196612
  0.1 5.6 %copy-start.11 = (f32[16,64]{1,0:T(8,128)S(1)}, f32[16,64]{1,0:T(8,128)}, u32[]{:S(2)}) copy-start(f32[16,64]{1,0:T(8,128)} %altimetry.1) | copy-start | bytes 12292
  2.2 3.4 %copy-start.12 = (s32[12,1,1]{0,2,1:T(1,128)S(1)}, s32[12,1,1]{0,2,1:T(1,128)}, u32[]{:S(2)}) copy-start(s32[12,1,1]{0,2,1:T(1,128)} %param.18) | copy-start | bytes 148
  2.3 5.6 %collective-permute-start = (f32[27,2,32,128]{3,2,1,0:T(8,128)}, f32[27,2,32,128]{3,2,1,0:T(8,128)S(1)}, u32[]{:S(2)}, u32[]{:S(2)}) collective-permute-start(f32[27,2,32,128]{3,2,1,0:T(8,128)} %shard_map.136), channel_id=1, source_target_pairs={{0,1},{1,0},{2,3},{3,2},{4,5},{5,4},{6,7},{7,6},{8,9},{9,8},{10,11... | collective-permute-start | bytes 2654216 | tf_op jit(solution)/shard_map/ppermute | solution.py:499
  7.9 15.6 %collective-permute-start.1 = (f32[27,32,128]{2,1,0:T(8,128)S(1)}, f32[27,32,128]{2,1,0:T(8,128)S(1)}, u32[]{:S(2)}, u32[]{:S(2)}) collective-permute-start(f32[27,32,128]{2,1,0:T(8,128)S(1)} %shard_map.138.near), channel_id=1, source_target_pairs={{0,2},{1,3},{2,0},{3,1},{4,6},{5,7},{6,4},{7,5},{8,10},{9,11},{10,... | collective-permute-start | bytes 1327112 | tf_op jit(solution)/shard_map/ppermute | solution.py:502
  9.8 24.0 %all-to-all-start = ((f32[128,1,128]{2,1,0:T(1,128)}), f32[128,1,128]{2,1,0:T(1,128)S(1)}, u32[]{:S(2)}, u32[]{:S(2)}) async-start(f32[128,1,128]{2,1,0:T(1,128)} %shard_map.139), calls=%async_computation | async-start | bytes 131072 | tf_op jit(solution)/shard_map/all_to_all | solution.py:505
  23.4 7.1 %copy-start.2 = (bf16[256,128]{1,0:T(8,128)(2,1)S(1)}, bf16[256,128]{1,0:T(8,128)(2,1)}, u32[]{:S(2)}) copy-start(bf16[256,128]{1,0:T(8,128)(2,1)} %constant.20.clone.refs_3_) | copy-start | bytes 196612
  23.4 7.1 %copy-start.3 = (bf16[256,128]{1,0:T(8,128)(2,1)S(1)}, bf16[256,128]{1,0:T(8,128)(2,1)}, u32[]{:S(2)}) copy-start(bf16[256,128]{1,0:T(8,128)(2,1)} %constant.19.clone.refs_2_) | copy-start | bytes 196612
  23.4 7.0 %copy-start.4 = (bf16[128,192]{1,0:T(8,128)(2,1)S(1)}, bf16[128,192]{1,0:T(8,128)(2,1)}, u32[]{:S(2)}) copy-start(bf16[128,192]{1,0:T(8,128)(2,1)} %constant.17.clone.refs_0_) | copy-start | bytes 147460
  23.5 7.0 %copy-start.5 = (bf16[128,128]{1,0:T(8,128)(2,1)S(1)}, bf16[128,128]{1,0:T(8,128)(2,1)}, u32[]{:S(2)}) copy-start(bf16[128,128]{1,0:T(8,128)(2,1)} %constant.21.clone.refs_4_) | copy-start | bytes 98308
  23.5 7.0 %copy-start.6 = (bf16[64,256]{1,0:T(8,128)(2,1)S(1)}, bf16[64,256]{1,0:T(8,128)(2,1)}, u32[]{:S(2)}) copy-start(bf16[64,256]{1,0:T(8,128)(2,1)} %constant.18.clone.refs_1_) | copy-start | bytes 98308
  23.5 6.1 %collective-permute-start.2 = (f32[5,32,128]{2,1,0:T(8,128)S(1)}, f32[5,32,128]{2,1,0:T(8,128)S(1)}, u32[]{:S(2)}, u32[]{:S(2)}) collective-permute-start(f32[5,32,128]{2,1,0:T(8,128)S(1)} %get-tuple-element.29), channel_id=1, source_target_pairs={{0,253},{1,4},{2,255},{3,6},{4,1},{5,8},{6,3},{7,10},{8,5},{9,12},... | collective-permute-start | bytes 245768 | tf_op jit(solution)/shard_map/ppermute | solution.py:468
  25.3 5.2 %collective-permute-start.3 = (f32[5,32,128]{2,1,0:T(8,128)S(1)}, f32[5,32,128]{2,1,0:T(8,128)S(1)}, u32[]{:S(2)}, u32[]{:S(2)}) collective-permute-start(f32[5,32,128]{2,1,0:T(8,128)S(1)} %get-tuple-element.30), channel_id=1, source_target_pairs={{0,1},{1,0},{2,3},{3,2},{4,5},{5,4},{6,7},{7,6},{8,9},{9,8},{10,11... | collective-permute-start | bytes 245768 | tf_op jit(solution)/shard_map/ppermute | solution.py:468
  35.7 4.5 %collective-permute-start.4 = (f32[5,32,128]{2,1,0:T(8,128)S(1)}, f32[5,32,128]{2,1,0:T(8,128)S(1)}, u32[]{:S(2)}, u32[]{:S(2)}) collective-permute-start(f32[5,32,128]{2,1,0:T(8,128)S(1)} %get-tuple-element.38), channel_id=1, source_target_pairs={{0,253},{1,4},{2,255},{3,6},{4,1},{5,8},{6,3},{7,10},{8,5},{9,12},... | collective-permute-start | bytes 245768 | tf_op jit(solution)/shard_map/ppermute | solution.py:468
  38.2 3.0 %collective-permute-start.5 = (f32[5,32,128]{2,1,0:T(8,128)S(1)}, f32[5,32,128]{2,1,0:T(8,128)S(1)}, u32[]{:S(2)}, u32[]{:S(2)}) collective-permute-start(f32[5,32,128]{2,1,0:T(8,128)S(1)} %get-tuple-element.39), channel_id=1, source_target_pairs={{0,1},{1,0},{2,3},{3,2},{4,5},{5,4},{6,7},{7,6},{8,9},{9,8},{10,11... | collective-permute-start | bytes 245768 | tf_op jit(solution)/shard_map/ppermute | solution.py:468
  43.3 7.3 %collective-permute-start.6 = (f32[5,32,128]{2,1,0:T(8,128)S(1)}, f32[5,32,128]{2,1,0:T(8,128)S(1)}, u32[]{:S(2)}, u32[]{:S(2)}) collective-permute-start(f32[5,32,128]{2,1,0:T(8,128)S(1)} %get-tuple-element.42), channel_id=1, source_target_pairs={{0,253},{1,4},{2,255},{3,6},{4,1},{5,8},{6,3},{7,10},{8,5},{9,12},... | collective-permute-start | bytes 245768 | tf_op jit(solution)/shard_map/ppermute | solution.py:468
  44.3 7.2 %collective-permute-start.7 = (f32[5,32,128]{2,1,0:T(8,128)S(1)}, f32[5,32,128]{2,1,0:T(8,128)S(1)}, u32[]{:S(2)}, u32[]{:S(2)}) collective-permute-start(f32[5,32,128]{2,1,0:T(8,128)S(1)} %get-tuple-element.43), channel_id=1, source_target_pairs={{0,1},{1,0},{2,3},{3,2},{4,5},{5,4},{6,7},{7,6},{8,9},{9,8},{10,11... | collective-permute-start | bytes 245768 | tf_op jit(solution)/shard_map/ppermute | solution.py:468
  53.7 7.3 %collective-permute-start.9 = (f32[4,24,128]{2,1,0:T(8,128)S(1)}, f32[4,24,128]{2,1,0:T(8,128)S(1)}, u32[]{:S(2)}, u32[]{:S(2)}) collective-permute-start(f32[4,24,128]{2,1,0:T(8,128)S(1)} %get-tuple-element.46), channel_id=1, source_target_pairs={{0,253},{1,4},{2,255},{3,6},{4,1},{5,8},{6,3},{7,10},{8,5},{9,12},... | collective-permute-start | bytes 147464 | tf_op jit(solution)/shard_map/ppermute | solution.py:468
  53.8 12.5 %collective-permute-start.8 = (f32[2,48,128]{2,1,0:T(8,128)S(1)}, f32[2,48,128]{2,1,0:T(8,128)S(1)}, u32[]{:S(2)}, u32[]{:S(2)}) collective-permute-start(f32[2,48,128]{2,1,0:T(8,128)S(1)} %get-tuple-element.45), channel_id=1, source_target_pairs={{0,1},{1,0},{2,3},{3,2},{4,5},{5,4},{6,7},{7,6},{8,9},{9,8},{10,11... | collective-permute-start | bytes 147464 | tf_op jit(solution)/shard_map/ppermute | solution.py:468
  60.9 6.2 %collective-permute-start.10 = (f32[2,16,128]{2,1,0:T(8,128)S(1)}, f32[2,16,128]{2,1,0:T(8,128)S(1)}, u32[]{:S(2)}, u32[]{:S(2)}) collective-permute-start(f32[2,16,128]{2,1,0:T(8,128)S(1)} %shard_map.145), channel_id=1, source_target_pairs={{0,1},{1,0},{2,3},{3,2},{4,5},{5,4},{6,7},{7,6},{8,9},{9,8},{10,11... | collective-permute-start | bytes 49160 | tf_op jit(solution)/shard_map/ppermute | solution.py:545

commit v10 on v9

--- a/solution.py
+++ b/solution.py
@@ -97,10 +97,11 @@
 
 
 def filter_lat(tiles, taps, count):
-    total = None
-    for part in pieces(with_sides(tiles), count):
-        term = dot(part, taps)
-        total = term if total is None else total + term
+    sums = dot(jnp.concatenate(pieces(with_sides(tiles), count), axis=0), taps)
+    size = sums.shape[0] // count
+    total = sums[0:size]
+    for i in range(1, count):
+        total = total + sums[i * size : (i + 1) * size]
     return total
 
 
@@ -293,8 +294,8 @@
     def part(row, count, j):
         return down[row : row + count, j * LANES : (j + 1) * LANES]
 
-    slope_lon[...] = TAP_SCALE * filter_lat([part(0, STRIP, j) for j in tiles], smooth[...], 3)
-    slope_lat[...] = TAP_SCALE * filter_lat([part(STRIP, STRIP, j) for j in tiles], slope[...], 3)
+    slope_lon[...] = TAP_SCALE * filter_lat([part(0, STRIP, j) for j in tiles], smooth[...], 2)
+    slope_lat[...] = TAP_SCALE * filter_lat([part(STRIP, STRIP, j) for j in tiles], slope[...], 2)
     sums = []
     for j in tiles:
         shift = shift_rows(aux, j)

time: 67.9 us -> 67.8 us (level)
  transfers between devices with their start and end apart: 12 -> 12, of which waited for: 6 -> 7; matrix products, arithmetic and copies ran while one was open for 1% -> 1% of each run, Pallas kernels for 2% -> 2%
where the time goes in v10:
time: 67.8 us; the launch traced here: 67.7 us
  starting transfers between devices  48.4 us (71%)
  Pallas kernels  10.4 us (15%)
  waiting for transfers between devices  8.08 us (12%)
    ppermute x4, starting transfers between devices, exchange(): lax.ppermute(intra, axes, across_cores)  19.7 us
    all_to_all x1, starting transfers between devices, per_device(): counts = lax.all_to_all(counts, axes, 0, 0, axis_index_groups=same_core)  13.6 us
    pallas_call x10, Pallas kernels, call(): pl.pallas_call(kernel, out_shape=out_shape, in_specs=[VMEM] * len(args),...  8.22 us
    ppermute x1, starting transfers between devices, per_device(): passed = lax.ppermute(passed, axes, across_cores)  5.37 us
    ppermute x4, starting transfers between devices, exchange(): lax.ppermute(inter, axes, across_strips)  5.26 us
    ppermute x1, starting transfers between devices, per_device(): received = lax.ppermute(sent, axes, across_cores)  3.31 us
    all_to_all x1, waiting for transfers between devices, per_device(): counts = lax.all_to_all(counts, axes, 0, 0, axis_index_groups=same_core)  2.84 us
    ppermute x4, waiting for transfers between devices, exchange(): lax.ppermute(intra, axes, across_cores)  2.6 us
  transfers between devices with their start and end apart: 12, of which 7 were waited for; matrix products, arithmetic and copies ran while one was open for 1% of the time, Pallas kernels for 2%

profile of v10, /device:TPU:1, one launch (start us, length us, event | category | flops | bytes accessed | tf_op | source)
XLA Modules:
  0.0 67.7 jit_solution(3019512745441553760)
XLA Ops:
  0.0 0.0 copy-start.7
  0.1 2.2 %shard_map.136 = f32[27,2,32,128]{3,2,1,0:T(8,128)} custom-call(bf16[12,64,256]{2,1,0:T(8,128)(2,1)} %images.1, s32[12,64,256]{2,1,0:T(8,128)} %lit_mask.1, f32[64,256]{1,0:T(8,128)} %height.1, f32[64,256]{1,0:T(8,128)} %albedo.1, s32[64,256]{1,0:T(8,128)} %owner.1, f32[16,64]{1,0:T(8,128)} %altimetry.1, s32[1,12]{1,0:T(1,128)} %bitcast.15, ...), custom_call_target="tpu_custom_call" | custom-call | tf_op jit(solution)/shard_map/pallas_call | solution.py:489
  2.2 0.0 copy-start.12
  2.3 3.3 %collective-permute-start = (f32[27,2,32,128]{3,2,1,0:T(8,128)}, f32[27,2,32,128]{3,2,1,0:T(8,128)S(1)}, u32[]{:S(2)}, u32[]{:S(2)}) collective-permute-start(f32[27,2,32,128]{3,2,1,0:T(8,128)} %shard_map.136), channel_id=1, source_target_pairs={{0,1},{1,0},{2,3},{3,2},{4,5},{5,4},{6,7},{7,6},{8,9},{9,8},{10,11... | collective-permute-start | bytes 2654216 | tf_op jit(solution)/shard_map/ppermute | solution.py:500
  5.7 0.2 shard_map.137.kept
  5.9 0.1 constant_dynamic-update-slice_fusion.6
  5.9 0.1 constant_dynamic-update-slice_fusion.5
  6.0 0.1 constant_dynamic-update-slice_fusion.4
  6.1 0.1 constant_dynamic-update-slice_fusion.3
  6.1 1.7 %collective-permute-done.received = f32[27,2,32,128]{3,2,1,0:T(8,128)S(1)} collective-permute-done((f32[27,2,32,128]{3,2,1,0:T(8,128)}, f32[27,2,32,128]{3,2,1,0:T(8,128)S(1)}, u32[]{:S(2)}, u32[]{:S(2)}) %collective-permute-start) | collective-permute-done | bytes 884768 | tf_op jit(solution)/shard_map/ppermute | solution.py:500
  7.9 1.1 %collective-permute-start.1 = (f32[27,32,128]{2,1,0:T(8,128)S(1)}, f32[27,32,128]{2,1,0:T(8,128)S(1)}, u32[]{:S(2)}, u32[]{:S(2)}) collective-permute-start(f32[27,32,128]{2,1,0:T(8,128)S(1)} %shard_map.138.near), channel_id=1, source_target_pairs={{0,2},{1,3},{2,0},{3,1},{4,6},{5,7},{6,4},{7,5},{8,10},{9,11},{10,... | collective-permute-start | bytes 1327112 | tf_op jit(solution)/shard_map/ppermute | solution.py:503
  9.0 0.1 constant_dynamic-update-slice_fusion.2
  9.0 0.1 constant_dynamic-update-slice_fusion.1
  9.1 0.7 shard_map.139
  9.8 13.6 %all-to-all-start = ((f32[128,1,128]{2,1,0:T(1,128)}), f32[128,1,128]{2,1,0:T(1,128)S(1)}, u32[]{:S(2)}, u32[]{:S(2)}) async-start(f32[128,1,128]{2,1,0:T(1,128)} %shard_map.139), calls=%async_computation | async-start | bytes 131072 | tf_op jit(solution)/shard_map/all_to_all | solution.py:506
  23.4 0.0 copy-start.2
  23.4 0.0 copy-start.3
  23.4 0.0 copy-start.4
  23.5 0.0 collective-permute-done.1.halo
  23.5 0.0 copy-start.5
  23.5 0.0 copy-start.6
  23.5 1.8 %collective-permute-start.2 = (f32[5,32,128]{2,1,0:T(8,128)S(1)}, f32[5,32,128]{2,1,0:T(8,128)S(1)}, u32[]{:S(2)}, u32[]{:S(2)}) collective-permute-start(f32[5,32,128]{2,1,0:T(8,128)S(1)} %get-tuple-element.29), channel_id=1, source_target_pairs={{0,253},{1,4},{2,255},{3,6},{4,1},{5,8},{6,3},{7,10},{8,5},{9,12},... | collective-permute-start | bytes 245768 | tf_op jit(solution)/shard_map/ppermute | solution.py:469
  25.3 4.3 %collective-permute-start.3 = (f32[5,32,128]{2,1,0:T(8,128)S(1)}, f32[5,32,128]{2,1,0:T(8,128)S(1)}, u32[]{:S(2)}, u32[]{:S(2)}) collective-permute-start(f32[5,32,128]{2,1,0:T(8,128)S(1)} %get-tuple-element.30), channel_id=1, source_target_pairs={{0,1},{1,0},{2,3},{3,2},{4,5},{5,4},{6,7},{7,6},{8,9},{9,8},{10,11... | collective-permute-start | bytes 245768 | tf_op jit(solution)/shard_map/ppermute | solution.py:469
  29.6 0.1 constant_dynamic-update-slice_fusion.coef
  29.6 0.0 collective-permute-done.2.inter
  29.6 0.8 %collective-permute-done.3.intra = f32[5,32,128]{2,1,0:T(8,128)S(1)} collective-permute-done((f32[5,32,128]{2,1,0:T(8,128)S(1)}, f32[5,32,128]{2,1,0:T(8,128)S(1)}, u32[]{:S(2)}, u32[]{:S(2)}) %collective-permute-start.3) | collective-permute-done | bytes 81952 | tf_op jit(solution)/shard_map/ppermute | solution.py:469
  30.5 0.0 copy-done.5
  30.5 0.0 copy-done.6
  30.5 0.4 shard_map.141
  30.9 2.8 %all-to-all-done.counts = f32[128,1,128]{2,1,0:T(1,128)S(1)} async-done(((f32[128,1,128]{2,1,0:T(1,128)}), f32[128,1,128]{2,1,0:T(1,128)S(1)}, u32[]{:S(2)}, u32[]{:S(2)}) %all-to-all-start) | async-done | bytes 65568 | tf_op jit(solution)/shard_map/all_to_all | solution.py:506
  33.8 1.9 %shard_map.142 = (f32[5,64,128]{2,1,0:T(8,128)S(1)}, f32[5,32,128]{2,1,0:T(8,128)S(1)}, f32[5,32,128]{2,1,0:T(8,128)S(1)}, f32[16,128]{1,0:T(8,128)S(1)}) custom-call(f32[7,12,128]{2,1,0:T(8,128)S(1)} %constant_dynamic-update-slice_fusion.coef, f32[128,1,128]{2,1,0:T(1,128)S(1)} %all-to-all-done.counts, f32[27,2,32,128]{3,2,1,0:T(8,128)S(1)} %shard_map.137.kept, ...), custom_call_target="tpu_custom_call" | custom-call | tf_op jit(solution)/shard_map/pallas_call | solution.py:446
  35.7 2.4 %collective-permute-start.4 = (f32[5,32,128]{2,1,0:T(8,128)S(1)}, f32[5,32,128]{2,1,0:T(8,128)S(1)}, u32[]{:S(2)}, u32[]{:S(2)}) collective-permute-start(f32[5,32,128]{2,1,0:T(8,128)S(1)} %get-tuple-element.38), channel_id=1, source_target_pairs={{0,253},{1,4},{2,255},{3,6},{4,1},{5,8},{6,3},{7,10},{8,5},{9,12},... | collective-permute-start | bytes 245768 | tf_op jit(solution)/shard_map/ppermute | solution.py:469
  38.1 2.0 %collective-permute-start.5 = (f32[5,32,128]{2,1,0:T(8,128)S(1)}, f32[5,32,128]{2,1,0:T(8,128)S(1)}, u32[]{:S(2)}, u32[]{:S(2)}) collective-permute-start(f32[5,32,128]{2,1,0:T(8,128)S(1)} %get-tuple-element.39), channel_id=1, source_target_pairs={{0,1},{1,0},{2,3},{3,2},{4,5},{5,4},{6,7},{7,6},{8,9},{9,8},{10,11... | collective-permute-start | bytes 245768 | tf_op jit(solution)/shard_map/ppermute | solution.py:469
  40.2 0.1 collective-permute-done.4.inter
  40.3 0.8 %collective-permute-done.5.intra = f32[5,32,128]{2,1,0:T(8,128)S(1)} collective-permute-done((f32[5,32,128]{2,1,0:T(8,128)S(1)}, f32[5,32,128]{2,1,0:T(8,128)S(1)}, u32[]{:S(2)}, u32[]{:S(2)}) %collective-permute-start.5) | collective-permute-done | bytes 81952 | tf_op jit(solution)/shard_map/ppermute | solution.py:469
  41.1 2.1 %shard_map.143 = (f32[5,64,128]{2,1,0:T(8,128)S(1)}, f32[5,32,128]{2,1,0:T(8,128)S(1)}, f32[5,32,128]{2,1,0:T(8,128)S(1)}) custom-call(f32[7,12,128]{2,1,0:T(8,128)S(1)} %constant_dynamic-update-slice_fusion.coef, f32[16,128]{1,0:T(8,128)S(1)} %get-tuple-element.36.weight, f32[27,2,32,128]{3,2,1,0:T(8,128)S(1)} %shard_map.137.kept, ...), custom_call_target="tpu_custom_call" | custom-call | tf_op jit(solution)/shard_map/pallas_call | solution.py:446
  43.2 1.0 %collective-permute-start.6 = (f32[5,32,128]{2,1,0:T(8,128)S(1)}, f32[5,32,128]{2,1,0:T(8,128)S(1)}, u32[]{:S(2)}, u32[]{:S(2)}) collective-permute-start(f32[5,32,128]{2,1,0:T(8,128)S(1)} %get-tuple-element.42), channel_id=1, source_target_pairs={{0,253},{1,4},{2,255},{3,6},{4,1},{5,8},{6,3},{7,10},{8,5},{9,12},... | collective-permute-start | bytes 245768 | tf_op jit(solution)/shard_map/ppermute | solution.py:469
  44.2 6.3 %collective-permute-start.7 = (f32[5,32,128]{2,1,0:T(8,128)S(1)}, f32[5,32,128]{2,1,0:T(8,128)S(1)}, u32[]{:S(2)}, u32[]{:S(2)}) collective-permute-start(f32[5,32,128]{2,1,0:T(8,128)S(1)} %get-tuple-element.43), channel_id=1, source_target_pairs={{0,1},{1,0},{2,3},{3,2},{4,5},{5,4},{6,7},{7,6},{8,9},{9,8},{10,11... | collective-permute-start | bytes 245768 | tf_op jit(solution)/shard_map/ppermute | solution.py:469
  50.5 0.0 collective-permute-done.6.inter
  50.5 0.9 %collective-permute-done.7.intra = f32[5,32,128]{2,1,0:T(8,128)S(1)} collective-permute-done((f32[5,32,128]{2,1,0:T(8,128)S(1)}, f32[5,32,128]{2,1,0:T(8,128)S(1)}, u32[]{:S(2)}, u32[]{:S(2)}) %collective-permute-start.7) | collective-permute-done | bytes 81952 | tf_op jit(solution)/shard_map/ppermute | solution.py:469
  51.4 2.2 %shard_map.144 = (f32[4,24,128]{2,1,0:T(8,128)S(1)}, f32[2,48,128]{2,1,0:T(8,128)S(1)}, f32[2,48,128]{2,1,0:T(8,128)S(1)}) custom-call(f32[7,12,128]{2,1,0:T(8,128)S(1)} %constant_dynamic-update-slice_fusion.coef, f32[16,128]{1,0:T(8,128)S(1)} %get-tuple-element.36.weight, f32[27,2,32,128]{3,2,1,0:T(8,128)S(1)} %shard_map.137.kept, ...), custom_call_target="tpu_custom_call" | custom-call | tf_op jit(solution)/shard_map/pallas_call | solution.py:446
  53.6 0.1 collective-permute-start.9
  53.7 7.2 %collective-permute-start.8 = (f32[2,48,128]{2,1,0:T(8,128)S(1)}, f32[2,48,128]{2,1,0:T(8,128)S(1)}, u32[]{:S(2)}, u32[]{:S(2)}) collective-permute-start(f32[2,48,128]{2,1,0:T(8,128)S(1)} %get-tuple-element.45), channel_id=1, source_target_pairs={{0,1},{1,0},{2,3},{3,2},{4,5},{5,4},{6,7},{7,6},{8,9},{9,8},{10,11... | collective-permute-start | bytes 147464 | tf_op jit(solution)/shard_map/ppermute | solution.py:469
  60.8 0.0 collective-permute-done.9.inter
  60.8 5.4 %collective-permute-start.10 = (f32[2,16,128]{2,1,0:T(8,128)S(1)}, f32[2,16,128]{2,1,0:T(8,128)S(1)}, u32[]{:S(2)}, u32[]{:S(2)}) collective-permute-start(f32[2,16,128]{2,1,0:T(8,128)S(1)} %shard_map.145), channel_id=1, source_target_pairs={{0,1},{1,0},{2,3},{3,2},{4,5},{5,4},{6,7},{7,6},{8,9},{9,8},{10,11... | collective-permute-start | bytes 49160 | tf_op jit(solution)/shard_map/ppermute | solution.py:546
  66.2 0.0 collective-permute-done.8.intra
  66.2 0.8 %collective-permute-done.10.forward = f32[2,16,128]{2,1,0:T(8,128)S(1)} collective-permute-done((f32[2,16,128]{2,1,0:T(8,128)S(1)}, f32[2,16,128]{2,1,0:T(8,128)S(1)}, u32[]{:S(2)}, u32[]{:S(2)}) %collective-permute-start.10) | collective-permute-done | bytes 16416 | tf_op jit(solution)/shard_map/ppermute | solution.py:546
  67.0 0.6 shard_map.146
  (23 shorter events, 0.1 us)
Async XLA Ops:
  0.0 5.6 %copy-start.13 = (f32[12,4]{0,1:T(4,128)S(1)}, f32[12,4]{0,1:T(4,128)}, u32[]{:S(2)}) copy-start(f32[12,4]{0,1:T(4,128)} %param.19) | copy-start | bytes 580
  0.0 5.6 %copy-start = (s32[12,64,256]{2,1,0:T(8,128)S(1)}, s32[12,64,256]{2,1,0:T(8,128)}, u32[]{:S(2)}) copy-start(s32[12,64,256]{2,1,0:T(8,128)} %lit_mask.1) | copy-start | bytes 2359300
  0.0 5.6 %copy-start.1 = (bf16[12,64,256]{2,1,0:T(8,128)(2,1)S(1)}, bf16[12,64,256]{2,1,0:T(8,128)(2,1)}, u32[]{:S(2)}) copy-start(bf16[12,64,256]{2,1,0:T(8,128)(2,1)} %images.1) | copy-start | bytes 1179652
  0.0 5.6 %copy-start.7 = (bf16[192,256]{1,0:T(8,128)(2,1)S(1)}, bf16[192,256]{1,0:T(8,128)(2,1)}, u32[]{:S(2)}) copy-start(bf16[192,256]{1,0:T(8,128)(2,1)} %constant.16.clone.expand_hbm.expand) | copy-start | bytes 294916
  0.0 5.6 %copy-start.8 = (f32[64,256]{1,0:T(8,128)S(1)}, f32[64,256]{1,0:T(8,128)}, u32[]{:S(2)}) copy-start(f32[64,256]{1,0:T(8,128)} %height.1) | copy-start | bytes 196612
  0.0 5.6 %copy-start.9 = (f32[64,256]{1,0:T(8,128)S(1)}, f32[64,256]{1,0:T(8,128)}, u32[]{:S(2)}) copy-start(f32[64,256]{1,0:T(8,128)} %albedo.1) | copy-start | bytes 196612
  0.0 5.6 %copy-start.10 = (s32[64,256]{1,0:T(8,128)S(1)}, s32[64,256]{1,0:T(8,128)}, u32[]{:S(2)}) copy-start(s32[64,256]{1,0:T(8,128)} %owner.1) | copy-start | bytes 196612
  0.1 5.6 %copy-start.11 = (f32[16,64]{1,0:T(8,128)S(1)}, f32[16,64]{1,0:T(8,128)}, u32[]{:S(2)}) copy-start(f32[16,64]{1,0:T(8,128)} %altimetry.1) | copy-start | bytes 12292
  2.2 3.4 %copy-start.12 = (s32[12,1,1]{0,2,1:T(1,128)S(1)}, s32[12,1,1]{0,2,1:T(1,128)}, u32[]{:S(2)}) copy-start(s32[12,1,1]{0,2,1:T(1,128)} %param.18) | copy-start | bytes 148
  2.3 5.6 %collective-permute-start = (f32[27,2,32,128]{3,2,1,0:T(8,128)}, f32[27,2,32,128]{3,2,1,0:T(8,128)S(1)}, u32[]{:S(2)}, u32[]{:S(2)}) collective-permute-start(f32[27,2,32,128]{3,2,1,0:T(8,128)} %shard_map.136), channel_id=1, source_target_pairs={{0,1},{1,0},{2,3},{3,2},{4,5},{5,4},{6,7},{7,6},{8,9},{9,8},{10,11... | collective-permute-start | bytes 2654216 | tf_op jit(solution)/shard_map/ppermute | solution.py:500
  7.9 15.6 %collective-permute-start.1 = (f32[27,32,128]{2,1,0:T(8,128)S(1)}, f32[27,32,128]{2,1,0:T(8,128)S(1)}, u32[]{:S(2)}, u32[]{:S(2)}) collective-permute-start(f32[27,32,128]{2,1,0:T(8,128)S(1)} %shard_map.138.near), channel_id=1, source_target_pairs={{0,2},{1,3},{2,0},{3,1},{4,6},{5,7},{6,4},{7,5},{8,10},{9,11},{10,... | collective-permute-start | bytes 1327112 | tf_op jit(solution)/shard_map/ppermute | solution.py:503
  9.8 24.0 %all-to-all-start = ((f32[128,1,128]{2,1,0:T(1,128)}), f32[128,1,128]{2,1,0:T(1,128)S(1)}, u32[]{:S(2)}, u32[]{:S(2)}) async-start(f32[128,1,128]{2,1,0:T(1,128)} %shard_map.139), calls=%async_computation | async-start | bytes 131072 | tf_op jit(solution)/shard_map/all_to_all | solution.py:506
  23.4 7.1 %copy-start.2 = (bf16[256,128]{1,0:T(8,128)(2,1)S(1)}, bf16[256,128]{1,0:T(8,128)(2,1)}, u32[]{:S(2)}) copy-start(bf16[256,128]{1,0:T(8,128)(2,1)} %constant.20.clone.refs_3_) | copy-start | bytes 196612
  23.4 7.1 %copy-start.3 = (bf16[256,128]{1,0:T(8,128)(2,1)S(1)}, bf16[256,128]{1,0:T(8,128)(2,1)}, u32[]{:S(2)}) copy-start(bf16[256,128]{1,0:T(8,128)(2,1)} %constant.19.clone.refs_2_) | copy-start | bytes 196612
  23.4 7.0 %copy-start.4 = (bf16[128,192]{1,0:T(8,128)(2,1)S(1)}, bf16[128,192]{1,0:T(8,128)(2,1)}, u32[]{:S(2)}) copy-start(bf16[128,192]{1,0:T(8,128)(2,1)} %constant.17.clone.refs_0_) | copy-start | bytes 147460
  23.5 7.0 %copy-start.5 = (bf16[128,128]{1,0:T(8,128)(2,1)S(1)}, bf16[128,128]{1,0:T(8,128)(2,1)}, u32[]{:S(2)}) copy-start(bf16[128,128]{1,0:T(8,128)(2,1)} %constant.21.clone.refs_4_) | copy-start | bytes 98308
  23.5 7.0 %copy-start.6 = (bf16[64,256]{1,0:T(8,128)(2,1)S(1)}, bf16[64,256]{1,0:T(8,128)(2,1)}, u32[]{:S(2)}) copy-start(bf16[64,256]{1,0:T(8,128)(2,1)} %constant.18.clone.refs_1_) | copy-start | bytes 98308
  23.5 6.1 %collective-permute-start.2 = (f32[5,32,128]{2,1,0:T(8,128)S(1)}, f32[5,32,128]{2,1,0:T(8,128)S(1)}, u32[]{:S(2)}, u32[]{:S(2)}) collective-permute-start(f32[5,32,128]{2,1,0:T(8,128)S(1)} %get-tuple-element.29), channel_id=1, source_target_pairs={{0,253},{1,4},{2,255},{3,6},{4,1},{5,8},{6,3},{7,10},{8,5},{9,12},... | collective-permute-start | bytes 245768 | tf_op jit(solution)/shard_map/ppermute | solution.py:469
  25.3 5.2 %collective-permute-start.3 = (f32[5,32,128]{2,1,0:T(8,128)S(1)}, f32[5,32,128]{2,1,0:T(8,128)S(1)}, u32[]{:S(2)}, u32[]{:S(2)}) collective-permute-start(f32[5,32,128]{2,1,0:T(8,128)S(1)} %get-tuple-element.30), channel_id=1, source_target_pairs={{0,1},{1,0},{2,3},{3,2},{4,5},{5,4},{6,7},{7,6},{8,9},{9,8},{10,11... | collective-permute-start | bytes 245768 | tf_op jit(solution)/shard_map/ppermute | solution.py:469
  35.7 4.5 %collective-permute-start.4 = (f32[5,32,128]{2,1,0:T(8,128)S(1)}, f32[5,32,128]{2,1,0:T(8,128)S(1)}, u32[]{:S(2)}, u32[]{:S(2)}) collective-permute-start(f32[5,32,128]{2,1,0:T(8,128)S(1)} %get-tuple-element.38), channel_id=1, source_target_pairs={{0,253},{1,4},{2,255},{3,6},{4,1},{5,8},{6,3},{7,10},{8,5},{9,12},... | collective-permute-start | bytes 245768 | tf_op jit(solution)/shard_map/ppermute | solution.py:469
  38.1 3.0 %collective-permute-start.5 = (f32[5,32,128]{2,1,0:T(8,128)S(1)}, f32[5,32,128]{2,1,0:T(8,128)S(1)}, u32[]{:S(2)}, u32[]{:S(2)}) collective-permute-start(f32[5,32,128]{2,1,0:T(8,128)S(1)} %get-tuple-element.39), channel_id=1, source_target_pairs={{0,1},{1,0},{2,3},{3,2},{4,5},{5,4},{6,7},{7,6},{8,9},{9,8},{10,11... | collective-permute-start | bytes 245768 | tf_op jit(solution)/shard_map/ppermute | solution.py:469
  43.2 7.3 %collective-permute-start.6 = (f32[5,32,128]{2,1,0:T(8,128)S(1)}, f32[5,32,128]{2,1,0:T(8,128)S(1)}, u32[]{:S(2)}, u32[]{:S(2)}) collective-permute-start(f32[5,32,128]{2,1,0:T(8,128)S(1)} %get-tuple-element.42), channel_id=1, source_target_pairs={{0,253},{1,4},{2,255},{3,6},{4,1},{5,8},{6,3},{7,10},{8,5},{9,12},... | collective-permute-start | bytes 245768 | tf_op jit(solution)/shard_map/ppermute | solution.py:469
  44.2 7.2 %collective-permute-start.7 = (f32[5,32,128]{2,1,0:T(8,128)S(1)}, f32[5,32,128]{2,1,0:T(8,128)S(1)}, u32[]{:S(2)}, u32[]{:S(2)}) collective-permute-start(f32[5,32,128]{2,1,0:T(8,128)S(1)} %get-tuple-element.43), channel_id=1, source_target_pairs={{0,1},{1,0},{2,3},{3,2},{4,5},{5,4},{6,7},{7,6},{8,9},{9,8},{10,11... | collective-permute-start | bytes 245768 | tf_op jit(solution)/shard_map/ppermute | solution.py:469
  53.6 7.3 %collective-permute-start.9 = (f32[4,24,128]{2,1,0:T(8,128)S(1)}, f32[4,24,128]{2,1,0:T(8,128)S(1)}, u32[]{:S(2)}, u32[]{:S(2)}) collective-permute-start(f32[4,24,128]{2,1,0:T(8,128)S(1)} %get-tuple-element.46), channel_id=1, source_target_pairs={{0,253},{1,4},{2,255},{3,6},{4,1},{5,8},{6,3},{7,10},{8,5},{9,12},... | collective-permute-start | bytes 147464 | tf_op jit(solution)/shard_map/ppermute | solution.py:469
  53.7 12.5 %collective-permute-start.8 = (f32[2,48,128]{2,1,0:T(8,128)S(1)}, f32[2,48,128]{2,1,0:T(8,128)S(1)}, u32[]{:S(2)}, u32[]{:S(2)}) collective-permute-start(f32[2,48,128]{2,1,0:T(8,128)S(1)} %get-tuple-element.45), channel_id=1, source_target_pairs={{0,1},{1,0},{2,3},{3,2},{4,5},{5,4},{6,7},{7,6},{8,9},{9,8},{10,11... | collective-permute-start | bytes 147464 | tf_op jit(solution)/shard_map/ppermute | solution.py:469
  60.8 6.2 %collective-permute-start.10 = (f32[2,16,128]{2,1,0:T(8,128)S(1)}, f32[2,16,128]{2,1,0:T(8,128)S(1)}, u32[]{:S(2)}, u32[]{:S(2)}) collective-permute-start(f32[2,16,128]{2,1,0:T(8,128)S(1)} %shard_map.145), channel_id=1, source_target_pairs={{0,1},{1,0},{2,3},{3,2},{4,5},{5,4},{6,7},{7,6},{8,9},{9,8},{10,11... | collective-permute-start | bytes 49160 | tf_op jit(solution)/shard_map/ppermute | solution.py:546
